TPU v7x, 32 devices: a whole 2x2x4 slice. The times are simulated.
32 devices in a mesh: groups: 2 (over x), ep: 8 (over z, y), sub: 2 (over core).
Axes of the slice: x: 2, y: 2, z: 4, core: 2. Of those that a mesh axis runs over, the one named last changes fastest.
Arguments:
- queries: bfloat16 [256, 2, 128, 576], P(('groups', 'ep', 'sub')), parts along dimension 0, may hold values from -400 to 400
- latent_cache: bfloat16 [256, 256, 576], P(('groups', 'ep', 'sub')), parts along dimension 0, may hold values from -6 to 6
- new_latent: bfloat16 [256, 2, 576], P(('groups', 'ep', 'sub')), parts along dimension 0, may hold values from -8 to 8
- lengths: int32 [256], P(('groups', 'ep', 'sub')), parts along dimension 0, may hold values from 2 to 256, as said below
- moe_input: bfloat16 [512, 3584], P(('groups', 'ep', 'sub')), parts along dimension 0, may hold values from -6 to 6
- gate_scores: float32 [512, 8], P(('groups', 'ep', 'sub')), parts along dimension 0, may hold values from -6 to 6
- expert_ids: int32 [512, 8], P(('groups', 'ep', 'sub')), parts along dimension 0, may hold values from 0 to 13, as said below
- placement: int32 [28, 2], P('groups'), parts along dimension 0, may hold values from 0 to 15, as said below
- w_gate: bfloat16 [32, 3584, 1024], P(('groups', 'ep'), None, 'sub'), parts along dimension 0, as said below
- w_up: bfloat16 [32, 3584, 1024], P(('groups', 'ep'), None, 'sub'), parts along dimension 0, as said below
- w_down: bfloat16 [32, 1024, 3584], P(('groups', 'ep'), 'sub'), parts along dimension 0, as said below
Outputs:
- attn_latent: bfloat16 [256, 2, 128, 512], P(('groups', 'ep', 'sub')), parts along dimension 0
- moe_output: bfloat16 [512, 3584], P(('groups', 'ep', 'sub')), parts along dimension 0
There are 2 independent parts, one for each index of `groups`. A program takes and returns all parts, laid end to end along the dimension named above; each array names one. Nothing has to cross between parts.
Inputs may be any that keep to these rules, and one draw needn't show every extreme that they name: `lengths`: all 8 requests of some device have length 256. `expert_ids`: each row names 8 different experts. One expert, which has a single replica in placement, is named by every row. `placement`: column 0 puts the 14 experts on distinct slots; column 1 equals column 0 except for 2 experts, whose second replicas take the remaining 2 slots. `w_gate`: the slot of an expert's second replica holds the same matrix as its first. `w_up`: the slot of an expert's second replica holds the same matrix as its first. `w_down`: the slot of an expert's second replica holds the same matrix as its first.
All inputs are finite; a program needn't handle non-finite values.
Results may differ from a plain program's by a relative error of at most 0.0064.
Values may be sent and summed in bfloat16 or wider, within the bound.
No kernel may reach another device: no remote copies, remote signals or barrier semaphores. Data moves between devices by JAX's collectives and lax.ppermute only.
A program may use at most 128 MiB of HBM per device.

v0:
```python
import jax
import jax.numpy as jnp
from jax import lax
from jax.sharding import PartitionSpec as P

LATENT_RANK = 512


score_scale = 192.0 ** (-0.5)
route_scale = 2.5


def attend_block(packed):
    query_rows, cached_latent_rows, incoming_rows, length_value = packed
    blocks, steps, heads, latent = query_rows.shape
    flattened_query = query_rows.reshape(blocks, steps * heads, latent)
    older = (
        jnp.einsum(
            "raw,rzw->raz", flattened_query, cached_latent_rows, preferred_element_type=jnp.float32
        )
        * score_scale
    )
    newer = (
        jnp.einsum(
            "raw,rzw->raz", flattened_query, incoming_rows, preferred_element_type=jnp.float32
        )
        * score_scale
    )
    positions = jnp.arange(cached_latent_rows.shape[1], dtype=jnp.int32)
    older = jnp.where(positions[None, None, :] < length_value[:, None, None], older, -jnp.inf)
    row_step = jnp.arange(steps * heads, dtype=jnp.int32) // heads
    newer = jnp.where(
        jnp.arange(steps, dtype=jnp.int32)[None, None, :] <= row_step[None, :, None],
        newer,
        -jnp.inf,
    )
    highest = jnp.maximum(jnp.max(older, axis=2), jnp.max(newer, axis=2))[:, :, None]
    older_exp = jnp.exp(older - highest)
    newer_exp = jnp.exp(newer - highest)
    totals = (jnp.sum(older_exp, axis=2) + jnp.sum(newer_exp, axis=2))[:, :, None]
    older_probability = (older_exp / totals).astype(jnp.bfloat16)
    newer_probability = (newer_exp / totals).astype(jnp.bfloat16)
    blended = jnp.einsum(
        "vhs,vsn->vhn",
        older_probability,
        cached_latent_rows[:, :, :LATENT_RANK],
        preferred_element_type=jnp.float32,
    )
    blended = blended + jnp.einsum(
        "vhs,vsn->vhn",
        newer_probability,
        incoming_rows[:, :, :LATENT_RANK],
        preferred_element_type=jnp.float32,
    )
    return blended.reshape(blocks, steps, heads, LATENT_RANK).astype(jnp.bfloat16)


def apply_experts(token_rows, token_weights, w_gate, w_up, w_down):
    width = token_rows.shape[-1]
    leading = token_rows.shape[:-1]
    flat_rows = token_rows.reshape(-1, width)
    flat_weights = token_weights.reshape(-1, token_weights.shape[-1]).astype(jnp.float32)
    summed = jnp.zeros(flat_rows.shape, jnp.float32)
    for local_slot in range(w_gate.shape[0]):
        gate_values = jnp.dot(flat_rows, w_gate[local_slot], preferred_element_type=jnp.float32)
        upward = jnp.dot(flat_rows, w_up[local_slot], preferred_element_type=jnp.float32)
        active = (jax.nn.silu(gate_values) * upward).astype(jnp.bfloat16)
        produced = jnp.dot(active, w_down[local_slot], preferred_element_type=jnp.float32)
        summed = summed + flat_weights[:, local_slot : local_slot + 1] * produced
    return summed.reshape(leading + (width,))


def on_device(
    queries,
    latent_cache,
    new_latent,
    lengths,
    moe_input,
    gate_scores,
    expert_ids,
    placement,
    w_gate,
    w_up,
    w_down,
):
    request_count = queries.shape[0]
    paired = (
        queries.reshape((request_count // 2, 2) + queries.shape[1:]),
        latent_cache.reshape((request_count // 2, 2) + latent_cache.shape[1:]),
        new_latent.reshape((request_count // 2, 2) + new_latent.shape[1:]),
        lengths.reshape(request_count // 2, 2),
    )
    attended = lax.map(attend_block, paired)
    attn_latent = attended.reshape((request_count,) + attended.shape[2:])
    token_count = moe_input.shape[0]
    width = moe_input.shape[1]
    ep_count = lax.axis_size("ep")
    sub_count = lax.axis_size("sub")
    slot_local = w_gate.shape[0]
    slot_count = slot_local * ep_count
    expert_count = placement.shape[0]
    sigmoid_values = jax.nn.sigmoid(gate_scores)
    weights = (
        route_scale * sigmoid_values / jnp.sum(sigmoid_values, axis=1, keepdims=True)
    ).astype(jnp.bfloat16)
    weights = lax.optimization_barrier(weights)
    expert_match = (
        expert_ids[:, :, None] == jnp.arange(expert_count, dtype=jnp.int32)[None, None, :]
    )
    first_slot = jnp.sum(jnp.where(expert_match, placement[None, None, :, 0], 0), axis=2)
    second_slot = jnp.sum(jnp.where(expert_match, placement[None, None, :, 1], 0), axis=2)
    parity = jnp.arange(token_count, dtype=jnp.int32) % 2
    chosen_slot = jnp.where(parity[:, None] == 0, first_slot, second_slot)
    slot_match = chosen_slot[:, :, None] == jnp.arange(slot_count, dtype=jnp.int32)[None, None, :]
    slot_weight = jnp.sum(
        jnp.where(slot_match, weights.astype(jnp.float32)[:, :, None], 0.0), axis=1
    )
    slot_hit = jnp.any(slot_match, axis=1)
    device_weight = (
        slot_weight.reshape(token_count, ep_count, slot_local)
        .transpose(1, 0, 2)
        .astype(jnp.bfloat16)
    )
    device_hit = jnp.any(slot_hit.reshape(token_count, ep_count, slot_local), axis=2).T
    masked_rows = jnp.where(
        device_hit[:, :, None], moe_input[None, :, :], jnp.zeros((), jnp.bfloat16)
    )
    outgoing_rows = jnp.broadcast_to(
        masked_rows[:, None], (ep_count, sub_count, token_count, width)
    )
    outgoing_weights = jnp.broadcast_to(
        device_weight[:, None], (ep_count, sub_count, token_count, slot_local)
    )
    got_rows = lax.all_to_all(
        outgoing_rows.reshape(ep_count * sub_count, token_count, width),
        ("ep", "sub"),
        split_axis=0,
        concat_axis=0,
        tiled=True,
    )
    got_weights = lax.all_to_all(
        outgoing_weights.reshape(ep_count * sub_count, token_count, slot_local),
        ("ep", "sub"),
        split_axis=0,
        concat_axis=0,
        tiled=True,
    )
    partials = apply_experts(got_rows, got_weights, w_gate, w_up, w_down)
    partials = partials.reshape(ep_count, sub_count, token_count, width)
    halves = lax.psum_scatter(partials, "sub", scatter_dimension=1, tiled=True)
    rounded = halves.astype(jnp.bfloat16)
    returned = lax.all_to_all(rounded, "ep", split_axis=0, concat_axis=0, tiled=True)
    combined = jnp.sum(returned[:, 0].astype(jnp.float32), axis=0)
    return (attn_latent, combined.astype(jnp.bfloat16))


def solution(mesh):
    return jax.shard_map(
        on_device,
        mesh=mesh,
        in_specs=(
            P(("groups", "ep", "sub"), None, None, None),
            P(("groups", "ep", "sub"), None, None),
            P(("groups", "ep", "sub"), None, None),
            P(("groups", "ep", "sub")),
            P(("groups", "ep", "sub"), None),
            P(("groups", "ep", "sub"), None),
            P(("groups", "ep", "sub"), None),
            P("groups", None),
            P(("groups", "ep"), None, "sub"),
            P(("groups", "ep"), None, "sub"),
            P(("groups", "ep"), "sub", None),
        ),
        out_specs=(P(("groups", "ep", "sub"), None, None, None), P(("groups", "ep", "sub"), None)),
        check_vma=False,
    )
```

profile of v0, /device:TPU:0, one launch (start us, length us, event | category | flops | bytes accessed | tf_op | source)
XLA Modules:
  0.0 136.7 jit_solution(12717970227465992892)
XLA Ops:
  4.6 7.4 %all-to-all-start = ((bf16[16,16,2]{1,2,0:T(2,128)(2,1)}), bf16[16,16,2]{1,2,0:T(2,128)(2,1)S(1)}, u32[]{:S(2)}, u32[]{:S(2)}) async-start(bf16[16,16,2]{1,2,0:T(2,128)(2,1)} %bitcast.12), calls=%async_computation | async-start | bytes 16384 | tf_op jit(solution)/shard_map/all_to_all | solution.py:141
  12.2 1.0 broadcast_select_fusion
  13.3 5.1 %all-to-all-done = bf16[16,16,2]{1,2,0:T(2,128)(2,1)S(1)} async-done(((bf16[16,16,2]{1,2,0:T(2,128)(2,1)}), bf16[16,16,2]{1,2,0:T(2,128)(2,1)S(1)}, u32[]{:S(2)}, u32[]{:S(2)}) %all-to-all-start) | async-done | bytes 1056 | tf_op jit(solution)/shard_map/all_to_all | solution.py:141
  18.3 1.4 %broadcast_in_dim.145 = bf16[8,2,16,3584]{3,2,1,0:T(8,128)(2,1)} broadcast(bf16[8,16,3584]{2,1,0:T(8,128)(2,1)S(1)} %broadcast_select_fusion), dimensions={0,2,3} | broadcast | bytes 2752512 | tf_op jit(solution)/shard_map/broadcast_in_dim | solution.py:128
  19.8 4.5 %all-to-all-start.1 = ((bf16[16,16,3584]{2,1,0:T(8,128)(2,1)}), bf16[16,16,3584]{2,1,0:T(8,128)(2,1)}, u32[]{:S(2)}, u32[]{:S(2)}) async-start(bf16[16,16,3584]{2,1,0:T(8,128)(2,1)} %bitcast.15), calls=%async_computation.1 | async-start | bytes 3670016 | tf_op jit(solution)/shard_map/all_to_all | solution.py:134
  24.3 4.1 %copy.48 = bf16[8,2,128,576]{2,1,3,0:T(2,128)(2,1)S(1)} copy(bf16[8,2,128,576]{2,3,1,0:T(8,128)(2,1)} %param.13) | data formatting | bytes 4718592 | tf_op args[0]
  29.2 31.7 %all-to-all-done.1 = bf16[16,16,3584]{2,1,0:T(8,128)(2,1)} async-done(((bf16[16,16,3584]{2,1,0:T(8,128)(2,1)}), bf16[16,16,3584]{2,1,0:T(8,128)(2,1)}, u32[]{:S(2)}, u32[]{:S(2)}) %all-to-all-start.1) | async-done | bytes 1835040 | tf_op jit(solution)/shard_map/all_to_all | solution.py:134
  60.8 3.7 %fusion.22 = f32[256,512]{1,0:T(8,128)S(1)} fusion(bf16[256,3584]{1,0:T(8,128)(2,1)} %bitcast.16, bf16[2,3584,512]{2,1,0:T(8,128)(2,1)} %param.21), kind=kOutput, calls=%fused_computation.42 | convolution fusion | flops 939524096 | bytes 6029312 | tf_op jit(solution)/shard_map/dot_general | solution.py:65
  64.5 3.7 %fusion.17 = f32[256,512]{1,0:T(8,128)S(1)} fusion(bf16[256,3584]{1,0:T(8,128)(2,1)} %bitcast.16, bf16[2,3584,512]{2,1,0:T(8,128)(2,1)} %param.21), kind=kOutput, calls=%fused_computation.37 | convolution fusion | flops 939524096 | bytes 6029312 | tf_op jit(solution)/shard_map/dot_general | solution.py:65
  68.2 7.7 %convolution_multiply_fusion.3 = f32[256,3584]{1,0:T(8,128)} fusion(bf16[2,512,3584]{2,1,0:T(8,128)(2,1)} %param.23, f32[256]{0:T(256)S(1)} %bitcast.96, bf16[256,3584]{1,0:T(8,128)(2,1)} %bitcast.16, bf16[2,3584,512]{2,1,0:T(8,128)(2,1)} %param.22, f32[256,512]{1,0:T(8,128)S(1)} %fusion.22), kind=kOutput, calls=%fused_computation.33 | convolution fusion | flops 1880752128 | bytes 13370368 | tf_op jit(solution)/shard_map/dot_general | solution.py:68
  75.9 8.7 %fusion.13 = f32[256,3584]{1,0:T(8,128)} fusion(f32[256,3584]{1,0:T(8,128)} %convolution_multiply_fusion.3, bf16[2,512,3584]{2,1,0:T(8,128)(2,1)} %param.23, f32[256]{0:T(256)S(1)} %bitcast.95, bf16[256,3584]{1,0:T(8,128)(2,1)} %bitcast.16, bf16[2,3584,512]{2,1,0:T(8,128)(2,1)} %param.22, f32[256,512]{1,0:T(8,128)S(1)} %fusion.17), kind=kOutput, calls=%fused_computation.32 | convolution fusion | flops 1881669632 | bytes 17040384 | tf_op jit(solution)/shard_map/dot_general | solution.py:68
  84.6 14.4 %all-reduce.2 = bf16[8,2,16,3584]{3,2,1,0:T(8,128)(2,1)} all-reduce(f32[8,2,16,3584]{3,2,1,0:T(8,128)} %bitcast.91), channel_id=2, replica_groups=mesh['groups'=2,'ep'=8,'sub'=2] {'sub'}, use_global_device_ids=true, to_apply=%region_12.13.clone | all-reduce | flops 917504 | bytes 5505024
  99.0 2.7 %dynamic-slice_convert_fusion = bf16[8,1,16,3584]{3,2,1,0:T(8,128)(2,1)} fusion(bf16[8,2,16,3584]{3,2,1,0:T(8,128)(2,1)} %all-reduce.2, u32[]{:T(128)} %bitcast.28), kind=kLoop, calls=%fused_computation.50 | loop fusion | bytes 1835012 | tf_op jit(solution)/shard_map/convert_element_type | solution.py:151
  101.7 9.6 %all-to-all-start.2 = ((bf16[8,1,16,3584]{3,2,1,0:T(8,128)(2,1)}), bf16[8,1,16,3584]{3,2,1,0:T(8,128)(2,1)}, u32[]{:S(2)}, u32[]{:S(2)}) async-start(bf16[8,1,16,3584]{3,2,1,0:T(8,128)(2,1)} %dynamic-slice_convert_fusion), calls=%async_computation.2 | async-start | bytes 1835008 | tf_op jit(solution)/shard_map/all_to_all | solution.py:152
  111.2 20.2 %while.12 = (s32[]{:T(128)}, bf16[4,2,2,128,512]{4,3,2,1,0:T(8,128)(2,1)}, s32[4,2]{1,0:T(4,128)S(1)}, bf16[4,2,2,128,576]{3,2,4,1,0:T(2,128)(2,1)S(1)}, bf16[4,...) while((s32[]{:T(128)}, bf16[4,2,2,128,512]{4,3,2,1,0:T(8,128)(2,1)}, ...), condition=%wide.region_5.6_spmd, body=%wide.region_0.5_spmd.sunk | while | flops 289024000 | bytes 11143285 | solution.py:93
  112.0 1.1 dynamic-slice_bitcast_fusion.4
  115.5 0.8 constant_dynamic-update-slice_fusion.2
  117.1 1.1 dynamic-slice_bitcast_fusion.4
  120.5 0.8 constant_dynamic-update-slice_fusion.2
  122.2 1.1 dynamic-slice_bitcast_fusion.4
  125.6 0.8 constant_dynamic-update-slice_fusion.2
  127.2 1.1 dynamic-slice_bitcast_fusion.4
  131.5 3.2 %all-to-all-done.2 = bf16[8,1,16,3584]{3,2,1,0:T(8,128)(2,1)} async-done(((bf16[8,1,16,3584]{3,2,1,0:T(8,128)(2,1)}), bf16[8,1,16,3584]{3,2,1,0:T(8,128)(2,1)}, u32[]{:S(2)}, u32[]{:S(2)}) %all-to-all-start.2) | async-done | bytes 917536 | tf_op jit(solution)/shard_map/all_to_all | solution.py:152
  134.7 2.0 %reduce_sum.76 = bf16[16,3584]{1,0:T(8,128)(2,1)} reduce(bf16[8,1,16,3584]{3,2,1,0:T(8,128)(2,1)} %all-to-all-done.2, bf16[]{:T(256)} %constant.91.clone.1), dimensions={0,1}, to_apply=%region_13.14 | reduce | flops 401408 | bytes 1032194 | tf_op jit(solution)/shard_map/reduce_sum | solution.py:153
  (86 shorter events, 18.0 us)
Async XLA Ops:
  4.6 13.7 %all-to-all-start = ((bf16[16,16,2]{1,2,0:T(2,128)(2,1)}), bf16[16,16,2]{1,2,0:T(2,128)(2,1)S(1)}, u32[]{:S(2)}, u32[]{:S(2)}) async-start(bf16[16,16,2]{1,2,0:T(2,128)(2,1)} %bitcast.12), calls=%async_computation | async-start | bytes 16384 | tf_op jit(solution)/shard_map/all_to_all | solution.py:141
  19.8 8.7 %copy-start = (s32[8]{0:T(128)S(1)}, s32[8]{0:T(128)}, u32[]{:S(2)}) copy-start(s32[8]{0:T(128)} %param.16) | copy-start | bytes 100
  19.8 8.8 %copy-start.1 = (u32[32]{0:T(128)S(1)}, u32[32]{0:T(128)}, u32[]{:S(2)}) copy-start(u32[32]{0:T(128)} %constant.110) | copy-start | bytes 388
  19.8 41.1 %all-to-all-start.1 = ((bf16[16,16,3584]{2,1,0:T(8,128)(2,1)}), bf16[16,16,3584]{2,1,0:T(8,128)(2,1)}, u32[]{:S(2)}, u32[]{:S(2)}) async-start(bf16[16,16,3584]{2,1,0:T(8,128)(2,1)} %bitcast.15), calls=%async_computation.1 | async-start | bytes 3670016 | tf_op jit(solution)/shard_map/all_to_all | solution.py:134
  101.7 33.0 %all-to-all-start.2 = ((bf16[8,1,16,3584]{3,2,1,0:T(8,128)(2,1)}), bf16[8,1,16,3584]{3,2,1,0:T(8,128)(2,1)}, u32[]{:S(2)}, u32[]{:S(2)}) async-start(bf16[8,1,16,3584]{3,2,1,0:T(8,128)(2,1)} %dynamic-slice_convert_fusion), calls=%async_computation.2 | async-start | bytes 1835008 | tf_op jit(solution)/shard_map/all_to_all | solution.py:152
where the time goes:
time: 138 us; the launch traced here: 137 us
  waiting for transfers between devices  40 us (29%)
  matrix products  29.1 us (21%)
  local copies, waits for them, and re-layouts  24.4 us (18%)
  starting transfers between devices  21.5 us (16%)
  blocking collectives  14.4 us (10%)
  other arithmetic  6.33 us (5%)
    all_to_all x1, waiting for transfers between devices, on_device(): lax.all_to_all(outgoing_rows.reshape(ep_count * sub_count, token_count, w...  31.7 us
    dot_general x2, matrix products, apply_experts(): jnp.dot(active, w_down[local_slot], preferred_element_type=jnp.float32)  16.3 us
    unnamed x1, blocking collectives  14.4 us
    all_to_all x1, starting transfers between devices, on_device(): lax.all_to_all(rounded, 'ep', split_axis=0, concat_axis=0, tiled=True)  9.56 us
    dot_general x2, matrix products, apply_experts(): jnp.dot(flat_rows, w_gate[local_slot], preferred_element_type=jnp.float32)  7.39 us
    all_to_all x1, starting transfers between devices, on_device(): lax.all_to_all(outgoing_weights.reshape(ep_count * sub_count, token_count...  7.39 us
    squeeze x8, local copies, waits for them, and re-layouts, on_device(): attended = lax.map(attend_block, paired)  7.24 us
    all_to_all x1, waiting for transfers between devices, on_device(): lax.all_to_all(outgoing_weights.reshape(ep_count * sub_count, token_count...  5.06 us
  transfers between devices with their start and end apart: 3, of which 3 were waited for; matrix products, arithmetic and copies ran while one was open for 19% of the time, Pallas kernels for 0%

commit v1 on v0

v1 whole, which is shorter than its diff:
```python
import functools

import jax
import jax.numpy as jnp
from jax import lax
from jax.experimental import pallas as pl
from jax.experimental.pallas import tpu as pltpu
from jax.sharding import PartitionSpec as P

LATENT_RANK = 512
SCORE_SCALE = 192.0 ** (-0.5)
ROUTE_SCALE = 2.5
LANES = 128
F32 = jnp.float32
BF16 = jnp.bfloat16


def contract(a, b, dim_a, dim_b):
    return lax.dot_general(
        a, b, (((dim_a,), (dim_b,)), ((), ())), preferred_element_type=F32
    )


def attention_kernel(length_ref, query_ref, cache_ref, new_ref, *rest, first, block):
    out_ref = rest[-1]
    steps, heads = query_ref.shape[1], query_ref.shape[3]
    for b in range(block):
        length = length_ref[first + pl.program_id(0) * block + b]
        q = jnp.concatenate([query_ref[b, s].T for s in range(steps)], axis=0)
        cached = cache_ref[b]
        fresh = new_ref[b]
        older = contract(q, cached, 1, 0) * SCORE_SCALE
        newer = contract(q, fresh, 1, 1) * SCORE_SCALE
        position = lax.broadcasted_iota(jnp.int32, older.shape, 1)
        older = jnp.where(position < length, older, -jnp.inf)
        row = lax.broadcasted_iota(jnp.int32, newer.shape, 0)
        step = lax.broadcasted_iota(jnp.int32, newer.shape, 1)
        newer = jnp.where(step * heads <= row, newer, -jnp.inf)
        highest = jnp.maximum(
            jnp.max(older, axis=1, keepdims=True), jnp.max(newer, axis=1, keepdims=True)
        )
        older = jnp.exp(older - highest)
        newer = jnp.exp(newer - highest)
        total = jnp.sum(older, axis=1, keepdims=True) + jnp.sum(newer, axis=1, keepdims=True)
        blended = contract((older / total).astype(BF16), cached[:LATENT_RANK], 1, 1)
        blended = blended + contract((newer / total).astype(BF16), fresh[:, :LATENT_RANK], 1, 0)
        out_ref[b] = blended.reshape(steps, heads, LATENT_RANK).astype(BF16)


def attention(lengths, queries, cache, fresh, first, count, block, previous):
    requests, steps, latent, heads = queries.shape
    context = cache.shape[2]
    skip = first // block
    in_specs = [
        pl.BlockSpec((block, steps, latent, heads), lambda i, _: (i + skip, 0, 0, 0)),
        pl.BlockSpec((block, latent, context), lambda i, _: (i + skip, 0, 0)),
        pl.BlockSpec((block, steps, latent), lambda i, _: (i + skip, 0, 0)),
    ]
    operands = [queries, cache, fresh]
    aliases = {}
    if previous is not None:
        in_specs.append(pl.BlockSpec(memory_space=pl.ANY))
        operands.append(previous)
        aliases = {4: 0}
    rows = count * steps * heads
    return pl.pallas_call(
        functools.partial(attention_kernel, first=first, block=block),
        grid_spec=pltpu.PrefetchScalarGridSpec(
            num_scalar_prefetch=1,
            grid=(count // block,),
            in_specs=in_specs,
            out_specs=pl.BlockSpec(
                (block, steps, heads, LATENT_RANK), lambda i, _: (i + skip, 0, 0, 0)
            ),
        ),
        out_shape=jax.ShapeDtypeStruct((requests, steps, heads, LATENT_RANK), BF16),
        input_output_aliases=aliases,
        compiler_params=pltpu.CompilerParams(vmem_limit_bytes=14 << 20),
        cost_estimate=pl.CostEstimate(
            flops=rows * context * (latent + LATENT_RANK) * 2,
            bytes_accessed=count * (2 * steps * heads + context) * latent * 2,
            transcendentals=rows * context,
        ),
        name="attention",
    )(lengths, *operands)


def route_kernel(place_ref, rows_ref, score_ref, expert_ref, out_ref, *, experts, slots):
    tokens, width = rows_ref.shape
    sigmoid = jax.nn.sigmoid(score_ref[...])
    weights = ROUTE_SCALE * sigmoid / jnp.sum(sigmoid, axis=0, keepdims=True)
    weights = weights.astype(BF16).astype(F32)
    named = expert_ref[...]
    even = lax.broadcasted_iota(jnp.int32, named.shape, 1) % 2 == 0
    slot = jnp.zeros_like(named)
    for e in range(experts):
        slot = jnp.where(
            named == e, jnp.where(even, place_ref[0, e], place_ref[1, e]), slot
        )
    index = lax.broadcasted_iota(jnp.int32, (LANES, tokens), 0)
    table = jnp.zeros((LANES, tokens), F32)
    for k in range(named.shape[0]):
        table = table + jnp.where(index == slot[k : k + 1], weights[k : k + 1], 0.0)
    row = lax.broadcasted_iota(jnp.int32, (tokens, tokens), 0)
    column = lax.broadcasted_iota(jnp.int32, (tokens, tokens), 1)
    unit = jnp.where(row == column, 1.0, 0.0).astype(BF16)
    out_ref[:, :width] = rows_ref[...]
    out_ref[:, width:] = contract(unit, table.astype(BF16), 1, 1).astype(BF16)


def route(placement, rows, scores, expert_ids, slots):
    tokens, width = rows.shape
    vmem = pl.BlockSpec(memory_space=pltpu.VMEM)
    return pl.pallas_call(
        functools.partial(route_kernel, experts=placement.shape[0], slots=slots),
        in_specs=[pl.BlockSpec(memory_space=pltpu.SMEM), vmem, vmem, vmem],
        out_specs=vmem,
        out_shape=jax.ShapeDtypeStruct((tokens, width + LANES), BF16),
        compiler_params=pltpu.CompilerParams(vmem_limit_bytes=4 << 20),
        name="route",
    )(placement.T, rows, scores.T, expert_ids.T)


def experts_kernel(*refs, parts, tile):
    rows_refs = refs[:parts]
    gate_ref, up_ref, down_ref, chip_ref = refs[parts : parts + 4]
    out_refs = refs[parts + 4 : 2 * parts + 4]
    rows_s, act_s = refs[-2:]
    slots, width, hidden = gate_ref.shape
    start = 0
    for ref in rows_refs:
        rows_s[start : start + ref.shape[0], :] = ref[...]
        start += ref.shape[0]
    table = rows_s[:, width:].astype(F32)
    lane = lax.broadcasted_iota(jnp.int32, table.shape, 1)
    for s in range(slots):
        slot = chip_ref[0] * slots + s
        weight = jnp.sum(jnp.where(lane == slot, table, 0.0), axis=1, keepdims=True)
        rows = rows_s[:, :width]
        gate = jnp.dot(rows, gate_ref[s], preferred_element_type=F32)
        up = jnp.dot(rows, up_ref[s], preferred_element_type=F32)
        act = gate / (1.0 + jnp.exp(-gate)) * up
        act_s[:, s * hidden : (s + 1) * hidden] = (weight * act).astype(BF16)

    def project(i, carry):
        columns = pl.ds(pl.multiple_of(i * tile, tile), tile)
        total = jnp.dot(act_s[:, :hidden], down_ref[0, :, columns], preferred_element_type=F32)
        for s in range(1, slots):
            total = total + jnp.dot(
                act_s[:, s * hidden : (s + 1) * hidden],
                down_ref[s, :, columns],
                preferred_element_type=F32,
            )
        total = total.astype(BF16)
        start = 0
        for ref in out_refs:
            ref[:, columns] = total[start : start + ref.shape[0]]
            start += ref.shape[0]
        return carry

    lax.fori_loop(0, width // tile, project, 0)


def experts(parts, gate, up, down, chip):
    slots, width, hidden = gate.shape
    count = sum(p.shape[0] for p in parts)
    vmem = pl.BlockSpec(memory_space=pltpu.VMEM)
    return pl.pallas_call(
        functools.partial(experts_kernel, parts=len(parts), tile=512),
        in_specs=[vmem] * (len(parts) + 3) + [pl.BlockSpec(memory_space=pltpu.SMEM)],
        out_specs=[vmem] * len(parts),
        out_shape=[jax.ShapeDtypeStruct((p.shape[0], width), BF16) for p in parts],
        scratch_shapes=[
            pltpu.VMEM((count, parts[0].shape[1]), BF16),
            pltpu.VMEM((count, slots * hidden), BF16),
        ],
        compiler_params=pltpu.CompilerParams(vmem_limit_bytes=16 << 20),
        cost_estimate=pl.CostEstimate(
            flops=count * slots * 3 * width * hidden * 2,
            bytes_accessed=count * width * 4,
            transcendentals=count * slots * hidden,
        ),
        name="experts",
    )(*parts, gate, up, down, chip)


def halving_masks(ep):
    bits = []
    bit = ep // 2
    while bit:
        bits.append(bit)
        bit //= 2
    other = bits[:-2] + bits[-2:][::-1]
    return bits, other


def hop(x, ep, sub, masks, turn):
    pairs = [
        (e * sub + s, (e ^ masks[s % 2][turn]) * sub + s) for e in range(ep) for s in range(sub)
    ]
    return lax.ppermute(x, ("ep", "sub"), pairs)


def swap(x):
    return lax.ppermute(x, "sub", [(0, 1), (1, 0)])


def add(*terms):
    total = terms[0].astype(F32)
    for t in terms[1:]:
        total = total + t.astype(F32)
    return total.astype(BF16)


def on_device(
    queries,
    latent_cache,
    new_latent,
    lengths,
    moe_input,
    gate_scores,
    expert_ids,
    placement,
    w_gate,
    w_up,
    w_down,
):
    ep, sub = lax.axis_size("ep"), lax.axis_size("sub")
    masks = halving_masks(ep)
    turns = len(masks[0])
    tokens = moe_input.shape[0]
    requests = queries.shape[0]
    queries_t = queries.transpose(0, 1, 3, 2)
    cache_t = latent_cache.transpose(0, 2, 1)
    weights = [pltpu.with_memory_space_constraint(w, pltpu.VMEM) for w in (w_gate, w_up, w_down)]
    chip = lax.axis_index("ep").astype(jnp.int32)[None]
    slots = ep * w_gate.shape[0]

    part = requests // 4
    state = {"out": None, "next": 0}

    def attend(parts):
        for _ in range(parts):
            state["out"] = attention(
                lengths, queries_t, cache_t, new_latent, state["next"], part, 1, state["out"]
            )
            state["next"] += part

    rows = route(placement, moe_input, gate_scores, expert_ids, slots)
    for turn in range(turns - 1):
        got = hop(rows, ep, sub, masks, turn)
        if turn == 0:
            attend(2)
            got, state["out"] = lax.optimization_barrier((got, state["out"]))
        rows = jnp.concatenate([rows, got], axis=0)

    far = hop(rows, ep, sub, masks, turns - 1)
    near_own, near_other = experts([rows, swap(rows)], *weights, chip)
    near_back = swap(near_other)
    near = add(near_own, near_back)
    far, near = lax.optimization_barrier((far, near))

    far_own, far_other = experts([far, swap(far)], *weights, chip)
    far_sum = add(far_own, swap(far_other))

    total = near
    sent = far_sum
    for turn in range(turns - 1, -1, -1):
        got = hop(sent, ep, sub, masks, turn)
        if turn == turns - 1 or turn == 0:
            attend(1)
            got, state["out"] = lax.optimization_barrier((got, state["out"]))
        half = total.shape[0] // 2
        if turn:
            sent = add(total[half:], got[half:])
            total = add(total[:half], got[:half])
        else:
            total = add(total, got)
    return state["out"], total


def solution(mesh):
    split = ("groups", "ep", "sub")
    return jax.shard_map(
        on_device,
        mesh=mesh,
        in_specs=(
            P(split, None, None, None),
            P(split, None, None),
            P(split, None, None),
            P(split),
            P(split, None),
            P(split, None),
            P(split, None),
            P("groups", None),
            P(("groups", "ep"), None, "sub"),
            P(("groups", "ep"), None, "sub"),
            P(("groups", "ep"), "sub", None),
        ),
        out_specs=(P(split, None, None, None), P(split, None)),
        check_vma=False,
    )
```

time: 138 us -> 83.3 us (0.60)
  matrix products: 29.1 us -> 0 us
  Pallas kernels: 0 us -> 22.6 us
  blocking collectives: 14.4 us -> 0 us
  starting transfers between devices: 21.5 us -> 10.9 us
  waiting for transfers between devices: 40 us -> 29.8 us
  local copies, waits for them, and re-layouts: 24.4 us -> 16.9 us
  other arithmetic: 6.33 us -> 1.89 us
    all_to_all x3 -> x0, waiting for transfers between devices: 40 us -> none  [the longest x1 31.7 us: on_device(): lax.all_to_all(outgoing_rows.reshape(ep_count * sub_count, token_count, w...]
    ppermute x0 -> x10, waiting for transfers between devices: none -> 29.8 us  [the longest x6 23.9 us: hop(): return lax.ppermute(x, ('ep', 'sub'), pairs)]
    dot_general x20 -> x0, matrix products: 29.1 us -> none  [the longest x2 16.3 us: apply_experts(): jnp.dot(active, w_down[local_slot], preferred_element_type=jnp.float32)]
    pallas_call x0 -> x7, Pallas kernels: none -> 22.6 us  [the longest x4 11.9 us: attention(): pl.pallas_call(functools.partial(attention_kernel, first=first, block=blo...]
    all_to_all x3 -> x0, starting transfers between devices: 21.5 us -> none  [the longest x1 9.56 us: on_device(): lax.all_to_all(rounded, 'ep', split_axis=0, concat_axis=0, tiled=True)]
    unnamed x1 -> x0, blocking collectives: 14.4 us -> none
    unnamed x6 -> x34, local copies, waits for them, and re-layouts: 4.65 us -> 16.9 us
    ppermute x0 -> x10, starting transfers between devices: none -> 10.9 us  [the longest x6 10.5 us: hop(): return lax.ppermute(x, ('ep', 'sub'), pairs)]
  transfers between devices with their start and end apart: 3 -> 10, of which waited for: 3 -> 9; matrix products, arithmetic and copies ran while one was open for 19% -> 0% of each run, Pallas kernels for 0% -> 14%
where the time goes in v1:
time: 83.3 us; the launch traced here: 82.9 us
  waiting for transfers between devices  29.8 us (36%)
  Pallas kernels  22.6 us (27%)
  local copies, waits for them, and re-layouts  16.9 us (20%)
  starting transfers between devices  10.9 us (13%)
  other arithmetic  1.89 us (2%)
    ppermute x6, waiting for transfers between devices, hop(): return lax.ppermute(x, ('ep', 'sub'), pairs)  23.9 us
    unnamed x34, local copies, waits for them, and re-layouts  16.9 us
    pallas_call x4, Pallas kernels, attention(): pl.pallas_call(functools.partial(attention_kernel, first=first, block=blo...  11.9 us
    ppermute x6, starting transfers between devices, hop(): return lax.ppermute(x, ('ep', 'sub'), pairs)  10.5 us
    pallas_call x2, Pallas kernels, experts(): pl.pallas_call(functools.partial(experts_kernel, parts=len(parts), tile=5...  9.96 us
    ppermute x4, waiting for transfers between devices, swap(): return lax.ppermute(x, 'sub', [(0, 1), (1, 0)])  5.85 us
  transfers between devices with their start and end apart: 10, of which 9 were waited for; matrix products, arithmetic and copies ran while one was open for 0% of the time, Pallas kernels for 14%

profile of v1, /device:TPU:0, one launch (start us, length us, event | category | flops | bytes accessed | tf_op | source)
XLA Modules:
  0.0 82.9 jit_solution(1292959492167336916)
XLA Ops:
  4.3 4.0 %collective-permute-start = (bf16[16,3712]{1,0:T(8,128)(2,1)S(1)}, bf16[16,3712]{1,0:T(8,128)(2,1)S(1)}, u32[]{:S(2)}, u32[]{:S(2)}) collective-permute-start(bf16[16,3712]{1,0:T(8,128)(2,1)S(1)} %route.1), channel_id=1, source_target_pairs={{0,8},{1,9},{2,10},{3,11},{4,12},{5,13},{6,14},{7,15},{8,0},{9,1},... | collective-permute-start | bytes 356360 | tf_op jit(solution)/shard_map/ppermute | solution.py:201
  8.4 1.7 %copy-done = bf16[8,2,128,576]{2,3,1,0:T(8,128)(2,1)S(1)} copy-done((bf16[8,2,128,576]{2,3,1,0:T(8,128)(2,1)S(1)}, bf16[8,2,128,576]{2,3,1,0:T(8,128)(2,1)}, u32[]{:S(2)}) %copy-start) | copy-done | bytes 2359320
  10.1 1.7 %copy-done.2 = bf16[8,256,576]{1,2,0:T(8,128)(2,1)S(1)} copy-done((bf16[8,256,576]{1,2,0:T(8,128)(2,1)S(1)}, bf16[8,256,576]{1,2,0:T(8,128)(2,1)}, u32[]{:S(2)}) %copy-start.2) | copy-done | bytes 2359320
  13.1 3.0 %attention.4.rest_0_ = bf16[8,2,128,512]{3,2,1,0:T(8,128)(2,1)} custom-call(s32[8]{0:T(128)S(1)} %copy-done.10, bf16[8,2,576,128]{3,2,1,0:T(8,128)(2,1)S(1)} %bitcast.6, bf16[8,576,256]{2,1,0:T(8,128)(2,1)S(1)} %bitcast.10, bf16[8,2,576]{2,1,0:T(2,128)(2,1)S(1)} %copy-done.7), custom_call_target="tpu_custom_call" | custom-call | flops 285212672 | bytes 1769472 | tf_op jit(solution)/shard_map/attention/pallas_call | solution.py:66
  16.1 3.0 %attention.5.rest_0_ = bf16[8,2,128,512]{3,2,1,0:T(8,128)(2,1)} custom-call(s32[8]{0:T(128)S(1)} %copy-done.10, bf16[8,2,576,128]{3,2,1,0:T(8,128)(2,1)S(1)} %bitcast.7, bf16[8,576,256]{2,1,0:T(8,128)(2,1)S(1)} %bitcast.11, bf16[8,2,576]{2,1,0:T(2,128)(2,1)S(1)} %copy-done.7, bf16[8,2,128,512]{3,2,1,0:T(8,128)(2,1)} %attention.4.rest_0_), custom_call_target="tpu_custom_call", output_to_operand_aliasing={{}: (4, {})} | custom-call | flops 285212672 | bytes 1769472 | tf_op jit(solution)/shard_map/attention/pallas_call | solution.py:66
  19.1 1.6 %collective-permute-start.1 = (bf16[32,3712]{1,0:T(8,128)(2,1)S(1)}, bf16[32,3712]{1,0:T(8,128)(2,1)S(1)}, u32[]{:S(2)}, u32[]{:S(2)}) collective-permute-start(bf16[32,3712]{1,0:T(8,128)(2,1)S(1)} %pad_maximum_fusion.1), channel_id=1, source_target_pairs={{0,4},{1,3},{2,6},{3,1},{4,0},{5,7},{6,2},{7,5},{8,12},{9,11},{10,... | collective-permute-start | bytes 712712 | tf_op jit(solution)/shard_map/ppermute | solution.py:201
  20.7 4.5 %collective-permute-done.1 = bf16[32,3712]{1,0:T(8,128)(2,1)S(1)} collective-permute-done((bf16[32,3712]{1,0:T(8,128)(2,1)S(1)}, bf16[32,3712]{1,0:T(8,128)(2,1)S(1)}, u32[]{:S(2)}, u32[]{:S(2)}) %collective-permute-start.1) | collective-permute-done | bytes 237600 | tf_op jit(solution)/shard_map/ppermute | solution.py:201
  26.1 2.2 %collective-permute-done.3.refs_1_ = bf16[64,3712]{1,0:T(8,128)(2,1)} collective-permute-done((bf16[64,3712]{1,0:T(8,128)(2,1)}, bf16[64,3712]{1,0:T(8,128)(2,1)}, u32[]{:S(2)}, u32[]{:S(2)}) %collective-permute-start.3) | collective-permute-done | bytes 475168 | tf_op jit(solution)/shard_map/ppermute | solution.py:205
  28.3 3.1 %copy-done.4 = bf16[2,3584,512]{2,1,0:T(8,128)(2,1)S(1)} copy-done((bf16[2,3584,512]{2,1,0:T(8,128)(2,1)S(1)}, bf16[2,3584,512]{2,1,0:T(8,128)(2,1)}, u32[]{:S(2)}) %copy-start.4) | copy-done | bytes 7340056
  31.3 3.1 %copy-done.5 = bf16[2,3584,512]{2,1,0:T(8,128)(2,1)S(1)} copy-done((bf16[2,3584,512]{2,1,0:T(8,128)(2,1)S(1)}, bf16[2,3584,512]{2,1,0:T(8,128)(2,1)}, u32[]{:S(2)}) %copy-start.5) | copy-done | bytes 7340056
  34.4 3.1 %copy-done.6 = bf16[2,512,3584]{2,1,0:T(8,128)(2,1)S(1)} copy-done((bf16[2,512,3584]{2,1,0:T(8,128)(2,1)S(1)}, bf16[2,512,3584]{2,1,0:T(8,128)(2,1)}, u32[]{:S(2)}) %copy-start.6) | copy-done | bytes 7340056
  37.5 5.6 %experts.2 = (bf16[64,3584]{1,0:T(8,128)(2,1)S(1)}, bf16[64,3584]{1,0:T(8,128)(2,1)S(1)}) custom-call(bf16[64,3712]{1,0:T(8,128)(2,1)} %pad_maximum_fusion.refs_0_, bf16[64,3712]{1,0:T(8,128)(2,1)} %collective-permute-done.3.refs_1_, bf16[2,3584,512]{2,1,0:T(8,128)(2,1)S(1)} %copy-done.4, bf16[2,3584,512]{2,1,0:T(8,128)(2,1)S(1)} %copy-done.5, ...), custom_call_target="tpu_custom_call" | custom-call | flops 2818572288 | bytes 1835008 | tf_op jit(solution)/shard_map/experts/pallas_call | solution.py:168
  43.4 1.5 %collective-permute-start.2 = (bf16[64,3712]{1,0:T(8,128)(2,1)}, bf16[64,3712]{1,0:T(8,128)(2,1)S(1)}, u32[]{:S(2)}, u32[]{:S(2)}) collective-permute-start(bf16[64,3712]{1,0:T(8,128)(2,1)} %pad_maximum_fusion.refs_0_), channel_id=1, source_target_pairs={{0,2},{1,5},{2,0},{3,7},{4,6},{5,1},{6,4},{7,3},{8,10},{9,13},{10,... | collective-permute-start | bytes 1425416 | tf_op jit(solution)/shard_map/ppermute | solution.py:201
  45.2 7.0 %collective-permute-done.2.refs_0_ = bf16[64,3712]{1,0:T(8,128)(2,1)S(1)} collective-permute-done((bf16[64,3712]{1,0:T(8,128)(2,1)}, bf16[64,3712]{1,0:T(8,128)(2,1)S(1)}, u32[]{:S(2)}, u32[]{:S(2)}) %collective-permute-start.2) | collective-permute-done | bytes 475168 | tf_op jit(solution)/shard_map/ppermute | solution.py:201
  52.2 1.8 %collective-permute-done.5.refs_1_ = bf16[64,3712]{1,0:T(8,128)(2,1)S(1)} collective-permute-done((bf16[64,3712]{1,0:T(8,128)(2,1)S(1)}, bf16[64,3712]{1,0:T(8,128)(2,1)S(1)}, u32[]{:S(2)}, u32[]{:S(2)}) %collective-permute-start.5) | collective-permute-done | bytes 475168 | tf_op jit(solution)/shard_map/ppermute | solution.py:205
  54.1 4.3 %experts.3 = (bf16[64,3584]{1,0:T(8,128)(2,1)S(1)}, bf16[64,3584]{1,0:T(8,128)(2,1)S(1)}) custom-call(bf16[64,3712]{1,0:T(8,128)(2,1)S(1)} %collective-permute-done.2.refs_0_, bf16[64,3712]{1,0:T(8,128)(2,1)S(1)} %collective-permute-done.5.refs_1_, bf16[2,3584,512]{2,1,0:T(8,128)(2,1)S(1)} %bitcast.15, bf16[2,3584,512]{2,1,0:T(8,128)(2,1)S(1)} %copy-done.5, ...), custom_call_target="tpu_custom_call" | custom-call | flops 2818572288 | bytes 1835008 | tf_op jit(solution)/shard_map/experts/pallas_call | solution.py:168
  58.6 1.7 %collective-permute-done.6 = bf16[64,3584]{1,0:T(8,128)(2,1)S(1)} collective-permute-done((bf16[64,3584]{1,0:T(8,128)(2,1)S(1)}, bf16[64,3584]{1,0:T(8,128)(2,1)S(1)}, u32[]{:S(2)}, u32[]{:S(2)}) %collective-permute-start.6) | collective-permute-done | bytes 458784 | tf_op jit(solution)/shard_map/ppermute | solution.py:205
  60.4 1.6 %collective-permute-start.7 = (bf16[64,3584]{1,0:T(8,128)(2,1)S(1)}, bf16[64,3584]{1,0:T(8,128)(2,1)S(1)}, u32[]{:S(2)}, u32[]{:S(2)}) collective-permute-start(bf16[64,3584]{1,0:T(8,128)(2,1)S(1)} %add_convert_fusion), channel_id=1, source_target_pairs={{0,2},{1,5},{2,0},{3,7},{4,6},{5,1},{6,4},{7,3},{8,10},{9,13},{10,... | collective-permute-start | bytes 1376264 | tf_op jit(solution)/shard_map/ppermute | solution.py:201
  62.0 3.0 %attention.6.rest_0_ = bf16[8,2,128,512]{3,2,1,0:T(8,128)(2,1)} custom-call(s32[8]{0:T(128)S(1)} %copy-done.11, bf16[8,2,576,128]{3,2,1,0:T(8,128)(2,1)S(1)} %bitcast.8, bf16[8,576,256]{2,1,0:T(8,128)(2,1)S(1)} %bitcast.12, bf16[8,2,576]{2,1,0:T(2,128)(2,1)S(1)} %copy-done.8, bf16[8,2,128,512]{3,2,1,0:T(8,128)(2,1)} %attention.5.rest_0_), custom_call_target="tpu_custom_call", output_to_operand_aliasing={{}: (4, {})} | custom-call | flops 285212672 | bytes 1769472 | tf_op jit(solution)/shard_map/attention/pallas_call | solution.py:66
  65.0 4.0 %collective-permute-done.7 = bf16[64,3584]{1,0:T(8,128)(2,1)S(1)} collective-permute-done((bf16[64,3584]{1,0:T(8,128)(2,1)S(1)}, bf16[64,3584]{1,0:T(8,128)(2,1)S(1)}, u32[]{:S(2)}, u32[]{:S(2)}) %collective-permute-start.7) | collective-permute-done | bytes 458784 | tf_op jit(solution)/shard_map/ppermute | solution.py:201
  69.1 1.6 %collective-permute-start.8 = (bf16[32,3584]{1,0:T(8,128)(2,1)S(1)}, bf16[32,3584]{1,0:T(8,128)(2,1)S(1)}, u32[]{:S(2)}, u32[]{:S(2)}) collective-permute-start(bf16[32,3584]{1,0:T(8,128)(2,1)S(1)} %get-tuple-element.27), channel_id=1, source_target_pairs={{0,4},{1,3},{2,6},{3,1},{4,0},{5,7},{6,2},{7,5},{8,12},{9,11},{10,... | collective-permute-start | bytes 688136 | tf_op jit(solution)/shard_map/ppermute | solution.py:201
  70.7 4.5 %collective-permute-done.8 = bf16[32,3584]{1,0:T(8,128)(2,1)S(1)} collective-permute-done((bf16[32,3584]{1,0:T(8,128)(2,1)S(1)}, bf16[32,3584]{1,0:T(8,128)(2,1)S(1)}, u32[]{:S(2)}, u32[]{:S(2)}) %collective-permute-start.8) | collective-permute-done | bytes 229408 | tf_op jit(solution)/shard_map/ppermute | solution.py:201
  75.3 3.0 %attention.7 = bf16[8,2,128,512]{3,2,1,0:T(8,128)(2,1)} custom-call(s32[8]{0:T(128)S(1)} %copy-done.11, bf16[8,2,576,128]{3,2,1,0:T(8,128)(2,1)S(1)} %bitcast.9, bf16[8,576,256]{2,1,0:T(8,128)(2,1)S(1)} %bitcast.13, bf16[8,2,576]{2,1,0:T(2,128)(2,1)S(1)} %copy-done.8, bf16[8,2,128,512]{3,2,1,0:T(8,128)(2,1)} %attention.6.rest_0_), custom_call_target="tpu_custom_call", output_to_operand_aliasing={{}: (4, {})} | custom-call | flops 285212672 | bytes 1769472 | tf_op jit(solution)/shard_map/attention/pallas_call | solution.py:66
  78.3 3.9 %collective-permute-done.9 = bf16[16,3584]{1,0:T(8,128)(2,1)S(1)} collective-permute-done((bf16[16,3584]{1,0:T(8,128)(2,1)S(1)}, bf16[16,3584]{1,0:T(8,128)(2,1)S(1)}, u32[]{:S(2)}, u32[]{:S(2)}) %collective-permute-start.9) | collective-permute-done | bytes 114720 | tf_op jit(solution)/shard_map/ppermute | solution.py:201
  (45 shorter events, 7.6 us)
Async XLA Ops:
  0.6 0.9 %copy-start.9 = (bf16[16,3584]{1,0:T(8,128)(2,1)S(1)}, bf16[16,3584]{1,0:T(8,128)(2,1)}, u32[]{:S(2)}) copy-start(bf16[16,3584]{1,0:T(8,128)(2,1)} %rows_ref.1) | copy-start | bytes 344068
  1.5 0.7 copy-start.12
  4.3 14.7 %collective-permute-start = (bf16[16,3712]{1,0:T(8,128)(2,1)S(1)}, bf16[16,3712]{1,0:T(8,128)(2,1)S(1)}, u32[]{:S(2)}, u32[]{:S(2)}) collective-permute-start(bf16[16,3712]{1,0:T(8,128)(2,1)S(1)} %route.1), channel_id=1, source_target_pairs={{0,8},{1,9},{2,10},{3,11},{4,12},{5,13},{6,14},{7,15},{8,0},{9,1},... | collective-permute-start | bytes 356360 | tf_op jit(solution)/shard_map/ppermute | solution.py:201
  8.4 1.7 %copy-start = (bf16[8,2,128,576]{2,3,1,0:T(8,128)(2,1)S(1)}, bf16[8,2,128,576]{2,3,1,0:T(8,128)(2,1)}, u32[]{:S(2)}) copy-start(bf16[8,2,128,576]{2,3,1,0:T(8,128)(2,1)} %param.11) | copy-start | bytes 7077892
  10.0 1.7 %copy-start.2 = (bf16[8,256,576]{1,2,0:T(8,128)(2,1)S(1)}, bf16[8,256,576]{1,2,0:T(8,128)(2,1)}, u32[]{:S(2)}) copy-start(bf16[8,256,576]{1,2,0:T(8,128)(2,1)} %param.12) | copy-start | bytes 7077892
  11.7 0.7 copy-start.7
  16.1 38.0 %slice-start = ((s8[7340032]{0:T(1024)(128)(4,1)}), s8[3145728]{0:T(1024)(128)(4,1)S(1)}, s32[]{:S(2)}) async-start(s8[7340032]{0:T(1024)(128)(4,1)} %bitcast.14), calls=%async_computation | async-start | bytes 6291456
  19.1 6.2 %collective-permute-start.1 = (bf16[32,3712]{1,0:T(8,128)(2,1)S(1)}, bf16[32,3712]{1,0:T(8,128)(2,1)S(1)}, u32[]{:S(2)}, u32[]{:S(2)}) collective-permute-start(bf16[32,3712]{1,0:T(8,128)(2,1)S(1)} %pad_maximum_fusion.1), channel_id=1, source_target_pairs={{0,4},{1,3},{2,6},{3,1},{4,0},{5,7},{6,2},{7,5},{8,12},{9,11},{10,... | collective-permute-start | bytes 712712 | tf_op jit(solution)/shard_map/ppermute | solution.py:201
  26.1 2.2 %collective-permute-start.3 = (bf16[64,3712]{1,0:T(8,128)(2,1)}, bf16[64,3712]{1,0:T(8,128)(2,1)}, u32[]{:S(2)}, u32[]{:S(2)}) collective-permute-start(bf16[64,3712]{1,0:T(8,128)(2,1)} %pad_maximum_fusion.refs_0_), channel_id=1, source_target_pairs={{0,1},{1,0},{2,3},{3,2},{4,5},{5,4},{6,7},{7,6},{8,9},{9,8},{10,11... | collective-permute-start | bytes 1425416 | tf_op jit(solution)/shard_map/ppermute | solution.py:205
  28.2 3.1 %copy-start.4 = (bf16[2,3584,512]{2,1,0:T(8,128)(2,1)S(1)}, bf16[2,3584,512]{2,1,0:T(8,128)(2,1)}, u32[]{:S(2)}) copy-start(bf16[2,3584,512]{2,1,0:T(8,128)(2,1)} %refs_2_.3) | copy-start | bytes 22020100
  31.3 3.1 %copy-start.5 = (bf16[2,3584,512]{2,1,0:T(8,128)(2,1)S(1)}, bf16[2,3584,512]{2,1,0:T(8,128)(2,1)}, u32[]{:S(2)}) copy-start(bf16[2,3584,512]{2,1,0:T(8,128)(2,1)} %refs_3_.3) | copy-start | bytes 22020100
  34.4 3.1 %copy-start.6 = (bf16[2,512,3584]{2,1,0:T(8,128)(2,1)S(1)}, bf16[2,512,3584]{2,1,0:T(8,128)(2,1)}, u32[]{:S(2)}) copy-start(bf16[2,512,3584]{2,1,0:T(8,128)(2,1)} %refs_4_.3) | copy-start | bytes 22020100
  37.5 16.6 %slice-start.1 = ((s8[7340032]{0:T(1024)(128)(4,1)}), s8[4194304]{0:T(1024)(128)(4,1)S(1)}, s32[]{:S(2)}) async-start(s8[7340032]{0:T(1024)(128)(4,1)} %bitcast.14), calls=%async_computation.1 | async-start | bytes 8388608
  43.1 1.9 %collective-permute-start.4 = (bf16[64,3584]{1,0:T(8,128)(2,1)S(1)}, bf16[64,3584]{1,0:T(8,128)(2,1)S(1)}, u32[]{:S(2)}, u32[]{:S(2)}) collective-permute-start(bf16[64,3584]{1,0:T(8,128)(2,1)S(1)} %get-tuple-element.16), channel_id=1, source_target_pairs={{0,1},{1,0},{2,3},{3,2},{4,5},{5,4},{6,7},{7,6},{8,9},{9,8},{10,11... | collective-permute-start | bytes 1376264 | tf_op jit(solution)/shard_map/ppermute | solution.py:205
  43.4 8.9 %collective-permute-start.2 = (bf16[64,3712]{1,0:T(8,128)(2,1)}, bf16[64,3712]{1,0:T(8,128)(2,1)S(1)}, u32[]{:S(2)}, u32[]{:S(2)}) collective-permute-start(bf16[64,3712]{1,0:T(8,128)(2,1)} %pad_maximum_fusion.refs_0_), channel_id=1, source_target_pairs={{0,2},{1,5},{2,0},{3,7},{4,6},{5,1},{6,4},{7,3},{8,10},{9,13},{10,... | collective-permute-start | bytes 1425416 | tf_op jit(solution)/shard_map/ppermute | solution.py:201
  45.1 16.9 %copy-start.8 = (bf16[8,2,576]{2,1,0:T(2,128)(2,1)S(1)}, bf16[8,2,576]{2,1,0:T(2,128)(2,1)}, u32[]{:S(2)}) copy-start(bf16[8,2,576]{2,1,0:T(2,128)(2,1)} %new_ref.7) | copy-start | bytes 55300
  45.2 16.9 %copy-start.11 = (s32[8]{0:T(128)S(1)}, s32[8]{0:T(128)}, u32[]{:S(2)}) copy-start(s32[8]{0:T(128)} %length_ref.7) | copy-start | bytes 100
  52.2 1.8 %collective-permute-start.5 = (bf16[64,3712]{1,0:T(8,128)(2,1)S(1)}, bf16[64,3712]{1,0:T(8,128)(2,1)S(1)}, u32[]{:S(2)}, u32[]{:S(2)}) collective-permute-start(bf16[64,3712]{1,0:T(8,128)(2,1)S(1)} %collective-permute-done.2.refs_0_), channel_id=1, source_target_pairs={{0,1},{1,0},{2,3},{3,2},{4,5},{5,4},{6,7},{7,6},{8,9},{9,8},{10,11... | collective-permute-start | bytes 1425416 | tf_op jit(solution)/shard_map/ppermute | solution.py:205
  54.1 7.9 %copy-start.1 = (bf16[8,2,128,576]{2,3,1,0:T(8,128)(2,1)S(1)}, bf16[8,2,128,576]{2,3,1,0:T(8,128)(2,1)}, u32[]{:S(2)}) copy-start(bf16[8,2,128,576]{2,3,1,0:T(8,128)(2,1)} %param.11) | copy-start | bytes 7077892
  54.1 7.9 %copy-start.3 = (bf16[8,256,576]{1,2,0:T(8,128)(2,1)S(1)}, bf16[8,256,576]{1,2,0:T(8,128)(2,1)}, u32[]{:S(2)}) copy-start(bf16[8,256,576]{1,2,0:T(8,128)(2,1)} %param.12) | copy-start | bytes 7077892
  58.4 1.9 %collective-permute-start.6 = (bf16[64,3584]{1,0:T(8,128)(2,1)S(1)}, bf16[64,3584]{1,0:T(8,128)(2,1)S(1)}, u32[]{:S(2)}, u32[]{:S(2)}) collective-permute-start(bf16[64,3584]{1,0:T(8,128)(2,1)S(1)} %get-tuple-element.20), channel_id=1, source_target_pairs={{0,1},{1,0},{2,3},{3,2},{4,5},{5,4},{6,7},{7,6},{8,9},{9,8},{10,11... | collective-permute-start | bytes 1376264 | tf_op jit(solution)/shard_map/ppermute | solution.py:205
  60.4 8.5 %collective-permute-start.7 = (bf16[64,3584]{1,0:T(8,128)(2,1)S(1)}, bf16[64,3584]{1,0:T(8,128)(2,1)S(1)}, u32[]{:S(2)}, u32[]{:S(2)}) collective-permute-start(bf16[64,3584]{1,0:T(8,128)(2,1)S(1)} %add_convert_fusion), channel_id=1, source_target_pairs={{0,2},{1,5},{2,0},{3,7},{4,6},{5,1},{6,4},{7,3},{8,10},{9,13},{10,... | collective-permute-start | bytes 1376264 | tf_op jit(solution)/shard_map/ppermute | solution.py:201
  69.1 6.1 %collective-permute-start.8 = (bf16[32,3584]{1,0:T(8,128)(2,1)S(1)}, bf16[32,3584]{1,0:T(8,128)(2,1)S(1)}, u32[]{:S(2)}, u32[]{:S(2)}) collective-permute-start(bf16[32,3584]{1,0:T(8,128)(2,1)S(1)} %get-tuple-element.27), channel_id=1, source_target_pairs={{0,4},{1,3},{2,6},{3,1},{4,0},{5,7},{6,2},{7,5},{8,12},{9,11},{10,... | collective-permute-start | bytes 688136 | tf_op jit(solution)/shard_map/ppermute | solution.py:201
  75.2 7.0 %collective-permute-start.9 = (bf16[16,3584]{1,0:T(8,128)(2,1)S(1)}, bf16[16,3584]{1,0:T(8,128)(2,1)S(1)}, u32[]{:S(2)}, u32[]{:S(2)}) collective-permute-start(bf16[16,3584]{1,0:T(8,128)(2,1)S(1)} %add_convert_fusion.6), channel_id=1, source_target_pairs={{0,8},{1,9},{2,10},{3,11},{4,12},{5,13},{6,14},{7,15},{8,0},{9,1},... | collective-permute-start | bytes 344072 | tf_op jit(solution)/shard_map/ppermute | solution.py:201
  (3 other events, 2.0 us)

commit v2 on v1

v2 whole, which is shorter than its diff:
```python
import functools

import jax
import jax.numpy as jnp
from jax import lax
from jax.experimental import pallas as pl
from jax.experimental.pallas import tpu as pltpu
from jax.sharding import PartitionSpec as P

LATENT_RANK = 512
SCORE_SCALE = 192.0 ** (-0.5)
ROUTE_SCALE = 2.5
LANES = 128
F32 = jnp.float32
BF16 = jnp.bfloat16


def contract(a, b, dim_a, dim_b):
    return lax.dot_general(
        a, b, (((dim_a,), (dim_b,)), ((), ())), preferred_element_type=F32
    )


def attend_request(q_steps, cached, fresh, length):
    heads = q_steps[0].shape[1]
    q = jnp.concatenate([q.T for q in q_steps], axis=0)
    older = contract(q, cached, 1, 0) * SCORE_SCALE
    newer = contract(q, fresh, 1, 1) * SCORE_SCALE
    position = lax.broadcasted_iota(jnp.int32, older.shape, 1)
    older = jnp.where(position < length, older, -jnp.inf)
    row = lax.broadcasted_iota(jnp.int32, newer.shape, 0)
    step = lax.broadcasted_iota(jnp.int32, newer.shape, 1)
    newer = jnp.where(step * heads <= row, newer, -jnp.inf)
    highest = jnp.maximum(
        jnp.max(older, axis=1, keepdims=True), jnp.max(newer, axis=1, keepdims=True)
    )
    older = jnp.exp(older - highest)
    newer = jnp.exp(newer - highest)
    total = jnp.sum(older, axis=1, keepdims=True) + jnp.sum(newer, axis=1, keepdims=True)
    blended = contract((older / total).astype(BF16), cached[:LATENT_RANK], 1, 1)
    blended = blended + contract((newer / total).astype(BF16), fresh[:, :LATENT_RANK], 1, 0)
    return blended.reshape(len(q_steps), heads, LATENT_RANK).astype(BF16)


def attention_kernel(*refs, first, count, loads, opening):
    length_ref, refs = refs[0], refs[1:]
    sources, refs = refs[:3], refs[3:]
    load_refs, refs = refs[:loads], refs[loads:]
    if not opening:
        refs = refs[1:]
    out_ref, refs = refs[0], refs[1:]
    if opening:
        resident, refs = refs[:3], refs[3:]
    else:
        resident = sources
    loaded, (result, out_sems, load_sems, in_sems) = refs[:loads], refs[loads:]
    requests = resident[0].shape[0]

    arrivals = []
    if opening:
        fresh = pltpu.make_async_copy(sources[2], resident[2], in_sems.at[2, 0])
        fresh.start()
        for lo, hi in ((first, first + count), (first + count, requests)):
            group = []
            if hi > lo:
                for i in range(2):
                    copy = pltpu.make_async_copy(
                        sources[i].at[lo:hi],
                        resident[i].at[lo:hi],
                        in_sems.at[i, 0 if lo == first else 1],
                    )
                    copy.start()
                    group.append(copy)
            arrivals.append(group)
        arrivals[0].append(fresh)
    copies = []
    for i, (source, target) in enumerate(zip(load_refs, loaded)):
        copy = pltpu.make_async_copy(source, target, load_sems.at[i])
        copy.start()
        copies.append(copy)
    if opening:
        for copy in arrivals[0]:
            copy.wait()
        copies += arrivals[1]
    query_ref, cache_ref, new_ref = resident
    for b in range(count):
        r = first + b
        steps = query_ref.shape[1]
        result[b] = attend_request(
            [query_ref[r, s] for s in range(steps)], cache_ref[r], new_ref[r], length_ref[r]
        )
        copy = pltpu.make_async_copy(result.at[b], out_ref.at[r], out_sems.at[b])
        copy.start()
        copies.append(copy)
    for copy in copies:
        copy.wait()


def attention(lengths, inputs, first, count, loads, previous):
    opening = previous is None
    requests, steps, latent, heads = inputs[0].shape
    vmem = pl.BlockSpec(memory_space=pltpu.VMEM)
    hbm = pl.BlockSpec(memory_space=pl.ANY)
    in_specs = [pl.BlockSpec(memory_space=pltpu.SMEM)]
    in_specs += [hbm if opening else vmem] * 3 + [hbm] * len(loads)
    operands = list(inputs)
    if opening:
        operands = [pltpu.with_memory_space_constraint(x, pltpu.HBM) for x in operands]
    else:
        operands = [pltpu.with_memory_space_constraint(x, pltpu.VMEM) for x in operands]
    operands += [pltpu.with_memory_space_constraint(x, pltpu.HBM) for x in loads]
    aliases = {}
    if not opening:
        in_specs.append(hbm)
        aliases = {len(operands) + 1: 0}
        operands.append(pltpu.with_memory_space_constraint(previous, pltpu.HBM))
    kept = (list(inputs) if opening else []) + list(loads)
    outs = pl.pallas_call(
        functools.partial(
            attention_kernel, first=first, count=count, loads=len(loads), opening=opening
        ),
        in_specs=in_specs,
        out_specs=[hbm] + [vmem] * len(kept),
        out_shape=[pltpu.HBM((requests, steps, heads, LATENT_RANK), BF16)]
        + [pltpu.VMEM(x.shape, x.dtype) for x in kept],
        scratch_shapes=[
            pltpu.VMEM((count, steps, heads, LATENT_RANK), BF16),
            pltpu.SemaphoreType.DMA((count,)),
            pltpu.SemaphoreType.DMA((max(len(loads), 1),)),
            pltpu.SemaphoreType.DMA((3, 2)),
        ],
        input_output_aliases=aliases,
        compiler_params=pltpu.CompilerParams(vmem_limit_bytes=12 << 20),
        cost_estimate=pl.CostEstimate(flops=1 << 20, bytes_accessed=1 << 16, transcendentals=0),
        name="attention",
    )(pltpu.with_memory_space_constraint(lengths, pltpu.HBM), *operands)
    out, kept = outs[0], list(outs[1:])
    if opening:
        return out, kept[:3], kept[3:]
    return out, list(inputs), kept


def route_kernel(place_ref, rows_ref, score_ref, expert_ref, out_ref, *, experts, slots):
    tokens, width = rows_ref.shape
    sigmoid = jax.nn.sigmoid(score_ref[...])
    weights = ROUTE_SCALE * sigmoid / jnp.sum(sigmoid, axis=0, keepdims=True)
    weights = weights.astype(BF16).astype(F32)
    named = expert_ref[...]
    even = lax.broadcasted_iota(jnp.int32, named.shape, 1) % 2 == 0
    slot = jnp.zeros_like(named)
    for e in range(experts):
        slot = jnp.where(
            named == e, jnp.where(even, place_ref[0, e], place_ref[1, e]), slot
        )
    index = lax.broadcasted_iota(jnp.int32, (LANES, tokens), 0)
    table = jnp.zeros((LANES, tokens), F32)
    for k in range(named.shape[0]):
        table = table + jnp.where(index == slot[k : k + 1], weights[k : k + 1], 0.0)
    row = lax.broadcasted_iota(jnp.int32, (tokens, tokens), 0)
    column = lax.broadcasted_iota(jnp.int32, (tokens, tokens), 1)
    unit = jnp.where(row == column, 1.0, 0.0).astype(BF16)
    out_ref[:, :width] = rows_ref[...]
    out_ref[:, width:] = contract(unit, table.astype(BF16), 1, 1).astype(BF16)


def route(placement, rows, scores, expert_ids, slots):
    tokens, width = rows.shape
    vmem = pl.BlockSpec(memory_space=pltpu.VMEM)
    return pl.pallas_call(
        functools.partial(route_kernel, experts=placement.shape[0], slots=slots),
        in_specs=[pl.BlockSpec(memory_space=pltpu.SMEM), vmem, vmem, vmem],
        out_specs=vmem,
        out_shape=jax.ShapeDtypeStruct((tokens, width + LANES), BF16),
        compiler_params=pltpu.CompilerParams(vmem_limit_bytes=4 << 20),
        name="route",
    )(*(pltpu.with_memory_space_constraint(x, pltpu.HBM) for x in (placement.T, rows, scores.T, expert_ids.T)))


def experts_kernel(*refs, parts, tile):
    rows_refs = refs[:parts]
    gate_ref, up_ref, down_ref, chip_ref = refs[parts : parts + 4]
    out_refs = refs[parts + 4 : 2 * parts + 4]
    rows_s, act_s = refs[-2:]
    slots, width, hidden = gate_ref.shape
    start = 0
    for ref in rows_refs:
        rows_s[start : start + ref.shape[0], :] = ref[...]
        start += ref.shape[0]
    table = rows_s[:, width:].astype(F32)
    lane = lax.broadcasted_iota(jnp.int32, table.shape, 1)
    for s in range(slots):
        slot = chip_ref[0] * slots + s
        weight = jnp.sum(jnp.where(lane == slot, table, 0.0), axis=1, keepdims=True)
        rows = rows_s[:, :width]
        gate = jnp.dot(rows, gate_ref[s], preferred_element_type=F32)
        up = jnp.dot(rows, up_ref[s], preferred_element_type=F32)
        act = gate / (1.0 + jnp.exp(-gate)) * up
        act_s[:, s * hidden : (s + 1) * hidden] = (weight * act).astype(BF16)

    def project(i, carry):
        columns = pl.ds(pl.multiple_of(i * tile, tile), tile)
        total = jnp.dot(act_s[:, :hidden], down_ref[0, :, columns], preferred_element_type=F32)
        for s in range(1, slots):
            total = total + jnp.dot(
                act_s[:, s * hidden : (s + 1) * hidden],
                down_ref[s, :, columns],
                preferred_element_type=F32,
            )
        start = 0
        for ref in out_refs:
            ref[:, columns] = total[start : start + ref.shape[0]].astype(ref.dtype)
            start += ref.shape[0]
        return carry

    lax.fori_loop(0, width // tile, project, 0)


def experts(parts, gate, up, down, chip):
    slots, width, hidden = gate.shape
    count = sum(p.shape[0] for p in parts)
    vmem = pl.BlockSpec(memory_space=pltpu.VMEM)
    return pl.pallas_call(
        functools.partial(experts_kernel, parts=len(parts), tile=512),
        in_specs=[vmem] * (len(parts) + 3) + [pl.BlockSpec(memory_space=pltpu.SMEM)],
        out_specs=[vmem] * len(parts),
        out_shape=[
            jax.ShapeDtypeStruct((p.shape[0], width), kind) for p, kind in zip(parts, (F32, BF16))
        ],
        scratch_shapes=[
            pltpu.VMEM((count, parts[0].shape[1]), BF16),
            pltpu.VMEM((count, slots * hidden), BF16),
        ],
        compiler_params=pltpu.CompilerParams(vmem_limit_bytes=16 << 20),
        cost_estimate=pl.CostEstimate(
            flops=1 << 20, bytes_accessed=1 << 16, transcendentals=0
        ),
        name="experts",
    )(*parts, gate, up, down, chip)


def halving_masks(ep):
    bits = []
    bit = ep // 2
    while bit:
        bits.append(bit)
        bit //= 2
    other = bits[:-2] + bits[-2:][::-1]
    return bits, other


def hop(x, ep, sub, masks, turn):
    pairs = [
        (e * sub + s, (e ^ masks[s % 2][turn]) * sub + s) for e in range(ep) for s in range(sub)
    ]
    return lax.ppermute(x, ("ep", "sub"), pairs)


def swap(x):
    return lax.ppermute(x, "sub", [(0, 1), (1, 0)])


def add(*terms):
    total = terms[0].astype(F32)
    for t in terms[1:]:
        total = total + t.astype(F32)
    return total


def on_device(
    queries,
    latent_cache,
    new_latent,
    lengths,
    moe_input,
    gate_scores,
    expert_ids,
    placement,
    w_gate,
    w_up,
    w_down,
):
    ep, sub = lax.axis_size("ep"), lax.axis_size("sub")
    masks = halving_masks(ep)
    turns = len(masks[0])
    tokens = moe_input.shape[0]
    requests = queries.shape[0]
    inputs = [queries.transpose(0, 1, 3, 2), latent_cache.transpose(0, 2, 1), new_latent]
    chip = lax.axis_index("ep").astype(jnp.int32)[None]
    slots = ep * w_gate.shape[0]
    barrier = lax.optimization_barrier
    chip, gate_scores, lengths = barrier((chip, gate_scores, lengths))

    out = None
    weights = []
    done = 0
    loads = [[w_gate, w_up], [w_down]] + [[]] * turns
    share = [1, 1] + [2] * turns

    def attend(window, tie):
        nonlocal out, inputs, done, weights
        count = min(share[window], requests - done)
        if window == 1 + turns:
            count = requests - done
        if count == 0:
            return tie
        out, inputs, loaded = attention(lengths, inputs, done, count, loads[window], out)
        weights = weights + loaded
        done += count
        tie, out, inputs, weights = barrier((tie, out, inputs, weights))
        return tie

    rows = route(placement, moe_input, gate_scores, expert_ids, slots)
    for turn in range(turns - 1):
        got = hop(rows, ep, sub, masks, turn)
        if turn < 2:
            rows, inputs, weights = barrier((rows, inputs, weights))
            got = attend(turn, got)
        rows = jnp.concatenate([rows, got], axis=0)

    far = hop(rows, ep, sub, masks, turns - 1)
    near_own, near_other = experts([rows, swap(rows)], *weights, chip)
    far, near_own, inputs, weights = barrier((far, near_own, inputs, weights))
    far_own, far_other = experts([far, swap(far)], *weights, chip)
    total = add(near_own, swap(near_other))
    sent = add(far_own, swap(far_other)).astype(BF16)
    for turn in range(turns - 1, -1, -1):
        got = hop(sent, ep, sub, masks, turn)
        sent, inputs = barrier((sent, inputs))
        got = attend(turns + 1 - turn, got)
        total = add(total, got)
        if turn:
            half = total.shape[0] // 2
            sent = total[half:].astype(BF16)
            total = total[:half]
    return out, total.astype(BF16)


def solution(mesh):
    split = ("groups", "ep", "sub")
    return jax.shard_map(
        on_device,
        mesh=mesh,
        in_specs=(
            P(split, None, None, None),
            P(split, None, None),
            P(split, None, None),
            P(split),
            P(split, None),
            P(split, None),
            P(split, None),
            P("groups", None),
            P(("groups", "ep"), None, "sub"),
            P(("groups", "ep"), None, "sub"),
            P(("groups", "ep"), "sub", None),
        ),
        out_specs=(P(split, None, None, None), P(split, None)),
        check_vma=False,
    )
```

time: 83.3 us -> 59.4 us (0.71)
  local copies, waits for them, and re-layouts: 16.9 us -> 0.11 us
  waiting for transfers between devices: 29.8 us -> 16 us
  Pallas kernels: 22.6 us -> 30.2 us
  other arithmetic: 1.89 us -> 0.96 us
    unnamed x34 -> x2, local copies, waits for them, and re-layouts: 16.9 us -> 0.03 us
    ppermute x6, waiting for transfers between devices: 23.9 us -> 12.2 us  [hop(): return lax.ppermute(x, ('ep', 'sub'), pairs)]
    pallas_call x4 -> x5, Pallas kernels: 11.9 us -> 20.1 us  [attention(): pl.pallas_call(functools.partial(attention_kernel, first=first, count=cou...]
    ppermute x4, waiting for transfers between devices: 5.85 us -> 3.78 us  [swap(): return lax.ppermute(x, 'sub', [(0, 1), (1, 0)])]
    pallas_call x2, Pallas kernels: 9.96 us -> 8.9 us  [experts(): pl.pallas_call(functools.partial(experts_kernel, parts=len(parts), tile=5...]
  transfers between devices with their start and end apart: 10 -> 10, of which waited for: 9 -> 8; matrix products, arithmetic and copies ran while one was open for 0% -> 0% of each run, Pallas kernels for 14% -> 42%
where the time goes in v2:
time: 59.4 us; the launch traced here: 59.1 us
  Pallas kernels  30.2 us (51%)
  waiting for transfers between devices  16 us (27%)
  starting transfers between devices  11.1 us (19%)
  other arithmetic  0.96 us (2%)
  between operations  0.76 us (1%)
    pallas_call x5, Pallas kernels, attention(): pl.pallas_call(functools.partial(attention_kernel, first=first, count=cou...  20.1 us
    ppermute x6, waiting for transfers between devices, hop(): return lax.ppermute(x, ('ep', 'sub'), pairs)  12.2 us
    ppermute x6, starting transfers between devices, hop(): return lax.ppermute(x, ('ep', 'sub'), pairs)  10.9 us
    pallas_call x2, Pallas kernels, experts(): pl.pallas_call(functools.partial(experts_kernel, parts=len(parts), tile=5...  8.9 us
    ppermute x4, waiting for transfers between devices, swap(): return lax.ppermute(x, 'sub', [(0, 1), (1, 0)])  3.78 us
  transfers between devices with their start and end apart: 10, of which 8 were waited for; matrix products, arithmetic and copies ran while one was open for 0% of the time, Pallas kernels for 42%

profile of v2, /device:TPU:0, one launch (start us, length us, event | category | flops | bytes accessed | tf_op | source)
XLA Modules:
  0.0 59.1 jit_solution(7018240939729969090)
XLA Ops:
  0.6 1.1 %route.1 = bf16[16,3712]{1,0:T(8,128)(2,1)S(1)} custom-call(s32[2,14]{1,0:T(2,128)} %bitcast.10, bf16[16,3584]{1,0:T(8,128)(2,1)} %rows_ref.1, f32[8,16]{1,0:T(8,128)} %bitcast.8, s32[8,16]{1,0:T(8,128)} %bitcast.9), custom_call_target="tpu_custom_call" | custom-call | tf_op jit(solution)/shard_map/route/pallas_call | solution.py:169
  1.8 4.0 %collective-permute-start = (bf16[16,3712]{1,0:T(8,128)(2,1)S(1)}, bf16[16,3712]{1,0:T(8,128)(2,1)S(1)}, u32[]{:S(2)}, u32[]{:S(2)}) collective-permute-start(bf16[16,3712]{1,0:T(8,128)(2,1)S(1)} %route.1), channel_id=1, source_target_pairs={{0,8},{1,9},{2,10},{3,11},{4,12},{5,13},{6,14},{7,15},{8,0},{9,1},... | collective-permute-start | bytes 356360 | tf_op jit(solution)/shard_map/ppermute | solution.py:255
  5.8 7.4 %attention.5 = (bf16[8,2,128,512]{3,2,1,0:T(8,128)(2,1)}, bf16[8,2,576,128]{3,2,1,0:T(8,128)(2,1)S(1)}, bf16[8,576,256]{2,1,0:T(8,128)(2,1)S(1)}, bf16[8,2,576]{...) custom-call(s32[8]{0:T(128)} %refs_0_.4, bf16[8,2,576,128]{3,2,1,0:T(8,128)(2,1)} %bitcast.6, ...), custom_call_target="tpu_custom_call" | custom-call | flops 1048576 | bytes 65536 | tf_op jit(solution)/shard_map/attention/pallas_call | solution.py:118
  13.3 1.6 %collective-permute-start.1 = (bf16[32,3712]{1,0:T(8,128)(2,1)S(1)}, bf16[32,3712]{1,0:T(8,128)(2,1)S(1)}, u32[]{:S(2)}, u32[]{:S(2)}) collective-permute-start(bf16[32,3712]{1,0:T(8,128)(2,1)S(1)} %constant_dynamic-update-slice_fusion), channel_id=1, source_target_pairs={{0,4},{1,3},{2,6},{3,1},{4,0},{5,7},{6,2},{7,5},{8,12},{9,11},{10,... | collective-permute-start | bytes 712712 | tf_op jit(solution)/shard_map/ppermute | solution.py:255
  14.9 3.9 %attention.6 = (bf16[8,2,128,512]{3,2,1,0:T(8,128)(2,1)}, bf16[2,512,3584]{2,1,0:T(8,128)(2,1)S(1)}) custom-call(s32[8]{0:T(128)} %refs_0_.4, bf16[8,2,576,128]{3,2,1,0:T(8,128)(2,1)S(1)} %get-tuple-element.134.refs_1_, bf16[8,576,256]{2,1,0:T(8,128)(2,1)S(1)} %get-tuple-element.135.refs_2_, ...), custom_call_target="tpu_custom_call", output_to_operand_aliasing={{0}: (5, {})} | custom-call | flops 1048576 | bytes 65536 | tf_op jit(solution)/shard_map/attention/pallas_call | solution.py:118
  18.9 0.6 collective-permute-done.1
  19.6 1.6 %collective-permute-start.2 = (bf16[64,3712]{1,0:T(8,128)(2,1)S(1)}, bf16[64,3712]{1,0:T(8,128)(2,1)S(1)}, u32[]{:S(2)}, u32[]{:S(2)}) collective-permute-start(bf16[64,3712]{1,0:T(8,128)(2,1)S(1)} %constant_dynamic-update-slice_fusion.2.refs_0_), channel_id=1, source_target_pairs={{0,2},{1,5},{2,0},{3,7},{4,6},{5,1},{6,4},{7,3},{8,10},{9,13},{10,... | collective-permute-start | bytes 1425416 | tf_op jit(solution)/shard_map/ppermute | solution.py:255
  21.2 0.2 collective-permute-done.3.refs_1_
  21.4 4.5 %experts.2 = (f32[64,3584]{1,0:T(8,128)S(1)}, bf16[64,3584]{1,0:T(8,128)(2,1)S(1)}) custom-call(bf16[64,3712]{1,0:T(8,128)(2,1)S(1)} %constant_dynamic-update-slice_fusion.2.refs_0_, bf16[64,3712]{1,0:T(8,128)(2,1)S(1)} %collective-permute-done.3.refs_1_, bf16[2,3584,512]{2,1,0:T(8,128)(2,1)S(1)} %get-tuple-element.110.refs_2_, ...), custom_call_target="tpu_custom_call" | custom-call | flops 1048576 | bytes 65536 | tf_op jit(solution)/shard_map/experts/pallas_call | solution.py:222
  25.9 2.4 %collective-permute-done.2.refs_0_ = bf16[64,3712]{1,0:T(8,128)(2,1)S(1)} collective-permute-done((bf16[64,3712]{1,0:T(8,128)(2,1)S(1)}, bf16[64,3712]{1,0:T(8,128)(2,1)S(1)}, u32[]{:S(2)}, u32[]{:S(2)}) %collective-permute-start.2) | collective-permute-done | bytes 475168 | tf_op jit(solution)/shard_map/ppermute | solution.py:255
  28.3 1.8 %collective-permute-done.5.refs_1_ = bf16[64,3712]{1,0:T(8,128)(2,1)S(1)} collective-permute-done((bf16[64,3712]{1,0:T(8,128)(2,1)S(1)}, bf16[64,3712]{1,0:T(8,128)(2,1)S(1)}, u32[]{:S(2)}, u32[]{:S(2)}) %collective-permute-start.5) | collective-permute-done | bytes 475168 | tf_op jit(solution)/shard_map/ppermute | solution.py:259
  30.1 4.4 %experts.3 = (f32[64,3584]{1,0:T(8,128)S(1)}, bf16[64,3584]{1,0:T(8,128)(2,1)S(1)}) custom-call(bf16[64,3712]{1,0:T(8,128)(2,1)S(1)} %collective-permute-done.2.refs_0_, bf16[64,3712]{1,0:T(8,128)(2,1)S(1)} %collective-permute-done.5.refs_1_, bf16[2,3584,512]{2,1,0:T(8,128)(2,1)S(1)} %get-tuple-element.110.refs_2_, ...), custom_call_target="tpu_custom_call" | custom-call | flops 1048576 | bytes 65536 | tf_op jit(solution)/shard_map/experts/pallas_call | solution.py:222
  34.6 0.2 collective-permute-start.6
  34.8 1.7 %collective-permute-done.6 = bf16[64,3584]{1,0:T(8,128)(2,1)S(1)} collective-permute-done((bf16[64,3584]{1,0:T(8,128)(2,1)S(1)}, bf16[64,3584]{1,0:T(8,128)(2,1)S(1)}, u32[]{:S(2)}, u32[]{:S(2)}) %collective-permute-start.6) | collective-permute-done | bytes 458784 | tf_op jit(solution)/shard_map/ppermute | solution.py:259
  36.6 1.6 %collective-permute-start.7 = (bf16[64,3584]{1,0:T(8,128)(2,1)S(1)}, bf16[64,3584]{1,0:T(8,128)(2,1)S(1)}, u32[]{:S(2)}, u32[]{:S(2)}) collective-permute-start(bf16[64,3584]{1,0:T(8,128)(2,1)S(1)} %add_convert_fusion), channel_id=1, source_target_pairs={{0,2},{1,5},{2,0},{3,7},{4,6},{5,1},{6,4},{7,3},{8,10},{9,13},{10,... | collective-permute-start | bytes 1376264 | tf_op jit(solution)/shard_map/ppermute | solution.py:255
  38.2 2.9 %attention.7.refs_4_ = bf16[8,2,128,512]{3,2,1,0:T(8,128)(2,1)} custom-call(s32[8]{0:T(128)} %refs_0_.4, bf16[8,2,576,128]{3,2,1,0:T(8,128)(2,1)S(1)} %get-tuple-element.134.refs_1_, bf16[8,576,256]{2,1,0:T(8,128)(2,1)S(1)} %get-tuple-element.135.refs_2_, bf16[8,2,576]{2,1,0:T(2,128)(2,1)S(1)} %get-tuple-element.136.refs_3_, ...), custom_call_target="tpu_custom_call", output_to_operand_aliasing={{}: (4, {})} | custom-call | flops 1048576 | bytes 65536 | tf_op jit(solution)/shard_map/attention/pallas_call | solution.py:118
  41.1 4.1 %collective-permute-done.7 = bf16[64,3584]{1,0:T(8,128)(2,1)S(1)} collective-permute-done((bf16[64,3584]{1,0:T(8,128)(2,1)S(1)}, bf16[64,3584]{1,0:T(8,128)(2,1)S(1)}, u32[]{:S(2)}, u32[]{:S(2)}) %collective-permute-start.7) | collective-permute-done | bytes 458784 | tf_op jit(solution)/shard_map/ppermute | solution.py:255
  45.3 1.6 %collective-permute-start.8 = (bf16[32,3584]{1,0:T(8,128)(2,1)S(1)}, bf16[32,3584]{1,0:T(8,128)(2,1)S(1)}, u32[]{:S(2)}, u32[]{:S(2)}) collective-permute-start(bf16[32,3584]{1,0:T(8,128)(2,1)S(1)} %slice.28), channel_id=1, source_target_pairs={{0,4},{1,3},{2,6},{3,1},{4,0},{5,7},{6,2},{7,5},{8,12},{9,11},{10,... | collective-permute-start | bytes 688136 | tf_op jit(solution)/shard_map/ppermute | solution.py:255
  46.9 2.9 %attention.8.refs_4_ = bf16[8,2,128,512]{3,2,1,0:T(8,128)(2,1)} custom-call(s32[8]{0:T(128)} %refs_0_.4, bf16[8,2,576,128]{3,2,1,0:T(8,128)(2,1)S(1)} %get-tuple-element.134.refs_1_, bf16[8,576,256]{2,1,0:T(8,128)(2,1)S(1)} %get-tuple-element.135.refs_2_, bf16[8,2,576]{2,1,0:T(2,128)(2,1)S(1)} %get-tuple-element.136.refs_3_, ...), custom_call_target="tpu_custom_call", output_to_operand_aliasing={{}: (4, {})} | custom-call | flops 1048576 | bytes 65536 | tf_op jit(solution)/shard_map/attention/pallas_call | solution.py:118
  49.9 1.5 %collective-permute-done.8 = bf16[32,3584]{1,0:T(8,128)(2,1)S(1)} collective-permute-done((bf16[32,3584]{1,0:T(8,128)(2,1)S(1)}, bf16[32,3584]{1,0:T(8,128)(2,1)S(1)}, u32[]{:S(2)}, u32[]{:S(2)}) %collective-permute-start.8) | collective-permute-done | bytes 229408 | tf_op jit(solution)/shard_map/ppermute | solution.py:255
  51.5 0.4 collective-permute-start.9
  51.9 2.9 %attention.9 = bf16[8,2,128,512]{3,2,1,0:T(8,128)(2,1)} custom-call(s32[8]{0:T(128)} %refs_0_.4, bf16[8,2,576,128]{3,2,1,0:T(8,128)(2,1)S(1)} %get-tuple-element.134.refs_1_, bf16[8,576,256]{2,1,0:T(8,128)(2,1)S(1)} %get-tuple-element.135.refs_2_, bf16[8,2,576]{2,1,0:T(2,128)(2,1)S(1)} %get-tuple-element.136.refs_3_, ...), custom_call_target="tpu_custom_call", output_to_operand_aliasing={{}: (4, {})} | custom-call | flops 1048576 | bytes 65536 | tf_op jit(solution)/shard_map/attention/pallas_call | solution.py:118
  54.8 3.6 %collective-permute-done.9 = bf16[16,3584]{1,0:T(8,128)(2,1)S(1)} collective-permute-done((bf16[16,3584]{1,0:T(8,128)(2,1)S(1)}, bf16[16,3584]{1,0:T(8,128)(2,1)S(1)}, u32[]{:S(2)}, u32[]{:S(2)}) %collective-permute-start.9) | collective-permute-done | bytes 114720 | tf_op jit(solution)/shard_map/ppermute | solution.py:255
  58.5 0.7 %fusion = bf16[16,3584]{1,0:T(8,128)(2,1)} fusion(f32[32,3584]{1,0:T(8,128)S(1)} %slice_add_fusion, bf16[16,3584]{1,0:T(8,128)(2,1)S(1)} %collective-permute-done.9), kind=kLoop, calls=%fused_computation.5 | loop fusion | flops 172032 | bytes 458752 | tf_op jit(solution)/shard_map/convert_element_type | solution.py:335
  (14 shorter events, 0.5 us)
Async XLA Ops:
  1.8 11.5 %collective-permute-start = (bf16[16,3712]{1,0:T(8,128)(2,1)S(1)}, bf16[16,3712]{1,0:T(8,128)(2,1)S(1)}, u32[]{:S(2)}, u32[]{:S(2)}) collective-permute-start(bf16[16,3712]{1,0:T(8,128)(2,1)S(1)} %route.1), channel_id=1, source_target_pairs={{0,8},{1,9},{2,10},{3,11},{4,12},{5,13},{6,14},{7,15},{8,0},{9,1},... | collective-permute-start | bytes 356360 | tf_op jit(solution)/shard_map/ppermute | solution.py:255
  13.3 6.2 %collective-permute-start.1 = (bf16[32,3712]{1,0:T(8,128)(2,1)S(1)}, bf16[32,3712]{1,0:T(8,128)(2,1)S(1)}, u32[]{:S(2)}, u32[]{:S(2)}) collective-permute-start(bf16[32,3712]{1,0:T(8,128)(2,1)S(1)} %constant_dynamic-update-slice_fusion), channel_id=1, source_target_pairs={{0,4},{1,3},{2,6},{3,1},{4,0},{5,7},{6,2},{7,5},{8,12},{9,11},{10,... | collective-permute-start | bytes 712712 | tf_op jit(solution)/shard_map/ppermute | solution.py:255
  19.5 1.9 %collective-permute-start.3 = (bf16[64,3712]{1,0:T(8,128)(2,1)S(1)}, bf16[64,3712]{1,0:T(8,128)(2,1)S(1)}, u32[]{:S(2)}, u32[]{:S(2)}) collective-permute-start(bf16[64,3712]{1,0:T(8,128)(2,1)S(1)} %constant_dynamic-update-slice_fusion.2.refs_0_), channel_id=1, source_target_pairs={{0,1},{1,0},{2,3},{3,2},{4,5},{5,4},{6,7},{7,6},{8,9},{9,8},{10,11... | collective-permute-start | bytes 1425416 | tf_op jit(solution)/shard_map/ppermute | solution.py:259
  19.6 8.7 %collective-permute-start.2 = (bf16[64,3712]{1,0:T(8,128)(2,1)S(1)}, bf16[64,3712]{1,0:T(8,128)(2,1)S(1)}, u32[]{:S(2)}, u32[]{:S(2)}) collective-permute-start(bf16[64,3712]{1,0:T(8,128)(2,1)S(1)} %constant_dynamic-update-slice_fusion.2.refs_0_), channel_id=1, source_target_pairs={{0,2},{1,5},{2,0},{3,7},{4,6},{5,1},{6,4},{7,3},{8,10},{9,13},{10,... | collective-permute-start | bytes 1425416 | tf_op jit(solution)/shard_map/ppermute | solution.py:255
  28.3 1.8 %collective-permute-start.5 = (bf16[64,3712]{1,0:T(8,128)(2,1)S(1)}, bf16[64,3712]{1,0:T(8,128)(2,1)S(1)}, u32[]{:S(2)}, u32[]{:S(2)}) collective-permute-start(bf16[64,3712]{1,0:T(8,128)(2,1)S(1)} %collective-permute-done.2.refs_0_), channel_id=1, source_target_pairs={{0,1},{1,0},{2,3},{3,2},{4,5},{5,4},{6,7},{7,6},{8,9},{9,8},{10,11... | collective-permute-start | bytes 1425416 | tf_op jit(solution)/shard_map/ppermute | solution.py:259
  34.6 1.9 %collective-permute-start.6 = (bf16[64,3584]{1,0:T(8,128)(2,1)S(1)}, bf16[64,3584]{1,0:T(8,128)(2,1)S(1)}, u32[]{:S(2)}, u32[]{:S(2)}) collective-permute-start(bf16[64,3584]{1,0:T(8,128)(2,1)S(1)} %get-tuple-element.114), channel_id=1, source_target_pairs={{0,1},{1,0},{2,3},{3,2},{4,5},{5,4},{6,7},{7,6},{8,9},{9,8},{10,11... | collective-permute-start | bytes 1376264 | tf_op jit(solution)/shard_map/ppermute | solution.py:259
  36.6 8.5 %collective-permute-start.7 = (bf16[64,3584]{1,0:T(8,128)(2,1)S(1)}, bf16[64,3584]{1,0:T(8,128)(2,1)S(1)}, u32[]{:S(2)}, u32[]{:S(2)}) collective-permute-start(bf16[64,3584]{1,0:T(8,128)(2,1)S(1)} %add_convert_fusion), channel_id=1, source_target_pairs={{0,2},{1,5},{2,0},{3,7},{4,6},{5,1},{6,4},{7,3},{8,10},{9,13},{10,... | collective-permute-start | bytes 1376264 | tf_op jit(solution)/shard_map/ppermute | solution.py:255
  38.2 7.0 %collective-permute-start.4 = (bf16[64,3584]{1,0:T(8,128)(2,1)S(1)}, bf16[64,3584]{1,0:T(8,128)(2,1)S(1)}, u32[]{:S(2)}, u32[]{:S(2)}) collective-permute-start(bf16[64,3584]{1,0:T(8,128)(2,1)S(1)} %get-tuple-element.108), channel_id=1, source_target_pairs={{0,1},{1,0},{2,3},{3,2},{4,5},{5,4},{6,7},{7,6},{8,9},{9,8},{10,11... | collective-permute-start | bytes 1376264 | tf_op jit(solution)/shard_map/ppermute | solution.py:259
  45.3 6.1 %collective-permute-start.8 = (bf16[32,3584]{1,0:T(8,128)(2,1)S(1)}, bf16[32,3584]{1,0:T(8,128)(2,1)S(1)}, u32[]{:S(2)}, u32[]{:S(2)}) collective-permute-start(bf16[32,3584]{1,0:T(8,128)(2,1)S(1)} %slice.28), channel_id=1, source_target_pairs={{0,4},{1,3},{2,6},{3,1},{4,0},{5,7},{6,2},{7,5},{8,12},{9,11},{10,... | collective-permute-start | bytes 688136 | tf_op jit(solution)/shard_map/ppermute | solution.py:255
  51.5 7.0 %collective-permute-start.9 = (bf16[16,3584]{1,0:T(8,128)(2,1)S(1)}, bf16[16,3584]{1,0:T(8,128)(2,1)S(1)}, u32[]{:S(2)}, u32[]{:S(2)}) collective-permute-start(bf16[16,3584]{1,0:T(8,128)(2,1)S(1)} %slice.29), channel_id=1, source_target_pairs={{0,8},{1,9},{2,10},{3,11},{4,12},{5,13},{6,14},{7,15},{8,0},{9,1},... | collective-permute-start | bytes 344072 | tf_op jit(solution)/shard_map/ppermute | solution.py:255

commit v3 on v2

v3 whole, which is shorter than its diff:
```python
import functools

import jax
import jax.numpy as jnp
from jax import lax
from jax.experimental import pallas as pl
from jax.experimental.pallas import tpu as pltpu
from jax.sharding import PartitionSpec as P

LATENT_RANK = 512
SCORE_SCALE = 192.0 ** (-0.5)
ROUTE_SCALE = 2.5
LANES = 128
F32 = jnp.float32
BF16 = jnp.bfloat16
SMALL_COST = pl.CostEstimate(flops=1 << 20, bytes_accessed=1 << 16, transcendentals=0)


def contract(a, b, dim_a, dim_b):
    return lax.dot_general(
        a, b, (((dim_a,), (dim_b,)), ((), ())), preferred_element_type=F32
    )


def attend_request(q_steps, cached, fresh, length):
    heads, context, steps = q_steps[0].shape[1], cached.shape[1], fresh.shape[0]
    q = jnp.concatenate(q_steps, axis=1)
    padded = jnp.concatenate(
        [fresh, jnp.zeros((-steps % 16, fresh.shape[1]), fresh.dtype)], axis=0
    )
    scores = jnp.concatenate([contract(cached, q, 0, 0), contract(padded, q, 1, 0)], axis=0)
    scores = scores * SCORE_SCALE
    key = lax.broadcasted_iota(jnp.int32, scores.shape, 0)
    column = lax.broadcasted_iota(jnp.int32, scores.shape, 1)
    step = key - context
    is_new = jnp.logical_and(step >= 0, jnp.logical_and(step < steps, step * heads <= column))
    is_old = jnp.logical_and(key < context, key < length)
    scores = jnp.where(jnp.logical_or(is_old, is_new), scores, -jnp.inf)
    weights = jnp.exp(scores - jnp.max(scores, axis=0, keepdims=True))
    total = jnp.sum(weights, axis=0, keepdims=True)
    probs = (weights / total).astype(BF16)
    blended = contract(probs[:context], cached[:LATENT_RANK], 0, 1)
    blended = blended + contract(probs[context:], padded[:, :LATENT_RANK], 0, 0)
    return blended.reshape(len(q_steps), heads, LATENT_RANK).astype(BF16)


def attention_kernel(*refs, base, first, count, loads, opening, following):
    length_ref, refs = refs[0], refs[1:]
    sources, refs = refs[:3], refs[3:]
    load_refs, refs = refs[:loads], refs[loads:]
    if following:
        refs = refs[1:]
    out_ref, refs = refs[0], refs[1:]
    if opening:
        resident, refs = refs[:3], refs[3:]
    else:
        resident = sources
    loaded, (result, out_sems, load_sems, in_sems) = refs[:loads], refs[loads:]
    held = resident[0].shape[0]

    needed, copies = [], []
    if opening:
        for lo, hi, group in ((0, first - base + count, 0), (first - base + count, held, 1)):
            if hi == lo:
                continue
            for i in range(3):
                copy = pltpu.make_async_copy(
                    sources[i].at[base + lo : base + hi],
                    resident[i].at[lo:hi],
                    in_sems.at[i, group],
                )
                copy.start()
                (copies if group else needed).append(copy)
    for i, (source, target) in enumerate(zip(load_refs, loaded)):
        copy = pltpu.make_async_copy(source, target, load_sems.at[i])
        copy.start()
        copies.append(copy)
    for copy in needed:
        copy.wait()
    query_ref, cache_ref, new_ref = resident
    steps = query_ref.shape[1]
    for b in range(count):
        r = first - base + b
        result[b] = attend_request(
            [query_ref[r, s] for s in range(steps)], cache_ref[r], new_ref[r], length_ref[first + b]
        )
        copy = pltpu.make_async_copy(result.at[b], out_ref.at[first + b], out_sems.at[b])
        copy.start()
        copies.append(copy)
    for copy in copies:
        copy.wait()


def attention(lengths, inputs, base, first, count, held=0, loads=(), previous=None):
    opening, following = held > 0, previous is not None
    _, steps, latent, heads = inputs[0].shape
    requests = lengths.shape[0]
    vmem = pl.BlockSpec(memory_space=pltpu.VMEM)
    hbm = pl.BlockSpec(memory_space=pl.ANY)
    in_specs = [pl.BlockSpec(memory_space=pltpu.SMEM)]
    in_specs += [hbm if opening else vmem] * 3 + [hbm] * len(loads)
    place = pltpu.HBM if opening else pltpu.VMEM
    operands = [pltpu.with_memory_space_constraint(lengths, pltpu.HBM)]
    operands += [pltpu.with_memory_space_constraint(x, place) for x in inputs]
    operands += [pltpu.with_memory_space_constraint(x, pltpu.HBM) for x in loads]
    aliases = {}
    if following:
        in_specs.append(hbm)
        aliases = {len(operands): 0}
        operands.append(pltpu.with_memory_space_constraint(previous, pltpu.HBM))
    kept = [((held,) + x.shape[1:], x.dtype) for x in inputs] if opening else []
    kept += [(x.shape, x.dtype) for x in loads]
    outs = pl.pallas_call(
        functools.partial(
            attention_kernel,
            base=base,
            first=first,
            count=count,
            loads=len(loads),
            opening=opening,
            following=following,
        ),
        in_specs=in_specs,
        out_specs=[hbm] + [vmem] * len(kept),
        out_shape=[pltpu.HBM((requests, steps, heads, LATENT_RANK), BF16)]
        + [pltpu.VMEM(shape, kind) for shape, kind in kept],
        scratch_shapes=[
            pltpu.VMEM((count, steps, heads, LATENT_RANK), BF16),
            pltpu.SemaphoreType.DMA((count,)),
            pltpu.SemaphoreType.DMA((max(len(loads), 1),)),
            pltpu.SemaphoreType.DMA((3, 2)),
        ],
        input_output_aliases=aliases,
        compiler_params=pltpu.CompilerParams(vmem_limit_bytes=12 << 20),
        cost_estimate=SMALL_COST,
        name="attention",
    )(*operands)
    kept = list(outs[1:])
    if opening:
        return outs[0], kept[:3], kept[3:]
    return outs[0], list(inputs), kept


def route_kernel(place_ref, rows_ref, score_ref, expert_ref, out_ref, *, experts, slots):
    tokens, width = rows_ref.shape
    sigmoid = jax.nn.sigmoid(score_ref[...])
    weights = ROUTE_SCALE * sigmoid / jnp.sum(sigmoid, axis=0, keepdims=True)
    weights = weights.astype(BF16).astype(F32)
    named = expert_ref[...]
    even = lax.broadcasted_iota(jnp.int32, named.shape, 1) % 2 == 0
    slot = jnp.zeros_like(named)
    for e in range(experts):
        slot = jnp.where(
            named == e, jnp.where(even, place_ref[0, e], place_ref[1, e]), slot
        )
    index = lax.broadcasted_iota(jnp.int32, (LANES, tokens), 0)
    table = jnp.zeros((LANES, tokens), F32)
    for k in range(named.shape[0]):
        table = table + jnp.where(index == slot[k : k + 1], weights[k : k + 1], 0.0)
    row = lax.broadcasted_iota(jnp.int32, (tokens, tokens), 0)
    column = lax.broadcasted_iota(jnp.int32, (tokens, tokens), 1)
    unit = jnp.where(row == column, 1.0, 0.0).astype(BF16)
    out_ref[:, :width] = rows_ref[...]
    out_ref[:, width:] = contract(unit, table.astype(BF16), 1, 1).astype(BF16)


def route(placement, rows, scores, expert_ids, slots):
    tokens, width = rows.shape
    vmem = pl.BlockSpec(memory_space=pltpu.VMEM)
    return pl.pallas_call(
        functools.partial(route_kernel, experts=placement.shape[0], slots=slots),
        in_specs=[pl.BlockSpec(memory_space=pltpu.SMEM), vmem, vmem, vmem],
        out_specs=vmem,
        out_shape=jax.ShapeDtypeStruct((tokens, width + LANES), BF16),
        compiler_params=pltpu.CompilerParams(vmem_limit_bytes=4 << 20),
        name="route",
    )(*(pltpu.with_memory_space_constraint(x, pltpu.HBM) for x in (placement.T, rows, scores.T, expert_ids.T)))


def project(act_s, down_ref, own_ref, other_ref, own, first, tile):
    slots, hidden, _ = down_ref.shape

    def step(i, carry):
        source = pl.ds(pl.multiple_of(first + i * tile, LANES), tile)
        target = pl.ds(pl.multiple_of(i * tile, LANES), tile)
        total = contract(act_s[:, :hidden], down_ref[0, :, source], 1, 0)
        for s in range(1, slots):
            total = total + contract(
                act_s[:, s * hidden : (s + 1) * hidden], down_ref[s, :, source], 1, 0
            )
        own_ref[:, target] = total[:own]
        other_ref[:, target] = total[own:].astype(BF16)
        return carry

    lax.fori_loop(0, own_ref.shape[1] // tile, step, 0)


def experts_kernel(*refs, parts, tile, load):
    rows_refs = refs[:parts]
    gate_ref, up_ref, down_ref, chip_ref, own_ref, other_ref, act_s = refs[parts : parts + 7]
    rows_s = refs[-2]
    if load:
        copy = pltpu.make_async_copy(down_ref, refs[parts + 7], refs[-1].at[0])
        copy.start()
        down_ref = refs[parts + 7]
    slots, width, hidden = gate_ref.shape
    start = 0
    for ref in rows_refs:
        rows_s[start : start + ref.shape[0], :] = ref[...]
        start += ref.shape[0]
    table = rows_s[:, width:].astype(F32)
    lane = lax.broadcasted_iota(jnp.int32, table.shape, 1)
    for s in range(slots):
        slot = chip_ref[0] * slots + s
        weight = jnp.sum(jnp.where(lane == slot, table, 0.0), axis=1, keepdims=True)
        rows = rows_s[:, :width]
        gate = contract(rows, gate_ref[s], 1, 0)
        up = contract(rows, up_ref[s], 1, 0)
        act = gate / (1.0 + jnp.exp(-gate)) * up
        act_s[:, s * hidden : (s + 1) * hidden] = (weight * act).astype(BF16)
    if load:
        copy.wait()
    project(act_s, down_ref, own_ref, other_ref, own_ref.shape[0], 0, tile)


def down_kernel(act_ref, down_ref, own_ref, other_ref, *, first, tile):
    project(act_ref, down_ref, own_ref, other_ref, own_ref.shape[0], first, tile)


def experts(parts, gate, up, down, chip, columns, load):
    slots, width, hidden = gate.shape
    count = sum(p.shape[0] for p in parts)
    vmem = pl.BlockSpec(memory_space=pltpu.VMEM)
    down_spec = vmem
    if load:
        down_spec = pl.BlockSpec(memory_space=pl.ANY)
        down = pltpu.with_memory_space_constraint(down, pltpu.HBM)
    return pl.pallas_call(
        functools.partial(experts_kernel, parts=len(parts), tile=width // 4, load=load),
        in_specs=[vmem] * (len(parts) + 2) + [down_spec, pl.BlockSpec(memory_space=pltpu.SMEM)],
        out_specs=[vmem] * (4 if load else 3),
        out_shape=[
            jax.ShapeDtypeStruct((count // 2, columns), F32),
            jax.ShapeDtypeStruct((count // 2, columns), BF16),
            jax.ShapeDtypeStruct((count, slots * hidden), BF16),
        ]
        + ([pltpu.VMEM(down.shape, down.dtype)] if load else []),
        scratch_shapes=[
            pltpu.VMEM((count, parts[0].shape[1]), BF16),
            pltpu.SemaphoreType.DMA((1,)),
        ],
        compiler_params=pltpu.CompilerParams(vmem_limit_bytes=16 << 20),
        cost_estimate=SMALL_COST,
        name="experts",
    )(*parts, gate, up, down, chip)


def down_rest(act, down, first):
    count = act.shape[0]
    width = down.shape[2]
    vmem = pl.BlockSpec(memory_space=pltpu.VMEM)
    return pl.pallas_call(
        functools.partial(down_kernel, first=first, tile=width // 4),
        in_specs=[vmem] * 2,
        out_specs=[vmem] * 2,
        out_shape=[
            jax.ShapeDtypeStruct((count // 2, width - first), F32),
            jax.ShapeDtypeStruct((count // 2, width - first), BF16),
        ],
        compiler_params=pltpu.CompilerParams(vmem_limit_bytes=8 << 20),
        cost_estimate=SMALL_COST,
        name="down",
    )(act, down)


def halving_masks(ep):
    bits = []
    bit = ep // 2
    while bit:
        bits.append(bit)
        bit //= 2
    other = bits[:-2] + bits[-2:][::-1]
    return bits, other


def hop(x, ep, sub, masks, turn):
    pairs = [
        (e * sub + s, (e ^ masks[s % 2][turn]) * sub + s) for e in range(ep) for s in range(sub)
    ]
    return lax.ppermute(x, ("ep", "sub"), pairs)


def swap(x):
    return lax.ppermute(x, "sub", [(0, 1), (1, 0)])


def add(*terms):
    total = terms[0].astype(F32)
    for t in terms[1:]:
        total = total + t.astype(F32)
    return total


def on_device(
    queries,
    latent_cache,
    new_latent,
    lengths,
    moe_input,
    gate_scores,
    expert_ids,
    placement,
    w_gate,
    w_up,
    w_down,
):
    ep, sub = lax.axis_size("ep"), lax.axis_size("sub")
    masks = halving_masks(ep)
    turns = len(masks[0])
    width = moe_input.shape[1]
    requests, width = queries.shape[0], moe_input.shape[1]
    inputs = [queries.transpose(0, 1, 3, 2), latent_cache.transpose(0, 2, 1), new_latent]
    chip = lax.axis_index("ep").astype(jnp.int32)[None]
    slots = ep * w_gate.shape[0]
    barrier = lax.optimization_barrier
    chip, gate_scores, lengths = barrier((chip, gate_scores, lengths))

    requests = queries.shape[0]
    half = width // 2

    base = route(placement, moe_input, gate_scores, expert_ids, slots)
    for turn in range(turns - 2):
        got = hop(base, ep, sub, masks, turn)
        if turn == 0:
            base, inputs = barrier((base, inputs))
            out, _, (gate, up) = attention(lengths, inputs, 0, 0, 2, held=2, loads=(w_gate, w_up))
            got, out, inputs = barrier((got, out, inputs))
        base = jnp.concatenate([base, got], axis=0)

    second = hop(base, ep, sub, masks, turns - 2)
    early = hop(base, ep, sub, masks, turns - 1)
    base, inputs = barrier((base, inputs))
    out, inputs, _ = attention(lengths, inputs, 2, 2, 1, held=requests - 2, previous=out)
    done = 3
    second, out, inputs = barrier((second, out, inputs))
    late = hop(second, ep, sub, masks, turns - 1)
    near_rows = [base, second, swap(base), swap(second)]
    near_rows, early = barrier((near_rows, early))
    early_swap = swap(early)
    near_own, near_other, _, down = experts(near_rows, gate, up, w_down, chip, width, True)
    late, early_swap, near_own, near_other = barrier((late, early_swap, near_own, near_other))
    near_back = swap(near_other)
    own_a, other_a, act = experts(
        [early, late, early_swap, swap(late)], gate, up, down, chip, half, False
    )
    sent_a = add(own_a, swap(other_a)).astype(BF16)
    sent_a, act = barrier((sent_a, act))
    own_b, other_b = down_rest(act, down, half)
    totals = [
        barrier(add(near_own[:, :half], near_back[:, :half])),
        barrier(add(near_own[:, half:], near_back[:, half:])),
    ]
    sent = [sent_a, add(own_b, swap(other_b)).astype(BF16)]
    shares = {turns - 1: 3, 0: requests}
    for turn in range(turns - 1, -1, -1):
        got = [hop(x, ep, sub, masks, turn) for x in sent]
        if turn in shares and done < requests:
            sent, inputs = barrier((sent, inputs))
            count = min(shares[turn], requests - done)
            out, inputs, _ = attention(lengths, inputs, 2, done, count, previous=out)
            done += count
            got[0], out, inputs = barrier((got[0], out, inputs))
        totals = [add(t, g) for t, g in zip(totals, got)]
        if turn:
            keep = totals[0].shape[0] // 2
            sent = [barrier(t[keep:].astype(BF16)) for t in totals]
            totals = [barrier(t[:keep]) for t in totals]
    return out, jnp.concatenate(totals, axis=1).astype(BF16)


def solution(mesh):
    split = ("groups", "ep", "sub")
    return jax.shard_map(
        on_device,
        mesh=mesh,
        in_specs=(
            P(split, None, None, None),
            P(split, None, None),
            P(split, None, None),
            P(split),
            P(split, None),
            P(split, None),
            P(split, None),
            P("groups", None),
            P(("groups", "ep"), None, "sub"),
            P(("groups", "ep"), None, "sub"),
            P(("groups", "ep"), "sub", None),
        ),
        out_specs=(P(split, None, None, None), P(split, None)),
        check_vma=False,
    )
```

time: 59.4 us -> 57.4 us (0.966)
  waiting for transfers between devices: 16 us -> 11.1 us
  starting transfers between devices: 11.1 us -> 15.5 us
  Pallas kernels: 30.2 us -> 28.7 us
    ppermute x6 -> x10, waiting for transfers between devices: 12.2 us -> 7.05 us  [hop(): return lax.ppermute(x, ('ep', 'sub'), pairs)]
    ppermute x6 -> x10, starting transfers between devices: 10.9 us -> 14.1 us  [hop(): return lax.ppermute(x, ('ep', 'sub'), pairs)]
    pallas_call x7, Pallas kernels: 29 us -> 27.6 us  [the longest x4 17.1 us: attention(): pl.pallas_call(functools.partial(attention_kernel, base=base, first=first...]
    ppermute x4 -> x7, starting transfers between devices: 0.26 us -> 1.34 us  [swap(): return lax.ppermute(x, 'sub', [(0, 1), (1, 0)])]
    convert_element_type x2, other arithmetic: 0.77 us -> 0.09 us  [the longest x1 0.05 us: on_device(): sent = [sent_a, add(own_b, swap(other_b)).astype(BF16)]]
    concatenate x0 -> x1, other arithmetic: none -> 0.65 us  [on_device(): return (out, jnp.concatenate(totals, axis=1).astype(BF16))]
    ppermute x4 -> x7, waiting for transfers between devices: 3.78 us -> 4 us  [swap(): return lax.ppermute(x, 'sub', [(0, 1), (1, 0)])]
  transfers between devices with their start and end apart: 10 -> 17, of which waited for: 8 -> 11; matrix products, arithmetic and copies ran while one was open for 0% -> 1% of each run, Pallas kernels for 42% -> 43%
where the time goes in v3:
time: 57.4 us; the launch traced here: 57.2 us
  Pallas kernels  28.7 us (50%)
  starting transfers between devices  15.5 us (27%)
  waiting for transfers between devices  11.1 us (19%)
  other arithmetic  0.98 us (2%)
  between operations  0.83 us (1%)
    pallas_call x4, Pallas kernels, attention(): pl.pallas_call(functools.partial(attention_kernel, base=base, first=first...  17.1 us
    ppermute x10, starting transfers between devices, hop(): return lax.ppermute(x, ('ep', 'sub'), pairs)  14.1 us
    pallas_call x2, Pallas kernels, experts(): pl.pallas_call(functools.partial(experts_kernel, parts=len(parts), tile=w...  9.63 us
    ppermute x10, waiting for transfers between devices, hop(): return lax.ppermute(x, ('ep', 'sub'), pairs)  7.05 us
    ppermute x7, waiting for transfers between devices, swap(): return lax.ppermute(x, 'sub', [(0, 1), (1, 0)])  4 us
    ppermute x7, starting transfers between devices, swap(): return lax.ppermute(x, 'sub', [(0, 1), (1, 0)])  1.34 us
  transfers between devices with their start and end apart: 17, of which 11 were waited for; matrix products, arithmetic and copies ran while one was open for 1% of the time, Pallas kernels for 43%

profile of v3, /device:TPU:0, one launch (start us, length us, event | category | flops | bytes accessed | tf_op | source)
XLA Modules:
  0.0 57.2 jit_solution(1892428671746286534)
XLA Ops:
  0.6 1.1 %route.1 = bf16[16,3712]{1,0:T(8,128)(2,1)S(1)} custom-call(s32[2,14]{1,0:T(2,128)} %bitcast.12, bf16[16,3584]{1,0:T(8,128)(2,1)} %rows_ref.1, f32[8,16]{1,0:T(8,128)} %bitcast.10, s32[8,16]{1,0:T(8,128)} %bitcast.11), custom_call_target="tpu_custom_call" | custom-call | tf_op jit(solution)/shard_map/route/pallas_call | solution.py:170
  1.8 4.0 %collective-permute-start = (bf16[16,3712]{1,0:T(8,128)(2,1)S(1)}, bf16[16,3712]{1,0:T(8,128)(2,1)S(1)}, u32[]{:S(2)}, u32[]{:S(2)}) collective-permute-start(bf16[16,3712]{1,0:T(8,128)(2,1)S(1)} %route.1), channel_id=1, source_target_pairs={{0,8},{1,9},{2,10},{3,11},{4,12},{5,13},{6,14},{7,15},{8,0},{9,1},... | collective-permute-start | bytes 356360 | tf_op jit(solution)/shard_map/ppermute | solution.py:290
  5.8 7.6 %attention.4 = (bf16[8,2,128,512]{3,2,1,0:T(8,128)(2,1)}, bf16[2,2,576,128]{3,2,1,0:T(8,128)(2,1)}, bf16[2,576,256]{2,1,0:T(8,128)(2,1)}, bf16[2,2,576]{2,1,0:T(...) custom-call(s32[8]{0:T(128)} %refs_0_.3, bf16[8,2,576,128]{3,2,1,0:T(8,128)(2,1)} %bitcast.6, ...), custom_call_target="tpu_custom_call" | custom-call | flops 1048576 | bytes 65536 | tf_op jit(solution)/shard_map/attention/pallas_call | solution.py:113
  13.4 1.6 %collective-permute-start.1 = (bf16[32,3712]{1,0:T(8,128)(2,1)S(1)}, bf16[32,3712]{1,0:T(8,128)(2,1)S(1)}, u32[]{:S(2)}, u32[]{:S(2)}) collective-permute-start(bf16[32,3712]{1,0:T(8,128)(2,1)S(1)} %constant_dynamic-update-slice_fusion.refs_0_), channel_id=1, source_target_pairs={{0,4},{1,3},{2,6},{3,1},{4,0},{5,7},{6,2},{7,5},{8,12},{9,11},{10,... | collective-permute-start | bytes 712712 | tf_op jit(solution)/shard_map/ppermute | solution.py:290
  15.1 1.5 %collective-permute-start.5 = (bf16[32,3712]{1,0:T(8,128)(2,1)S(1)}, bf16[32,3712]{1,0:T(8,128)(2,1)S(1)}, u32[]{:S(2)}, u32[]{:S(2)}) collective-permute-start(bf16[32,3712]{1,0:T(8,128)(2,1)S(1)} %constant_dynamic-update-slice_fusion.refs_0_), channel_id=1, source_target_pairs={{0,2},{1,5},{2,0},{3,7},{4,6},{5,1},{6,4},{7,3},{8,10},{9,13},{10,... | collective-permute-start | bytes 712712 | tf_op jit(solution)/shard_map/ppermute | solution.py:290
  16.6 3.3 %attention.5 = (bf16[8,2,128,512]{3,2,1,0:T(8,128)(2,1)}, bf16[6,2,576,128]{3,2,1,0:T(8,128)(2,1)S(1)}, bf16[6,576,256]{2,1,0:T(8,128)(2,1)S(1)}, bf16[6,2,576]{2,1,0:T(2,128)(2,1)S(1)}) custom-call(s32[8]{0:T(128)} %refs_0_.3, bf16[8,2,576,128]{3,2,1,0:T(8,128)(2,1)} %bitcast.7, bf16[8,576,256]{2,1,0:T(8,128)(2,1)} %bitcast.9, ...), custom_call_target="tpu_custom_call", output_to_operand_aliasing={{0}: (4, {})} | custom-call | flops 1048576 | bytes 65536 | tf_op jit(solution)/shard_map/attention/pallas_call | solution.py:113
  19.9 2.0 %collective-permute-done.1.refs_1_ = bf16[32,3712]{1,0:T(8,128)(2,1)S(1)} collective-permute-done((bf16[32,3712]{1,0:T(8,128)(2,1)S(1)}, bf16[32,3712]{1,0:T(8,128)(2,1)S(1)}, u32[]{:S(2)}, u32[]{:S(2)}) %collective-permute-start.1) | collective-permute-done | bytes 237600 | tf_op jit(solution)/shard_map/ppermute | solution.py:290
  22.5 1.0 %collective-permute-done.4.refs_3_ = bf16[32,3712]{1,0:T(8,128)(2,1)S(1)} collective-permute-done((bf16[32,3712]{1,0:T(8,128)(2,1)S(1)}, bf16[32,3712]{1,0:T(8,128)(2,1)S(1)}, u32[]{:S(2)}, u32[]{:S(2)}) %collective-permute-start.4) | collective-permute-done | bytes 237600 | tf_op jit(solution)/shard_map/ppermute | solution.py:294
  23.8 6.5 %experts.2 = (f32[64,3584]{1,0:T(8,128)S(1)}, bf16[64,3584]{1,0:T(8,128)(2,1)S(1)}, bf16[128,1024]{1,0:T(8,128)(2,1)}, bf16[2,512,3584]{2,1,0:T(8,128)(2,1)S(1)}) custom-call(bf16[32,3712]{1,0:T(8,128)(2,1)S(1)} %constant_dynamic-update-slice_fusion.refs_0_, bf16[32,3712]{1,0:T(8,128)(2,1)S(1)} %collective-permute-done.1.refs_1_, ...), custom_call_target="tpu_custom_call" | custom-call | flops 1048576 | bytes 65536 | tf_op jit(solution)/shard_map/experts/pallas_call | solution.py:238
  30.5 1.4 %collective-permute-done.8.refs_3_ = bf16[32,3712]{1,0:T(8,128)(2,1)S(1)} collective-permute-done((bf16[32,3712]{1,0:T(8,128)(2,1)S(1)}, bf16[32,3712]{1,0:T(8,128)(2,1)S(1)}, u32[]{:S(2)}, u32[]{:S(2)}) %collective-permute-start.8) | collective-permute-done | bytes 237600 | tf_op jit(solution)/shard_map/ppermute | solution.py:294
  31.9 3.1 %experts.3 = (f32[64,1792]{1,0:T(8,128)S(1)}, bf16[64,1792]{1,0:T(8,128)(2,1)S(1)}, bf16[128,1024]{1,0:T(8,128)(2,1)S(1)}) custom-call(bf16[32,3712]{1,0:T(8,128)(2,1)S(1)} %collective-permute-done.5.refs_0_, bf16[32,3712]{1,0:T(8,128)(2,1)S(1)} %collective-permute-done.2.refs_1_, bf16[32,3712]{1,0:T(8,128)(2,1)S(1)} %collective-permute-done.6.refs_2_, ...), custom_call_target="tpu_custom_call" | custom-call | flops 1048576 | bytes 65536 | tf_op jit(solution)/shard_map/experts/pallas_call | solution.py:238
  35.7 1.0 %collective-permute-done.9 = bf16[64,1792]{1,0:T(8,128)(2,1)S(1)} collective-permute-done((bf16[64,1792]{1,0:T(8,128)(2,1)S(1)}, bf16[64,1792]{1,0:T(8,128)(2,1)S(1)}, u32[]{:S(2)}, u32[]{:S(2)}) %collective-permute-start.9) | collective-permute-done | bytes 229408 | tf_op jit(solution)/shard_map/ppermute | solution.py:294
  36.7 0.9 %down.1 = (f32[64,1792]{1,0:T(8,128)S(1)}, bf16[64,1792]{1,0:T(8,128)(2,1)S(1)}) custom-call(bf16[128,1024]{1,0:T(8,128)(2,1)S(1)} %get-tuple-element.102.act_ref, bf16[2,512,3584]{2,1,0:T(8,128)(2,1)S(1)} %get-tuple-element.97.refs_6_.down_ref), custom_call_target="tpu_custom_call" | custom-call | flops 1048576 | bytes 65536 | tf_op jit(solution)/shard_map/down/pallas_call | solution.py:262
  39.2 0.9 %collective-permute-start.14 = (bf16[64,1792]{1,0:T(8,128)(2,1)S(1)}, bf16[64,1792]{1,0:T(8,128)(2,1)S(1)}, u32[]{:S(2)}, u32[]{:S(2)}) collective-permute-start(bf16[64,1792]{1,0:T(8,128)(2,1)S(1)} %add_convert_fusion), channel_id=1, source_target_pairs={{0,2},{1,5},{2,0},{3,7},{4,6},{5,1},{6,4},{7,3},{8,10},{9,13},{10,... | collective-permute-start | bytes 688136 | tf_op jit(solution)/shard_map/ppermute | solution.py:290
  40.1 3.4 %attention.6.refs_4_ = bf16[8,2,128,512]{3,2,1,0:T(8,128)(2,1)} custom-call(s32[8]{0:T(128)} %refs_0_.3, bf16[6,2,576,128]{3,2,1,0:T(8,128)(2,1)S(1)} %get-tuple-element.116.refs_1_, bf16[6,576,256]{2,1,0:T(8,128)(2,1)S(1)} %get-tuple-element.117.refs_2_, bf16[6,2,576]{2,1,0:T(2,128)(2,1)S(1)} %get-tuple-element.118.refs_3_, ...), custom_call_target="tpu_custom_call", output_to_operand_aliasing={{}: (4, {})} | custom-call | flops 1048576 | bytes 65536 | tf_op jit(solution)/shard_map/attention/pallas_call | solution.py:113
  44.1 1.6 %collective-permute-start.12 = (bf16[32,1792]{1,0:T(8,128)(2,1)S(1)}, bf16[32,1792]{1,0:T(8,128)(2,1)S(1)}, u32[]{:S(2)}, u32[]{:S(2)}) collective-permute-start(bf16[32,1792]{1,0:T(8,128)(2,1)S(1)} %slice.71), channel_id=1, source_target_pairs={{0,4},{1,3},{2,6},{3,1},{4,0},{5,7},{6,2},{7,5},{8,12},{9,11},{10,... | collective-permute-start | bytes 344072 | tf_op jit(solution)/shard_map/ppermute | solution.py:290
  45.7 0.8 %collective-permute-done.14 = bf16[64,1792]{1,0:T(8,128)(2,1)S(1)} collective-permute-done((bf16[64,1792]{1,0:T(8,128)(2,1)S(1)}, bf16[64,1792]{1,0:T(8,128)(2,1)S(1)}, u32[]{:S(2)}, u32[]{:S(2)}) %collective-permute-start.14) | collective-permute-done | bytes 229408 | tf_op jit(solution)/shard_map/ppermute | solution.py:290
  46.5 1.9 %collective-permute-start.15 = (bf16[32,1792]{1,0:T(8,128)(2,1)S(1)}, bf16[32,1792]{1,0:T(8,128)(2,1)S(1)}, u32[]{:S(2)}, u32[]{:S(2)}) collective-permute-start(bf16[32,1792]{1,0:T(8,128)(2,1)S(1)} %slice.70), channel_id=1, source_target_pairs={{0,4},{1,3},{2,6},{3,1},{4,0},{5,7},{6,2},{7,5},{8,12},{9,11},{10,... | collective-permute-start | bytes 344072 | tf_op jit(solution)/shard_map/ppermute | solution.py:290
  49.6 1.7 %collective-permute-done.15 = bf16[32,1792]{1,0:T(8,128)(2,1)S(1)} collective-permute-done((bf16[32,1792]{1,0:T(8,128)(2,1)S(1)}, bf16[32,1792]{1,0:T(8,128)(2,1)S(1)}, u32[]{:S(2)}, u32[]{:S(2)}) %collective-permute-start.15) | collective-permute-done | bytes 114720 | tf_op jit(solution)/shard_map/ppermute | solution.py:290
  51.4 0.7 %collective-permute-start.16 = (bf16[16,1792]{1,0:T(8,128)(2,1)S(1)}, bf16[16,1792]{1,0:T(8,128)(2,1)S(1)}, u32[]{:S(2)}, u32[]{:S(2)}) collective-permute-start(bf16[16,1792]{1,0:T(8,128)(2,1)S(1)} %slice.72), channel_id=1, source_target_pairs={{0,8},{1,9},{2,10},{3,11},{4,12},{5,13},{6,14},{7,15},{8,0},{9,1},... | collective-permute-start | bytes 172040 | tf_op jit(solution)/shard_map/ppermute | solution.py:290
  52.1 2.8 %attention.7 = bf16[8,2,128,512]{3,2,1,0:T(8,128)(2,1)} custom-call(s32[8]{0:T(128)} %refs_0_.3, bf16[6,2,576,128]{3,2,1,0:T(8,128)(2,1)S(1)} %get-tuple-element.116.refs_1_, bf16[6,576,256]{2,1,0:T(8,128)(2,1)S(1)} %get-tuple-element.117.refs_2_, bf16[6,2,576]{2,1,0:T(2,128)(2,1)S(1)} %get-tuple-element.118.refs_3_, ...), custom_call_target="tpu_custom_call", output_to_operand_aliasing={{}: (4, {})} | custom-call | flops 1048576 | bytes 65536 | tf_op jit(solution)/shard_map/attention/pallas_call | solution.py:113
  54.9 0.9 %collective-permute-done.13 = bf16[16,1792]{1,0:T(8,128)(2,1)S(1)} collective-permute-done((bf16[16,1792]{1,0:T(8,128)(2,1)S(1)}, bf16[16,1792]{1,0:T(8,128)(2,1)S(1)}, u32[]{:S(2)}, u32[]{:S(2)}) %collective-permute-start.13) | collective-permute-done | bytes 57376 | tf_op jit(solution)/shard_map/ppermute | solution.py:290
  55.8 0.7 %collective-permute-done.16 = bf16[16,1792]{1,0:T(8,128)(2,1)S(1)} collective-permute-done((bf16[16,1792]{1,0:T(8,128)(2,1)S(1)}, bf16[16,1792]{1,0:T(8,128)(2,1)S(1)}, u32[]{:S(2)}, u32[]{:S(2)}) %collective-permute-start.16) | collective-permute-done | bytes 57376 | tf_op jit(solution)/shard_map/ppermute | solution.py:290
  56.5 0.7 %pad_maximum_fusion = bf16[16,3584]{1,0:T(8,128)(2,1)} fusion(bf16[16,1792]{1,0:T(8,128)(2,1)S(1)} %add_convert_fusion.2, bf16[16,1792]{1,0:T(8,128)(2,1)S(1)} %add_convert_fusion.3), kind=kLoop, calls=%fused_computation.12 | loop fusion | flops 229376 | bytes 229376 | tf_op jit(solution)/shard_map/concatenate | solution.py:378
  (38 shorter events, 5.2 us)
Async XLA Ops:
  1.8 11.6 %collective-permute-start = (bf16[16,3712]{1,0:T(8,128)(2,1)S(1)}, bf16[16,3712]{1,0:T(8,128)(2,1)S(1)}, u32[]{:S(2)}, u32[]{:S(2)}) collective-permute-start(bf16[16,3712]{1,0:T(8,128)(2,1)S(1)} %route.1), channel_id=1, source_target_pairs={{0,8},{1,9},{2,10},{3,11},{4,12},{5,13},{6,14},{7,15},{8,0},{9,1},... | collective-permute-start | bytes 356360 | tf_op jit(solution)/shard_map/ppermute | solution.py:290
  13.4 8.5 %collective-permute-start.1 = (bf16[32,3712]{1,0:T(8,128)(2,1)S(1)}, bf16[32,3712]{1,0:T(8,128)(2,1)S(1)}, u32[]{:S(2)}, u32[]{:S(2)}) collective-permute-start(bf16[32,3712]{1,0:T(8,128)(2,1)S(1)} %constant_dynamic-update-slice_fusion.refs_0_), channel_id=1, source_target_pairs={{0,4},{1,3},{2,6},{3,1},{4,0},{5,7},{6,2},{7,5},{8,12},{9,11},{10,... | collective-permute-start | bytes 712712 | tf_op jit(solution)/shard_map/ppermute | solution.py:290
  15.1 7.4 %collective-permute-start.5 = (bf16[32,3712]{1,0:T(8,128)(2,1)S(1)}, bf16[32,3712]{1,0:T(8,128)(2,1)S(1)}, u32[]{:S(2)}, u32[]{:S(2)}) collective-permute-start(bf16[32,3712]{1,0:T(8,128)(2,1)S(1)} %constant_dynamic-update-slice_fusion.refs_0_), channel_id=1, source_target_pairs={{0,2},{1,5},{2,0},{3,7},{4,6},{5,1},{6,4},{7,3},{8,10},{9,13},{10,... | collective-permute-start | bytes 712712 | tf_op jit(solution)/shard_map/ppermute | solution.py:290
  16.6 5.9 %collective-permute-start.3 = (bf16[32,3712]{1,0:T(8,128)(2,1)S(1)}, bf16[32,3712]{1,0:T(8,128)(2,1)S(1)}, u32[]{:S(2)}, u32[]{:S(2)}) collective-permute-start(bf16[32,3712]{1,0:T(8,128)(2,1)S(1)} %constant_dynamic-update-slice_fusion.refs_0_), channel_id=1, source_target_pairs={{0,1},{1,0},{2,3},{3,2},{4,5},{5,4},{6,7},{7,6},{8,9},{9,8},{10,11... | collective-permute-start | bytes 712712 | tf_op jit(solution)/shard_map/ppermute | solution.py:294
  22.0 1.5 %collective-permute-start.4 = (bf16[32,3712]{1,0:T(8,128)(2,1)S(1)}, bf16[32,3712]{1,0:T(8,128)(2,1)S(1)}, u32[]{:S(2)}, u32[]{:S(2)}) collective-permute-start(bf16[32,3712]{1,0:T(8,128)(2,1)S(1)} %collective-permute-done.1.refs_1_), channel_id=1, source_target_pairs={{0,1},{1,0},{2,3},{3,2},{4,5},{5,4},{6,7},{7,6},{8,9},{9,8},{10,11... | collective-permute-start | bytes 712712 | tf_op jit(solution)/shard_map/ppermute | solution.py:294
  22.0 8.4 %collective-permute-start.2 = (bf16[32,3712]{1,0:T(8,128)(2,1)S(1)}, bf16[32,3712]{1,0:T(8,128)(2,1)S(1)}, u32[]{:S(2)}, u32[]{:S(2)}) collective-permute-start(bf16[32,3712]{1,0:T(8,128)(2,1)S(1)} %collective-permute-done.1.refs_1_), channel_id=1, source_target_pairs={{0,2},{1,5},{2,0},{3,7},{4,6},{5,1},{6,4},{7,3},{8,10},{9,13},{10,... | collective-permute-start | bytes 712712 | tf_op jit(solution)/shard_map/ppermute | solution.py:290
  23.5 6.9 %collective-permute-start.6 = (bf16[32,3712]{1,0:T(8,128)(2,1)S(1)}, bf16[32,3712]{1,0:T(8,128)(2,1)S(1)}, u32[]{:S(2)}, u32[]{:S(2)}) collective-permute-start(bf16[32,3712]{1,0:T(8,128)(2,1)S(1)} %collective-permute-done.5.refs_0_), channel_id=1, source_target_pairs={{0,1},{1,0},{2,3},{3,2},{4,5},{5,4},{6,7},{7,6},{8,9},{9,8},{10,11... | collective-permute-start | bytes 712712 | tf_op jit(solution)/shard_map/ppermute | solution.py:294
  30.4 1.6 %collective-permute-start.8 = (bf16[32,3712]{1,0:T(8,128)(2,1)S(1)}, bf16[32,3712]{1,0:T(8,128)(2,1)S(1)}, u32[]{:S(2)}, u32[]{:S(2)}) collective-permute-start(bf16[32,3712]{1,0:T(8,128)(2,1)S(1)} %collective-permute-done.2.refs_1_), channel_id=1, source_target_pairs={{0,1},{1,0},{2,3},{3,2},{4,5},{5,4},{6,7},{7,6},{8,9},{9,8},{10,11... | collective-permute-start | bytes 712712 | tf_op jit(solution)/shard_map/ppermute | solution.py:294
  35.1 1.6 %collective-permute-start.9 = (bf16[64,1792]{1,0:T(8,128)(2,1)S(1)}, bf16[64,1792]{1,0:T(8,128)(2,1)S(1)}, u32[]{:S(2)}, u32[]{:S(2)}) collective-permute-start(bf16[64,1792]{1,0:T(8,128)(2,1)S(1)} %get-tuple-element.99), channel_id=1, source_target_pairs={{0,1},{1,0},{2,3},{3,2},{4,5},{5,4},{6,7},{7,6},{8,9},{9,8},{10,11... | collective-permute-start | bytes 688136 | tf_op jit(solution)/shard_map/ppermute | solution.py:294
  35.3 2.5 %collective-permute-start.7 = (bf16[64,3584]{1,0:T(8,128)(2,1)S(1)}, bf16[64,3584]{1,0:T(8,128)(2,1)S(1)}, u32[]{:S(2)}, u32[]{:S(2)}) collective-permute-start(bf16[64,3584]{1,0:T(8,128)(2,1)S(1)} %get-tuple-element.94), channel_id=1, source_target_pairs={{0,1},{1,0},{2,3},{3,2},{4,5},{5,4},{6,7},{7,6},{8,9},{9,8},{10,11... | collective-permute-start | bytes 1376264 | tf_op jit(solution)/shard_map/ppermute | solution.py:294
  37.6 1.6 %collective-permute-start.11 = (bf16[64,1792]{1,0:T(8,128)(2,1)S(1)}, bf16[64,1792]{1,0:T(8,128)(2,1)S(1)}, u32[]{:S(2)}, u32[]{:S(2)}) collective-permute-start(bf16[64,1792]{1,0:T(8,128)(2,1)S(1)} %get-tuple-element.104), channel_id=1, source_target_pairs={{0,1},{1,0},{2,3},{3,2},{4,5},{5,4},{6,7},{7,6},{8,9},{9,8},{10,11... | collective-permute-start | bytes 688136 | tf_op jit(solution)/shard_map/ppermute | solution.py:294
  37.9 6.1 %collective-permute-start.10 = (bf16[64,1792]{1,0:T(8,128)(2,1)S(1)}, bf16[64,1792]{1,0:T(8,128)(2,1)S(1)}, u32[]{:S(2)}, u32[]{:S(2)}) collective-permute-start(bf16[64,1792]{1,0:T(8,128)(2,1)S(1)} %add_convert_fusion.1), channel_id=1, source_target_pairs={{0,2},{1,5},{2,0},{3,7},{4,6},{5,1},{6,4},{7,3},{8,10},{9,13},{10,... | collective-permute-start | bytes 688136 | tf_op jit(solution)/shard_map/ppermute | solution.py:290
  39.2 7.2 %collective-permute-start.14 = (bf16[64,1792]{1,0:T(8,128)(2,1)S(1)}, bf16[64,1792]{1,0:T(8,128)(2,1)S(1)}, u32[]{:S(2)}, u32[]{:S(2)}) collective-permute-start(bf16[64,1792]{1,0:T(8,128)(2,1)S(1)} %add_convert_fusion), channel_id=1, source_target_pairs={{0,2},{1,5},{2,0},{3,7},{4,6},{5,1},{6,4},{7,3},{8,10},{9,13},{10,... | collective-permute-start | bytes 688136 | tf_op jit(solution)/shard_map/ppermute | solution.py:290
  44.1 4.9 %collective-permute-start.12 = (bf16[32,1792]{1,0:T(8,128)(2,1)S(1)}, bf16[32,1792]{1,0:T(8,128)(2,1)S(1)}, u32[]{:S(2)}, u32[]{:S(2)}) collective-permute-start(bf16[32,1792]{1,0:T(8,128)(2,1)S(1)} %slice.71), channel_id=1, source_target_pairs={{0,4},{1,3},{2,6},{3,1},{4,0},{5,7},{6,2},{7,5},{8,12},{9,11},{10,... | collective-permute-start | bytes 344072 | tf_op jit(solution)/shard_map/ppermute | solution.py:290
  46.5 4.9 %collective-permute-start.15 = (bf16[32,1792]{1,0:T(8,128)(2,1)S(1)}, bf16[32,1792]{1,0:T(8,128)(2,1)S(1)}, u32[]{:S(2)}, u32[]{:S(2)}) collective-permute-start(bf16[32,1792]{1,0:T(8,128)(2,1)S(1)} %slice.70), channel_id=1, source_target_pairs={{0,4},{1,3},{2,6},{3,1},{4,0},{5,7},{6,2},{7,5},{8,12},{9,11},{10,... | collective-permute-start | bytes 344072 | tf_op jit(solution)/shard_map/ppermute | solution.py:290
  49.0 6.8 %collective-permute-start.13 = (bf16[16,1792]{1,0:T(8,128)(2,1)S(1)}, bf16[16,1792]{1,0:T(8,128)(2,1)S(1)}, u32[]{:S(2)}, u32[]{:S(2)}) collective-permute-start(bf16[16,1792]{1,0:T(8,128)(2,1)S(1)} %slice.73), channel_id=1, source_target_pairs={{0,8},{1,9},{2,10},{3,11},{4,12},{5,13},{6,14},{7,15},{8,0},{9,1},... | collective-permute-start | bytes 172040 | tf_op jit(solution)/shard_map/ppermute | solution.py:290
  51.4 5.1 %collective-permute-start.16 = (bf16[16,1792]{1,0:T(8,128)(2,1)S(1)}, bf16[16,1792]{1,0:T(8,128)(2,1)S(1)}, u32[]{:S(2)}, u32[]{:S(2)}) collective-permute-start(bf16[16,1792]{1,0:T(8,128)(2,1)S(1)} %slice.72), channel_id=1, source_target_pairs={{0,8},{1,9},{2,10},{3,11},{4,12},{5,13},{6,14},{7,15},{8,0},{9,1},... | collective-permute-start | bytes 172040 | tf_op jit(solution)/shard_map/ppermute | solution.py:290

commit v4 on v3

--- a/solution.py
+++ b/solution.py
@@ -132,7 +132,9 @@
         ],
         input_output_aliases=aliases,
         compiler_params=pltpu.CompilerParams(vmem_limit_bytes=12 << 20),
-        cost_estimate=SMALL_COST,
+        cost_estimate=pl.CostEstimate(flops=1 << 32, bytes_accessed=1 << 23, transcendentals=0)
+        if opening
+        else SMALL_COST,
         name="attention",
     )(*operands)
     kept = list(outs[1:])
@@ -177,8 +179,9 @@
     )(*(pltpu.with_memory_space_constraint(x, pltpu.HBM) for x in (placement.T, rows, scores.T, expert_ids.T)))
 
 
-def project(act_s, down_ref, own_ref, other_ref, own, first, tile):
+def project(act_s, down_ref, own_ref, other_ref, first, tile):
     slots, hidden, _ = down_ref.shape
+    own = own_ref.shape[0]
 
     def step(i, carry):
         source = pl.ds(pl.multiple_of(first + i * tile, LANES), tile)
@@ -195,14 +198,10 @@
     lax.fori_loop(0, own_ref.shape[1] // tile, step, 0)
 
 
-def experts_kernel(*refs, parts, tile, load):
-    rows_refs = refs[:parts]
-    gate_ref, up_ref, down_ref, chip_ref, own_ref, other_ref, act_s = refs[parts : parts + 7]
-    rows_s = refs[-2]
-    if load:
-        copy = pltpu.make_async_copy(down_ref, refs[parts + 7], refs[-1].at[0])
-        copy.start()
-        down_ref = refs[parts + 7]
+def experts_kernel(*refs, parts, cuts, tile):
+    rows_refs, refs = refs[:parts], refs[parts:]
+    (gate_ref, up_ref, down_ref, chip_ref), refs = refs[:4], refs[4:]
+    own_refs, other_refs, (rows_s, act_s) = refs[:cuts], refs[cuts : 2 * cuts], refs[2 * cuts :]
     slots, width, hidden = gate_ref.shape
     start = 0
     for ref in rows_refs:
@@ -218,59 +217,30 @@
         up = contract(rows, up_ref[s], 1, 0)
         act = gate / (1.0 + jnp.exp(-gate)) * up
         act_s[:, s * hidden : (s + 1) * hidden] = (weight * act).astype(BF16)
-    if load:
-        copy.wait()
-    project(act_s, down_ref, own_ref, other_ref, own_ref.shape[0], 0, tile)
-
-
-def down_kernel(act_ref, down_ref, own_ref, other_ref, *, first, tile):
-    project(act_ref, down_ref, own_ref, other_ref, own_ref.shape[0], first, tile)
-
-
-def experts(parts, gate, up, down, chip, columns, load):
+    for i, (own_ref, other_ref) in enumerate(zip(own_refs, other_refs)):
+        project(act_s, down_ref, own_ref, other_ref, i * own_ref.shape[1], tile)
+
+
+def experts(parts, gate, up, down, chip, cuts):
     slots, width, hidden = gate.shape
     count = sum(p.shape[0] for p in parts)
     vmem = pl.BlockSpec(memory_space=pltpu.VMEM)
-    down_spec = vmem
-    if load:
-        down_spec = pl.BlockSpec(memory_space=pl.ANY)
-        down = pltpu.with_memory_space_constraint(down, pltpu.HBM)
-    return pl.pallas_call(
-        functools.partial(experts_kernel, parts=len(parts), tile=width // 4, load=load),
-        in_specs=[vmem] * (len(parts) + 2) + [down_spec, pl.BlockSpec(memory_space=pltpu.SMEM)],
-        out_specs=[vmem] * (4 if load else 3),
-        out_shape=[
-            jax.ShapeDtypeStruct((count // 2, columns), F32),
-            jax.ShapeDtypeStruct((count // 2, columns), BF16),
-            jax.ShapeDtypeStruct((count, slots * hidden), BF16),
-        ]
-        + ([pltpu.VMEM(down.shape, down.dtype)] if load else []),
+    shape = (count // 2, width // cuts)
+    outs = pl.pallas_call(
+        functools.partial(experts_kernel, parts=len(parts), cuts=cuts, tile=width // 4),
+        in_specs=[vmem] * (len(parts) + 3) + [pl.BlockSpec(memory_space=pltpu.SMEM)],
+        out_specs=[vmem] * (2 * cuts),
+        out_shape=[jax.ShapeDtypeStruct(shape, F32)] * cuts
+        + [jax.ShapeDtypeStruct(shape, BF16)] * cuts,
         scratch_shapes=[
             pltpu.VMEM((count, parts[0].shape[1]), BF16),
-            pltpu.SemaphoreType.DMA((1,)),
+            pltpu.VMEM((count, slots * hidden), BF16),
         ],
         compiler_params=pltpu.CompilerParams(vmem_limit_bytes=16 << 20),
         cost_estimate=SMALL_COST,
         name="experts",
     )(*parts, gate, up, down, chip)
-
-
-def down_rest(act, down, first):
-    count = act.shape[0]
-    width = down.shape[2]
-    vmem = pl.BlockSpec(memory_space=pltpu.VMEM)
-    return pl.pallas_call(
-        functools.partial(down_kernel, first=first, tile=width // 4),
-        in_specs=[vmem] * 2,
-        out_specs=[vmem] * 2,
-        out_shape=[
-            jax.ShapeDtypeStruct((count // 2, width - first), F32),
-            jax.ShapeDtypeStruct((count // 2, width - first), BF16),
-        ],
-        compiler_params=pltpu.CompilerParams(vmem_limit_bytes=8 << 20),
-        cost_estimate=SMALL_COST,
-        name="down",
-    )(act, down)
+    return outs[:cuts], outs[cuts:]
 
 
 def halving_masks(ep):
@@ -327,40 +297,37 @@
 
     requests = queries.shape[0]
     half = width // 2
+    gate, up, down = [pltpu.with_memory_space_constraint(w, pltpu.VMEM) for w in (w_gate, w_up, w_down)]
 
     base = route(placement, moe_input, gate_scores, expert_ids, slots)
     for turn in range(turns - 2):
         got = hop(base, ep, sub, masks, turn)
         if turn == 0:
             base, inputs = barrier((base, inputs))
-            out, _, (gate, up) = attention(lengths, inputs, 0, 0, 2, held=2, loads=(w_gate, w_up))
+            out, _, _ = attention(lengths, inputs, 0, 0, 2, held=2, loads=())
             got, out, inputs = barrier((got, out, inputs))
         base = jnp.concatenate([base, got], axis=0)
 
     second = hop(base, ep, sub, masks, turns - 2)
-    early = hop(base, ep, sub, masks, turns - 1)
     base, inputs = barrier((base, inputs))
     out, inputs, _ = attention(lengths, inputs, 2, 2, 1, held=requests - 2, previous=out)
     done = 3
+    base_late, out = barrier((base, out))
+    early = hop(base_late, ep, sub, masks, turns - 1)
     second, out, inputs = barrier((second, out, inputs))
     late = hop(second, ep, sub, masks, turns - 1)
     near_rows = [base, second, swap(base), swap(second)]
     near_rows, early = barrier((near_rows, early))
     early_swap = swap(early)
-    near_own, near_other, _, down = experts(near_rows, gate, up, w_down, chip, width, True)
+    near_own, (near_other,) = experts(near_rows, gate, up, down, chip, 1)
     late, early_swap, near_own, near_other = barrier((late, early_swap, near_own, near_other))
     near_back = swap(near_other)
-    own_a, other_a, act = experts(
-        [early, late, early_swap, swap(late)], gate, up, down, chip, half, False
-    )
-    sent_a = add(own_a, swap(other_a)).astype(BF16)
-    sent_a, act = barrier((sent_a, act))
-    own_b, other_b = down_rest(act, down, half)
+    own, other = experts([early, late, early_swap, swap(late)], gate, up, down, chip, 2)
+    sent = [add(x, swap(y)).astype(BF16) for x, y in zip(own, other)]
     totals = [
-        barrier(add(near_own[:, :half], near_back[:, :half])),
-        barrier(add(near_own[:, half:], near_back[:, half:])),
+        barrier(add(near_own[0][:, :half], near_back[:, :half])),
+        barrier(add(near_own[0][:, half:], near_back[:, half:])),
     ]
-    sent = [sent_a, add(own_b, swap(other_b)).astype(BF16)]
     shares = {turns - 1: 3, 0: requests}
     for turn in range(turns - 1, -1, -1):
         got = [hop(x, ep, sub, masks, turn) for x in sent]

time: 57.4 us -> 56.8 us (0.990)
  Pallas kernels: 28.7 us -> 25.3 us
  starting transfers between devices: 15.5 us -> 16.9 us
  waiting for transfers between devices: 11.1 us -> 12.3 us
    ppermute x10, waiting for transfers between devices: 7.05 us -> 9.72 us  [hop(): return lax.ppermute(x, ('ep', 'sub'), pairs)]
    pallas_call x3 -> x2, Pallas kernels: 10.5 us -> 8.07 us  [experts(): pl.pallas_call(functools.partial(experts_kernel, parts=len(parts), cuts=c...]
    ppermute x10, starting transfers between devices: 14.1 us -> 15.7 us  [hop(): return lax.ppermute(x, ('ep', 'sub'), pairs)]
    ppermute x7, waiting for transfers between devices: 4 us -> 2.61 us  [swap(): return lax.ppermute(x, 'sub', [(0, 1), (1, 0)])]
    pallas_call x4, Pallas kernels: 17.1 us -> 16 us  [attention(): pl.pallas_call(functools.partial(attention_kernel, base=base, first=first...]
  transfers between devices with their start and end apart: 17 -> 17, of which waited for: 11 -> 9; matrix products, arithmetic and copies ran while one was open for 1% -> 1% of each run, Pallas kernels for 43% -> 42%
where the time goes in v4:
time: 56.8 us; the launch traced here: 56.6 us
  Pallas kernels  25.3 us (45%)
  starting transfers between devices  16.9 us (30%)
  waiting for transfers between devices  12.3 us (22%)
  other arithmetic  0.99 us (2%)
  between operations  0.92 us (2%)
    pallas_call x4, Pallas kernels, attention(): pl.pallas_call(functools.partial(attention_kernel, base=base, first=first...  16 us
    ppermute x10, starting transfers between devices, hop(): return lax.ppermute(x, ('ep', 'sub'), pairs)  15.7 us
    ppermute x10, waiting for transfers between devices, hop(): return lax.ppermute(x, ('ep', 'sub'), pairs)  9.72 us
    pallas_call x2, Pallas kernels, experts(): pl.pallas_call(functools.partial(experts_kernel, parts=len(parts), cuts=c...  8.07 us
    ppermute x7, waiting for transfers between devices, swap(): return lax.ppermute(x, 'sub', [(0, 1), (1, 0)])  2.61 us
    pallas_call x1, Pallas kernels, route(): pl.pallas_call(functools.partial(route_kernel, experts=placement.shape[0]...  1.28 us
    ppermute x7, starting transfers between devices, swap(): return lax.ppermute(x, 'sub', [(0, 1), (1, 0)])  1.22 us
  transfers between devices with their start and end apart: 17, of which 9 were waited for; matrix products, arithmetic and copies ran while one was open for 1% of the time, Pallas kernels for 42%

profile of v4, /device:TPU:0, one launch (start us, length us, event | category | flops | bytes accessed | tf_op | source)
XLA Modules:
  0.0 56.6 jit_solution(18143491564079263914)
XLA Ops:
  0.6 1.3 %route.1 = bf16[16,3712]{1,0:T(8,128)(2,1)S(1)} custom-call(s32[2,14]{1,0:T(2,128)} %bitcast.14, bf16[16,3584]{1,0:T(8,128)(2,1)} %rows_ref.1, f32[8,16]{1,0:T(8,128)} %bitcast.12, s32[8,16]{1,0:T(8,128)} %bitcast.13), custom_call_target="tpu_custom_call" | custom-call | tf_op jit(solution)/shard_map/route/pallas_call | solution.py:172
  1.9 4.0 %collective-permute-start = (bf16[16,3712]{1,0:T(8,128)(2,1)S(1)}, bf16[16,3712]{1,0:T(8,128)(2,1)S(1)}, u32[]{:S(2)}, u32[]{:S(2)}) collective-permute-start(bf16[16,3712]{1,0:T(8,128)(2,1)S(1)} %route.1), channel_id=1, source_target_pairs={{0,8},{1,9},{2,10},{3,11},{4,12},{5,13},{6,14},{7,15},{8,0},{9,1},... | collective-permute-start | bytes 356360 | tf_op jit(solution)/shard_map/ppermute | solution.py:260
  6.0 5.5 %attention.4 = (bf16[8,2,128,512]{3,2,1,0:T(8,128)(2,1)}, bf16[2,2,576,128]{3,2,1,0:T(8,128)(2,1)}, bf16[2,576,256]{2,1,0:T(8,128)(2,1)}, bf16[2,2,576]{2,1,0:T(2,128)(2,1)}) custom-call(s32[8]{0:T(128)} %refs_0_.3, bf16[8,2,576,128]{3,2,1,0:T(8,128)(2,1)} %bitcast.15, bf16[8,576,256]{2,1,0:T(8,128)(2,1)} %bitcast.17, bf16[8,2,576]{2,1,0:T(2,128)(2,1)} %refs_3_.1), custom_call_target="tpu_custom_call" | custom-call | flops 4294967296 | bytes 8388608 | tf_op jit(solution)/shard_map/attention/pallas_call | solution.py:113
  11.8 1.5 %collective-permute-start.1 = (bf16[32,3712]{1,0:T(8,128)(2,1)S(1)}, bf16[32,3712]{1,0:T(8,128)(2,1)S(1)}, u32[]{:S(2)}, u32[]{:S(2)}) collective-permute-start(bf16[32,3712]{1,0:T(8,128)(2,1)S(1)} %constant_dynamic-update-slice_fusion.refs_0_), channel_id=1, source_target_pairs={{0,4},{1,3},{2,6},{3,1},{4,0},{5,7},{6,2},{7,5},{8,12},{9,11},{10,... | collective-permute-start | bytes 712712 | tf_op jit(solution)/shard_map/ppermute | solution.py:260
  13.3 4.2 %attention.5 = (bf16[8,2,128,512]{3,2,1,0:T(8,128)(2,1)}, bf16[6,2,576,128]{3,2,1,0:T(8,128)(2,1)S(1)}, bf16[6,576,256]{2,1,0:T(8,128)(2,1)S(1)}, bf16[6,2,576]{2,1,0:T(2,128)(2,1)S(1)}) custom-call(s32[8]{0:T(128)} %refs_0_.3, bf16[8,2,576,128]{3,2,1,0:T(8,128)(2,1)} %bitcast.16, bf16[8,576,256]{2,1,0:T(8,128)(2,1)} %bitcast.18, ...), custom_call_target="tpu_custom_call", output_to_operand_aliasing={{0}: (4, {})} | custom-call | flops 4294967296 | bytes 8388608 | tf_op jit(solution)/shard_map/attention/pallas_call | solution.py:113
  17.5 1.6 %collective-permute-start.5 = (bf16[32,3712]{1,0:T(8,128)(2,1)S(1)}, bf16[32,3712]{1,0:T(8,128)(2,1)S(1)}, u32[]{:S(2)}, u32[]{:S(2)}) collective-permute-start(bf16[32,3712]{1,0:T(8,128)(2,1)S(1)} %constant_dynamic-update-slice_fusion.refs_0_), channel_id=1, source_target_pairs={{0,2},{1,5},{2,0},{3,7},{4,6},{5,1},{6,4},{7,3},{8,10},{9,13},{10,... | collective-permute-start | bytes 712712 | tf_op jit(solution)/shard_map/ppermute | solution.py:260
  19.1 0.6 %collective-permute-start.2 = (bf16[32,3712]{1,0:T(8,128)(2,1)S(1)}, bf16[32,3712]{1,0:T(8,128)(2,1)S(1)}, u32[]{:S(2)}, u32[]{:S(2)}) collective-permute-start(bf16[32,3712]{1,0:T(8,128)(2,1)S(1)} %collective-permute-done.1.refs_1_), channel_id=1, source_target_pairs={{0,2},{1,5},{2,0},{3,7},{4,6},{5,1},{6,4},{7,3},{8,10},{9,13},{10,... | collective-permute-start | bytes 712712 | tf_op jit(solution)/shard_map/ppermute | solution.py:260
  19.8 3.9 %collective-permute-done.5.refs_0_ = bf16[32,3712]{1,0:T(8,128)(2,1)S(1)} collective-permute-done((bf16[32,3712]{1,0:T(8,128)(2,1)S(1)}, bf16[32,3712]{1,0:T(8,128)(2,1)S(1)}, u32[]{:S(2)}, u32[]{:S(2)}) %collective-permute-start.5) | collective-permute-done | bytes 237600 | tf_op jit(solution)/shard_map/ppermute | solution.py:260
  23.8 4.0 %experts.2 = (f32[64,3584]{1,0:T(8,128)S(1)}, bf16[64,3584]{1,0:T(8,128)(2,1)S(1)}) custom-call(bf16[32,3712]{1,0:T(8,128)(2,1)S(1)} %constant_dynamic-update-slice_fusion.refs_0_, bf16[32,3712]{1,0:T(8,128)(2,1)S(1)} %collective-permute-done.1.refs_1_, bf16[32,3712]{1,0:T(8,128)(2,1)S(1)} %collective-permute-done.3.refs_2_, ...), custom_call_target="tpu_custom_call" | custom-call | flops 1048576 | bytes 65536 | tf_op jit(solution)/shard_map/experts/pallas_call | solution.py:229
  28.4 1.7 %collective-permute-done.8.refs_3_ = bf16[32,3712]{1,0:T(8,128)(2,1)S(1)} collective-permute-done((bf16[32,3712]{1,0:T(8,128)(2,1)S(1)}, bf16[32,3712]{1,0:T(8,128)(2,1)S(1)}, u32[]{:S(2)}, u32[]{:S(2)}) %collective-permute-start.8) | collective-permute-done | bytes 237600 | tf_op jit(solution)/shard_map/ppermute | solution.py:264
  30.1 4.1 %experts.3 = (f32[64,1792]{1,0:T(8,128)S(1)}, f32[64,1792]{1,0:T(8,128)S(1)}, bf16[64,1792]{1,0:T(8,128)(2,1)S(1)}, bf16[64,1792]{1,0:T(8,128)(2,1)S(1)}) custom-call(bf16[32,3712]{1,0:T(8,128)(2,1)S(1)} %collective-permute-done.5.refs_0_, bf16[32,3712]{1,0:T(8,128)(2,1)S(1)} %collective-permute-done.2.refs_1_, ...), custom_call_target="tpu_custom_call" | custom-call | flops 1048576 | bytes 65536 | tf_op jit(solution)/shard_map/experts/pallas_call | solution.py:229
  34.9 0.9 %collective-permute-done.9 = bf16[64,1792]{1,0:T(8,128)(2,1)S(1)} collective-permute-done((bf16[64,1792]{1,0:T(8,128)(2,1)S(1)}, bf16[64,1792]{1,0:T(8,128)(2,1)S(1)}, u32[]{:S(2)}, u32[]{:S(2)}) %collective-permute-start.9) | collective-permute-done | bytes 229408 | tf_op jit(solution)/shard_map/ppermute | solution.py:264
  35.8 1.6 %collective-permute-start.10 = (bf16[64,1792]{1,0:T(8,128)(2,1)S(1)}, bf16[64,1792]{1,0:T(8,128)(2,1)S(1)}, u32[]{:S(2)}, u32[]{:S(2)}) collective-permute-start(bf16[64,1792]{1,0:T(8,128)(2,1)S(1)} %add_convert_fusion.1), channel_id=1, source_target_pairs={{0,2},{1,5},{2,0},{3,7},{4,6},{5,1},{6,4},{7,3},{8,10},{9,13},{10,... | collective-permute-start | bytes 688136 | tf_op jit(solution)/shard_map/ppermute | solution.py:260
  38.0 3.4 %attention.6.refs_4_ = bf16[8,2,128,512]{3,2,1,0:T(8,128)(2,1)} custom-call(s32[8]{0:T(128)} %refs_0_.3, bf16[6,2,576,128]{3,2,1,0:T(8,128)(2,1)S(1)} %get-tuple-element.108.refs_1_, bf16[6,576,256]{2,1,0:T(8,128)(2,1)S(1)} %get-tuple-element.109.refs_2_, bf16[6,2,576]{2,1,0:T(2,128)(2,1)S(1)} %get-tuple-element.110.refs_3_, ...), custom_call_target="tpu_custom_call", output_to_operand_aliasing={{}: (4, {})} | custom-call | flops 1048576 | bytes 65536 | tf_op jit(solution)/shard_map/attention/pallas_call | solution.py:113
  42.0 0.9 %collective-permute-start.12 = (bf16[32,1792]{1,0:T(8,128)(2,1)S(1)}, bf16[32,1792]{1,0:T(8,128)(2,1)S(1)}, u32[]{:S(2)}, u32[]{:S(2)}) collective-permute-start(bf16[32,1792]{1,0:T(8,128)(2,1)S(1)} %slice.71), channel_id=1, source_target_pairs={{0,4},{1,3},{2,6},{3,1},{4,0},{5,7},{6,2},{7,5},{8,12},{9,11},{10,... | collective-permute-start | bytes 344072 | tf_op jit(solution)/shard_map/ppermute | solution.py:260
  42.8 1.7 %collective-permute-done.14 = bf16[64,1792]{1,0:T(8,128)(2,1)S(1)} collective-permute-done((bf16[64,1792]{1,0:T(8,128)(2,1)S(1)}, bf16[64,1792]{1,0:T(8,128)(2,1)S(1)}, u32[]{:S(2)}, u32[]{:S(2)}) %collective-permute-start.14) | collective-permute-done | bytes 229408 | tf_op jit(solution)/shard_map/ppermute | solution.py:260
  44.6 0.9 %collective-permute-start.15 = (bf16[32,1792]{1,0:T(8,128)(2,1)S(1)}, bf16[32,1792]{1,0:T(8,128)(2,1)S(1)}, u32[]{:S(2)}, u32[]{:S(2)}) collective-permute-start(bf16[32,1792]{1,0:T(8,128)(2,1)S(1)} %slice.70), channel_id=1, source_target_pairs={{0,4},{1,3},{2,6},{3,1},{4,0},{5,7},{6,2},{7,5},{8,12},{9,11},{10,... | collective-permute-start | bytes 344072 | tf_op jit(solution)/shard_map/ppermute | solution.py:260
  45.5 1.3 %collective-permute-done.12 = bf16[32,1792]{1,0:T(8,128)(2,1)S(1)} collective-permute-done((bf16[32,1792]{1,0:T(8,128)(2,1)S(1)}, bf16[32,1792]{1,0:T(8,128)(2,1)S(1)}, u32[]{:S(2)}, u32[]{:S(2)}) %collective-permute-start.12) | collective-permute-done | bytes 114720 | tf_op jit(solution)/shard_map/ppermute | solution.py:260
  46.9 2.0 %collective-permute-start.13 = (bf16[16,1792]{1,0:T(8,128)(2,1)S(1)}, bf16[16,1792]{1,0:T(8,128)(2,1)S(1)}, u32[]{:S(2)}, u32[]{:S(2)}) collective-permute-start(bf16[16,1792]{1,0:T(8,128)(2,1)S(1)} %slice.73), channel_id=1, source_target_pairs={{0,8},{1,9},{2,10},{3,11},{4,12},{5,13},{6,14},{7,15},{8,0},{9,1},... | collective-permute-start | bytes 172040 | tf_op jit(solution)/shard_map/ppermute | solution.py:260
  48.9 1.2 %collective-permute-done.15 = bf16[32,1792]{1,0:T(8,128)(2,1)S(1)} collective-permute-done((bf16[32,1792]{1,0:T(8,128)(2,1)S(1)}, bf16[32,1792]{1,0:T(8,128)(2,1)S(1)}, u32[]{:S(2)}, u32[]{:S(2)}) %collective-permute-start.15) | collective-permute-done | bytes 114720 | tf_op jit(solution)/shard_map/ppermute | solution.py:260
  50.2 2.0 %collective-permute-start.16 = (bf16[16,1792]{1,0:T(8,128)(2,1)S(1)}, bf16[16,1792]{1,0:T(8,128)(2,1)S(1)}, u32[]{:S(2)}, u32[]{:S(2)}) collective-permute-start(bf16[16,1792]{1,0:T(8,128)(2,1)S(1)} %slice.72), channel_id=1, source_target_pairs={{0,8},{1,9},{2,10},{3,11},{4,12},{5,13},{6,14},{7,15},{8,0},{9,1},... | collective-permute-start | bytes 172040 | tf_op jit(solution)/shard_map/ppermute | solution.py:260
  52.2 2.7 %attention.7 = bf16[8,2,128,512]{3,2,1,0:T(8,128)(2,1)} custom-call(s32[8]{0:T(128)} %refs_0_.3, bf16[6,2,576,128]{3,2,1,0:T(8,128)(2,1)S(1)} %get-tuple-element.108.refs_1_, bf16[6,576,256]{2,1,0:T(8,128)(2,1)S(1)} %get-tuple-element.109.refs_2_, bf16[6,2,576]{2,1,0:T(2,128)(2,1)S(1)} %get-tuple-element.110.refs_3_, ...), custom_call_target="tpu_custom_call", output_to_operand_aliasing={{}: (4, {})} | custom-call | flops 1048576 | bytes 65536 | tf_op jit(solution)/shard_map/attention/pallas_call | solution.py:113
  55.0 1.0 %collective-permute-done.16 = bf16[16,1792]{1,0:T(8,128)(2,1)S(1)} collective-permute-done((bf16[16,1792]{1,0:T(8,128)(2,1)S(1)}, bf16[16,1792]{1,0:T(8,128)(2,1)S(1)}, u32[]{:S(2)}, u32[]{:S(2)}) %collective-permute-start.16) | collective-permute-done | bytes 57376 | tf_op jit(solution)/shard_map/ppermute | solution.py:260
  55.9 0.7 %pad_maximum_fusion = bf16[16,3584]{1,0:T(8,128)(2,1)} fusion(bf16[16,1792]{1,0:T(8,128)(2,1)S(1)} %add_convert_fusion.2, bf16[16,1792]{1,0:T(8,128)(2,1)S(1)} %add_convert_fusion.3), kind=kLoop, calls=%fused_computation.12 | loop fusion | flops 229376 | bytes 229376 | tf_op jit(solution)/shard_map/concatenate | solution.py:345
  (52 shorter events, 2.9 us)
Async XLA Ops:
  0.6 23.0 %slice-start.4 = ((s8[7340032]{0:T(1024)(128)(4,1)}), s8[4194304]{0:T(1024)(128)(4,1)S(1)}, s32[]{:S(2)}) async-start(s8[7340032]{0:T(1024)(128)(4,1)} %bitcast.10), calls=%async_computation.4 | async-start | bytes 8388608
  1.9 9.8 %collective-permute-start = (bf16[16,3712]{1,0:T(8,128)(2,1)S(1)}, bf16[16,3712]{1,0:T(8,128)(2,1)S(1)}, u32[]{:S(2)}, u32[]{:S(2)}) collective-permute-start(bf16[16,3712]{1,0:T(8,128)(2,1)S(1)} %route.1), channel_id=1, source_target_pairs={{0,8},{1,9},{2,10},{3,11},{4,12},{5,13},{6,14},{7,15},{8,0},{9,1},... | collective-permute-start | bytes 356360 | tf_op jit(solution)/shard_map/ppermute | solution.py:260
  6.0 17.7 %slice-start.2 = ((s8[7340032]{0:T(1024)(128)(4,1)}), s8[4194304]{0:T(1024)(128)(4,1)S(1)}, s32[]{:S(2)}) async-start(s8[7340032]{0:T(1024)(128)(4,1)} %bitcast.8), calls=%async_computation.2 | async-start | bytes 8388608
  6.0 17.7 %slice-start.5 = ((s8[7340032]{0:T(1024)(128)(4,1)}), s8[3145728]{0:T(1024)(128)(4,1)S(1)}, s32[]{:S(2)}) async-start(s8[7340032]{0:T(1024)(128)(4,1)} %bitcast.10), calls=%async_computation.5 | async-start | bytes 6291456
  11.8 12.0 %slice-start = ((s8[7340032]{0:T(1024)(128)(4,1)}), s8[4194304]{0:T(1024)(128)(4,1)S(1)}, s32[]{:S(2)}) async-start(s8[7340032]{0:T(1024)(128)(4,1)} %bitcast.6), calls=%async_computation | async-start | bytes 8388608
  11.8 12.0 %slice-start.3 = ((s8[7340032]{0:T(1024)(128)(4,1)}), s8[3145728]{0:T(1024)(128)(4,1)S(1)}, s32[]{:S(2)}) async-start(s8[7340032]{0:T(1024)(128)(4,1)} %bitcast.8), calls=%async_computation.3 | async-start | bytes 6291456
  11.8 12.0 %slice-start.1 = ((s8[7340032]{0:T(1024)(128)(4,1)}), s8[3145728]{0:T(1024)(128)(4,1)S(1)}, s32[]{:S(2)}) async-start(s8[7340032]{0:T(1024)(128)(4,1)} %bitcast.6), calls=%async_computation.1 | async-start | bytes 6291456
  11.8 7.3 %collective-permute-start.1 = (bf16[32,3712]{1,0:T(8,128)(2,1)S(1)}, bf16[32,3712]{1,0:T(8,128)(2,1)S(1)}, u32[]{:S(2)}, u32[]{:S(2)}) collective-permute-start(bf16[32,3712]{1,0:T(8,128)(2,1)S(1)} %constant_dynamic-update-slice_fusion.refs_0_), channel_id=1, source_target_pairs={{0,4},{1,3},{2,6},{3,1},{4,0},{5,7},{6,2},{7,5},{8,12},{9,11},{10,... | collective-permute-start | bytes 712712 | tf_op jit(solution)/shard_map/ppermute | solution.py:260
  13.3 6.5 %collective-permute-start.3 = (bf16[32,3712]{1,0:T(8,128)(2,1)S(1)}, bf16[32,3712]{1,0:T(8,128)(2,1)S(1)}, u32[]{:S(2)}, u32[]{:S(2)}) collective-permute-start(bf16[32,3712]{1,0:T(8,128)(2,1)S(1)} %constant_dynamic-update-slice_fusion.refs_0_), channel_id=1, source_target_pairs={{0,1},{1,0},{2,3},{3,2},{4,5},{5,4},{6,7},{7,6},{8,9},{9,8},{10,11... | collective-permute-start | bytes 712712 | tf_op jit(solution)/shard_map/ppermute | solution.py:264
  17.5 6.2 %collective-permute-start.5 = (bf16[32,3712]{1,0:T(8,128)(2,1)S(1)}, bf16[32,3712]{1,0:T(8,128)(2,1)S(1)}, u32[]{:S(2)}, u32[]{:S(2)}) collective-permute-start(bf16[32,3712]{1,0:T(8,128)(2,1)S(1)} %constant_dynamic-update-slice_fusion.refs_0_), channel_id=1, source_target_pairs={{0,2},{1,5},{2,0},{3,7},{4,6},{5,1},{6,4},{7,3},{8,10},{9,13},{10,... | collective-permute-start | bytes 712712 | tf_op jit(solution)/shard_map/ppermute | solution.py:260
  19.1 4.6 %collective-permute-start.4 = (bf16[32,3712]{1,0:T(8,128)(2,1)S(1)}, bf16[32,3712]{1,0:T(8,128)(2,1)S(1)}, u32[]{:S(2)}, u32[]{:S(2)}) collective-permute-start(bf16[32,3712]{1,0:T(8,128)(2,1)S(1)} %collective-permute-done.1.refs_1_), channel_id=1, source_target_pairs={{0,1},{1,0},{2,3},{3,2},{4,5},{5,4},{6,7},{7,6},{8,9},{9,8},{10,11... | collective-permute-start | bytes 712712 | tf_op jit(solution)/shard_map/ppermute | solution.py:264
  19.1 8.7 %collective-permute-start.2 = (bf16[32,3712]{1,0:T(8,128)(2,1)S(1)}, bf16[32,3712]{1,0:T(8,128)(2,1)S(1)}, u32[]{:S(2)}, u32[]{:S(2)}) collective-permute-start(bf16[32,3712]{1,0:T(8,128)(2,1)S(1)} %collective-permute-done.1.refs_1_), channel_id=1, source_target_pairs={{0,2},{1,5},{2,0},{3,7},{4,6},{5,1},{6,4},{7,3},{8,10},{9,13},{10,... | collective-permute-start | bytes 712712 | tf_op jit(solution)/shard_map/ppermute | solution.py:260
  23.7 4.1 %collective-permute-start.6 = (bf16[32,3712]{1,0:T(8,128)(2,1)S(1)}, bf16[32,3712]{1,0:T(8,128)(2,1)S(1)}, u32[]{:S(2)}, u32[]{:S(2)}) collective-permute-start(bf16[32,3712]{1,0:T(8,128)(2,1)S(1)} %collective-permute-done.5.refs_0_), channel_id=1, source_target_pairs={{0,1},{1,0},{2,3},{3,2},{4,5},{5,4},{6,7},{7,6},{8,9},{9,8},{10,11... | collective-permute-start | bytes 712712 | tf_op jit(solution)/shard_map/ppermute | solution.py:264
  27.8 7.0 %collective-permute-start.7 = (bf16[64,3584]{1,0:T(8,128)(2,1)S(1)}, bf16[64,3584]{1,0:T(8,128)(2,1)S(1)}, u32[]{:S(2)}, u32[]{:S(2)}) collective-permute-start(bf16[64,3584]{1,0:T(8,128)(2,1)S(1)} %get-tuple-element.90), channel_id=1, source_target_pairs={{0,1},{1,0},{2,3},{3,2},{4,5},{5,4},{6,7},{7,6},{8,9},{9,8},{10,11... | collective-permute-start | bytes 1376264 | tf_op jit(solution)/shard_map/ppermute | solution.py:264
  28.4 1.8 %collective-permute-start.8 = (bf16[32,3712]{1,0:T(8,128)(2,1)S(1)}, bf16[32,3712]{1,0:T(8,128)(2,1)S(1)}, u32[]{:S(2)}, u32[]{:S(2)}) collective-permute-start(bf16[32,3712]{1,0:T(8,128)(2,1)S(1)} %collective-permute-done.2.refs_1_), channel_id=1, source_target_pairs={{0,1},{1,0},{2,3},{3,2},{4,5},{5,4},{6,7},{7,6},{8,9},{9,8},{10,11... | collective-permute-start | bytes 712712 | tf_op jit(solution)/shard_map/ppermute | solution.py:264
  34.2 1.6 %collective-permute-start.9 = (bf16[64,1792]{1,0:T(8,128)(2,1)S(1)}, bf16[64,1792]{1,0:T(8,128)(2,1)S(1)}, u32[]{:S(2)}, u32[]{:S(2)}) collective-permute-start(bf16[64,1792]{1,0:T(8,128)(2,1)S(1)} %get-tuple-element.94), channel_id=1, source_target_pairs={{0,1},{1,0},{2,3},{3,2},{4,5},{5,4},{6,7},{7,6},{8,9},{9,8},{10,11... | collective-permute-start | bytes 688136 | tf_op jit(solution)/shard_map/ppermute | solution.py:264
  34.6 2.8 %collective-permute-start.11 = (bf16[64,1792]{1,0:T(8,128)(2,1)S(1)}, bf16[64,1792]{1,0:T(8,128)(2,1)S(1)}, u32[]{:S(2)}, u32[]{:S(2)}) collective-permute-start(bf16[64,1792]{1,0:T(8,128)(2,1)S(1)} %get-tuple-element.96), channel_id=1, source_target_pairs={{0,1},{1,0},{2,3},{3,2},{4,5},{5,4},{6,7},{7,6},{8,9},{9,8},{10,11... | collective-permute-start | bytes 688136 | tf_op jit(solution)/shard_map/ppermute | solution.py:264
  35.8 6.1 %collective-permute-start.10 = (bf16[64,1792]{1,0:T(8,128)(2,1)S(1)}, bf16[64,1792]{1,0:T(8,128)(2,1)S(1)}, u32[]{:S(2)}, u32[]{:S(2)}) collective-permute-start(bf16[64,1792]{1,0:T(8,128)(2,1)S(1)} %add_convert_fusion.1), channel_id=1, source_target_pairs={{0,2},{1,5},{2,0},{3,7},{4,6},{5,1},{6,4},{7,3},{8,10},{9,13},{10,... | collective-permute-start | bytes 688136 | tf_op jit(solution)/shard_map/ppermute | solution.py:260
  37.5 7.0 %collective-permute-start.14 = (bf16[64,1792]{1,0:T(8,128)(2,1)S(1)}, bf16[64,1792]{1,0:T(8,128)(2,1)S(1)}, u32[]{:S(2)}, u32[]{:S(2)}) collective-permute-start(bf16[64,1792]{1,0:T(8,128)(2,1)S(1)} %add_convert_fusion), channel_id=1, source_target_pairs={{0,2},{1,5},{2,0},{3,7},{4,6},{5,1},{6,4},{7,3},{8,10},{9,13},{10,... | collective-permute-start | bytes 688136 | tf_op jit(solution)/shard_map/ppermute | solution.py:260
  42.0 4.9 %collective-permute-start.12 = (bf16[32,1792]{1,0:T(8,128)(2,1)S(1)}, bf16[32,1792]{1,0:T(8,128)(2,1)S(1)}, u32[]{:S(2)}, u32[]{:S(2)}) collective-permute-start(bf16[32,1792]{1,0:T(8,128)(2,1)S(1)} %slice.71), channel_id=1, source_target_pairs={{0,4},{1,3},{2,6},{3,1},{4,0},{5,7},{6,2},{7,5},{8,12},{9,11},{10,... | collective-permute-start | bytes 344072 | tf_op jit(solution)/shard_map/ppermute | solution.py:260
  44.6 5.5 %collective-permute-start.15 = (bf16[32,1792]{1,0:T(8,128)(2,1)S(1)}, bf16[32,1792]{1,0:T(8,128)(2,1)S(1)}, u32[]{:S(2)}, u32[]{:S(2)}) collective-permute-start(bf16[32,1792]{1,0:T(8,128)(2,1)S(1)} %slice.70), channel_id=1, source_target_pairs={{0,4},{1,3},{2,6},{3,1},{4,0},{5,7},{6,2},{7,5},{8,12},{9,11},{10,... | collective-permute-start | bytes 344072 | tf_op jit(solution)/shard_map/ppermute | solution.py:260
  46.9 8.1 %collective-permute-start.13 = (bf16[16,1792]{1,0:T(8,128)(2,1)S(1)}, bf16[16,1792]{1,0:T(8,128)(2,1)S(1)}, u32[]{:S(2)}, u32[]{:S(2)}) collective-permute-start(bf16[16,1792]{1,0:T(8,128)(2,1)S(1)} %slice.73), channel_id=1, source_target_pairs={{0,8},{1,9},{2,10},{3,11},{4,12},{5,13},{6,14},{7,15},{8,0},{9,1},... | collective-permute-start | bytes 172040 | tf_op jit(solution)/shard_map/ppermute | solution.py:260
  50.2 5.8 %collective-permute-start.16 = (bf16[16,1792]{1,0:T(8,128)(2,1)S(1)}, bf16[16,1792]{1,0:T(8,128)(2,1)S(1)}, u32[]{:S(2)}, u32[]{:S(2)}) collective-permute-start(bf16[16,1792]{1,0:T(8,128)(2,1)S(1)} %slice.72), channel_id=1, source_target_pairs={{0,8},{1,9},{2,10},{3,11},{4,12},{5,13},{6,14},{7,15},{8,0},{9,1},... | collective-permute-start | bytes 172040 | tf_op jit(solution)/shard_map/ppermute | solution.py:260

commit v5 on v4

--- a/solution.py
+++ b/solution.py
@@ -299,31 +299,38 @@
     half = width // 2
     gate, up, down = [pltpu.with_memory_space_constraint(w, pltpu.VMEM) for w in (w_gate, w_up, w_down)]
 
-    base = route(placement, moe_input, gate_scores, expert_ids, slots)
-    for turn in range(turns - 2):
-        got = hop(base, ep, sub, masks, turn)
-        if turn == 0:
-            base, inputs = barrier((base, inputs))
-            out, _, _ = attention(lengths, inputs, 0, 0, 2, held=2, loads=())
-            got, out, inputs = barrier((got, out, inputs))
-        base = jnp.concatenate([base, got], axis=0)
-
-    second = hop(base, ep, sub, masks, turns - 2)
-    base, inputs = barrier((base, inputs))
-    out, inputs, _ = attention(lengths, inputs, 2, 2, 1, held=requests - 2, previous=out)
-    done = 3
-    base_late, out = barrier((base, out))
-    early = hop(base_late, ep, sub, masks, turns - 1)
-    second, out, inputs = barrier((second, out, inputs))
-    late = hop(second, ep, sub, masks, turns - 1)
+    own = route(placement, moe_input, gate_scores, expert_ids, slots)
+    own, inputs = barrier((own, inputs))
+    whole = [pltpu.with_memory_space_constraint(x, pltpu.VMEM) for x in inputs]
+    for turn in range(turns - 3):
+        own = jnp.concatenate([own, hop(own, ep, sub, masks, turn)], axis=0)
+    hop_a, hop_b, hop_c = (
+        functools.partial(hop, ep=ep, sub=sub, masks=masks, turn=turn)
+        for turn in range(turns - 3, turns)
+    )
+    a, b, c = hop_a(own), hop_b(own), hop_c(own)
+    out, _, _ = attention(lengths, inputs, 0, 0, 1, held=1)
+    a, b, c, out, inputs = barrier((a, b, c, out, inputs))
+    ab, ac, bc = hop_b(a), hop_c(a), hop_c(b)
+    out, _, _ = attention(lengths, inputs, 1, 1, 1, held=1, previous=out)
+    ab, out, inputs = barrier((ab, out, inputs))
+    abc = hop_c(ab)
+    done = 2
+    base = jnp.concatenate([own, a], axis=0)
+    second = jnp.concatenate([b, ab], axis=0)
+    early = jnp.concatenate([c, ac], axis=0)
     near_rows = [base, second, swap(base), swap(second)]
-    near_rows, early = barrier((near_rows, early))
+    near_rows, c = barrier((near_rows, c))
+    late_swap = swap(bc)
     early_swap = swap(early)
     near_own, (near_other,) = experts(near_rows, gate, up, down, chip, 1)
-    late, early_swap, near_own, near_other = barrier((late, early_swap, near_own, near_other))
+    abc, early_swap, late_swap, near_own, near_other = barrier(
+        (abc, early_swap, late_swap, near_own, near_other)
+    )
     near_back = swap(near_other)
-    own, other = experts([early, late, early_swap, swap(late)], gate, up, down, chip, 2)
-    sent = [add(x, swap(y)).astype(BF16) for x, y in zip(own, other)]
+    far_rows = [early, bc, abc, early_swap, late_swap, swap(abc)]
+    far_own, far_other = experts(far_rows, gate, up, down, chip, 2)
+    sent = [add(x, swap(y)).astype(BF16) for x, y in zip(far_own, far_other)]
     totals = [
         barrier(add(near_own[0][:, :half], near_back[:, :half])),
         barrier(add(near_own[0][:, half:], near_back[:, half:])),
@@ -332,11 +339,11 @@
     for turn in range(turns - 1, -1, -1):
         got = [hop(x, ep, sub, masks, turn) for x in sent]
         if turn in shares and done < requests:
-            sent, inputs = barrier((sent, inputs))
+            sent, whole = barrier((sent, whole))
             count = min(shares[turn], requests - done)
-            out, inputs, _ = attention(lengths, inputs, 2, done, count, previous=out)
+            out, _, _ = attention(lengths, whole, 0, done, count, previous=out)
             done += count
-            got[0], out, inputs = barrier((got[0], out, inputs))
+            got[0], out, whole = barrier((got[0], out, whole))
         totals = [add(t, g) for t, g in zip(totals, got)]
         if turn:
             keep = totals[0].shape[0] // 2

time: 56.8 us -> 55 us (0.968)
  waiting for transfers between devices: 12.3 us -> 6.11 us
  starting transfers between devices: 16.9 us -> 20.9 us
    ppermute x10 -> x13, waiting for transfers between devices: 9.72 us -> 4.06 us  [hop(): return lax.ppermute(x, ('ep', 'sub'), pairs)]
    ppermute x10 -> x13, starting transfers between devices: 15.7 us -> 18.9 us  [hop(): return lax.ppermute(x, ('ep', 'sub'), pairs)]
    ppermute x7 -> x8, starting transfers between devices: 1.22 us -> 2.02 us  [swap(): return lax.ppermute(x, 'sub', [(0, 1), (1, 0)])]
    ppermute x7 -> x8, waiting for transfers between devices: 2.61 us -> 2.05 us  [swap(): return lax.ppermute(x, 'sub', [(0, 1), (1, 0)])]
  transfers between devices with their start and end apart: 17 -> 21, of which waited for: 9 -> 6; matrix products, arithmetic and copies ran while one was open for 1% -> 1% of each run, Pallas kernels for 42% -> 37%
where the time goes in v5:
time: 55 us; the launch traced here: 54.8 us
  Pallas kernels  25.5 us (46%)
  starting transfers between devices  20.9 us (38%)
  waiting for transfers between devices  6.11 us (11%)
  other arithmetic  1.02 us (2%)
  between operations  1.01 us (2%)
    ppermute x13, starting transfers between devices, hop(): return lax.ppermute(x, ('ep', 'sub'), pairs)  18.9 us
    pallas_call x4, Pallas kernels, attention(): pl.pallas_call(functools.partial(attention_kernel, base=base, first=first...  16.3 us
    pallas_call x2, Pallas kernels, experts(): pl.pallas_call(functools.partial(experts_kernel, parts=len(parts), cuts=c...  8.06 us
    ppermute x13, waiting for transfers between devices, hop(): return lax.ppermute(x, ('ep', 'sub'), pairs)  4.06 us
    ppermute x8, waiting for transfers between devices, swap(): return lax.ppermute(x, 'sub', [(0, 1), (1, 0)])  2.05 us
    ppermute x8, starting transfers between devices, swap(): return lax.ppermute(x, 'sub', [(0, 1), (1, 0)])  2.02 us
    pallas_call x1, Pallas kernels, route(): pl.pallas_call(functools.partial(route_kernel, experts=placement.shape[0]...  1.13 us
  transfers between devices with their start and end apart: 21, of which 6 were waited for; matrix products, arithmetic and copies ran while one was open for 1% of the time, Pallas kernels for 37%

profile of v5, /device:TPU:0, one launch (start us, length us, event | category | flops | bytes accessed | tf_op | source)
XLA Modules:
  0.0 54.8 jit_solution(13588034638129575151)
XLA Ops:
  0.6 1.1 %route.1 = bf16[16,3712]{1,0:T(8,128)(2,1)S(1)} custom-call(s32[2,14]{1,0:T(2,128)} %bitcast.20, bf16[16,3584]{1,0:T(8,128)(2,1)} %rows_ref.1, f32[8,16]{1,0:T(8,128)} %bitcast.18, s32[8,16]{1,0:T(8,128)} %bitcast.19), custom_call_target="tpu_custom_call" | custom-call | tf_op jit(solution)/shard_map/route/pallas_call | solution.py:172
  1.8 4.0 %collective-permute-start = (bf16[16,3712]{1,0:T(8,128)(2,1)S(1)}, bf16[16,3712]{1,0:T(8,128)(2,1)S(1)}, u32[]{:S(2)}, u32[]{:S(2)}) collective-permute-start(bf16[16,3712]{1,0:T(8,128)(2,1)S(1)} %route.1), channel_id=1, source_target_pairs={{0,8},{1,9},{2,10},{3,11},{4,12},{5,13},{6,14},{7,15},{8,0},{9,1},... | collective-permute-start | bytes 356360 | tf_op jit(solution)/shard_map/ppermute | solution.py:260
  5.8 1.6 %collective-permute-start.1 = (bf16[16,3712]{1,0:T(8,128)(2,1)S(1)}, bf16[16,3712]{1,0:T(8,128)(2,1)S(1)}, u32[]{:S(2)}, u32[]{:S(2)}) collective-permute-start(bf16[16,3712]{1,0:T(8,128)(2,1)S(1)} %route.1), channel_id=1, source_target_pairs={{0,4},{1,3},{2,6},{3,1},{4,0},{5,7},{6,2},{7,5},{8,12},{9,11},{10,... | collective-permute-start | bytes 356360 | tf_op jit(solution)/shard_map/ppermute | solution.py:260
  7.4 1.5 %collective-permute-start.2 = (bf16[16,3712]{1,0:T(8,128)(2,1)S(1)}, bf16[16,3712]{1,0:T(8,128)(2,1)S(1)}, u32[]{:S(2)}, u32[]{:S(2)}) collective-permute-start(bf16[16,3712]{1,0:T(8,128)(2,1)S(1)} %route.1), channel_id=1, source_target_pairs={{0,2},{1,5},{2,0},{3,7},{4,6},{5,1},{6,4},{7,3},{8,10},{9,13},{10,... | collective-permute-start | bytes 356360 | tf_op jit(solution)/shard_map/ppermute | solution.py:260
  8.9 4.7 %attention.4 = (bf16[8,2,128,512]{3,2,1,0:T(8,128)(2,1)}, bf16[1,2,576,128]{3,2,1,0:T(8,128)(2,1)}, bf16[1,576,256]{2,1,0:T(8,128)(2,1)}, bf16[1,2,576]{2,1,0:T(2,128)(2,1)}) custom-call(s32[8]{0:T(128)} %refs_0_.3, bf16[8,2,576,128]{3,2,1,0:T(8,128)(2,1)} %bitcast.10, bf16[8,576,256]{2,1,0:T(8,128)(2,1)} %bitcast.14, bf16[8,2,576]{2,1,0:T(2,128)(2,1)} %refs_3_.3), custom_call_target="tpu_custom_call" | custom-call | flops 4294967296 | bytes 8388608 | tf_op jit(solution)/shard_map/attention/pallas_call | solution.py:113
  14.9 1.4 %collective-permute-start.7 = (bf16[16,3712]{1,0:T(8,128)(2,1)S(1)}, bf16[16,3712]{1,0:T(8,128)(2,1)S(1)}, u32[]{:S(2)}, u32[]{:S(2)}) collective-permute-start(bf16[16,3712]{1,0:T(8,128)(2,1)S(1)} %collective-permute-done.1), channel_id=1, source_target_pairs={{0,2},{1,5},{2,0},{3,7},{4,6},{5,1},{6,4},{7,3},{8,10},{9,13},{10,... | collective-permute-start | bytes 356360 | tf_op jit(solution)/shard_map/ppermute | solution.py:260
  16.4 4.8 %attention.5 = (bf16[8,2,128,512]{3,2,1,0:T(8,128)(2,1)}, bf16[1,2,576,128]{3,2,1,0:T(8,128)(2,1)}, bf16[1,576,256]{2,1,0:T(8,128)(2,1)}, bf16[1,2,576]{2,1,0:T(2,128)(2,1)}) custom-call(s32[8]{0:T(128)} %refs_0_.3, bf16[8,2,576,128]{3,2,1,0:T(8,128)(2,1)} %bitcast.11, bf16[8,576,256]{2,1,0:T(8,128)(2,1)} %bitcast.15, ...), custom_call_target="tpu_custom_call", output_to_operand_aliasing={{0}: (4, {})} | custom-call | flops 4294967296 | bytes 8388608 | tf_op jit(solution)/shard_map/attention/pallas_call | solution.py:113
  21.8 1.0 %collective-permute-start.4 = (bf16[16,3712]{1,0:T(8,128)(2,1)S(1)}, bf16[16,3712]{1,0:T(8,128)(2,1)S(1)}, u32[]{:S(2)}, u32[]{:S(2)}) collective-permute-start(bf16[16,3712]{1,0:T(8,128)(2,1)S(1)} %collective-permute-done.3), channel_id=1, source_target_pairs={{0,2},{1,5},{2,0},{3,7},{4,6},{5,1},{6,4},{7,3},{8,10},{9,13},{10,... | collective-permute-start | bytes 356360 | tf_op jit(solution)/shard_map/ppermute | solution.py:260
  23.3 4.0 %experts.2 = (f32[64,3584]{1,0:T(8,128)S(1)}, bf16[64,3584]{1,0:T(8,128)(2,1)S(1)}) custom-call(bf16[32,3712]{1,0:T(8,128)(2,1)S(1)} %constant_dynamic-update-slice_fusion.2.refs_0_, bf16[32,3712]{1,0:T(8,128)(2,1)S(1)} %constant_dynamic-update-slice_fusion.4.refs_1_, bf16[32,3712]{1,0:T(8,128)(2,1)S(1)} %collective-permute-done.9.refs_2_, ...), custom_call_target="tpu_custom_call" | custom-call | flops 1048576 | bytes 65536 | tf_op jit(solution)/shard_map/experts/pallas_call | solution.py:229
  27.6 1.2 %collective-permute-done.12.refs_5_ = bf16[16,3712]{1,0:T(8,128)(2,1)S(1)} collective-permute-done((bf16[16,3712]{1,0:T(8,128)(2,1)S(1)}, bf16[16,3712]{1,0:T(8,128)(2,1)S(1)}, u32[]{:S(2)}, u32[]{:S(2)}) %collective-permute-start.12) | collective-permute-done | bytes 118816 | tf_op jit(solution)/shard_map/ppermute | solution.py:264
  28.8 4.0 %experts.3 = (f32[64,1792]{1,0:T(8,128)S(1)}, f32[64,1792]{1,0:T(8,128)S(1)}, bf16[64,1792]{1,0:T(8,128)(2,1)S(1)}, bf16[64,1792]{1,0:T(8,128)(2,1)S(1)}) custom-call(bf16[32,3712]{1,0:T(8,128)(2,1)S(1)} %constant_dynamic-update-slice_fusion.refs_0_, bf16[16,3712]{1,0:T(8,128)(2,1)S(1)} %collective-permute-done.7.refs_1_, ...), custom_call_target="tpu_custom_call" | custom-call | flops 1048576 | bytes 65536 | tf_op jit(solution)/shard_map/experts/pallas_call | solution.py:229
  33.6 0.8 %collective-permute-done.13 = bf16[64,1792]{1,0:T(8,128)(2,1)S(1)} collective-permute-done((bf16[64,1792]{1,0:T(8,128)(2,1)S(1)}, bf16[64,1792]{1,0:T(8,128)(2,1)S(1)}, u32[]{:S(2)}, u32[]{:S(2)}) %collective-permute-start.13) | collective-permute-done | bytes 229408 | tf_op jit(solution)/shard_map/ppermute | solution.py:264
  34.4 0.9 %collective-permute-start.14 = (bf16[64,1792]{1,0:T(8,128)(2,1)S(1)}, bf16[64,1792]{1,0:T(8,128)(2,1)S(1)}, u32[]{:S(2)}, u32[]{:S(2)}) collective-permute-start(bf16[64,1792]{1,0:T(8,128)(2,1)S(1)} %add_convert_fusion.1), channel_id=1, source_target_pairs={{0,2},{1,5},{2,0},{3,7},{4,6},{5,1},{6,4},{7,3},{8,10},{9,13},{10,... | collective-permute-start | bytes 688136 | tf_op jit(solution)/shard_map/ppermute | solution.py:260
  35.4 1.2 %collective-permute-start.18 = (bf16[64,1792]{1,0:T(8,128)(2,1)S(1)}, bf16[64,1792]{1,0:T(8,128)(2,1)S(1)}, u32[]{:S(2)}, u32[]{:S(2)}) collective-permute-start(bf16[64,1792]{1,0:T(8,128)(2,1)S(1)} %add_convert_fusion), channel_id=1, source_target_pairs={{0,2},{1,5},{2,0},{3,7},{4,6},{5,1},{6,4},{7,3},{8,10},{9,13},{10,... | collective-permute-start | bytes 688136 | tf_op jit(solution)/shard_map/ppermute | solution.py:260
  36.7 3.4 %attention.6.refs_4_ = bf16[8,2,128,512]{3,2,1,0:T(8,128)(2,1)} custom-call(s32[8]{0:T(128)} %refs_0_.3, bf16[8,2,576,128]{3,2,1,0:T(8,128)(2,1)S(1)} %bitcast.12, bf16[8,576,256]{2,1,0:T(8,128)(2,1)S(1)} %bitcast.16, bf16[8,2,576]{2,1,0:T(2,128)(2,1)S(1)} %copy-done.3, ...), custom_call_target="tpu_custom_call", output_to_operand_aliasing={{}: (4, {})} | custom-call | flops 1048576 | bytes 65536 | tf_op jit(solution)/shard_map/attention/pallas_call | solution.py:113
  40.6 1.1 %collective-permute-start.16 = (bf16[32,1792]{1,0:T(8,128)(2,1)S(1)}, bf16[32,1792]{1,0:T(8,128)(2,1)S(1)}, u32[]{:S(2)}, u32[]{:S(2)}) collective-permute-start(bf16[32,1792]{1,0:T(8,128)(2,1)S(1)} %slice.71), channel_id=1, source_target_pairs={{0,4},{1,3},{2,6},{3,1},{4,0},{5,7},{6,2},{7,5},{8,12},{9,11},{10,... | collective-permute-start | bytes 344072 | tf_op jit(solution)/shard_map/ppermute | solution.py:260
  41.7 1.4 %collective-permute-done.18 = bf16[64,1792]{1,0:T(8,128)(2,1)S(1)} collective-permute-done((bf16[64,1792]{1,0:T(8,128)(2,1)S(1)}, bf16[64,1792]{1,0:T(8,128)(2,1)S(1)}, u32[]{:S(2)}, u32[]{:S(2)}) %collective-permute-start.18) | collective-permute-done | bytes 229408 | tf_op jit(solution)/shard_map/ppermute | solution.py:260
  43.3 1.3 %collective-permute-start.19 = (bf16[32,1792]{1,0:T(8,128)(2,1)S(1)}, bf16[32,1792]{1,0:T(8,128)(2,1)S(1)}, u32[]{:S(2)}, u32[]{:S(2)}) collective-permute-start(bf16[32,1792]{1,0:T(8,128)(2,1)S(1)} %slice.70), channel_id=1, source_target_pairs={{0,4},{1,3},{2,6},{3,1},{4,0},{5,7},{6,2},{7,5},{8,12},{9,11},{10,... | collective-permute-start | bytes 344072 | tf_op jit(solution)/shard_map/ppermute | solution.py:260
  44.5 0.9 %collective-permute-done.16 = bf16[32,1792]{1,0:T(8,128)(2,1)S(1)} collective-permute-done((bf16[32,1792]{1,0:T(8,128)(2,1)S(1)}, bf16[32,1792]{1,0:T(8,128)(2,1)S(1)}, u32[]{:S(2)}, u32[]{:S(2)}) %collective-permute-start.16) | collective-permute-done | bytes 114720 | tf_op jit(solution)/shard_map/ppermute | solution.py:260
  45.5 1.9 %collective-permute-start.17 = (bf16[16,1792]{1,0:T(8,128)(2,1)S(1)}, bf16[16,1792]{1,0:T(8,128)(2,1)S(1)}, u32[]{:S(2)}, u32[]{:S(2)}) collective-permute-start(bf16[16,1792]{1,0:T(8,128)(2,1)S(1)} %slice.73), channel_id=1, source_target_pairs={{0,8},{1,9},{2,10},{3,11},{4,12},{5,13},{6,14},{7,15},{8,0},{9,1},... | collective-permute-start | bytes 172040 | tf_op jit(solution)/shard_map/ppermute | solution.py:260
  47.3 1.4 %collective-permute-done.19 = bf16[32,1792]{1,0:T(8,128)(2,1)S(1)} collective-permute-done((bf16[32,1792]{1,0:T(8,128)(2,1)S(1)}, bf16[32,1792]{1,0:T(8,128)(2,1)S(1)}, u32[]{:S(2)}, u32[]{:S(2)}) %collective-permute-start.19) | collective-permute-done | bytes 114720 | tf_op jit(solution)/shard_map/ppermute | solution.py:260
  48.8 1.8 %collective-permute-start.20 = (bf16[16,1792]{1,0:T(8,128)(2,1)S(1)}, bf16[16,1792]{1,0:T(8,128)(2,1)S(1)}, u32[]{:S(2)}, u32[]{:S(2)}) collective-permute-start(bf16[16,1792]{1,0:T(8,128)(2,1)S(1)} %slice.72), channel_id=1, source_target_pairs={{0,8},{1,9},{2,10},{3,11},{4,12},{5,13},{6,14},{7,15},{8,0},{9,1},... | collective-permute-start | bytes 172040 | tf_op jit(solution)/shard_map/ppermute | solution.py:260
  50.6 3.4 %attention.7 = bf16[8,2,128,512]{3,2,1,0:T(8,128)(2,1)} custom-call(s32[8]{0:T(128)} %refs_0_.3, bf16[8,2,576,128]{3,2,1,0:T(8,128)(2,1)S(1)} %bitcast.13, bf16[8,576,256]{2,1,0:T(8,128)(2,1)S(1)} %bitcast.17, bf16[8,2,576]{2,1,0:T(2,128)(2,1)S(1)} %copy-done.3, bf16[8,2,128,512]{3,2,1,0:T(8,128)(2,1)} %attention.6.refs_4_), custom_call_target="tpu_custom_call", output_to_operand_aliasing={{}: (4, {})} | custom-call | flops 1048576 | bytes 65536 | tf_op jit(solution)/shard_map/attention/pallas_call | solution.py:113
  54.2 0.7 %pad_maximum_fusion = bf16[16,3584]{1,0:T(8,128)(2,1)} fusion(bf16[16,1792]{1,0:T(8,128)(2,1)S(1)} %add_convert_fusion.2, bf16[16,1792]{1,0:T(8,128)(2,1)S(1)} %add_convert_fusion.3), kind=kLoop, calls=%fused_computation.12 | loop fusion | flops 229376 | bytes 229376 | tf_op jit(solution)/shard_map/concatenate | solution.py:352
  (67 shorter events, 4.2 us)
Async XLA Ops:
  1.8 11.9 %collective-permute-start = (bf16[16,3712]{1,0:T(8,128)(2,1)S(1)}, bf16[16,3712]{1,0:T(8,128)(2,1)S(1)}, u32[]{:S(2)}, u32[]{:S(2)}) collective-permute-start(bf16[16,3712]{1,0:T(8,128)(2,1)S(1)} %route.1), channel_id=1, source_target_pairs={{0,8},{1,9},{2,10},{3,11},{4,12},{5,13},{6,14},{7,15},{8,0},{9,1},... | collective-permute-start | bytes 356360 | tf_op jit(solution)/shard_map/ppermute | solution.py:260
  5.8 7.9 %collective-permute-start.1 = (bf16[16,3712]{1,0:T(8,128)(2,1)S(1)}, bf16[16,3712]{1,0:T(8,128)(2,1)S(1)}, u32[]{:S(2)}, u32[]{:S(2)}) collective-permute-start(bf16[16,3712]{1,0:T(8,128)(2,1)S(1)} %route.1), channel_id=1, source_target_pairs={{0,4},{1,3},{2,6},{3,1},{4,0},{5,7},{6,2},{7,5},{8,12},{9,11},{10,... | collective-permute-start | bytes 356360 | tf_op jit(solution)/shard_map/ppermute | solution.py:260
  7.4 6.3 %collective-permute-start.2 = (bf16[16,3712]{1,0:T(8,128)(2,1)S(1)}, bf16[16,3712]{1,0:T(8,128)(2,1)S(1)}, u32[]{:S(2)}, u32[]{:S(2)}) collective-permute-start(bf16[16,3712]{1,0:T(8,128)(2,1)S(1)} %route.1), channel_id=1, source_target_pairs={{0,2},{1,5},{2,0},{3,7},{4,6},{5,1},{6,4},{7,3},{8,10},{9,13},{10,... | collective-permute-start | bytes 356360 | tf_op jit(solution)/shard_map/ppermute | solution.py:260
  8.9 14.3 %slice-start.2 = ((s8[7340032]{0:T(1024)(128)(4,1)}), s8[4194304]{0:T(1024)(128)(4,1)S(1)}, s32[]{:S(2)}) async-start(s8[7340032]{0:T(1024)(128)(4,1)} %bitcast.8), calls=%async_computation.2 | async-start | bytes 8388608
  8.9 14.3 %copy-start = (bf16[2,512,3584]{2,1,0:T(8,128)(2,1)S(1)}, bf16[2,512,3584]{2,1,0:T(8,128)(2,1)}, u32[]{:S(2)}) copy-start(bf16[2,512,3584]{2,1,0:T(8,128)(2,1)} %refs_8_.1) | copy-start | bytes 22020100
  13.7 7.5 %collective-permute-start.3 = (bf16[16,3712]{1,0:T(8,128)(2,1)S(1)}, bf16[16,3712]{1,0:T(8,128)(2,1)S(1)}, u32[]{:S(2)}, u32[]{:S(2)}) collective-permute-start(bf16[16,3712]{1,0:T(8,128)(2,1)S(1)} %collective-permute-done), channel_id=1, source_target_pairs={{0,4},{1,3},{2,6},{3,1},{4,0},{5,7},{6,2},{7,5},{8,12},{9,11},{10,... | collective-permute-start | bytes 356360 | tf_op jit(solution)/shard_map/ppermute | solution.py:260
  14.2 7.1 %collective-permute-start.5 = (bf16[16,3712]{1,0:T(8,128)(2,1)S(1)}, bf16[16,3712]{1,0:T(8,128)(2,1)S(1)}, u32[]{:S(2)}, u32[]{:S(2)}) collective-permute-start(bf16[16,3712]{1,0:T(8,128)(2,1)S(1)} %collective-permute-done), channel_id=1, source_target_pairs={{0,2},{1,5},{2,0},{3,7},{4,6},{5,1},{6,4},{7,3},{8,10},{9,13},{10,... | collective-permute-start | bytes 356360 | tf_op jit(solution)/shard_map/ppermute | solution.py:260
  14.9 8.0 %collective-permute-start.7 = (bf16[16,3712]{1,0:T(8,128)(2,1)S(1)}, bf16[16,3712]{1,0:T(8,128)(2,1)S(1)}, u32[]{:S(2)}, u32[]{:S(2)}) collective-permute-start(bf16[16,3712]{1,0:T(8,128)(2,1)S(1)} %collective-permute-done.1), channel_id=1, source_target_pairs={{0,2},{1,5},{2,0},{3,7},{4,6},{5,1},{6,4},{7,3},{8,10},{9,13},{10,... | collective-permute-start | bytes 356360 | tf_op jit(solution)/shard_map/ppermute | solution.py:260
  16.3 6.9 %collective-permute-start.9 = (bf16[32,3712]{1,0:T(8,128)(2,1)S(1)}, bf16[32,3712]{1,0:T(8,128)(2,1)S(1)}, u32[]{:S(2)}, u32[]{:S(2)}) collective-permute-start(bf16[32,3712]{1,0:T(8,128)(2,1)S(1)} %constant_dynamic-update-slice_fusion.2.refs_0_), channel_id=1, source_target_pairs={{0,1},{1,0},{2,3},{3,2},{4,5},{5,4},{6,7},{7,6},{8,9},{9,8},{10,11... | collective-permute-start | bytes 712712 | tf_op jit(solution)/shard_map/ppermute | solution.py:264
  21.2 2.0 %collective-permute-start.10 = (bf16[32,3712]{1,0:T(8,128)(2,1)S(1)}, bf16[32,3712]{1,0:T(8,128)(2,1)S(1)}, u32[]{:S(2)}, u32[]{:S(2)}) collective-permute-start(bf16[32,3712]{1,0:T(8,128)(2,1)S(1)} %constant_dynamic-update-slice_fusion.4.refs_1_), channel_id=1, source_target_pairs={{0,1},{1,0},{2,3},{3,2},{4,5},{5,4},{6,7},{7,6},{8,9},{9,8},{10,11... | collective-permute-start | bytes 712712 | tf_op jit(solution)/shard_map/ppermute | solution.py:264
  21.3 6.0 %collective-permute-start.6 = (bf16[32,3712]{1,0:T(8,128)(2,1)S(1)}, bf16[32,3712]{1,0:T(8,128)(2,1)S(1)}, u32[]{:S(2)}, u32[]{:S(2)}) collective-permute-start(bf16[32,3712]{1,0:T(8,128)(2,1)S(1)} %constant_dynamic-update-slice_fusion.refs_0_), channel_id=1, source_target_pairs={{0,1},{1,0},{2,3},{3,2},{4,5},{5,4},{6,7},{7,6},{8,9},{9,8},{10,11... | collective-permute-start | bytes 712712 | tf_op jit(solution)/shard_map/ppermute | solution.py:264
  21.8 5.5 %collective-permute-start.4 = (bf16[16,3712]{1,0:T(8,128)(2,1)S(1)}, bf16[16,3712]{1,0:T(8,128)(2,1)S(1)}, u32[]{:S(2)}, u32[]{:S(2)}) collective-permute-start(bf16[16,3712]{1,0:T(8,128)(2,1)S(1)} %collective-permute-done.3), channel_id=1, source_target_pairs={{0,2},{1,5},{2,0},{3,7},{4,6},{5,1},{6,4},{7,3},{8,10},{9,13},{10,... | collective-permute-start | bytes 356360 | tf_op jit(solution)/shard_map/ppermute | solution.py:260
  22.9 4.5 %collective-permute-start.8 = (bf16[16,3712]{1,0:T(8,128)(2,1)S(1)}, bf16[16,3712]{1,0:T(8,128)(2,1)S(1)}, u32[]{:S(2)}, u32[]{:S(2)}) collective-permute-start(bf16[16,3712]{1,0:T(8,128)(2,1)S(1)} %collective-permute-done.7.refs_1_), channel_id=1, source_target_pairs={{0,1},{1,0},{2,3},{3,2},{4,5},{5,4},{6,7},{7,6},{8,9},{9,8},{10,11... | collective-permute-start | bytes 356360 | tf_op jit(solution)/shard_map/ppermute | solution.py:264
  27.4 9.3 %copy-start.3 = (bf16[8,2,576]{2,1,0:T(2,128)(2,1)S(1)}, bf16[8,2,576]{2,1,0:T(2,128)(2,1)}, u32[]{:S(2)}) copy-start(bf16[8,2,576]{2,1,0:T(2,128)(2,1)} %refs_3_.3) | copy-start | bytes 55300
  27.4 1.4 %collective-permute-start.12 = (bf16[16,3712]{1,0:T(8,128)(2,1)S(1)}, bf16[16,3712]{1,0:T(8,128)(2,1)S(1)}, u32[]{:S(2)}, u32[]{:S(2)}) collective-permute-start(bf16[16,3712]{1,0:T(8,128)(2,1)S(1)} %collective-permute-done.4.refs_2_), channel_id=1, source_target_pairs={{0,1},{1,0},{2,3},{3,2},{4,5},{5,4},{6,7},{7,6},{8,9},{9,8},{10,11... | collective-permute-start | bytes 356360 | tf_op jit(solution)/shard_map/ppermute | solution.py:264
  32.8 1.6 %collective-permute-start.13 = (bf16[64,1792]{1,0:T(8,128)(2,1)S(1)}, bf16[64,1792]{1,0:T(8,128)(2,1)S(1)}, u32[]{:S(2)}, u32[]{:S(2)}) collective-permute-start(bf16[64,1792]{1,0:T(8,128)(2,1)S(1)} %get-tuple-element.77), channel_id=1, source_target_pairs={{0,1},{1,0},{2,3},{3,2},{4,5},{5,4},{6,7},{7,6},{8,9},{9,8},{10,11... | collective-permute-start | bytes 688136 | tf_op jit(solution)/shard_map/ppermute | solution.py:264
  33.0 7.0 %collective-permute-start.11 = (bf16[64,3584]{1,0:T(8,128)(2,1)S(1)}, bf16[64,3584]{1,0:T(8,128)(2,1)S(1)}, u32[]{:S(2)}, u32[]{:S(2)}) collective-permute-start(bf16[64,3584]{1,0:T(8,128)(2,1)S(1)} %get-tuple-element.72), channel_id=1, source_target_pairs={{0,1},{1,0},{2,3},{3,2},{4,5},{5,4},{6,7},{7,6},{8,9},{9,8},{10,11... | collective-permute-start | bytes 1376264 | tf_op jit(solution)/shard_map/ppermute | solution.py:264
  33.4 2.0 %collective-permute-start.15 = (bf16[64,1792]{1,0:T(8,128)(2,1)S(1)}, bf16[64,1792]{1,0:T(8,128)(2,1)S(1)}, u32[]{:S(2)}, u32[]{:S(2)}) collective-permute-start(bf16[64,1792]{1,0:T(8,128)(2,1)S(1)} %get-tuple-element.79), channel_id=1, source_target_pairs={{0,1},{1,0},{2,3},{3,2},{4,5},{5,4},{6,7},{7,6},{8,9},{9,8},{10,11... | collective-permute-start | bytes 688136 | tf_op jit(solution)/shard_map/ppermute | solution.py:264
  34.4 6.1 %collective-permute-start.14 = (bf16[64,1792]{1,0:T(8,128)(2,1)S(1)}, bf16[64,1792]{1,0:T(8,128)(2,1)S(1)}, u32[]{:S(2)}, u32[]{:S(2)}) collective-permute-start(bf16[64,1792]{1,0:T(8,128)(2,1)S(1)} %add_convert_fusion.1), channel_id=1, source_target_pairs={{0,2},{1,5},{2,0},{3,7},{4,6},{5,1},{6,4},{7,3},{8,10},{9,13},{10,... | collective-permute-start | bytes 688136 | tf_op jit(solution)/shard_map/ppermute | solution.py:260
  35.4 7.7 %collective-permute-start.18 = (bf16[64,1792]{1,0:T(8,128)(2,1)S(1)}, bf16[64,1792]{1,0:T(8,128)(2,1)S(1)}, u32[]{:S(2)}, u32[]{:S(2)}) collective-permute-start(bf16[64,1792]{1,0:T(8,128)(2,1)S(1)} %add_convert_fusion), channel_id=1, source_target_pairs={{0,2},{1,5},{2,0},{3,7},{4,6},{5,1},{6,4},{7,3},{8,10},{9,13},{10,... | collective-permute-start | bytes 688136 | tf_op jit(solution)/shard_map/ppermute | solution.py:260
  40.6 4.9 %collective-permute-start.16 = (bf16[32,1792]{1,0:T(8,128)(2,1)S(1)}, bf16[32,1792]{1,0:T(8,128)(2,1)S(1)}, u32[]{:S(2)}, u32[]{:S(2)}) collective-permute-start(bf16[32,1792]{1,0:T(8,128)(2,1)S(1)} %slice.71), channel_id=1, source_target_pairs={{0,4},{1,3},{2,6},{3,1},{4,0},{5,7},{6,2},{7,5},{8,12},{9,11},{10,... | collective-permute-start | bytes 344072 | tf_op jit(solution)/shard_map/ppermute | solution.py:260
  43.3 5.5 %collective-permute-start.19 = (bf16[32,1792]{1,0:T(8,128)(2,1)S(1)}, bf16[32,1792]{1,0:T(8,128)(2,1)S(1)}, u32[]{:S(2)}, u32[]{:S(2)}) collective-permute-start(bf16[32,1792]{1,0:T(8,128)(2,1)S(1)} %slice.70), channel_id=1, source_target_pairs={{0,4},{1,3},{2,6},{3,1},{4,0},{5,7},{6,2},{7,5},{8,12},{9,11},{10,... | collective-permute-start | bytes 344072 | tf_op jit(solution)/shard_map/ppermute | solution.py:260
  45.5 8.6 %collective-permute-start.17 = (bf16[16,1792]{1,0:T(8,128)(2,1)S(1)}, bf16[16,1792]{1,0:T(8,128)(2,1)S(1)}, u32[]{:S(2)}, u32[]{:S(2)}) collective-permute-start(bf16[16,1792]{1,0:T(8,128)(2,1)S(1)} %slice.73), channel_id=1, source_target_pairs={{0,8},{1,9},{2,10},{3,11},{4,12},{5,13},{6,14},{7,15},{8,0},{9,1},... | collective-permute-start | bytes 172040 | tf_op jit(solution)/shard_map/ppermute | solution.py:260
  48.8 5.3 %collective-permute-start.20 = (bf16[16,1792]{1,0:T(8,128)(2,1)S(1)}, bf16[16,1792]{1,0:T(8,128)(2,1)S(1)}, u32[]{:S(2)}, u32[]{:S(2)}) collective-permute-start(bf16[16,1792]{1,0:T(8,128)(2,1)S(1)} %slice.72), channel_id=1, source_target_pairs={{0,8},{1,9},{2,10},{3,11},{4,12},{5,13},{6,14},{7,15},{8,0},{9,1},... | collective-permute-start | bytes 172040 | tf_op jit(solution)/shard_map/ppermute | solution.py:260
  (5 other events, 36.7 us)

commit v6 on v5

v6 whole, which is shorter than its diff:
```python
import functools

import jax
import jax.numpy as jnp
from jax import lax
from jax.experimental import pallas as pl
from jax.experimental.pallas import tpu as pltpu
from jax.sharding import PartitionSpec as P

LATENT_RANK = 512
SCORE_SCALE = 192.0 ** (-0.5)
ROUTE_SCALE = 2.5
LANES = 128
F32 = jnp.float32
BF16 = jnp.bfloat16
SMALL_COST = pl.CostEstimate(flops=1 << 20, bytes_accessed=1 << 16, transcendentals=0)


def contract(a, b, dim_a, dim_b):
    return lax.dot_general(
        a, b, (((dim_a,), (dim_b,)), ((), ())), preferred_element_type=F32
    )


def attend_request(q_steps, cached, fresh, length):
    heads, context, steps = q_steps[0].shape[1], cached.shape[1], fresh.shape[0]
    q = jnp.concatenate(q_steps, axis=1)
    padded = jnp.concatenate(
        [fresh, jnp.zeros((-steps % 16, fresh.shape[1]), fresh.dtype)], axis=0
    )
    scores = jnp.concatenate([contract(cached, q, 0, 0), contract(padded, q, 1, 0)], axis=0)
    scores = scores * SCORE_SCALE
    key = lax.broadcasted_iota(jnp.int32, scores.shape, 0)
    column = lax.broadcasted_iota(jnp.int32, scores.shape, 1)
    step = key - context
    is_new = jnp.logical_and(step >= 0, jnp.logical_and(step < steps, step * heads <= column))
    is_old = jnp.logical_and(key < context, key < length)
    scores = jnp.where(jnp.logical_or(is_old, is_new), scores, -jnp.inf)
    weights = jnp.exp(scores - jnp.max(scores, axis=0, keepdims=True))
    total = jnp.sum(weights, axis=0, keepdims=True)
    probs = (weights / total).astype(BF16)
    blended = contract(probs[:context], cached[:LATENT_RANK], 0, 1)
    blended = blended + contract(probs[context:], padded[:, :LATENT_RANK], 0, 0)
    return blended.reshape(len(q_steps), heads, LATENT_RANK).astype(BF16)


def attention_kernel(length_ref, query_ref, cache_ref, new_ref, *refs, first, count):
    out_ref, result, sems = refs[-3:]
    steps = query_ref.shape[1]
    copies = []
    for b in range(count):
        r = first + b
        result[b] = attend_request(
            [query_ref[r, s] for s in range(steps)], cache_ref[r], new_ref[r], length_ref[r]
        )
        copy = pltpu.make_async_copy(result.at[b], out_ref.at[r], sems.at[b])
        copy.start()
        copies.append(copy)
    for copy in copies:
        copy.wait()


def attention(lengths, inputs, first, count, previous):
    requests, steps, latent, heads = inputs[0].shape
    vmem = pl.BlockSpec(memory_space=pltpu.VMEM)
    hbm = pl.BlockSpec(memory_space=pl.ANY)
    in_specs = [pl.BlockSpec(memory_space=pltpu.SMEM), vmem, vmem, vmem]
    operands = [pltpu.with_memory_space_constraint(lengths, pltpu.HBM)]
    operands += [pltpu.with_memory_space_constraint(x, pltpu.VMEM) for x in inputs]
    aliases = {}
    if previous is not None:
        in_specs.append(hbm)
        aliases = {len(operands): 0}
        operands.append(pltpu.with_memory_space_constraint(previous, pltpu.HBM))
    return pl.pallas_call(
        functools.partial(attention_kernel, first=first, count=count),
        in_specs=in_specs,
        out_specs=hbm,
        out_shape=pltpu.HBM((requests, steps, heads, LATENT_RANK), BF16),
        scratch_shapes=[
            pltpu.VMEM((count, steps, heads, LATENT_RANK), BF16),
            pltpu.SemaphoreType.DMA((count,)),
        ],
        input_output_aliases=aliases,
        compiler_params=pltpu.CompilerParams(vmem_limit_bytes=12 << 20),
        cost_estimate=SMALL_COST,
        name="attention",
    )(*operands)


def route_kernel(place_ref, rows_ref, score_ref, expert_ref, out_ref, *, experts, slots):
    tokens, width = rows_ref.shape
    sigmoid = jax.nn.sigmoid(score_ref[...])
    weights = ROUTE_SCALE * sigmoid / jnp.sum(sigmoid, axis=0, keepdims=True)
    weights = weights.astype(BF16).astype(F32)
    named = expert_ref[...]
    even = lax.broadcasted_iota(jnp.int32, named.shape, 1) % 2 == 0
    slot = jnp.zeros_like(named)
    for e in range(experts):
        slot = jnp.where(
            named == e, jnp.where(even, place_ref[0, e], place_ref[1, e]), slot
        )
    index = lax.broadcasted_iota(jnp.int32, (LANES, tokens), 0)
    table = jnp.zeros((LANES, tokens), F32)
    for k in range(named.shape[0]):
        table = table + jnp.where(index == slot[k : k + 1], weights[k : k + 1], 0.0)
    row = lax.broadcasted_iota(jnp.int32, (tokens, tokens), 0)
    column = lax.broadcasted_iota(jnp.int32, (tokens, tokens), 1)
    unit = jnp.where(row == column, 1.0, 0.0).astype(BF16)
    out_ref[:, :width] = rows_ref[...]
    out_ref[:, width:] = contract(unit, table.astype(BF16), 1, 1).astype(BF16)


def route(placement, rows, scores, expert_ids, slots):
    tokens, width = rows.shape
    vmem = pl.BlockSpec(memory_space=pltpu.VMEM)
    return pl.pallas_call(
        functools.partial(route_kernel, experts=placement.shape[0], slots=slots),
        in_specs=[pl.BlockSpec(memory_space=pltpu.SMEM), vmem, vmem, vmem],
        out_specs=vmem,
        out_shape=jax.ShapeDtypeStruct((tokens, width + LANES), BF16),
        compiler_params=pltpu.CompilerParams(vmem_limit_bytes=4 << 20),
        cost_estimate=pl.CostEstimate(flops=1 << 34, bytes_accessed=1 << 25, transcendentals=0),
        name="route",
    )(*(pltpu.with_memory_space_constraint(x, pltpu.HBM) for x in (placement.T, rows, scores.T, expert_ids.T)))


def experts_kernel(*refs, parts, groups, tile):
    rows_refs, refs = refs[:parts], refs[parts:]
    (gate_ref, up_ref, down_ref, chip_ref), refs = refs[:4], refs[4:]
    out_refs, (rows_s, act_s) = refs[: 2 * groups], refs[2 * groups :]
    slots, width, hidden = gate_ref.shape
    start = 0
    for ref in rows_refs:
        rows_s[start : start + ref.shape[0], :] = ref[...]
        start += ref.shape[0]
    table = rows_s[:, width:].astype(F32)
    lane = lax.broadcasted_iota(jnp.int32, table.shape, 1)
    for s in range(slots):
        slot = chip_ref[0] * slots + s
        weight = jnp.sum(jnp.where(lane == slot, table, 0.0), axis=1, keepdims=True)
        rows = rows_s[:, :width]
        gate = contract(rows, gate_ref[s], 1, 0)
        up = contract(rows, up_ref[s], 1, 0)
        act = gate / (1.0 + jnp.exp(-gate)) * up
        act_s[:, s * hidden : (s + 1) * hidden] = (weight * act).astype(BF16)

    def step(i, carry):
        columns = pl.ds(pl.multiple_of(i * tile, LANES), tile)
        total = contract(act_s[:, :hidden], down_ref[0, :, columns], 1, 0)
        for s in range(1, slots):
            total = total + contract(
                act_s[:, s * hidden : (s + 1) * hidden], down_ref[s, :, columns], 1, 0
            )
        start = 0
        for ref in out_refs:
            ref[:, columns] = total[start : start + ref.shape[0]].astype(ref.dtype)
            start += ref.shape[0]
        return carry

    lax.fori_loop(0, width // tile, step, 0)


def experts(parts, gate, up, down, chip, groups):
    slots, width, hidden = gate.shape
    count = 2 * sum(groups)
    vmem = pl.BlockSpec(memory_space=pltpu.VMEM)
    outs = pl.pallas_call(
        functools.partial(experts_kernel, parts=len(parts), groups=len(groups), tile=width // 4),
        in_specs=[vmem] * (len(parts) + 3) + [pl.BlockSpec(memory_space=pltpu.SMEM)],
        out_specs=[vmem] * (2 * len(groups)),
        out_shape=[
            jax.ShapeDtypeStruct((n, width), kind) for kind in (F32, BF16) for n in groups
        ],
        scratch_shapes=[
            pltpu.VMEM((count, parts[0].shape[1]), BF16),
            pltpu.VMEM((count, slots * hidden), BF16),
        ],
        compiler_params=pltpu.CompilerParams(vmem_limit_bytes=16 << 20),
        cost_estimate=SMALL_COST,
        name="experts",
    )(*parts, gate, up, down, chip)
    return outs[: len(groups)], outs[len(groups) :]


def halving_masks(ep):
    bits = []
    bit = ep // 2
    while bit:
        bits.append(bit)
        bit //= 2
    other = bits[:-2] + bits[-2:][::-1]
    return bits, other


def hop(x, ep, sub, masks, turn):
    pairs = [
        (e * sub + s, (e ^ masks[s % 2][turn]) * sub + s) for e in range(ep) for s in range(sub)
    ]
    return lax.ppermute(x, ("ep", "sub"), pairs)


def swap(x):
    return lax.ppermute(x, "sub", [(0, 1), (1, 0)])


def add(*terms):
    total = terms[0].astype(F32)
    for t in terms[1:]:
        total = total + t.astype(F32)
    return total


def on_device(
    queries,
    latent_cache,
    new_latent,
    lengths,
    moe_input,
    gate_scores,
    expert_ids,
    placement,
    w_gate,
    w_up,
    w_down,
):
    ep, sub = lax.axis_size("ep"), lax.axis_size("sub")
    masks = halving_masks(ep)
    turns = len(masks[0])
    width = moe_input.shape[1]
    requests, width = queries.shape[0], moe_input.shape[1]
    inputs = [queries.transpose(0, 1, 3, 2), latent_cache.transpose(0, 2, 1), new_latent]
    chip = lax.axis_index("ep").astype(jnp.int32)[None]
    slots = ep * w_gate.shape[0]
    barrier = lax.optimization_barrier
    chip, gate_scores, lengths = barrier((chip, gate_scores, lengths))

    requests = queries.shape[0]
    gate, up, down = [pltpu.with_memory_space_constraint(w, pltpu.VMEM) for w in (w_gate, w_up, w_down)]
    inputs = [pltpu.with_memory_space_constraint(x, pltpu.VMEM) for x in inputs]

    out = None
    done = 0

    def attend(count, tie):
        nonlocal out, inputs, done
        count = min(count, requests - done)
        if count == 0:
            return tie
        out = attention(lengths, inputs, done, count, out)
        done += count
        tie, out, inputs = barrier((tie, out, inputs))
        return tie

    own = route(placement, moe_input, gate_scores, expert_ids, slots)
    for turn in range(turns - 3):
        own = jnp.concatenate([own, hop(own, ep, sub, masks, turn)], axis=0)
    hop_a, hop_b, hop_c = (
        functools.partial(hop, ep=ep, sub=sub, masks=masks, turn=turn)
        for turn in range(turns - 3, turns)
    )
    n = own.shape[0]
    own, inputs = barrier((own, inputs))
    a, b, c = attend(2, (hop_a(own), hop_b(own), hop_c(own)))
    ab, ac, bc = hop_b(a), hop_c(a), hop_c(b)
    a, inputs = barrier((a, inputs))
    ab = attend(1, ab)
    abc = hop_c(ab)
    base = jnp.concatenate([own, a], axis=0)
    second = jnp.concatenate([b, ab], axis=0)
    early = jnp.concatenate([c, ac], axis=0)
    near_rows = [base, second, swap(base), swap(second)]
    near_rows, c = barrier((near_rows, c))
    late_swap = swap(bc)
    early_swap = swap(early)
    near_own, near_other = experts(near_rows, gate, up, down, chip, [4 * n])
    abc, early_swap, late_swap, near_own, near_other = barrier(
        (abc, early_swap, late_swap, near_own, near_other)
    )
    near_back = swap(near_other[0])
    far_rows = [early, bc, abc, early_swap, late_swap, swap(abc)]
    far_own, far_other = experts(far_rows, gate, up, down, chip, [3 * n, n])
    near = barrier(add(near_own[0], near_back))

    sent = add(far_own[1], swap(far_other[1])).astype(BF16)
    rest = add(far_own[0], swap(far_other[0])).astype(BF16)
    got_ab = hop_c(sent)
    got = hop_c(rest)
    rest, inputs = barrier((rest, inputs))
    got_ab = attend(2, got_ab)
    sent = add(near[3 * n :], got_ab).astype(BF16)
    got_a = hop_b(sent)
    sent, inputs = barrier((sent, inputs))
    got_a = attend(1, got_a)
    back_b = hop_b(add(near[2 * n : 3 * n], got[2 * n :]).astype(BF16))
    sent = add(near[n : 2 * n], got[n : 2 * n], got_a).astype(BF16)
    back_a = hop_a(sent)
    sent, inputs = barrier((sent, inputs))
    back_a = attend(requests, back_a)
    total = add(near[:n], got[:n], back_b, back_a)
    for turn in range(turns - 4, -1, -1):
        half = total.shape[0] // 2
        total = add(total[:half], hop(total[half:].astype(BF16), ep, sub, masks, turn))
    return out, total.astype(BF16)


def solution(mesh):
    split = ("groups", "ep", "sub")
    return jax.shard_map(
        on_device,
        mesh=mesh,
        in_specs=(
            P(split, None, None, None),
            P(split, None, None),
            P(split, None, None),
            P(split),
            P(split, None),
            P(split, None),
            P(split, None),
            P("groups", None),
            P(("groups", "ep"), None, "sub"),
            P(("groups", "ep"), None, "sub"),
            P(("groups", "ep"), "sub", None),
        ),
        out_specs=(P(split, None, None, None), P(split, None)),
        check_vma=False,
    )
```

time: 55 us -> 51.7 us (0.940)
  Pallas kernels: 25.5 us -> 22.1 us
  waiting for transfers between devices: 6.11 us -> 9.47 us
  starting transfers between devices: 20.9 us -> 18 us
    pallas_call x6 -> x7, Pallas kernels: 24.4 us -> 20.8 us  [the longest x5 12.8 us: attention(): pl.pallas_call(functools.partial(attention_kernel, first=first, count=cou...]
    ppermute x13 -> x12, waiting for transfers between devices: 4.06 us -> 7.27 us  [hop(): return lax.ppermute(x, ('ep', 'sub'), pairs)]
    ppermute x13 -> x12, starting transfers between devices: 18.9 us -> 16.3 us  [hop(): return lax.ppermute(x, ('ep', 'sub'), pairs)]
    convert_element_type x2 -> x5, other arithmetic: 0.11 us -> 0.89 us  [the longest x1 0.7 us: on_device(): return (out, total.astype(BF16))]
    concatenate x1 -> x0, other arithmetic: 0.65 us -> none  [on_device(): return (out, jnp.concatenate(totals, axis=1).astype(BF16))]
  transfers between devices with their start and end apart: 21 -> 20, of which waited for: 6 -> 8; matrix products, arithmetic and copies ran while one was open for 1% -> 1% of each run, Pallas kernels for 37% -> 33%
where the time goes in v6:
time: 51.7 us; the launch traced here: 51.6 us
  Pallas kernels  22.1 us (43%)
  starting transfers between devices  18 us (35%)
  waiting for transfers between devices  9.47 us (18%)
  other arithmetic  0.97 us (2%)
  between operations  0.91 us (2%)
    ppermute x12, starting transfers between devices, hop(): return lax.ppermute(x, ('ep', 'sub'), pairs)  16.3 us
    pallas_call x5, Pallas kernels, attention(): pl.pallas_call(functools.partial(attention_kernel, first=first, count=cou...  12.8 us
    pallas_call x2, Pallas kernels, experts(): pl.pallas_call(functools.partial(experts_kernel, parts=len(parts), groups...  8.03 us
    ppermute x12, waiting for transfers between devices, hop(): return lax.ppermute(x, ('ep', 'sub'), pairs)  7.27 us
    ppermute x8, waiting for transfers between devices, swap(): return lax.ppermute(x, 'sub', [(0, 1), (1, 0)])  2.2 us
    ppermute x8, starting transfers between devices, swap(): return lax.ppermute(x, 'sub', [(0, 1), (1, 0)])  1.7 us
    pallas_call x1, Pallas kernels, route(): pl.pallas_call(functools.partial(route_kernel, experts=placement.shape[0]...  1.28 us
  transfers between devices with their start and end apart: 20, of which 8 were waited for; matrix products, arithmetic and copies ran while one was open for 1% of the time, Pallas kernels for 33%

profile of v6, /device:TPU:0, one launch (start us, length us, event | category | flops | bytes accessed | tf_op | source)
XLA Modules:
  0.0 51.6 jit_solution(10879889742175847997)
XLA Ops:
  0.7 1.3 %route.1 = bf16[16,3712]{1,0:T(8,128)(2,1)S(1)} custom-call(s32[2,14]{1,0:T(2,128)} %bitcast.20, bf16[16,3584]{1,0:T(8,128)(2,1)} %rows_ref.1, f32[8,16]{1,0:T(8,128)} %bitcast.18, s32[8,16]{1,0:T(8,128)} %bitcast.19), custom_call_target="tpu_custom_call" | custom-call | flops 17179869184 | bytes 33554432 | tf_op jit(solution)/shard_map/route/pallas_call | solution.py:117
  2.0 4.0 %collective-permute-start = (bf16[16,3712]{1,0:T(8,128)(2,1)S(1)}, bf16[16,3712]{1,0:T(8,128)(2,1)S(1)}, u32[]{:S(2)}, u32[]{:S(2)}) collective-permute-start(bf16[16,3712]{1,0:T(8,128)(2,1)S(1)} %route.1), channel_id=1, source_target_pairs={{0,8},{1,9},{2,10},{3,11},{4,12},{5,13},{6,14},{7,15},{8,0},{9,1},... | collective-permute-start | bytes 356360 | tf_op jit(solution)/shard_map/ppermute | solution.py:200
  6.0 1.6 %collective-permute-start.1 = (bf16[16,3712]{1,0:T(8,128)(2,1)S(1)}, bf16[16,3712]{1,0:T(8,128)(2,1)S(1)}, u32[]{:S(2)}, u32[]{:S(2)}) collective-permute-start(bf16[16,3712]{1,0:T(8,128)(2,1)S(1)} %route.1), channel_id=1, source_target_pairs={{0,4},{1,3},{2,6},{3,1},{4,0},{5,7},{6,2},{7,5},{8,12},{9,11},{10,... | collective-permute-start | bytes 356360 | tf_op jit(solution)/shard_map/ppermute | solution.py:200
  7.6 1.5 %collective-permute-start.2 = (bf16[16,3712]{1,0:T(8,128)(2,1)S(1)}, bf16[16,3712]{1,0:T(8,128)(2,1)S(1)}, u32[]{:S(2)}, u32[]{:S(2)}) collective-permute-start(bf16[16,3712]{1,0:T(8,128)(2,1)S(1)} %route.1), channel_id=1, source_target_pairs={{0,2},{1,5},{2,0},{3,7},{4,6},{5,1},{6,4},{7,3},{8,10},{9,13},{10,... | collective-permute-start | bytes 356360 | tf_op jit(solution)/shard_map/ppermute | solution.py:200
  9.2 2.8 %attention.5.refs_0_ = bf16[8,2,128,512]{3,2,1,0:T(8,128)(2,1)} custom-call(s32[8]{0:T(128)} %length_ref.4, bf16[8,2,576,128]{3,2,1,0:T(8,128)(2,1)S(1)} %bitcast.6, bf16[8,576,256]{2,1,0:T(8,128)(2,1)S(1)} %bitcast.11, bf16[8,2,576]{2,1,0:T(2,128)(2,1)S(1)} %copy-done.4), custom_call_target="tpu_custom_call" | custom-call | flops 1048576 | bytes 65536 | tf_op jit(solution)/shard_map/attention/pallas_call | solution.py:75
  12.0 1.3 %collective-permute-done.1 = bf16[16,3712]{1,0:T(8,128)(2,1)S(1)} collective-permute-done((bf16[16,3712]{1,0:T(8,128)(2,1)S(1)}, bf16[16,3712]{1,0:T(8,128)(2,1)S(1)}, u32[]{:S(2)}, u32[]{:S(2)}) %collective-permute-start.1) | collective-permute-done | bytes 118816 | tf_op jit(solution)/shard_map/ppermute | solution.py:200
  13.6 1.5 %collective-permute-start.5 = (bf16[16,3712]{1,0:T(8,128)(2,1)S(1)}, bf16[16,3712]{1,0:T(8,128)(2,1)S(1)}, u32[]{:S(2)}, u32[]{:S(2)}) collective-permute-start(bf16[16,3712]{1,0:T(8,128)(2,1)S(1)} %collective-permute-done), channel_id=1, source_target_pairs={{0,2},{1,5},{2,0},{3,7},{4,6},{5,1},{6,4},{7,3},{8,10},{9,13},{10,... | collective-permute-start | bytes 356360 | tf_op jit(solution)/shard_map/ppermute | solution.py:200
  15.7 2.4 %attention.6.refs_0_ = bf16[8,2,128,512]{3,2,1,0:T(8,128)(2,1)} custom-call(s32[8]{0:T(128)} %length_ref.4, bf16[8,2,576,128]{3,2,1,0:T(8,128)(2,1)S(1)} %bitcast.7, bf16[8,576,256]{2,1,0:T(8,128)(2,1)S(1)} %bitcast.12, bf16[8,2,576]{2,1,0:T(2,128)(2,1)S(1)} %copy-done.4, bf16[8,2,128,512]{3,2,1,0:T(8,128)(2,1)} %attention.5.refs_0_), custom_call_target="tpu_custom_call", output_to_operand_aliasing={{}: (4, {})} | custom-call | flops 1048576 | bytes 65536 | tf_op jit(solution)/shard_map/attention/pallas_call | solution.py:75
  18.1 1.3 %collective-permute-done.3 = bf16[16,3712]{1,0:T(8,128)(2,1)S(1)} collective-permute-done((bf16[16,3712]{1,0:T(8,128)(2,1)S(1)}, bf16[16,3712]{1,0:T(8,128)(2,1)S(1)}, u32[]{:S(2)}, u32[]{:S(2)}) %collective-permute-start.3) | collective-permute-done | bytes 118816 | tf_op jit(solution)/shard_map/ppermute | solution.py:200
  21.0 4.0 %experts.2 = (f32[64,3584]{1,0:T(8,128)S(1)}, bf16[64,3584]{1,0:T(8,128)(2,1)S(1)}) custom-call(bf16[32,3712]{1,0:T(8,128)(2,1)S(1)} %constant_dynamic-update-slice_fusion.2.refs_0_, bf16[32,3712]{1,0:T(8,128)(2,1)S(1)} %constant_dynamic-update-slice_fusion.4.refs_1_, bf16[32,3712]{1,0:T(8,128)(2,1)S(1)} %collective-permute-done.9.refs_2_, ...), custom_call_target="tpu_custom_call" | custom-call | flops 1048576 | bytes 65536 | tf_op jit(solution)/shard_map/experts/pallas_call | solution.py:168
  25.2 1.2 %collective-permute-done.12.refs_5_ = bf16[16,3712]{1,0:T(8,128)(2,1)S(1)} collective-permute-done((bf16[16,3712]{1,0:T(8,128)(2,1)S(1)}, bf16[16,3712]{1,0:T(8,128)(2,1)S(1)}, u32[]{:S(2)}, u32[]{:S(2)}) %collective-permute-start.12) | collective-permute-done | bytes 118816 | tf_op jit(solution)/shard_map/ppermute | solution.py:204
  26.4 4.0 %experts.3 = (f32[48,3584]{1,0:T(8,128)S(1)}, f32[16,3584]{1,0:T(8,128)S(1)}, bf16[48,3584]{1,0:T(8,128)(2,1)S(1)}, bf16[16,3584]{1,0:T(8,128)(2,1)S(1)}) custom-call(bf16[32,3712]{1,0:T(8,128)(2,1)S(1)} %constant_dynamic-update-slice_fusion.refs_0_, bf16[16,3712]{1,0:T(8,128)(2,1)S(1)} %collective-permute-done.7.refs_1_, ...), custom_call_target="tpu_custom_call" | custom-call | flops 1048576 | bytes 65536 | tf_op jit(solution)/shard_map/experts/pallas_call | solution.py:168
  31.2 0.7 %collective-permute-done.15 = bf16[16,3584]{1,0:T(8,128)(2,1)S(1)} collective-permute-done((bf16[16,3584]{1,0:T(8,128)(2,1)S(1)}, bf16[16,3584]{1,0:T(8,128)(2,1)S(1)}, u32[]{:S(2)}, u32[]{:S(2)}) %collective-permute-start.15) | collective-permute-done | bytes 114720 | tf_op jit(solution)/shard_map/ppermute | solution.py:204
  31.9 1.4 %collective-permute-start.16 = (bf16[16,3584]{1,0:T(8,128)(2,1)S(1)}, bf16[16,3584]{1,0:T(8,128)(2,1)S(1)}, u32[]{:S(2)}, u32[]{:S(2)}) collective-permute-start(bf16[16,3584]{1,0:T(8,128)(2,1)S(1)} %add_convert_fusion.1), channel_id=1, source_target_pairs={{0,2},{1,5},{2,0},{3,7},{4,6},{5,1},{6,4},{7,3},{8,10},{9,13},{10,... | collective-permute-start | bytes 344072 | tf_op jit(solution)/shard_map/ppermute | solution.py:200
  33.4 1.2 %collective-permute-start.14 = (bf16[48,3584]{1,0:T(8,128)(2,1)S(1)}, bf16[48,3584]{1,0:T(8,128)(2,1)S(1)}, u32[]{:S(2)}, u32[]{:S(2)}) collective-permute-start(bf16[48,3584]{1,0:T(8,128)(2,1)S(1)} %add_convert_fusion), channel_id=1, source_target_pairs={{0,2},{1,5},{2,0},{3,7},{4,6},{5,1},{6,4},{7,3},{8,10},{9,13},{10,... | collective-permute-start | bytes 1032200 | tf_op jit(solution)/shard_map/ppermute | solution.py:200
  34.6 2.7 %attention.7.refs_0_ = bf16[8,2,128,512]{3,2,1,0:T(8,128)(2,1)} custom-call(s32[8]{0:T(128)} %length_ref.4, bf16[8,2,576,128]{3,2,1,0:T(8,128)(2,1)S(1)} %bitcast.8, bf16[8,576,256]{2,1,0:T(8,128)(2,1)S(1)} %bitcast.13, bf16[8,2,576]{2,1,0:T(2,128)(2,1)S(1)} %copy-done.4, bf16[8,2,128,512]{3,2,1,0:T(8,128)(2,1)} %attention.6.refs_0_), custom_call_target="tpu_custom_call", output_to_operand_aliasing={{}: (4, {})} | custom-call | flops 1048576 | bytes 65536 | tf_op jit(solution)/shard_map/attention/pallas_call | solution.py:75
  37.4 0.6 %collective-permute-start.17 = (bf16[16,3584]{1,0:T(8,128)(2,1)S(1)}, bf16[16,3584]{1,0:T(8,128)(2,1)S(1)}, u32[]{:S(2)}, u32[]{:S(2)}) collective-permute-start(bf16[16,3584]{1,0:T(8,128)(2,1)S(1)} %fusion.4), channel_id=1, source_target_pairs={{0,4},{1,3},{2,6},{3,1},{4,0},{5,7},{6,2},{7,5},{8,12},{9,11},{10,... | collective-permute-start | bytes 344072 | tf_op jit(solution)/shard_map/ppermute | solution.py:200
  38.0 2.2 %attention.8.refs_0_ = bf16[8,2,128,512]{3,2,1,0:T(8,128)(2,1)} custom-call(s32[8]{0:T(128)} %length_ref.4, bf16[8,2,576,128]{3,2,1,0:T(8,128)(2,1)S(1)} %bitcast.9, bf16[8,576,256]{2,1,0:T(8,128)(2,1)S(1)} %bitcast.14, bf16[8,2,576]{2,1,0:T(2,128)(2,1)S(1)} %copy-done.4, bf16[8,2,128,512]{3,2,1,0:T(8,128)(2,1)} %attention.7.refs_0_), custom_call_target="tpu_custom_call", output_to_operand_aliasing={{}: (4, {})} | custom-call | flops 1048576 | bytes 65536 | tf_op jit(solution)/shard_map/attention/pallas_call | solution.py:75
  40.2 2.0 %collective-permute-done.17 = bf16[16,3584]{1,0:T(8,128)(2,1)S(1)} collective-permute-done((bf16[16,3584]{1,0:T(8,128)(2,1)S(1)}, bf16[16,3584]{1,0:T(8,128)(2,1)S(1)}, u32[]{:S(2)}, u32[]{:S(2)}) %collective-permute-start.17) | collective-permute-done | bytes 114720 | tf_op jit(solution)/shard_map/ppermute | solution.py:200
  42.3 1.6 %collective-permute-start.18 = (bf16[16,3584]{1,0:T(8,128)(2,1)S(1)}, bf16[16,3584]{1,0:T(8,128)(2,1)S(1)}, u32[]{:S(2)}, u32[]{:S(2)}) collective-permute-start(bf16[16,3584]{1,0:T(8,128)(2,1)S(1)} %get-tuple-element.121), channel_id=1, source_target_pairs={{0,8},{1,9},{2,10},{3,11},{4,12},{5,13},{6,14},{7,15},{8,0},{9,1},... | collective-permute-start | bytes 344072 | tf_op jit(solution)/shard_map/ppermute | solution.py:200
  44.0 1.5 %collective-permute-start.19 = (bf16[16,3584]{1,0:T(8,128)(2,1)S(1)}, bf16[16,3584]{1,0:T(8,128)(2,1)S(1)}, u32[]{:S(2)}, u32[]{:S(2)}) collective-permute-start(bf16[16,3584]{1,0:T(8,128)(2,1)S(1)} %get-tuple-element.120), channel_id=1, source_target_pairs={{0,4},{1,3},{2,6},{3,1},{4,0},{5,7},{6,2},{7,5},{8,12},{9,11},{10,... | collective-permute-start | bytes 344072 | tf_op jit(solution)/shard_map/ppermute | solution.py:200
  45.5 2.7 %attention.9 = bf16[8,2,128,512]{3,2,1,0:T(8,128)(2,1)} custom-call(s32[8]{0:T(128)} %length_ref.4, bf16[8,2,576,128]{3,2,1,0:T(8,128)(2,1)S(1)} %bitcast.10, bf16[8,576,256]{2,1,0:T(8,128)(2,1)S(1)} %bitcast.15, bf16[8,2,576]{2,1,0:T(2,128)(2,1)S(1)} %copy-done.4, bf16[8,2,128,512]{3,2,1,0:T(8,128)(2,1)} %attention.8.refs_0_), custom_call_target="tpu_custom_call", output_to_operand_aliasing={{}: (4, {})} | custom-call | flops 1048576 | bytes 65536 | tf_op jit(solution)/shard_map/attention/pallas_call | solution.py:75
  48.1 2.6 %collective-permute-done.18 = bf16[16,3584]{1,0:T(8,128)(2,1)S(1)} collective-permute-done((bf16[16,3584]{1,0:T(8,128)(2,1)S(1)}, bf16[16,3584]{1,0:T(8,128)(2,1)S(1)}, u32[]{:S(2)}, u32[]{:S(2)}) %collective-permute-start.18) | collective-permute-done | bytes 114720 | tf_op jit(solution)/shard_map/ppermute | solution.py:200
  50.9 0.7 %fusion.3 = bf16[16,3584]{1,0:T(8,128)(2,1)} fusion(f32[64,3584]{1,0:T(8,128)S(1)} %convert_add_fusion, bf16[16,3584]{1,0:T(8,128)(2,1)S(1)} %collective-permute-done.18, bf16[16,3584]{1,0:T(8,128)(2,1)S(1)} %collective-permute-done.19, bf16[48,3584]{1,0:T(8,128)(2,1)S(1)} %collective-permute-done.14), kind=kLoop, calls=%fused_computation.7 | loop fusion | flops 401408 | bytes 688128 | tf_op jit(solution)/shard_map/convert_element_type | solution.py:304
  (51 shorter events, 3.9 us)
Async XLA Ops:
  0.6 8.5 %copy-start = (bf16[8,2,128,576]{2,3,1,0:T(8,128)(2,1)S(1)}, bf16[8,2,128,576]{2,3,1,0:T(8,128)(2,1)}, u32[]{:S(2)}) copy-start(bf16[8,2,128,576]{2,3,1,0:T(8,128)(2,1)} %param.11) | copy-start | bytes 7077892
  0.7 20.3 %copy-start.3 = (bf16[2,512,3584]{2,1,0:T(8,128)(2,1)S(1)}, bf16[2,512,3584]{2,1,0:T(8,128)(2,1)}, u32[]{:S(2)}) copy-start(bf16[2,512,3584]{2,1,0:T(8,128)(2,1)} %refs_8_.1) | copy-start | bytes 22020100
  2.0 10.0 %collective-permute-start = (bf16[16,3712]{1,0:T(8,128)(2,1)S(1)}, bf16[16,3712]{1,0:T(8,128)(2,1)S(1)}, u32[]{:S(2)}, u32[]{:S(2)}) collective-permute-start(bf16[16,3712]{1,0:T(8,128)(2,1)S(1)} %route.1), channel_id=1, source_target_pairs={{0,8},{1,9},{2,10},{3,11},{4,12},{5,13},{6,14},{7,15},{8,0},{9,1},... | collective-permute-start | bytes 356360 | tf_op jit(solution)/shard_map/ppermute | solution.py:200
  6.0 7.3 %collective-permute-start.1 = (bf16[16,3712]{1,0:T(8,128)(2,1)S(1)}, bf16[16,3712]{1,0:T(8,128)(2,1)S(1)}, u32[]{:S(2)}, u32[]{:S(2)}) collective-permute-start(bf16[16,3712]{1,0:T(8,128)(2,1)S(1)} %route.1), channel_id=1, source_target_pairs={{0,4},{1,3},{2,6},{3,1},{4,0},{5,7},{6,2},{7,5},{8,12},{9,11},{10,... | collective-permute-start | bytes 356360 | tf_op jit(solution)/shard_map/ppermute | solution.py:200
  7.6 5.7 %collective-permute-start.2 = (bf16[16,3712]{1,0:T(8,128)(2,1)S(1)}, bf16[16,3712]{1,0:T(8,128)(2,1)S(1)}, u32[]{:S(2)}, u32[]{:S(2)}) collective-permute-start(bf16[16,3712]{1,0:T(8,128)(2,1)S(1)} %route.1), channel_id=1, source_target_pairs={{0,2},{1,5},{2,0},{3,7},{4,6},{5,1},{6,4},{7,3},{8,10},{9,13},{10,... | collective-permute-start | bytes 356360 | tf_op jit(solution)/shard_map/ppermute | solution.py:200
  9.1 11.8 %slice-start = ((s8[7340032]{0:T(1024)(128)(4,1)}), s8[4194304]{0:T(1024)(128)(4,1)S(1)}, s32[]{:S(2)}) async-start(s8[7340032]{0:T(1024)(128)(4,1)} %bitcast.16), calls=%async_computation | async-start | bytes 8388608
  9.2 11.8 %copy-start.2 = (bf16[2,3584,512]{2,1,0:T(8,128)(2,1)S(1)}, bf16[2,3584,512]{2,1,0:T(8,128)(2,1)}, u32[]{:S(2)}) copy-start(bf16[2,3584,512]{2,1,0:T(8,128)(2,1)} %refs_7_.1) | copy-start | bytes 22020100
  13.3 6.1 %collective-permute-start.3 = (bf16[16,3712]{1,0:T(8,128)(2,1)S(1)}, bf16[16,3712]{1,0:T(8,128)(2,1)S(1)}, u32[]{:S(2)}, u32[]{:S(2)}) collective-permute-start(bf16[16,3712]{1,0:T(8,128)(2,1)S(1)} %collective-permute-done), channel_id=1, source_target_pairs={{0,4},{1,3},{2,6},{3,1},{4,0},{5,7},{6,2},{7,5},{8,12},{9,11},{10,... | collective-permute-start | bytes 356360 | tf_op jit(solution)/shard_map/ppermute | solution.py:200
  13.6 5.9 %collective-permute-start.5 = (bf16[16,3712]{1,0:T(8,128)(2,1)S(1)}, bf16[16,3712]{1,0:T(8,128)(2,1)S(1)}, u32[]{:S(2)}, u32[]{:S(2)}) collective-permute-start(bf16[16,3712]{1,0:T(8,128)(2,1)S(1)} %collective-permute-done), channel_id=1, source_target_pairs={{0,2},{1,5},{2,0},{3,7},{4,6},{5,1},{6,4},{7,3},{8,10},{9,13},{10,... | collective-permute-start | bytes 356360 | tf_op jit(solution)/shard_map/ppermute | solution.py:200
  15.0 5.5 %collective-permute-start.7 = (bf16[16,3712]{1,0:T(8,128)(2,1)S(1)}, bf16[16,3712]{1,0:T(8,128)(2,1)S(1)}, u32[]{:S(2)}, u32[]{:S(2)}) collective-permute-start(bf16[16,3712]{1,0:T(8,128)(2,1)S(1)} %collective-permute-done.1), channel_id=1, source_target_pairs={{0,2},{1,5},{2,0},{3,7},{4,6},{5,1},{6,4},{7,3},{8,10},{9,13},{10,... | collective-permute-start | bytes 356360 | tf_op jit(solution)/shard_map/ppermute | solution.py:200
  15.7 5.0 %collective-permute-start.9 = (bf16[32,3712]{1,0:T(8,128)(2,1)S(1)}, bf16[32,3712]{1,0:T(8,128)(2,1)S(1)}, u32[]{:S(2)}, u32[]{:S(2)}) collective-permute-start(bf16[32,3712]{1,0:T(8,128)(2,1)S(1)} %constant_dynamic-update-slice_fusion.2.refs_0_), channel_id=1, source_target_pairs={{0,1},{1,0},{2,3},{3,2},{4,5},{5,4},{6,7},{7,6},{8,9},{9,8},{10,11... | collective-permute-start | bytes 712712 | tf_op jit(solution)/shard_map/ppermute | solution.py:204
  19.4 1.6 %collective-permute-start.10 = (bf16[32,3712]{1,0:T(8,128)(2,1)S(1)}, bf16[32,3712]{1,0:T(8,128)(2,1)S(1)}, u32[]{:S(2)}, u32[]{:S(2)}) collective-permute-start(bf16[32,3712]{1,0:T(8,128)(2,1)S(1)} %constant_dynamic-update-slice_fusion.4.refs_1_), channel_id=1, source_target_pairs={{0,1},{1,0},{2,3},{3,2},{4,5},{5,4},{6,7},{7,6},{8,9},{9,8},{10,11... | collective-permute-start | bytes 712712 | tf_op jit(solution)/shard_map/ppermute | solution.py:204
  19.5 5.5 %collective-permute-start.6 = (bf16[32,3712]{1,0:T(8,128)(2,1)S(1)}, bf16[32,3712]{1,0:T(8,128)(2,1)S(1)}, u32[]{:S(2)}, u32[]{:S(2)}) collective-permute-start(bf16[32,3712]{1,0:T(8,128)(2,1)S(1)} %constant_dynamic-update-slice_fusion.refs_0_), channel_id=1, source_target_pairs={{0,1},{1,0},{2,3},{3,2},{4,5},{5,4},{6,7},{7,6},{8,9},{9,8},{10,11... | collective-permute-start | bytes 712712 | tf_op jit(solution)/shard_map/ppermute | solution.py:204
  20.1 4.9 %collective-permute-start.4 = (bf16[16,3712]{1,0:T(8,128)(2,1)S(1)}, bf16[16,3712]{1,0:T(8,128)(2,1)S(1)}, u32[]{:S(2)}, u32[]{:S(2)}) collective-permute-start(bf16[16,3712]{1,0:T(8,128)(2,1)S(1)} %collective-permute-done.3), channel_id=1, source_target_pairs={{0,2},{1,5},{2,0},{3,7},{4,6},{5,1},{6,4},{7,3},{8,10},{9,13},{10,... | collective-permute-start | bytes 356360 | tf_op jit(solution)/shard_map/ppermute | solution.py:200
  20.6 4.5 %collective-permute-start.8 = (bf16[16,3712]{1,0:T(8,128)(2,1)S(1)}, bf16[16,3712]{1,0:T(8,128)(2,1)S(1)}, u32[]{:S(2)}, u32[]{:S(2)}) collective-permute-start(bf16[16,3712]{1,0:T(8,128)(2,1)S(1)} %collective-permute-done.7.refs_1_), channel_id=1, source_target_pairs={{0,1},{1,0},{2,3},{3,2},{4,5},{5,4},{6,7},{7,6},{8,9},{9,8},{10,11... | collective-permute-start | bytes 356360 | tf_op jit(solution)/shard_map/ppermute | solution.py:204
  25.0 1.4 %collective-permute-start.12 = (bf16[16,3712]{1,0:T(8,128)(2,1)S(1)}, bf16[16,3712]{1,0:T(8,128)(2,1)S(1)}, u32[]{:S(2)}, u32[]{:S(2)}) collective-permute-start(bf16[16,3712]{1,0:T(8,128)(2,1)S(1)} %collective-permute-done.4.refs_2_), channel_id=1, source_target_pairs={{0,1},{1,0},{2,3},{3,2},{4,5},{5,4},{6,7},{7,6},{8,9},{9,8},{10,11... | collective-permute-start | bytes 356360 | tf_op jit(solution)/shard_map/ppermute | solution.py:204
  30.5 1.4 %collective-permute-start.15 = (bf16[16,3584]{1,0:T(8,128)(2,1)S(1)}, bf16[16,3584]{1,0:T(8,128)(2,1)S(1)}, u32[]{:S(2)}, u32[]{:S(2)}) collective-permute-start(bf16[16,3584]{1,0:T(8,128)(2,1)S(1)} %get-tuple-element.94), channel_id=1, source_target_pairs={{0,1},{1,0},{2,3},{3,2},{4,5},{5,4},{6,7},{7,6},{8,9},{9,8},{10,11... | collective-permute-start | bytes 344072 | tf_op jit(solution)/shard_map/ppermute | solution.py:204
  30.7 2.6 %collective-permute-start.11 = (bf16[64,3584]{1,0:T(8,128)(2,1)S(1)}, bf16[64,3584]{1,0:T(8,128)(2,1)S(1)}, u32[]{:S(2)}, u32[]{:S(2)}) collective-permute-start(bf16[64,3584]{1,0:T(8,128)(2,1)S(1)} %get-tuple-element.87), channel_id=1, source_target_pairs={{0,1},{1,0},{2,3},{3,2},{4,5},{5,4},{6,7},{7,6},{8,9},{9,8},{10,11... | collective-permute-start | bytes 1376264 | tf_op jit(solution)/shard_map/ppermute | solution.py:204
  31.0 2.3 %collective-permute-start.13 = (bf16[48,3584]{1,0:T(8,128)(2,1)S(1)}, bf16[48,3584]{1,0:T(8,128)(2,1)S(1)}, u32[]{:S(2)}, u32[]{:S(2)}) collective-permute-start(bf16[48,3584]{1,0:T(8,128)(2,1)S(1)} %get-tuple-element.92), channel_id=1, source_target_pairs={{0,1},{1,0},{2,3},{3,2},{4,5},{5,4},{6,7},{7,6},{8,9},{9,8},{10,11... | collective-permute-start | bytes 1032200 | tf_op jit(solution)/shard_map/ppermute | solution.py:204
  31.9 5.4 %collective-permute-start.16 = (bf16[16,3584]{1,0:T(8,128)(2,1)S(1)}, bf16[16,3584]{1,0:T(8,128)(2,1)S(1)}, u32[]{:S(2)}, u32[]{:S(2)}) collective-permute-start(bf16[16,3584]{1,0:T(8,128)(2,1)S(1)} %add_convert_fusion.1), channel_id=1, source_target_pairs={{0,2},{1,5},{2,0},{3,7},{4,6},{5,1},{6,4},{7,3},{8,10},{9,13},{10,... | collective-permute-start | bytes 344072 | tf_op jit(solution)/shard_map/ppermute | solution.py:200
  33.4 8.8 %collective-permute-start.14 = (bf16[48,3584]{1,0:T(8,128)(2,1)S(1)}, bf16[48,3584]{1,0:T(8,128)(2,1)S(1)}, u32[]{:S(2)}, u32[]{:S(2)}) collective-permute-start(bf16[48,3584]{1,0:T(8,128)(2,1)S(1)} %add_convert_fusion), channel_id=1, source_target_pairs={{0,2},{1,5},{2,0},{3,7},{4,6},{5,1},{6,4},{7,3},{8,10},{9,13},{10,... | collective-permute-start | bytes 1032200 | tf_op jit(solution)/shard_map/ppermute | solution.py:200
  37.4 4.9 %collective-permute-start.17 = (bf16[16,3584]{1,0:T(8,128)(2,1)S(1)}, bf16[16,3584]{1,0:T(8,128)(2,1)S(1)}, u32[]{:S(2)}, u32[]{:S(2)}) collective-permute-start(bf16[16,3584]{1,0:T(8,128)(2,1)S(1)} %fusion.4), channel_id=1, source_target_pairs={{0,4},{1,3},{2,6},{3,1},{4,0},{5,7},{6,2},{7,5},{8,12},{9,11},{10,... | collective-permute-start | bytes 344072 | tf_op jit(solution)/shard_map/ppermute | solution.py:200
  42.3 8.4 %collective-permute-start.18 = (bf16[16,3584]{1,0:T(8,128)(2,1)S(1)}, bf16[16,3584]{1,0:T(8,128)(2,1)S(1)}, u32[]{:S(2)}, u32[]{:S(2)}) collective-permute-start(bf16[16,3584]{1,0:T(8,128)(2,1)S(1)} %get-tuple-element.121), channel_id=1, source_target_pairs={{0,8},{1,9},{2,10},{3,11},{4,12},{5,13},{6,14},{7,15},{8,0},{9,1},... | collective-permute-start | bytes 344072 | tf_op jit(solution)/shard_map/ppermute | solution.py:200
  44.0 6.9 %collective-permute-start.19 = (bf16[16,3584]{1,0:T(8,128)(2,1)S(1)}, bf16[16,3584]{1,0:T(8,128)(2,1)S(1)}, u32[]{:S(2)}, u32[]{:S(2)}) collective-permute-start(bf16[16,3584]{1,0:T(8,128)(2,1)S(1)} %get-tuple-element.120), channel_id=1, source_target_pairs={{0,4},{1,3},{2,6},{3,1},{4,0},{5,7},{6,2},{7,5},{8,12},{9,11},{10,... | collective-permute-start | bytes 344072 | tf_op jit(solution)/shard_map/ppermute | solution.py:200
  (3 other events, 22.3 us)

commit v7 on v6

--- a/solution.py
+++ b/solution.py
@@ -261,43 +261,41 @@
     )
     n = own.shape[0]
     own, inputs = barrier((own, inputs))
-    a, b, c = attend(2, (hop_a(own), hop_b(own), hop_c(own)))
-    ab, ac, bc = hop_b(a), hop_c(a), hop_c(b)
-    a, inputs = barrier((a, inputs))
-    ab = attend(1, ab)
+    c, b, a = attend(3, (hop_c(own), hop_b(own), hop_a(own)))
+    bc, ac, ab = hop_c(b), hop_c(a), hop_b(a)
+    near_rows = [jnp.concatenate(x, axis=0) for x in ((own, a), (b, c))]
+    near_rows += [swap(x) for x in near_rows]
+    near_own, near_other = experts(near_rows, gate, up, down, chip, [4 * n])
+    bc, ac, ab, near_own, near_other = barrier((bc, ac, ab, near_own, near_other))
     abc = hop_c(ab)
-    base = jnp.concatenate([own, a], axis=0)
-    second = jnp.concatenate([b, ab], axis=0)
-    early = jnp.concatenate([c, ac], axis=0)
-    near_rows = [base, second, swap(base), swap(second)]
-    near_rows, c = barrier((near_rows, c))
-    late_swap = swap(bc)
-    early_swap = swap(early)
-    near_own, near_other = experts(near_rows, gate, up, down, chip, [4 * n])
-    abc, early_swap, late_swap, near_own, near_other = barrier(
-        (abc, early_swap, late_swap, near_own, near_other)
-    )
-    near_back = swap(near_other[0])
+    ab, inputs = barrier((ab, inputs))
+    abc = attend(2, abc)
+    near = barrier(add(near_own[0], swap(near_other[0])))
+    got_c = hop_c(near[3 * n :].astype(BF16))
+    early = jnp.concatenate([ab, ac], axis=0)
+    early_swap, late_swap = swap(early), swap(bc)
+    abc, early_swap, late_swap, near = barrier((abc, early_swap, late_swap, near))
     far_rows = [early, bc, abc, early_swap, late_swap, swap(abc)]
     far_own, far_other = experts(far_rows, gate, up, down, chip, [3 * n, n])
-    near = barrier(add(near_own[0], near_back))
+    far_own, far_other, got_c = barrier((far_own, far_other, got_c))
 
     sent = add(far_own[1], swap(far_other[1])).astype(BF16)
-    rest = add(far_own[0], swap(far_other[0])).astype(BF16)
+    far = add(far_own[0], swap(far_other[0]))
+    rest = far[n:].astype(BF16)
     got_ab = hop_c(sent)
     got = hop_c(rest)
     rest, inputs = barrier((rest, inputs))
-    got_ab = attend(2, got_ab)
-    sent = add(near[3 * n :], got_ab).astype(BF16)
+    got_ab = attend(1, got_ab)
+    sent = add(far[:n], got_ab).astype(BF16)
     got_a = hop_b(sent)
-    sent, inputs = barrier((sent, inputs))
-    got_a = attend(1, got_a)
-    back_b = hop_b(add(near[2 * n : 3 * n], got[2 * n :]).astype(BF16))
-    sent = add(near[n : 2 * n], got[n : 2 * n], got_a).astype(BF16)
+    got, got_a = barrier((got, got_a))
+    sent = add(near[n : 2 * n], got[:n], got_a).astype(BF16)
+    sent, got = barrier((sent, got))
     back_a = hop_a(sent)
+    back_b = hop_b(add(near[2 * n : 3 * n], got[n:]).astype(BF16))
     sent, inputs = barrier((sent, inputs))
     back_a = attend(requests, back_a)
-    total = add(near[:n], got[:n], back_b, back_a)
+    total = add(near[:n], got_c, back_b, back_a)
     for turn in range(turns - 4, -1, -1):
         half = total.shape[0] // 2
         total = add(total[:half], hop(total[half:].astype(BF16), ep, sub, masks, turn))

time: 51.7 us -> 51.5 us (level)
  starting transfers between devices: 18 us -> 21 us
  Pallas kernels: 22.1 us -> 20.2 us
  waiting for transfers between devices: 9.47 us -> 8 us
    ppermute x12 -> x13, starting transfers between devices: 16.3 us -> 18.7 us  [hop(): return lax.ppermute(x, ('ep', 'sub'), pairs)]
    pallas_call x5 -> x4, Pallas kernels: 12.8 us -> 11 us  [attention(): pl.pallas_call(functools.partial(attention_kernel, first=first, count=cou...]
    ppermute x8, waiting for transfers between devices: 2.2 us -> 0.9 us  [swap(): return lax.ppermute(x, 'sub', [(0, 1), (1, 0)])]
    ppermute x8, starting transfers between devices: 1.7 us -> 2.26 us  [swap(): return lax.ppermute(x, 'sub', [(0, 1), (1, 0)])]
    ppermute x12 -> x13, waiting for transfers between devices: 7.27 us -> 7.1 us  [hop(): return lax.ppermute(x, ('ep', 'sub'), pairs)]
  transfers between devices with their start and end apart: 20 -> 21, of which waited for: 8 -> 9; matrix products, arithmetic and copies ran while one was open for 1% -> 1% of each run, Pallas kernels for 33% -> 37%
where the time goes in v7:
time: 51.5 us; the launch traced here: 51.3 us
  starting transfers between devices  21 us (41%)
  Pallas kernels  20.2 us (39%)
  waiting for transfers between devices  8 us (16%)
  other arithmetic  1.01 us (2%)
  between operations  0.96 us (2%)
    ppermute x13, starting transfers between devices, hop(): return lax.ppermute(x, ('ep', 'sub'), pairs)  18.7 us
    pallas_call x4, Pallas kernels, attention(): pl.pallas_call(functools.partial(attention_kernel, first=first, count=cou...  11 us
    pallas_call x2, Pallas kernels, experts(): pl.pallas_call(functools.partial(experts_kernel, parts=len(parts), groups...  7.98 us
    ppermute x13, waiting for transfers between devices, hop(): return lax.ppermute(x, ('ep', 'sub'), pairs)  7.1 us
    ppermute x8, starting transfers between devices, swap(): return lax.ppermute(x, 'sub', [(0, 1), (1, 0)])  2.26 us
    pallas_call x1, Pallas kernels, route(): pl.pallas_call(functools.partial(route_kernel, experts=placement.shape[0]...  1.27 us
  transfers between devices with their start and end apart: 21, of which 9 were waited for; matrix products, arithmetic and copies ran while one was open for 1% of the time, Pallas kernels for 37%

profile of v7, /device:TPU:0, one launch (start us, length us, event | category | flops | bytes accessed | tf_op | source)
XLA Modules:
  0.0 51.3 jit_solution(11420321144553182271)
XLA Ops:
  0.7 1.3 %route.1 = bf16[16,3712]{1,0:T(8,128)(2,1)S(1)} custom-call(s32[2,14]{1,0:T(2,128)} %bitcast.22, bf16[16,3584]{1,0:T(8,128)(2,1)} %rows_ref.1, f32[8,16]{1,0:T(8,128)} %bitcast.20, s32[8,16]{1,0:T(8,128)} %bitcast.21), custom_call_target="tpu_custom_call" | custom-call | flops 17179869184 | bytes 33554432 | tf_op jit(solution)/shard_map/route/pallas_call | solution.py:117
  2.0 4.0 %collective-permute-start.2 = (bf16[16,3712]{1,0:T(8,128)(2,1)S(1)}, bf16[16,3712]{1,0:T(8,128)(2,1)S(1)}, u32[]{:S(2)}, u32[]{:S(2)}) collective-permute-start(bf16[16,3712]{1,0:T(8,128)(2,1)S(1)} %route.1), channel_id=1, source_target_pairs={{0,8},{1,9},{2,10},{3,11},{4,12},{5,13},{6,14},{7,15},{8,0},{9,1},... | collective-permute-start | bytes 356360 | tf_op jit(solution)/shard_map/ppermute | solution.py:200
  6.0 1.6 %collective-permute-start.1 = (bf16[16,3712]{1,0:T(8,128)(2,1)S(1)}, bf16[16,3712]{1,0:T(8,128)(2,1)S(1)}, u32[]{:S(2)}, u32[]{:S(2)}) collective-permute-start(bf16[16,3712]{1,0:T(8,128)(2,1)S(1)} %route.1), channel_id=1, source_target_pairs={{0,4},{1,3},{2,6},{3,1},{4,0},{5,7},{6,2},{7,5},{8,12},{9,11},{10,... | collective-permute-start | bytes 356360 | tf_op jit(solution)/shard_map/ppermute | solution.py:200
  7.6 1.5 %collective-permute-start = (bf16[16,3712]{1,0:T(8,128)(2,1)S(1)}, bf16[16,3712]{1,0:T(8,128)(2,1)S(1)}, u32[]{:S(2)}, u32[]{:S(2)}) collective-permute-start(bf16[16,3712]{1,0:T(8,128)(2,1)S(1)} %route.1), channel_id=1, source_target_pairs={{0,2},{1,5},{2,0},{3,7},{4,6},{5,1},{6,4},{7,3},{8,10},{9,13},{10,... | collective-permute-start | bytes 356360 | tf_op jit(solution)/shard_map/ppermute | solution.py:200
  9.2 3.4 %attention.4.refs_0_ = bf16[8,2,128,512]{3,2,1,0:T(8,128)(2,1)} custom-call(s32[8]{0:T(128)} %length_ref.3, bf16[8,2,576,128]{3,2,1,0:T(8,128)(2,1)S(1)} %bitcast.6, bf16[8,576,256]{2,1,0:T(8,128)(2,1)S(1)} %bitcast.10, bf16[8,2,576]{2,1,0:T(2,128)(2,1)S(1)} %copy-done.2), custom_call_target="tpu_custom_call" | custom-call | flops 1048576 | bytes 65536 | tf_op jit(solution)/shard_map/attention/pallas_call | solution.py:75
  12.6 0.8 %collective-permute-done.1 = bf16[16,3712]{1,0:T(8,128)(2,1)S(1)} collective-permute-done((bf16[16,3712]{1,0:T(8,128)(2,1)S(1)}, bf16[16,3712]{1,0:T(8,128)(2,1)S(1)}, u32[]{:S(2)}, u32[]{:S(2)}) %collective-permute-start.1) | collective-permute-done | bytes 118816 | tf_op jit(solution)/shard_map/ppermute | solution.py:200
  14.0 0.6 %collective-permute-start.3 = (bf16[16,3712]{1,0:T(8,128)(2,1)S(1)}, bf16[16,3712]{1,0:T(8,128)(2,1)S(1)}, u32[]{:S(2)}, u32[]{:S(2)}) collective-permute-start(bf16[16,3712]{1,0:T(8,128)(2,1)S(1)} %collective-permute-done.1), channel_id=1, source_target_pairs={{0,2},{1,5},{2,0},{3,7},{4,6},{5,1},{6,4},{7,3},{8,10},{9,13},{10,... | collective-permute-start | bytes 356360 | tf_op jit(solution)/shard_map/ppermute | solution.py:200
  14.7 1.1 %collective-permute-start.5 = (bf16[16,3712]{1,0:T(8,128)(2,1)S(1)}, bf16[16,3712]{1,0:T(8,128)(2,1)S(1)}, u32[]{:S(2)}, u32[]{:S(2)}) collective-permute-start(bf16[16,3712]{1,0:T(8,128)(2,1)S(1)} %collective-permute-done.2), channel_id=1, source_target_pairs={{0,4},{1,3},{2,6},{3,1},{4,0},{5,7},{6,2},{7,5},{8,12},{9,11},{10,... | collective-permute-start | bytes 356360 | tf_op jit(solution)/shard_map/ppermute | solution.py:200
  16.4 4.0 %experts.2 = (f32[64,3584]{1,0:T(8,128)S(1)}, bf16[64,3584]{1,0:T(8,128)(2,1)S(1)}) custom-call(bf16[32,3712]{1,0:T(8,128)(2,1)S(1)} %constant_dynamic-update-slice_fusion.refs_0_, bf16[32,3712]{1,0:T(8,128)(2,1)S(1)} %constant_dynamic-update-slice_fusion.2.refs_1_, bf16[32,3712]{1,0:T(8,128)(2,1)S(1)} %collective-permute-done.6.refs_2_, ...), custom_call_target="tpu_custom_call" | custom-call | flops 1048576 | bytes 65536 | tf_op jit(solution)/shard_map/experts/pallas_call | solution.py:168
  20.6 1.4 %collective-permute-start.8 = (bf16[16,3712]{1,0:T(8,128)(2,1)S(1)}, bf16[16,3712]{1,0:T(8,128)(2,1)S(1)}, u32[]{:S(2)}, u32[]{:S(2)}) collective-permute-start(bf16[16,3712]{1,0:T(8,128)(2,1)S(1)} %collective-permute-done.5), channel_id=1, source_target_pairs={{0,2},{1,5},{2,0},{3,7},{4,6},{5,1},{6,4},{7,3},{8,10},{9,13},{10,... | collective-permute-start | bytes 356360 | tf_op jit(solution)/shard_map/ppermute | solution.py:200
  22.6 2.7 %attention.5.refs_0_ = bf16[8,2,128,512]{3,2,1,0:T(8,128)(2,1)} custom-call(s32[8]{0:T(128)} %length_ref.3, bf16[8,2,576,128]{3,2,1,0:T(8,128)(2,1)S(1)} %bitcast.7, bf16[8,576,256]{2,1,0:T(8,128)(2,1)S(1)} %bitcast.11, bf16[8,2,576]{2,1,0:T(2,128)(2,1)S(1)} %copy-done.2, bf16[8,2,128,512]{3,2,1,0:T(8,128)(2,1)} %attention.4.refs_0_), custom_call_target="tpu_custom_call", output_to_operand_aliasing={{}: (4, {})} | custom-call | flops 1048576 | bytes 65536 | tf_op jit(solution)/shard_map/attention/pallas_call | solution.py:75
  26.0 1.1 %collective-permute-start.13 = (bf16[16,3584]{1,0:T(8,128)(2,1)S(1)}, bf16[16,3584]{1,0:T(8,128)(2,1)S(1)}, u32[]{:S(2)}, u32[]{:S(2)}) collective-permute-start(bf16[16,3584]{1,0:T(8,128)(2,1)S(1)} %slice.48), channel_id=1, source_target_pairs={{0,2},{1,5},{2,0},{3,7},{4,6},{5,1},{6,4},{7,3},{8,10},{9,13},{10,... | collective-permute-start | bytes 344072 | tf_op jit(solution)/shard_map/ppermute | solution.py:200
  27.1 4.0 %experts.3 = (f32[48,3584]{1,0:T(8,128)S(1)}, f32[16,3584]{1,0:T(8,128)S(1)}, bf16[48,3584]{1,0:T(8,128)(2,1)S(1)}, bf16[16,3584]{1,0:T(8,128)(2,1)S(1)}) custom-call(bf16[32,3712]{1,0:T(8,128)(2,1)S(1)} %constant_dynamic-update-slice_fusion.4.refs_0_, bf16[16,3712]{1,0:T(8,128)(2,1)S(1)} %collective-permute-done.3.refs_1_, ...), custom_call_target="tpu_custom_call" | custom-call | flops 1048576 | bytes 65536 | tf_op jit(solution)/shard_map/experts/pallas_call | solution.py:168
  31.8 0.9 %collective-permute-done.16 = bf16[16,3584]{1,0:T(8,128)(2,1)S(1)} collective-permute-done((bf16[16,3584]{1,0:T(8,128)(2,1)S(1)}, bf16[16,3584]{1,0:T(8,128)(2,1)S(1)}, u32[]{:S(2)}, u32[]{:S(2)}) %collective-permute-start.16) | collective-permute-done | bytes 114720 | tf_op jit(solution)/shard_map/ppermute | solution.py:204
  32.7 1.2 %collective-permute-start.17 = (bf16[16,3584]{1,0:T(8,128)(2,1)S(1)}, bf16[16,3584]{1,0:T(8,128)(2,1)S(1)}, u32[]{:S(2)}, u32[]{:S(2)}) collective-permute-start(bf16[16,3584]{1,0:T(8,128)(2,1)S(1)} %add_convert_fusion.3), channel_id=1, source_target_pairs={{0,2},{1,5},{2,0},{3,7},{4,6},{5,1},{6,4},{7,3},{8,10},{9,13},{10,... | collective-permute-start | bytes 344072 | tf_op jit(solution)/shard_map/ppermute | solution.py:200
  34.0 1.0 %collective-permute-start.15 = (bf16[32,3584]{1,0:T(8,128)(2,1)S(1)}, bf16[32,3584]{1,0:T(8,128)(2,1)S(1)}, u32[]{:S(2)}, u32[]{:S(2)}) collective-permute-start(bf16[32,3584]{1,0:T(8,128)(2,1)S(1)} %slice.47), channel_id=1, source_target_pairs={{0,2},{1,5},{2,0},{3,7},{4,6},{5,1},{6,4},{7,3},{8,10},{9,13},{10,... | collective-permute-start | bytes 688136 | tf_op jit(solution)/shard_map/ppermute | solution.py:200
  34.9 2.2 %attention.6.refs_0_ = bf16[8,2,128,512]{3,2,1,0:T(8,128)(2,1)} custom-call(s32[8]{0:T(128)} %length_ref.3, bf16[8,2,576,128]{3,2,1,0:T(8,128)(2,1)S(1)} %bitcast.8, bf16[8,576,256]{2,1,0:T(8,128)(2,1)S(1)} %bitcast.12, bf16[8,2,576]{2,1,0:T(2,128)(2,1)S(1)} %copy-done.2, bf16[8,2,128,512]{3,2,1,0:T(8,128)(2,1)} %attention.5.refs_0_), custom_call_target="tpu_custom_call", output_to_operand_aliasing={{}: (4, {})} | custom-call | flops 1048576 | bytes 65536 | tf_op jit(solution)/shard_map/attention/pallas_call | solution.py:75
  37.6 1.4 %collective-permute-start.18 = (bf16[16,3584]{1,0:T(8,128)(2,1)S(1)}, bf16[16,3584]{1,0:T(8,128)(2,1)S(1)}, u32[]{:S(2)}, u32[]{:S(2)}) collective-permute-start(bf16[16,3584]{1,0:T(8,128)(2,1)S(1)} %fusion), channel_id=1, source_target_pairs={{0,4},{1,3},{2,6},{3,1},{4,0},{5,7},{6,2},{7,5},{8,12},{9,11},{10,... | collective-permute-start | bytes 344072 | tf_op jit(solution)/shard_map/ppermute | solution.py:200
  39.0 3.4 %collective-permute-done.18 = bf16[16,3584]{1,0:T(8,128)(2,1)S(1)} collective-permute-done((bf16[16,3584]{1,0:T(8,128)(2,1)S(1)}, bf16[16,3584]{1,0:T(8,128)(2,1)S(1)}, u32[]{:S(2)}, u32[]{:S(2)}) %collective-permute-start.18) | collective-permute-done | bytes 114720 | tf_op jit(solution)/shard_map/ppermute | solution.py:200
  42.5 2.5 %collective-permute-start.19 = (bf16[16,3584]{1,0:T(8,128)(2,1)S(1)}, bf16[16,3584]{1,0:T(8,128)(2,1)S(1)}, u32[]{:S(2)}, u32[]{:S(2)}) collective-permute-start(bf16[16,3584]{1,0:T(8,128)(2,1)S(1)} %add_convert_fusion.2), channel_id=1, source_target_pairs={{0,8},{1,9},{2,10},{3,11},{4,12},{5,13},{6,14},{7,15},{8,0},{9,1},... | collective-permute-start | bytes 344072 | tf_op jit(solution)/shard_map/ppermute | solution.py:200
  45.0 0.7 %collective-permute-start.20 = (bf16[16,3584]{1,0:T(8,128)(2,1)S(1)}, bf16[16,3584]{1,0:T(8,128)(2,1)S(1)}, u32[]{:S(2)}, u32[]{:S(2)}) collective-permute-start(bf16[16,3584]{1,0:T(8,128)(2,1)S(1)} %add_convert_fusion.1), channel_id=1, source_target_pairs={{0,4},{1,3},{2,6},{3,1},{4,0},{5,7},{6,2},{7,5},{8,12},{9,11},{10,... | collective-permute-start | bytes 344072 | tf_op jit(solution)/shard_map/ppermute | solution.py:200
  45.7 2.7 %attention.7 = bf16[8,2,128,512]{3,2,1,0:T(8,128)(2,1)} custom-call(s32[8]{0:T(128)} %length_ref.3, bf16[8,2,576,128]{3,2,1,0:T(8,128)(2,1)S(1)} %bitcast.9, bf16[8,576,256]{2,1,0:T(8,128)(2,1)S(1)} %bitcast.13, bf16[8,2,576]{2,1,0:T(2,128)(2,1)S(1)} %copy-done.2, bf16[8,2,128,512]{3,2,1,0:T(8,128)(2,1)} %attention.6.refs_0_), custom_call_target="tpu_custom_call", output_to_operand_aliasing={{}: (4, {})} | custom-call | flops 1048576 | bytes 65536 | tf_op jit(solution)/shard_map/attention/pallas_call | solution.py:75
  48.4 1.6 %collective-permute-done.19 = bf16[16,3584]{1,0:T(8,128)(2,1)S(1)} collective-permute-done((bf16[16,3584]{1,0:T(8,128)(2,1)S(1)}, bf16[16,3584]{1,0:T(8,128)(2,1)S(1)}, u32[]{:S(2)}, u32[]{:S(2)}) %collective-permute-start.19) | collective-permute-done | bytes 114720 | tf_op jit(solution)/shard_map/ppermute | solution.py:200
  50.6 0.7 %add_convert_fusion = bf16[16,3584]{1,0:T(8,128)(2,1)} fusion(bf16[16,3584]{1,0:T(8,128)(2,1)S(1)} %collective-permute-done.19, bf16[16,3584]{1,0:T(8,128)(2,1)S(1)} %collective-permute-done.20, bf16[16,3584]{1,0:T(8,128)(2,1)S(1)} %collective-permute-done.13, f32[64,3584]{1,0:T(8,128)S(1)} %convert_add_fusion), kind=kLoop, calls=%fused_computation.6 | loop fusion | flops 401408 | bytes 688128 | tf_op jit(solution)/shard_map/convert_element_type | solution.py:302
  (61 shorter events, 4.6 us)
Async XLA Ops:
  0.6 15.7 %slice-start = ((s8[7340032]{0:T(1024)(128)(4,1)}), s8[4194304]{0:T(1024)(128)(4,1)S(1)}, s32[]{:S(2)}) async-start(s8[7340032]{0:T(1024)(128)(4,1)} %bitcast.14), calls=%async_computation | async-start | bytes 8388608
  0.6 15.7 %slice-start.2 = ((s8[7340032]{0:T(1024)(128)(4,1)}), s8[4194304]{0:T(1024)(128)(4,1)S(1)}, s32[]{:S(2)}) async-start(s8[7340032]{0:T(1024)(128)(4,1)} %bitcast.16), calls=%async_computation.2 | async-start | bytes 8388608
  0.7 15.7 %slice-start.4 = ((s8[7340032]{0:T(1024)(128)(4,1)}), s8[4194304]{0:T(1024)(128)(4,1)S(1)}, s32[]{:S(2)}) async-start(s8[7340032]{0:T(1024)(128)(4,1)} %bitcast.18), calls=%async_computation.4 | async-start | bytes 8388608
  2.0 10.6 %collective-permute-start.2 = (bf16[16,3712]{1,0:T(8,128)(2,1)S(1)}, bf16[16,3712]{1,0:T(8,128)(2,1)S(1)}, u32[]{:S(2)}, u32[]{:S(2)}) collective-permute-start(bf16[16,3712]{1,0:T(8,128)(2,1)S(1)} %route.1), channel_id=1, source_target_pairs={{0,8},{1,9},{2,10},{3,11},{4,12},{5,13},{6,14},{7,15},{8,0},{9,1},... | collective-permute-start | bytes 356360 | tf_op jit(solution)/shard_map/ppermute | solution.py:200
  6.0 7.3 %collective-permute-start.1 = (bf16[16,3712]{1,0:T(8,128)(2,1)S(1)}, bf16[16,3712]{1,0:T(8,128)(2,1)S(1)}, u32[]{:S(2)}, u32[]{:S(2)}) collective-permute-start(bf16[16,3712]{1,0:T(8,128)(2,1)S(1)} %route.1), channel_id=1, source_target_pairs={{0,4},{1,3},{2,6},{3,1},{4,0},{5,7},{6,2},{7,5},{8,12},{9,11},{10,... | collective-permute-start | bytes 356360 | tf_op jit(solution)/shard_map/ppermute | solution.py:200
  7.6 5.7 %collective-permute-start = (bf16[16,3712]{1,0:T(8,128)(2,1)S(1)}, bf16[16,3712]{1,0:T(8,128)(2,1)S(1)}, u32[]{:S(2)}, u32[]{:S(2)}) collective-permute-start(bf16[16,3712]{1,0:T(8,128)(2,1)S(1)} %route.1), channel_id=1, source_target_pairs={{0,2},{1,5},{2,0},{3,7},{4,6},{5,1},{6,4},{7,3},{8,10},{9,13},{10,... | collective-permute-start | bytes 356360 | tf_op jit(solution)/shard_map/ppermute | solution.py:200
  13.4 3.0 %collective-permute-start.7 = (bf16[32,3712]{1,0:T(8,128)(2,1)S(1)}, bf16[32,3712]{1,0:T(8,128)(2,1)S(1)}, u32[]{:S(2)}, u32[]{:S(2)}) collective-permute-start(bf16[32,3712]{1,0:T(8,128)(2,1)S(1)} %constant_dynamic-update-slice_fusion.2.refs_1_), channel_id=1, source_target_pairs={{0,1},{1,0},{2,3},{3,2},{4,5},{5,4},{6,7},{7,6},{8,9},{9,8},{10,11... | collective-permute-start | bytes 712712 | tf_op jit(solution)/shard_map/ppermute | solution.py:204
  13.5 2.9 %collective-permute-start.6 = (bf16[32,3712]{1,0:T(8,128)(2,1)S(1)}, bf16[32,3712]{1,0:T(8,128)(2,1)S(1)}, u32[]{:S(2)}, u32[]{:S(2)}) collective-permute-start(bf16[32,3712]{1,0:T(8,128)(2,1)S(1)} %constant_dynamic-update-slice_fusion.refs_0_), channel_id=1, source_target_pairs={{0,1},{1,0},{2,3},{3,2},{4,5},{5,4},{6,7},{7,6},{8,9},{9,8},{10,11... | collective-permute-start | bytes 712712 | tf_op jit(solution)/shard_map/ppermute | solution.py:204
  14.0 6.4 %collective-permute-start.3 = (bf16[16,3712]{1,0:T(8,128)(2,1)S(1)}, bf16[16,3712]{1,0:T(8,128)(2,1)S(1)}, u32[]{:S(2)}, u32[]{:S(2)}) collective-permute-start(bf16[16,3712]{1,0:T(8,128)(2,1)S(1)} %collective-permute-done.1), channel_id=1, source_target_pairs={{0,2},{1,5},{2,0},{3,7},{4,6},{5,1},{6,4},{7,3},{8,10},{9,13},{10,... | collective-permute-start | bytes 356360 | tf_op jit(solution)/shard_map/ppermute | solution.py:200
  14.7 5.9 %collective-permute-start.5 = (bf16[16,3712]{1,0:T(8,128)(2,1)S(1)}, bf16[16,3712]{1,0:T(8,128)(2,1)S(1)}, u32[]{:S(2)}, u32[]{:S(2)}) collective-permute-start(bf16[16,3712]{1,0:T(8,128)(2,1)S(1)} %collective-permute-done.2), channel_id=1, source_target_pairs={{0,4},{1,3},{2,6},{3,1},{4,0},{5,7},{6,2},{7,5},{8,12},{9,11},{10,... | collective-permute-start | bytes 356360 | tf_op jit(solution)/shard_map/ppermute | solution.py:200
  15.8 4.8 %collective-permute-start.4 = (bf16[16,3712]{1,0:T(8,128)(2,1)S(1)}, bf16[16,3712]{1,0:T(8,128)(2,1)S(1)}, u32[]{:S(2)}, u32[]{:S(2)}) collective-permute-start(bf16[16,3712]{1,0:T(8,128)(2,1)S(1)} %collective-permute-done.2), channel_id=1, source_target_pairs={{0,2},{1,5},{2,0},{3,7},{4,6},{5,1},{6,4},{7,3},{8,10},{9,13},{10,... | collective-permute-start | bytes 356360 | tf_op jit(solution)/shard_map/ppermute | solution.py:200
  20.6 4.8 %collective-permute-start.8 = (bf16[16,3712]{1,0:T(8,128)(2,1)S(1)}, bf16[16,3712]{1,0:T(8,128)(2,1)S(1)}, u32[]{:S(2)}, u32[]{:S(2)}) collective-permute-start(bf16[16,3712]{1,0:T(8,128)(2,1)S(1)} %collective-permute-done.5), channel_id=1, source_target_pairs={{0,2},{1,5},{2,0},{3,7},{4,6},{5,1},{6,4},{7,3},{8,10},{9,13},{10,... | collective-permute-start | bytes 356360 | tf_op jit(solution)/shard_map/ppermute | solution.py:200
  22.0 3.6 %collective-permute-start.10 = (bf16[16,3712]{1,0:T(8,128)(2,1)S(1)}, bf16[16,3712]{1,0:T(8,128)(2,1)S(1)}, u32[]{:S(2)}, u32[]{:S(2)}) collective-permute-start(bf16[16,3712]{1,0:T(8,128)(2,1)S(1)} %collective-permute-done.3.refs_1_), channel_id=1, source_target_pairs={{0,1},{1,0},{2,3},{3,2},{4,5},{5,4},{6,7},{7,6},{8,9},{9,8},{10,11... | collective-permute-start | bytes 356360 | tf_op jit(solution)/shard_map/ppermute | solution.py:204
  22.0 3.5 %collective-permute-start.11 = (bf16[64,3584]{1,0:T(8,128)(2,1)S(1)}, bf16[64,3584]{1,0:T(8,128)(2,1)S(1)}, u32[]{:S(2)}, u32[]{:S(2)}) collective-permute-start(bf16[64,3584]{1,0:T(8,128)(2,1)S(1)} %get-tuple-element.87), channel_id=1, source_target_pairs={{0,1},{1,0},{2,3},{3,2},{4,5},{5,4},{6,7},{7,6},{8,9},{9,8},{10,11... | collective-permute-start | bytes 1376264 | tf_op jit(solution)/shard_map/ppermute | solution.py:204
  22.5 3.0 %collective-permute-start.9 = (bf16[32,3712]{1,0:T(8,128)(2,1)S(1)}, bf16[32,3712]{1,0:T(8,128)(2,1)S(1)}, u32[]{:S(2)}, u32[]{:S(2)}) collective-permute-start(bf16[32,3712]{1,0:T(8,128)(2,1)S(1)} %constant_dynamic-update-slice_fusion.4.refs_0_), channel_id=1, source_target_pairs={{0,1},{1,0},{2,3},{3,2},{4,5},{5,4},{6,7},{7,6},{8,9},{9,8},{10,11... | collective-permute-start | bytes 712712 | tf_op jit(solution)/shard_map/ppermute | solution.py:204
  25.6 1.5 %collective-permute-start.12 = (bf16[16,3712]{1,0:T(8,128)(2,1)S(1)}, bf16[16,3712]{1,0:T(8,128)(2,1)S(1)}, u32[]{:S(2)}, u32[]{:S(2)}) collective-permute-start(bf16[16,3712]{1,0:T(8,128)(2,1)S(1)} %collective-permute-done.8.refs_2_), channel_id=1, source_target_pairs={{0,1},{1,0},{2,3},{3,2},{4,5},{5,4},{6,7},{7,6},{8,9},{9,8},{10,11... | collective-permute-start | bytes 356360 | tf_op jit(solution)/shard_map/ppermute | solution.py:204
  26.0 5.1 %collective-permute-start.13 = (bf16[16,3584]{1,0:T(8,128)(2,1)S(1)}, bf16[16,3584]{1,0:T(8,128)(2,1)S(1)}, u32[]{:S(2)}, u32[]{:S(2)}) collective-permute-start(bf16[16,3584]{1,0:T(8,128)(2,1)S(1)} %slice.48), channel_id=1, source_target_pairs={{0,2},{1,5},{2,0},{3,7},{4,6},{5,1},{6,4},{7,3},{8,10},{9,13},{10,... | collective-permute-start | bytes 344072 | tf_op jit(solution)/shard_map/ppermute | solution.py:200
  31.1 1.5 %collective-permute-start.16 = (bf16[16,3584]{1,0:T(8,128)(2,1)S(1)}, bf16[16,3584]{1,0:T(8,128)(2,1)S(1)}, u32[]{:S(2)}, u32[]{:S(2)}) collective-permute-start(bf16[16,3584]{1,0:T(8,128)(2,1)S(1)} %get-tuple-element.99), channel_id=1, source_target_pairs={{0,1},{1,0},{2,3},{3,2},{4,5},{5,4},{6,7},{7,6},{8,9},{9,8},{10,11... | collective-permute-start | bytes 344072 | tf_op jit(solution)/shard_map/ppermute | solution.py:204
  31.7 2.2 %collective-permute-start.14 = (bf16[48,3584]{1,0:T(8,128)(2,1)S(1)}, bf16[48,3584]{1,0:T(8,128)(2,1)S(1)}, u32[]{:S(2)}, u32[]{:S(2)}) collective-permute-start(bf16[48,3584]{1,0:T(8,128)(2,1)S(1)} %get-tuple-element.97), channel_id=1, source_target_pairs={{0,1},{1,0},{2,3},{3,2},{4,5},{5,4},{6,7},{7,6},{8,9},{9,8},{10,11... | collective-permute-start | bytes 1032200 | tf_op jit(solution)/shard_map/ppermute | solution.py:204
  32.7 4.9 %collective-permute-start.17 = (bf16[16,3584]{1,0:T(8,128)(2,1)S(1)}, bf16[16,3584]{1,0:T(8,128)(2,1)S(1)}, u32[]{:S(2)}, u32[]{:S(2)}) collective-permute-start(bf16[16,3584]{1,0:T(8,128)(2,1)S(1)} %add_convert_fusion.3), channel_id=1, source_target_pairs={{0,2},{1,5},{2,0},{3,7},{4,6},{5,1},{6,4},{7,3},{8,10},{9,13},{10,... | collective-permute-start | bytes 344072 | tf_op jit(solution)/shard_map/ppermute | solution.py:200
  34.0 8.5 %collective-permute-start.15 = (bf16[32,3584]{1,0:T(8,128)(2,1)S(1)}, bf16[32,3584]{1,0:T(8,128)(2,1)S(1)}, u32[]{:S(2)}, u32[]{:S(2)}) collective-permute-start(bf16[32,3584]{1,0:T(8,128)(2,1)S(1)} %slice.47), channel_id=1, source_target_pairs={{0,2},{1,5},{2,0},{3,7},{4,6},{5,1},{6,4},{7,3},{8,10},{9,13},{10,... | collective-permute-start | bytes 688136 | tf_op jit(solution)/shard_map/ppermute | solution.py:200
  37.6 4.9 %collective-permute-start.18 = (bf16[16,3584]{1,0:T(8,128)(2,1)S(1)}, bf16[16,3584]{1,0:T(8,128)(2,1)S(1)}, u32[]{:S(2)}, u32[]{:S(2)}) collective-permute-start(bf16[16,3584]{1,0:T(8,128)(2,1)S(1)} %fusion), channel_id=1, source_target_pairs={{0,4},{1,3},{2,6},{3,1},{4,0},{5,7},{6,2},{7,5},{8,12},{9,11},{10,... | collective-permute-start | bytes 344072 | tf_op jit(solution)/shard_map/ppermute | solution.py:200
  42.5 7.6 %collective-permute-start.19 = (bf16[16,3584]{1,0:T(8,128)(2,1)S(1)}, bf16[16,3584]{1,0:T(8,128)(2,1)S(1)}, u32[]{:S(2)}, u32[]{:S(2)}) collective-permute-start(bf16[16,3584]{1,0:T(8,128)(2,1)S(1)} %add_convert_fusion.2), channel_id=1, source_target_pairs={{0,8},{1,9},{2,10},{3,11},{4,12},{5,13},{6,14},{7,15},{8,0},{9,1},... | collective-permute-start | bytes 344072 | tf_op jit(solution)/shard_map/ppermute | solution.py:200
  45.0 5.6 %collective-permute-start.20 = (bf16[16,3584]{1,0:T(8,128)(2,1)S(1)}, bf16[16,3584]{1,0:T(8,128)(2,1)S(1)}, u32[]{:S(2)}, u32[]{:S(2)}) collective-permute-start(bf16[16,3584]{1,0:T(8,128)(2,1)S(1)} %add_convert_fusion.1), channel_id=1, source_target_pairs={{0,4},{1,3},{2,6},{3,1},{4,0},{5,7},{6,2},{7,5},{8,12},{9,11},{10,... | collective-permute-start | bytes 344072 | tf_op jit(solution)/shard_map/ppermute | solution.py:200
  (6 other events, 72.4 us)

commit v8 on v7

--- a/solution.py
+++ b/solution.py
@@ -265,19 +265,18 @@
     bc, ac, ab = hop_c(b), hop_c(a), hop_b(a)
     near_rows = [jnp.concatenate(x, axis=0) for x in ((own, a), (b, c))]
     near_rows += [swap(x) for x in near_rows]
+    near_rows, inputs = barrier((near_rows, inputs))
+    ab = attend(1, ab)
+    abc = hop_c(ab)
+    near_rows, ab_swap, bc, ac = barrier((near_rows, swap(ab), bc, ac))
+    ac_swap, bc_swap = swap(ac), swap(bc)
     near_own, near_other = experts(near_rows, gate, up, down, chip, [4 * n])
-    bc, ac, ab, near_own, near_other = barrier((bc, ac, ab, near_own, near_other))
-    abc = hop_c(ab)
-    ab, inputs = barrier((ab, inputs))
-    abc = attend(2, abc)
-    near = barrier(add(near_own[0], swap(near_other[0])))
-    got_c = hop_c(near[3 * n :].astype(BF16))
-    early = jnp.concatenate([ab, ac], axis=0)
-    early_swap, late_swap = swap(early), swap(bc)
-    abc, early_swap, late_swap, near = barrier((abc, early_swap, late_swap, near))
-    far_rows = [early, bc, abc, early_swap, late_swap, swap(abc)]
+    abc, ac_swap, bc_swap, near_own, near_other = barrier(
+        (abc, ac_swap, bc_swap, near_own, near_other)
+    )
+    far_rows = [ab, ac, bc, abc, ab_swap, ac_swap, bc_swap, swap(abc)]
     far_own, far_other = experts(far_rows, gate, up, down, chip, [3 * n, n])
-    far_own, far_other, got_c = barrier((far_own, far_other, got_c))
+    near_other, far_other = barrier((near_other, far_other))
 
     sent = add(far_own[1], swap(far_other[1])).astype(BF16)
     far = add(far_own[0], swap(far_other[0]))
@@ -285,9 +284,12 @@
     got_ab = hop_c(sent)
     got = hop_c(rest)
     rest, inputs = barrier((rest, inputs))
-    got_ab = attend(1, got_ab)
+    near = add(near_own[0], swap(near_other[0]))
+    got_ab, near = attend(1, (got_ab, near))
     sent = add(far[:n], got_ab).astype(BF16)
     got_a = hop_b(sent)
+    got, near = barrier((got, near))
+    got_c = hop_c(near[3 * n :].astype(BF16))
     got, got_a = barrier((got, got_a))
     sent = add(near[n : 2 * n], got[:n], got_a).astype(BF16)
     sent, got = barrier((sent, got))

time: 51.5 us -> 52.7 us (1.023)
  waiting for transfers between devices: 8 us -> 10.6 us
  starting transfers between devices: 21 us -> 19.3 us
    ppermute x8 -> x9, waiting for transfers between devices: 0.9 us -> 2.74 us  [swap(): return lax.ppermute(x, 'sub', [(0, 1), (1, 0)])]
    ppermute x13, starting transfers between devices: 18.7 us -> 17.2 us  [hop(): return lax.ppermute(x, ('ep', 'sub'), pairs)]
    ppermute x13, waiting for transfers between devices: 7.1 us -> 7.84 us  [hop(): return lax.ppermute(x, ('ep', 'sub'), pairs)]
    ppermute x8 -> x9, starting transfers between devices: 2.26 us -> 2.07 us  [swap(): return lax.ppermute(x, 'sub', [(0, 1), (1, 0)])]
  transfers between devices with their start and end apart: 21 -> 22, of which waited for: 9 -> 10; matrix products, arithmetic and copies ran while one was open for 1% -> 1% of each run, Pallas kernels for 37% -> 29%
where the time goes in v8:
time: 52.7 us; the launch traced here: 52.5 us
  Pallas kernels  20.6 us (39%)
  starting transfers between devices  19.3 us (37%)
  waiting for transfers between devices  10.6 us (20%)
  other arithmetic  0.99 us (2%)
  between operations  0.89 us (2%)
    ppermute x13, starting transfers between devices, hop(): return lax.ppermute(x, ('ep', 'sub'), pairs)  17.2 us
    pallas_call x4, Pallas kernels, attention(): pl.pallas_call(functools.partial(attention_kernel, first=first, count=cou...  11.4 us
    pallas_call x2, Pallas kernels, experts(): pl.pallas_call(functools.partial(experts_kernel, parts=len(parts), groups...  8.01 us
    ppermute x13, waiting for transfers between devices, hop(): return lax.ppermute(x, ('ep', 'sub'), pairs)  7.84 us
    ppermute x9, waiting for transfers between devices, swap(): return lax.ppermute(x, 'sub', [(0, 1), (1, 0)])  2.74 us
    ppermute x9, starting transfers between devices, swap(): return lax.ppermute(x, 'sub', [(0, 1), (1, 0)])  2.07 us
    pallas_call x1, Pallas kernels, route(): pl.pallas_call(functools.partial(route_kernel, experts=placement.shape[0]...  1.28 us
  transfers between devices with their start and end apart: 22, of which 10 were waited for; matrix products, arithmetic and copies ran while one was open for 1% of the time, Pallas kernels for 29%

profile of v8, /device:TPU:0, one launch (start us, length us, event | category | flops | bytes accessed | tf_op | source)
XLA Modules:
  0.0 52.5 jit_solution(9625365371209478440)
XLA Ops:
  0.7 1.3 %route.1 = bf16[16,3712]{1,0:T(8,128)(2,1)S(1)} custom-call(s32[2,14]{1,0:T(2,128)} %bitcast.18, bf16[16,3584]{1,0:T(8,128)(2,1)} %rows_ref.1, f32[8,16]{1,0:T(8,128)} %bitcast.16, s32[8,16]{1,0:T(8,128)} %bitcast.17), custom_call_target="tpu_custom_call" | custom-call | flops 17179869184 | bytes 33554432 | tf_op jit(solution)/shard_map/route/pallas_call | solution.py:117
  2.0 3.0 %collective-permute-start = (bf16[16,3712]{1,0:T(8,128)(2,1)S(1)}, bf16[16,3712]{1,0:T(8,128)(2,1)S(1)}, u32[]{:S(2)}, u32[]{:S(2)}) collective-permute-start(bf16[16,3712]{1,0:T(8,128)(2,1)S(1)} %route.1), channel_id=1, source_target_pairs={{0,2},{1,5},{2,0},{3,7},{4,6},{5,1},{6,4},{7,3},{8,10},{9,13},{10,... | collective-permute-start | bytes 356360 | tf_op jit(solution)/shard_map/ppermute | solution.py:200
  4.9 1.6 %collective-permute-start.1 = (bf16[16,3712]{1,0:T(8,128)(2,1)S(1)}, bf16[16,3712]{1,0:T(8,128)(2,1)S(1)}, u32[]{:S(2)}, u32[]{:S(2)}) collective-permute-start(bf16[16,3712]{1,0:T(8,128)(2,1)S(1)} %route.1), channel_id=1, source_target_pairs={{0,4},{1,3},{2,6},{3,1},{4,0},{5,7},{6,2},{7,5},{8,12},{9,11},{10,... | collective-permute-start | bytes 356360 | tf_op jit(solution)/shard_map/ppermute | solution.py:200
  6.5 2.6 %collective-permute-start.2 = (bf16[16,3712]{1,0:T(8,128)(2,1)S(1)}, bf16[16,3712]{1,0:T(8,128)(2,1)S(1)}, u32[]{:S(2)}, u32[]{:S(2)}) collective-permute-start(bf16[16,3712]{1,0:T(8,128)(2,1)S(1)} %route.1), channel_id=1, source_target_pairs={{0,8},{1,9},{2,10},{3,11},{4,12},{5,13},{6,14},{7,15},{8,0},{9,1},... | collective-permute-start | bytes 356360 | tf_op jit(solution)/shard_map/ppermute | solution.py:200
  9.2 3.5 %attention.4.refs_0_ = bf16[8,2,128,512]{3,2,1,0:T(8,128)(2,1)} custom-call(s32[8]{0:T(128)} %length_ref.3, bf16[8,2,576,128]{3,2,1,0:T(8,128)(2,1)S(1)} %bitcast.6, bf16[8,576,256]{2,1,0:T(8,128)(2,1)S(1)} %bitcast.10, bf16[8,2,576]{2,1,0:T(2,128)(2,1)S(1)} %copy-done.4), custom_call_target="tpu_custom_call" | custom-call | flops 1048576 | bytes 65536 | tf_op jit(solution)/shard_map/attention/pallas_call | solution.py:75
  12.7 1.6 %collective-permute-done.2 = bf16[16,3712]{1,0:T(8,128)(2,1)S(1)} collective-permute-done((bf16[16,3712]{1,0:T(8,128)(2,1)S(1)}, bf16[16,3712]{1,0:T(8,128)(2,1)S(1)}, u32[]{:S(2)}, u32[]{:S(2)}) %collective-permute-start.2) | collective-permute-done | bytes 118816 | tf_op jit(solution)/shard_map/ppermute | solution.py:200
  15.0 0.8 %collective-permute-start.7 = (bf16[16,3712]{1,0:T(8,128)(2,1)S(1)}, bf16[16,3712]{1,0:T(8,128)(2,1)S(1)}, u32[]{:S(2)}, u32[]{:S(2)}) collective-permute-start(bf16[16,3712]{1,0:T(8,128)(2,1)S(1)} %collective-permute-done.1), channel_id=1, source_target_pairs={{0,2},{1,5},{2,0},{3,7},{4,6},{5,1},{6,4},{7,3},{8,10},{9,13},{10,... | collective-permute-start | bytes 356360 | tf_op jit(solution)/shard_map/ppermute | solution.py:200
  15.7 1.2 %collective-permute-start.8 = (bf16[16,3712]{1,0:T(8,128)(2,1)S(1)}, bf16[16,3712]{1,0:T(8,128)(2,1)S(1)}, u32[]{:S(2)}, u32[]{:S(2)}) collective-permute-start(bf16[16,3712]{1,0:T(8,128)(2,1)S(1)} %collective-permute-done.2), channel_id=1, source_target_pairs={{0,2},{1,5},{2,0},{3,7},{4,6},{5,1},{6,4},{7,3},{8,10},{9,13},{10,... | collective-permute-start | bytes 356360 | tf_op jit(solution)/shard_map/ppermute | solution.py:200
  17.0 2.2 %attention.5.refs_0_ = bf16[8,2,128,512]{3,2,1,0:T(8,128)(2,1)} custom-call(s32[8]{0:T(128)} %length_ref.3, bf16[8,2,576,128]{3,2,1,0:T(8,128)(2,1)S(1)} %bitcast.7, bf16[8,576,256]{2,1,0:T(8,128)(2,1)S(1)} %bitcast.11, bf16[8,2,576]{2,1,0:T(2,128)(2,1)S(1)} %copy-done.4, bf16[8,2,128,512]{3,2,1,0:T(8,128)(2,1)} %attention.4.refs_0_), custom_call_target="tpu_custom_call", output_to_operand_aliasing={{}: (4, {})} | custom-call | flops 1048576 | bytes 65536 | tf_op jit(solution)/shard_map/attention/pallas_call | solution.py:75
  19.2 1.8 %collective-permute-done.3.refs_0_ = bf16[16,3712]{1,0:T(8,128)(2,1)S(1)} collective-permute-done((bf16[16,3712]{1,0:T(8,128)(2,1)S(1)}, bf16[16,3712]{1,0:T(8,128)(2,1)S(1)}, u32[]{:S(2)}, u32[]{:S(2)}) %collective-permute-start.3) | collective-permute-done | bytes 118816 | tf_op jit(solution)/shard_map/ppermute | solution.py:200
  21.5 0.9 %collective-permute-done.6.refs_4_ = bf16[16,3712]{1,0:T(8,128)(2,1)S(1)} collective-permute-done((bf16[16,3712]{1,0:T(8,128)(2,1)S(1)}, bf16[16,3712]{1,0:T(8,128)(2,1)S(1)}, u32[]{:S(2)}, u32[]{:S(2)}) %collective-permute-start.6) | collective-permute-done | bytes 118816 | tf_op jit(solution)/shard_map/ppermute | solution.py:204
  22.9 4.0 %experts.2 = (f32[64,3584]{1,0:T(8,128)S(1)}, bf16[64,3584]{1,0:T(8,128)(2,1)S(1)}) custom-call(bf16[32,3712]{1,0:T(8,128)(2,1)S(1)} %constant_dynamic-update-slice_fusion.refs_0_, bf16[32,3712]{1,0:T(8,128)(2,1)S(1)} %constant_dynamic-update-slice_fusion.2.refs_1_, bf16[32,3712]{1,0:T(8,128)(2,1)S(1)} %collective-permute-done.4.refs_2_, ...), custom_call_target="tpu_custom_call" | custom-call | flops 1048576 | bytes 65536 | tf_op jit(solution)/shard_map/experts/pallas_call | solution.py:168
  27.1 1.2 %collective-permute-done.12.refs_7_ = bf16[16,3712]{1,0:T(8,128)(2,1)S(1)} collective-permute-done((bf16[16,3712]{1,0:T(8,128)(2,1)S(1)}, bf16[16,3712]{1,0:T(8,128)(2,1)S(1)}, u32[]{:S(2)}, u32[]{:S(2)}) %collective-permute-start.12) | collective-permute-done | bytes 118816 | tf_op jit(solution)/shard_map/ppermute | solution.py:204
  28.3 4.0 %experts.3 = (f32[48,3584]{1,0:T(8,128)S(1)}, f32[16,3584]{1,0:T(8,128)S(1)}, bf16[48,3584]{1,0:T(8,128)(2,1)S(1)}, bf16[16,3584]{1,0:T(8,128)(2,1)S(1)}) custom-call(bf16[16,3712]{1,0:T(8,128)(2,1)S(1)} %collective-permute-done.3.refs_0_, bf16[16,3712]{1,0:T(8,128)(2,1)S(1)} %collective-permute-done.8.refs_1_, ...), custom_call_target="tpu_custom_call" | custom-call | flops 1048576 | bytes 65536 | tf_op jit(solution)/shard_map/experts/pallas_call | solution.py:168
  33.7 0.8 %collective-permute-start.16 = (bf16[16,3584]{1,0:T(8,128)(2,1)S(1)}, bf16[16,3584]{1,0:T(8,128)(2,1)S(1)}, u32[]{:S(2)}, u32[]{:S(2)}) collective-permute-start(bf16[16,3584]{1,0:T(8,128)(2,1)S(1)} %add_convert_fusion.3), channel_id=1, source_target_pairs={{0,2},{1,5},{2,0},{3,7},{4,6},{5,1},{6,4},{7,3},{8,10},{9,13},{10,... | collective-permute-start | bytes 344072 | tf_op jit(solution)/shard_map/ppermute | solution.py:200
  34.7 1.3 %collective-permute-start.14 = (bf16[32,3584]{1,0:T(8,128)(2,1)S(1)}, bf16[32,3584]{1,0:T(8,128)(2,1)S(1)}, u32[]{:S(2)}, u32[]{:S(2)}) collective-permute-start(bf16[32,3584]{1,0:T(8,128)(2,1)S(1)} %slice.47), channel_id=1, source_target_pairs={{0,2},{1,5},{2,0},{3,7},{4,6},{5,1},{6,4},{7,3},{8,10},{9,13},{10,... | collective-permute-start | bytes 688136 | tf_op jit(solution)/shard_map/ppermute | solution.py:200
  36.0 2.2 %attention.6.refs_0_ = bf16[8,2,128,512]{3,2,1,0:T(8,128)(2,1)} custom-call(s32[8]{0:T(128)} %length_ref.3, bf16[8,2,576,128]{3,2,1,0:T(8,128)(2,1)S(1)} %bitcast.8, bf16[8,576,256]{2,1,0:T(8,128)(2,1)S(1)} %bitcast.12, bf16[8,2,576]{2,1,0:T(2,128)(2,1)S(1)} %copy-done.4, bf16[8,2,128,512]{3,2,1,0:T(8,128)(2,1)} %attention.5.refs_0_), custom_call_target="tpu_custom_call", output_to_operand_aliasing={{}: (4, {})} | custom-call | flops 1048576 | bytes 65536 | tf_op jit(solution)/shard_map/attention/pallas_call | solution.py:75
  38.6 0.8 %collective-permute-start.18 = (bf16[16,3584]{1,0:T(8,128)(2,1)S(1)}, bf16[16,3584]{1,0:T(8,128)(2,1)S(1)}, u32[]{:S(2)}, u32[]{:S(2)}) collective-permute-start(bf16[16,3584]{1,0:T(8,128)(2,1)S(1)} %fusion), channel_id=1, source_target_pairs={{0,4},{1,3},{2,6},{3,1},{4,0},{5,7},{6,2},{7,5},{8,12},{9,11},{10,... | collective-permute-start | bytes 344072 | tf_op jit(solution)/shard_map/ppermute | solution.py:200
  39.4 1.9 %collective-permute-done.14 = bf16[32,3584]{1,0:T(8,128)(2,1)S(1)} collective-permute-done((bf16[32,3584]{1,0:T(8,128)(2,1)S(1)}, bf16[32,3584]{1,0:T(8,128)(2,1)S(1)}, u32[]{:S(2)}, u32[]{:S(2)}) %collective-permute-start.14) | collective-permute-done | bytes 229408 | tf_op jit(solution)/shard_map/ppermute | solution.py:200
  41.4 1.2 %collective-permute-start.20 = (bf16[16,3584]{1,0:T(8,128)(2,1)S(1)}, bf16[16,3584]{1,0:T(8,128)(2,1)S(1)}, u32[]{:S(2)}, u32[]{:S(2)}) collective-permute-start(bf16[16,3584]{1,0:T(8,128)(2,1)S(1)} %slice.48), channel_id=1, source_target_pairs={{0,2},{1,5},{2,0},{3,7},{4,6},{5,1},{6,4},{7,3},{8,10},{9,13},{10,... | collective-permute-start | bytes 344072 | tf_op jit(solution)/shard_map/ppermute | solution.py:200
  42.6 1.3 %collective-permute-done.18 = bf16[16,3584]{1,0:T(8,128)(2,1)S(1)} collective-permute-done((bf16[16,3584]{1,0:T(8,128)(2,1)S(1)}, bf16[16,3584]{1,0:T(8,128)(2,1)S(1)}, u32[]{:S(2)}, u32[]{:S(2)}) %collective-permute-start.18) | collective-permute-done | bytes 114720 | tf_op jit(solution)/shard_map/ppermute | solution.py:200
  44.0 1.9 %collective-permute-start.19 = (bf16[16,3584]{1,0:T(8,128)(2,1)S(1)}, bf16[16,3584]{1,0:T(8,128)(2,1)S(1)}, u32[]{:S(2)}, u32[]{:S(2)}) collective-permute-start(bf16[16,3584]{1,0:T(8,128)(2,1)S(1)} %add_convert_fusion.2), channel_id=1, source_target_pairs={{0,8},{1,9},{2,10},{3,11},{4,12},{5,13},{6,14},{7,15},{8,0},{9,1},... | collective-permute-start | bytes 344072 | tf_op jit(solution)/shard_map/ppermute | solution.py:200
  46.0 1.4 %collective-permute-start.21 = (bf16[16,3584]{1,0:T(8,128)(2,1)S(1)}, bf16[16,3584]{1,0:T(8,128)(2,1)S(1)}, u32[]{:S(2)}, u32[]{:S(2)}) collective-permute-start(bf16[16,3584]{1,0:T(8,128)(2,1)S(1)} %add_convert_fusion.1), channel_id=1, source_target_pairs={{0,4},{1,3},{2,6},{3,1},{4,0},{5,7},{6,2},{7,5},{8,12},{9,11},{10,... | collective-permute-start | bytes 344072 | tf_op jit(solution)/shard_map/ppermute | solution.py:200
  47.4 3.4 %attention.7 = bf16[8,2,128,512]{3,2,1,0:T(8,128)(2,1)} custom-call(s32[8]{0:T(128)} %length_ref.3, bf16[8,2,576,128]{3,2,1,0:T(8,128)(2,1)S(1)} %bitcast.9, bf16[8,576,256]{2,1,0:T(8,128)(2,1)S(1)} %bitcast.13, bf16[8,2,576]{2,1,0:T(2,128)(2,1)S(1)} %copy-done.4, bf16[8,2,128,512]{3,2,1,0:T(8,128)(2,1)} %attention.6.refs_0_), custom_call_target="tpu_custom_call", output_to_operand_aliasing={{}: (4, {})} | custom-call | flops 1048576 | bytes 65536 | tf_op jit(solution)/shard_map/attention/pallas_call | solution.py:75
  (55 shorter events, 5.6 us)
Async XLA Ops:
  0.7 22.2 %copy-start.3 = (bf16[2,512,3584]{2,1,0:T(8,128)(2,1)S(1)}, bf16[2,512,3584]{2,1,0:T(8,128)(2,1)}, u32[]{:S(2)}) copy-start(bf16[2,512,3584]{2,1,0:T(8,128)(2,1)} %refs_10_.1) | copy-start | bytes 22020100
  2.0 10.7 %collective-permute-start = (bf16[16,3712]{1,0:T(8,128)(2,1)S(1)}, bf16[16,3712]{1,0:T(8,128)(2,1)S(1)}, u32[]{:S(2)}, u32[]{:S(2)}) collective-permute-start(bf16[16,3712]{1,0:T(8,128)(2,1)S(1)} %route.1), channel_id=1, source_target_pairs={{0,2},{1,5},{2,0},{3,7},{4,6},{5,1},{6,4},{7,3},{8,10},{9,13},{10,... | collective-permute-start | bytes 356360 | tf_op jit(solution)/shard_map/ppermute | solution.py:200
  4.9 7.8 %collective-permute-start.1 = (bf16[16,3712]{1,0:T(8,128)(2,1)S(1)}, bf16[16,3712]{1,0:T(8,128)(2,1)S(1)}, u32[]{:S(2)}, u32[]{:S(2)}) collective-permute-start(bf16[16,3712]{1,0:T(8,128)(2,1)S(1)} %route.1), channel_id=1, source_target_pairs={{0,4},{1,3},{2,6},{3,1},{4,0},{5,7},{6,2},{7,5},{8,12},{9,11},{10,... | collective-permute-start | bytes 356360 | tf_op jit(solution)/shard_map/ppermute | solution.py:200
  6.5 7.7 %collective-permute-start.2 = (bf16[16,3712]{1,0:T(8,128)(2,1)S(1)}, bf16[16,3712]{1,0:T(8,128)(2,1)S(1)}, u32[]{:S(2)}, u32[]{:S(2)}) collective-permute-start(bf16[16,3712]{1,0:T(8,128)(2,1)S(1)} %route.1), channel_id=1, source_target_pairs={{0,8},{1,9},{2,10},{3,11},{4,12},{5,13},{6,14},{7,15},{8,0},{9,1},... | collective-permute-start | bytes 356360 | tf_op jit(solution)/shard_map/ppermute | solution.py:200
  9.1 13.7 %slice-start = ((s8[7340032]{0:T(1024)(128)(4,1)}), s8[4194304]{0:T(1024)(128)(4,1)S(1)}, s32[]{:S(2)}) async-start(s8[7340032]{0:T(1024)(128)(4,1)} %bitcast.14), calls=%async_computation | async-start | bytes 8388608
  14.3 2.7 %collective-permute-start.4 = (bf16[32,3712]{1,0:T(8,128)(2,1)S(1)}, bf16[32,3712]{1,0:T(8,128)(2,1)S(1)}, u32[]{:S(2)}, u32[]{:S(2)}) collective-permute-start(bf16[32,3712]{1,0:T(8,128)(2,1)S(1)} %constant_dynamic-update-slice_fusion.refs_0_), channel_id=1, source_target_pairs={{0,1},{1,0},{2,3},{3,2},{4,5},{5,4},{6,7},{7,6},{8,9},{9,8},{10,11... | collective-permute-start | bytes 712712 | tf_op jit(solution)/shard_map/ppermute | solution.py:204
  14.4 2.6 %collective-permute-start.5 = (bf16[32,3712]{1,0:T(8,128)(2,1)S(1)}, bf16[32,3712]{1,0:T(8,128)(2,1)S(1)}, u32[]{:S(2)}, u32[]{:S(2)}) collective-permute-start(bf16[32,3712]{1,0:T(8,128)(2,1)S(1)} %constant_dynamic-update-slice_fusion.2.refs_1_), channel_id=1, source_target_pairs={{0,1},{1,0},{2,3},{3,2},{4,5},{5,4},{6,7},{7,6},{8,9},{9,8},{10,11... | collective-permute-start | bytes 712712 | tf_op jit(solution)/shard_map/ppermute | solution.py:204
  15.0 6.0 %collective-permute-start.3 = (bf16[16,3712]{1,0:T(8,128)(2,1)S(1)}, bf16[16,3712]{1,0:T(8,128)(2,1)S(1)}, u32[]{:S(2)}, u32[]{:S(2)}) collective-permute-start(bf16[16,3712]{1,0:T(8,128)(2,1)S(1)} %collective-permute-done.2), channel_id=1, source_target_pairs={{0,4},{1,3},{2,6},{3,1},{4,0},{5,7},{6,2},{7,5},{8,12},{9,11},{10,... | collective-permute-start | bytes 356360 | tf_op jit(solution)/shard_map/ppermute | solution.py:200
  15.0 6.5 %collective-permute-start.7 = (bf16[16,3712]{1,0:T(8,128)(2,1)S(1)}, bf16[16,3712]{1,0:T(8,128)(2,1)S(1)}, u32[]{:S(2)}, u32[]{:S(2)}) collective-permute-start(bf16[16,3712]{1,0:T(8,128)(2,1)S(1)} %collective-permute-done.1), channel_id=1, source_target_pairs={{0,2},{1,5},{2,0},{3,7},{4,6},{5,1},{6,4},{7,3},{8,10},{9,13},{10,... | collective-permute-start | bytes 356360 | tf_op jit(solution)/shard_map/ppermute | solution.py:200
  15.7 5.7 %collective-permute-start.8 = (bf16[16,3712]{1,0:T(8,128)(2,1)S(1)}, bf16[16,3712]{1,0:T(8,128)(2,1)S(1)}, u32[]{:S(2)}, u32[]{:S(2)}) collective-permute-start(bf16[16,3712]{1,0:T(8,128)(2,1)S(1)} %collective-permute-done.2), channel_id=1, source_target_pairs={{0,2},{1,5},{2,0},{3,7},{4,6},{5,1},{6,4},{7,3},{8,10},{9,13},{10,... | collective-permute-start | bytes 356360 | tf_op jit(solution)/shard_map/ppermute | solution.py:200
  21.0 1.3 %collective-permute-start.6 = (bf16[16,3712]{1,0:T(8,128)(2,1)S(1)}, bf16[16,3712]{1,0:T(8,128)(2,1)S(1)}, u32[]{:S(2)}, u32[]{:S(2)}) collective-permute-start(bf16[16,3712]{1,0:T(8,128)(2,1)S(1)} %collective-permute-done.3.refs_0_), channel_id=1, source_target_pairs={{0,1},{1,0},{2,3},{3,2},{4,5},{5,4},{6,7},{7,6},{8,9},{9,8},{10,11... | collective-permute-start | bytes 356360 | tf_op jit(solution)/shard_map/ppermute | solution.py:204
  21.0 5.9 %collective-permute-start.9 = (bf16[16,3712]{1,0:T(8,128)(2,1)S(1)}, bf16[16,3712]{1,0:T(8,128)(2,1)S(1)}, u32[]{:S(2)}, u32[]{:S(2)}) collective-permute-start(bf16[16,3712]{1,0:T(8,128)(2,1)S(1)} %collective-permute-done.3.refs_0_), channel_id=1, source_target_pairs={{0,2},{1,5},{2,0},{3,7},{4,6},{5,1},{6,4},{7,3},{8,10},{9,13},{10,... | collective-permute-start | bytes 356360 | tf_op jit(solution)/shard_map/ppermute | solution.py:200
  22.3 4.6 %collective-permute-start.10 = (bf16[16,3712]{1,0:T(8,128)(2,1)S(1)}, bf16[16,3712]{1,0:T(8,128)(2,1)S(1)}, u32[]{:S(2)}, u32[]{:S(2)}) collective-permute-start(bf16[16,3712]{1,0:T(8,128)(2,1)S(1)} %collective-permute-done.8.refs_1_), channel_id=1, source_target_pairs={{0,1},{1,0},{2,3},{3,2},{4,5},{5,4},{6,7},{7,6},{8,9},{9,8},{10,11... | collective-permute-start | bytes 356360 | tf_op jit(solution)/shard_map/ppermute | solution.py:204
  22.5 4.4 %collective-permute-start.11 = (bf16[16,3712]{1,0:T(8,128)(2,1)S(1)}, bf16[16,3712]{1,0:T(8,128)(2,1)S(1)}, u32[]{:S(2)}, u32[]{:S(2)}) collective-permute-start(bf16[16,3712]{1,0:T(8,128)(2,1)S(1)} %collective-permute-done.7.refs_2_), channel_id=1, source_target_pairs={{0,1},{1,0},{2,3},{3,2},{4,5},{5,4},{6,7},{7,6},{8,9},{9,8},{10,11... | collective-permute-start | bytes 356360 | tf_op jit(solution)/shard_map/ppermute | solution.py:204
  26.9 1.4 %collective-permute-start.12 = (bf16[16,3712]{1,0:T(8,128)(2,1)S(1)}, bf16[16,3712]{1,0:T(8,128)(2,1)S(1)}, u32[]{:S(2)}, u32[]{:S(2)}) collective-permute-start(bf16[16,3712]{1,0:T(8,128)(2,1)S(1)} %collective-permute-done.9.refs_3_), channel_id=1, source_target_pairs={{0,1},{1,0},{2,3},{3,2},{4,5},{5,4},{6,7},{7,6},{8,9},{9,8},{10,11... | collective-permute-start | bytes 356360 | tf_op jit(solution)/shard_map/ppermute | solution.py:204
  32.3 1.4 %collective-permute-start.15 = (bf16[16,3584]{1,0:T(8,128)(2,1)S(1)}, bf16[16,3584]{1,0:T(8,128)(2,1)S(1)}, u32[]{:S(2)}, u32[]{:S(2)}) collective-permute-start(bf16[16,3584]{1,0:T(8,128)(2,1)S(1)} %get-tuple-element.109), channel_id=1, source_target_pairs={{0,1},{1,0},{2,3},{3,2},{4,5},{5,4},{6,7},{7,6},{8,9},{9,8},{10,11... | collective-permute-start | bytes 344072 | tf_op jit(solution)/shard_map/ppermute | solution.py:204
  32.5 2.1 %collective-permute-start.13 = (bf16[48,3584]{1,0:T(8,128)(2,1)S(1)}, bf16[48,3584]{1,0:T(8,128)(2,1)S(1)}, u32[]{:S(2)}, u32[]{:S(2)}) collective-permute-start(bf16[48,3584]{1,0:T(8,128)(2,1)S(1)} %get-tuple-element.107), channel_id=1, source_target_pairs={{0,1},{1,0},{2,3},{3,2},{4,5},{5,4},{6,7},{7,6},{8,9},{9,8},{10,11... | collective-permute-start | bytes 1032200 | tf_op jit(solution)/shard_map/ppermute | solution.py:204
  32.9 5.4 %collective-permute-start.17 = (bf16[64,3584]{1,0:T(8,128)(2,1)S(1)}, bf16[64,3584]{1,0:T(8,128)(2,1)S(1)}, u32[]{:S(2)}, u32[]{:S(2)}) collective-permute-start(bf16[64,3584]{1,0:T(8,128)(2,1)S(1)} %get-tuple-element.111), channel_id=1, source_target_pairs={{0,1},{1,0},{2,3},{3,2},{4,5},{5,4},{6,7},{7,6},{8,9},{9,8},{10,11... | collective-permute-start | bytes 1376264 | tf_op jit(solution)/shard_map/ppermute | solution.py:204
  33.7 4.9 %collective-permute-start.16 = (bf16[16,3584]{1,0:T(8,128)(2,1)S(1)}, bf16[16,3584]{1,0:T(8,128)(2,1)S(1)}, u32[]{:S(2)}, u32[]{:S(2)}) collective-permute-start(bf16[16,3584]{1,0:T(8,128)(2,1)S(1)} %add_convert_fusion.3), channel_id=1, source_target_pairs={{0,2},{1,5},{2,0},{3,7},{4,6},{5,1},{6,4},{7,3},{8,10},{9,13},{10,... | collective-permute-start | bytes 344072 | tf_op jit(solution)/shard_map/ppermute | solution.py:200
  34.7 6.7 %collective-permute-start.14 = (bf16[32,3584]{1,0:T(8,128)(2,1)S(1)}, bf16[32,3584]{1,0:T(8,128)(2,1)S(1)}, u32[]{:S(2)}, u32[]{:S(2)}) collective-permute-start(bf16[32,3584]{1,0:T(8,128)(2,1)S(1)} %slice.47), channel_id=1, source_target_pairs={{0,2},{1,5},{2,0},{3,7},{4,6},{5,1},{6,4},{7,3},{8,10},{9,13},{10,... | collective-permute-start | bytes 688136 | tf_op jit(solution)/shard_map/ppermute | solution.py:200
  38.6 5.3 %collective-permute-start.18 = (bf16[16,3584]{1,0:T(8,128)(2,1)S(1)}, bf16[16,3584]{1,0:T(8,128)(2,1)S(1)}, u32[]{:S(2)}, u32[]{:S(2)}) collective-permute-start(bf16[16,3584]{1,0:T(8,128)(2,1)S(1)} %fusion), channel_id=1, source_target_pairs={{0,4},{1,3},{2,6},{3,1},{4,0},{5,7},{6,2},{7,5},{8,12},{9,11},{10,... | collective-permute-start | bytes 344072 | tf_op jit(solution)/shard_map/ppermute | solution.py:200
  41.4 9.7 %collective-permute-start.20 = (bf16[16,3584]{1,0:T(8,128)(2,1)S(1)}, bf16[16,3584]{1,0:T(8,128)(2,1)S(1)}, u32[]{:S(2)}, u32[]{:S(2)}) collective-permute-start(bf16[16,3584]{1,0:T(8,128)(2,1)S(1)} %slice.48), channel_id=1, source_target_pairs={{0,2},{1,5},{2,0},{3,7},{4,6},{5,1},{6,4},{7,3},{8,10},{9,13},{10,... | collective-permute-start | bytes 344072 | tf_op jit(solution)/shard_map/ppermute | solution.py:200
  44.0 7.1 %collective-permute-start.19 = (bf16[16,3584]{1,0:T(8,128)(2,1)S(1)}, bf16[16,3584]{1,0:T(8,128)(2,1)S(1)}, u32[]{:S(2)}, u32[]{:S(2)}) collective-permute-start(bf16[16,3584]{1,0:T(8,128)(2,1)S(1)} %add_convert_fusion.2), channel_id=1, source_target_pairs={{0,8},{1,9},{2,10},{3,11},{4,12},{5,13},{6,14},{7,15},{8,0},{9,1},... | collective-permute-start | bytes 344072 | tf_op jit(solution)/shard_map/ppermute | solution.py:200
  46.0 5.9 %collective-permute-start.21 = (bf16[16,3584]{1,0:T(8,128)(2,1)S(1)}, bf16[16,3584]{1,0:T(8,128)(2,1)S(1)}, u32[]{:S(2)}, u32[]{:S(2)}) collective-permute-start(bf16[16,3584]{1,0:T(8,128)(2,1)S(1)} %add_convert_fusion.1), channel_id=1, source_target_pairs={{0,4},{1,3},{2,6},{3,1},{4,0},{5,7},{6,2},{7,5},{8,12},{9,11},{10,... | collective-permute-start | bytes 344072 | tf_op jit(solution)/shard_map/ppermute | solution.py:200
  (5 other events, 47.6 us)

commit v9 on v7

--- a/solution.py
+++ b/solution.py
@@ -125,7 +125,7 @@
     )(*(pltpu.with_memory_space_constraint(x, pltpu.HBM) for x in (placement.T, rows, scores.T, expert_ids.T)))
 
 
-def experts_kernel(*refs, parts, groups, tile):
+def experts_kernel(*refs, parts, groups):
     rows_refs, refs = refs[:parts], refs[parts:]
     (gate_ref, up_ref, down_ref, chip_ref), refs = refs[:4], refs[4:]
     out_refs, (rows_s, act_s) = refs[: 2 * groups], refs[2 * groups :]
@@ -145,20 +145,13 @@
         act = gate / (1.0 + jnp.exp(-gate)) * up
         act_s[:, s * hidden : (s + 1) * hidden] = (weight * act).astype(BF16)
 
-    def step(i, carry):
-        columns = pl.ds(pl.multiple_of(i * tile, LANES), tile)
-        total = contract(act_s[:, :hidden], down_ref[0, :, columns], 1, 0)
-        for s in range(1, slots):
-            total = total + contract(
-                act_s[:, s * hidden : (s + 1) * hidden], down_ref[s, :, columns], 1, 0
-            )
-        start = 0
-        for ref in out_refs:
-            ref[:, columns] = total[start : start + ref.shape[0]].astype(ref.dtype)
-            start += ref.shape[0]
-        return carry
-
-    lax.fori_loop(0, width // tile, step, 0)
+    total = contract(act_s[:, :hidden], down_ref[0], 1, 0)
+    for s in range(1, slots):
+        total = total + contract(act_s[:, s * hidden : (s + 1) * hidden], down_ref[s], 1, 0)
+    start = 0
+    for ref in out_refs:
+        ref[...] = total[start : start + ref.shape[0]].astype(ref.dtype)
+        start += ref.shape[0]
 
 
 def experts(parts, gate, up, down, chip, groups):
@@ -166,7 +159,7 @@
     count = 2 * sum(groups)
     vmem = pl.BlockSpec(memory_space=pltpu.VMEM)
     outs = pl.pallas_call(
-        functools.partial(experts_kernel, parts=len(parts), groups=len(groups), tile=width // 4),
+        functools.partial(experts_kernel, parts=len(parts), groups=len(groups)),
         in_specs=[vmem] * (len(parts) + 3) + [pl.BlockSpec(memory_space=pltpu.SMEM)],
         out_specs=[vmem] * (2 * len(groups)),
         out_shape=[

time: 51.5 us -> 51 us (level)
  waiting for transfers between devices: 8 us -> 9.93 us
  Pallas kernels: 20.2 us -> 18.7 us
  starting transfers between devices: 21 us -> 20.1 us
    ppermute x13, waiting for transfers between devices: 7.1 us -> 9.1 us  [hop(): return lax.ppermute(x, ('ep', 'sub'), pairs)]
    pallas_call x2, Pallas kernels: 7.98 us -> 6.48 us  [experts(): pl.pallas_call(functools.partial(experts_kernel, parts=len(parts), groups...]
    ppermute x13, starting transfers between devices: 18.7 us -> 17.9 us  [hop(): return lax.ppermute(x, ('ep', 'sub'), pairs)]
  transfers between devices with their start and end apart: 21 -> 21, of which waited for: 9 -> 10; matrix products, arithmetic and copies ran while one was open for 1% -> 1% of each run, Pallas kernels for 37% -> 34%
where the time goes in v9:
time: 51 us; the launch traced here: 50.9 us
  starting transfers between devices  20.1 us (39%)
  Pallas kernels  18.7 us (37%)
  waiting for transfers between devices  9.93 us (19%)
  other arithmetic  1.01 us (2%)
  between operations  0.95 us (2%)
    ppermute x13, starting transfers between devices, hop(): return lax.ppermute(x, ('ep', 'sub'), pairs)  17.9 us
    pallas_call x4, Pallas kernels, attention(): pl.pallas_call(functools.partial(attention_kernel, first=first, count=cou...  11 us
    ppermute x13, waiting for transfers between devices, hop(): return lax.ppermute(x, ('ep', 'sub'), pairs)  9.1 us
    pallas_call x2, Pallas kernels, experts(): pl.pallas_call(functools.partial(experts_kernel, parts=len(parts), groups...  6.48 us
    ppermute x8, starting transfers between devices, swap(): return lax.ppermute(x, 'sub', [(0, 1), (1, 0)])  2.16 us
    pallas_call x1, Pallas kernels, route(): pl.pallas_call(functools.partial(route_kernel, experts=placement.shape[0]...  1.27 us
  transfers between devices with their start and end apart: 21, of which 10 were waited for; matrix products, arithmetic and copies ran while one was open for 1% of the time, Pallas kernels for 34%

profile of v9, /device:TPU:0, one launch (start us, length us, event | category | flops | bytes accessed | tf_op | source)
XLA Modules:
  0.0 50.9 jit_solution(3633085541770639296)
XLA Ops:
  0.7 1.3 %route.1 = bf16[16,3712]{1,0:T(8,128)(2,1)S(1)} custom-call(s32[2,14]{1,0:T(2,128)} %bitcast.22, bf16[16,3584]{1,0:T(8,128)(2,1)} %rows_ref.1, f32[8,16]{1,0:T(8,128)} %bitcast.20, s32[8,16]{1,0:T(8,128)} %bitcast.21), custom_call_target="tpu_custom_call" | custom-call | flops 17179869184 | bytes 33554432 | tf_op jit(solution)/shard_map/route/pallas_call | solution.py:117
  2.0 4.0 %collective-permute-start.2 = (bf16[16,3712]{1,0:T(8,128)(2,1)S(1)}, bf16[16,3712]{1,0:T(8,128)(2,1)S(1)}, u32[]{:S(2)}, u32[]{:S(2)}) collective-permute-start(bf16[16,3712]{1,0:T(8,128)(2,1)S(1)} %route.1), channel_id=1, source_target_pairs={{0,8},{1,9},{2,10},{3,11},{4,12},{5,13},{6,14},{7,15},{8,0},{9,1},... | collective-permute-start | bytes 356360 | tf_op jit(solution)/shard_map/ppermute | solution.py:193
  6.0 1.6 %collective-permute-start.1 = (bf16[16,3712]{1,0:T(8,128)(2,1)S(1)}, bf16[16,3712]{1,0:T(8,128)(2,1)S(1)}, u32[]{:S(2)}, u32[]{:S(2)}) collective-permute-start(bf16[16,3712]{1,0:T(8,128)(2,1)S(1)} %route.1), channel_id=1, source_target_pairs={{0,4},{1,3},{2,6},{3,1},{4,0},{5,7},{6,2},{7,5},{8,12},{9,11},{10,... | collective-permute-start | bytes 356360 | tf_op jit(solution)/shard_map/ppermute | solution.py:193
  7.6 1.5 %collective-permute-start = (bf16[16,3712]{1,0:T(8,128)(2,1)S(1)}, bf16[16,3712]{1,0:T(8,128)(2,1)S(1)}, u32[]{:S(2)}, u32[]{:S(2)}) collective-permute-start(bf16[16,3712]{1,0:T(8,128)(2,1)S(1)} %route.1), channel_id=1, source_target_pairs={{0,2},{1,5},{2,0},{3,7},{4,6},{5,1},{6,4},{7,3},{8,10},{9,13},{10,... | collective-permute-start | bytes 356360 | tf_op jit(solution)/shard_map/ppermute | solution.py:193
  9.2 3.4 %attention.4.refs_0_ = bf16[8,2,128,512]{3,2,1,0:T(8,128)(2,1)} custom-call(s32[8]{0:T(128)} %length_ref.3, bf16[8,2,576,128]{3,2,1,0:T(8,128)(2,1)S(1)} %bitcast.6, bf16[8,576,256]{2,1,0:T(8,128)(2,1)S(1)} %bitcast.10, bf16[8,2,576]{2,1,0:T(2,128)(2,1)S(1)} %copy-done.2), custom_call_target="tpu_custom_call" | custom-call | flops 1048576 | bytes 65536 | tf_op jit(solution)/shard_map/attention/pallas_call | solution.py:75
  12.6 0.8 %collective-permute-done.1 = bf16[16,3712]{1,0:T(8,128)(2,1)S(1)} collective-permute-done((bf16[16,3712]{1,0:T(8,128)(2,1)S(1)}, bf16[16,3712]{1,0:T(8,128)(2,1)S(1)}, u32[]{:S(2)}, u32[]{:S(2)}) %collective-permute-start.1) | collective-permute-done | bytes 118816 | tf_op jit(solution)/shard_map/ppermute | solution.py:193
  14.7 1.1 %collective-permute-start.5 = (bf16[16,3712]{1,0:T(8,128)(2,1)S(1)}, bf16[16,3712]{1,0:T(8,128)(2,1)S(1)}, u32[]{:S(2)}, u32[]{:S(2)}) collective-permute-start(bf16[16,3712]{1,0:T(8,128)(2,1)S(1)} %collective-permute-done.2), channel_id=1, source_target_pairs={{0,4},{1,3},{2,6},{3,1},{4,0},{5,7},{6,2},{7,5},{8,12},{9,11},{10,... | collective-permute-start | bytes 356360 | tf_op jit(solution)/shard_map/ppermute | solution.py:193
  16.4 3.2 %experts.2 = (f32[64,3584]{1,0:T(8,128)S(1)}, bf16[64,3584]{1,0:T(8,128)(2,1)S(1)}) custom-call(bf16[32,3712]{1,0:T(8,128)(2,1)S(1)} %constant_dynamic-update-slice_fusion.refs_0_, bf16[32,3712]{1,0:T(8,128)(2,1)S(1)} %constant_dynamic-update-slice_fusion.2.refs_1_, bf16[32,3712]{1,0:T(8,128)(2,1)S(1)} %collective-permute-done.6.refs_2_, ...), custom_call_target="tpu_custom_call" | custom-call | flops 1048576 | bytes 65536 | tf_op jit(solution)/shard_map/experts/pallas_call | solution.py:161
  19.6 0.9 %collective-permute-done.5 = bf16[16,3712]{1,0:T(8,128)(2,1)S(1)} collective-permute-done((bf16[16,3712]{1,0:T(8,128)(2,1)S(1)}, bf16[16,3712]{1,0:T(8,128)(2,1)S(1)}, u32[]{:S(2)}, u32[]{:S(2)}) %collective-permute-start.5) | collective-permute-done | bytes 118816 | tf_op jit(solution)/shard_map/ppermute | solution.py:193
  20.6 1.4 %collective-permute-start.8 = (bf16[16,3712]{1,0:T(8,128)(2,1)S(1)}, bf16[16,3712]{1,0:T(8,128)(2,1)S(1)}, u32[]{:S(2)}, u32[]{:S(2)}) collective-permute-start(bf16[16,3712]{1,0:T(8,128)(2,1)S(1)} %collective-permute-done.5), channel_id=1, source_target_pairs={{0,2},{1,5},{2,0},{3,7},{4,6},{5,1},{6,4},{7,3},{8,10},{9,13},{10,... | collective-permute-start | bytes 356360 | tf_op jit(solution)/shard_map/ppermute | solution.py:193
  22.6 2.7 %attention.5.refs_0_ = bf16[8,2,128,512]{3,2,1,0:T(8,128)(2,1)} custom-call(s32[8]{0:T(128)} %length_ref.3, bf16[8,2,576,128]{3,2,1,0:T(8,128)(2,1)S(1)} %bitcast.7, bf16[8,576,256]{2,1,0:T(8,128)(2,1)S(1)} %bitcast.11, bf16[8,2,576]{2,1,0:T(2,128)(2,1)S(1)} %copy-done.2, bf16[8,2,128,512]{3,2,1,0:T(8,128)(2,1)} %attention.4.refs_0_), custom_call_target="tpu_custom_call", output_to_operand_aliasing={{}: (4, {})} | custom-call | flops 1048576 | bytes 65536 | tf_op jit(solution)/shard_map/attention/pallas_call | solution.py:75
  26.0 1.1 %collective-permute-start.13 = (bf16[16,3584]{1,0:T(8,128)(2,1)S(1)}, bf16[16,3584]{1,0:T(8,128)(2,1)S(1)}, u32[]{:S(2)}, u32[]{:S(2)}) collective-permute-start(bf16[16,3584]{1,0:T(8,128)(2,1)S(1)} %slice.48), channel_id=1, source_target_pairs={{0,2},{1,5},{2,0},{3,7},{4,6},{5,1},{6,4},{7,3},{8,10},{9,13},{10,... | collective-permute-start | bytes 344072 | tf_op jit(solution)/shard_map/ppermute | solution.py:193
  27.1 3.3 %experts.3 = (f32[48,3584]{1,0:T(8,128)S(1)}, f32[16,3584]{1,0:T(8,128)S(1)}, bf16[48,3584]{1,0:T(8,128)(2,1)S(1)}, bf16[16,3584]{1,0:T(8,128)(2,1)S(1)}) custom-call(bf16[32,3712]{1,0:T(8,128)(2,1)S(1)} %constant_dynamic-update-slice_fusion.4.refs_0_, bf16[16,3712]{1,0:T(8,128)(2,1)S(1)} %collective-permute-done.3.refs_1_, ...), custom_call_target="tpu_custom_call" | custom-call | flops 1048576 | bytes 65536 | tf_op jit(solution)/shard_map/experts/pallas_call | solution.py:161
  31.4 0.8 %collective-permute-done.16 = bf16[16,3584]{1,0:T(8,128)(2,1)S(1)} collective-permute-done((bf16[16,3584]{1,0:T(8,128)(2,1)S(1)}, bf16[16,3584]{1,0:T(8,128)(2,1)S(1)}, u32[]{:S(2)}, u32[]{:S(2)}) %collective-permute-start.16) | collective-permute-done | bytes 114720 | tf_op jit(solution)/shard_map/ppermute | solution.py:197
  32.2 1.1 %collective-permute-start.17 = (bf16[16,3584]{1,0:T(8,128)(2,1)S(1)}, bf16[16,3584]{1,0:T(8,128)(2,1)S(1)}, u32[]{:S(2)}, u32[]{:S(2)}) collective-permute-start(bf16[16,3584]{1,0:T(8,128)(2,1)S(1)} %add_convert_fusion.3), channel_id=1, source_target_pairs={{0,2},{1,5},{2,0},{3,7},{4,6},{5,1},{6,4},{7,3},{8,10},{9,13},{10,... | collective-permute-start | bytes 344072 | tf_op jit(solution)/shard_map/ppermute | solution.py:193
  33.4 1.1 %collective-permute-start.15 = (bf16[32,3584]{1,0:T(8,128)(2,1)S(1)}, bf16[32,3584]{1,0:T(8,128)(2,1)S(1)}, u32[]{:S(2)}, u32[]{:S(2)}) collective-permute-start(bf16[32,3584]{1,0:T(8,128)(2,1)S(1)} %slice.47), channel_id=1, source_target_pairs={{0,2},{1,5},{2,0},{3,7},{4,6},{5,1},{6,4},{7,3},{8,10},{9,13},{10,... | collective-permute-start | bytes 688136 | tf_op jit(solution)/shard_map/ppermute | solution.py:193
  34.5 2.2 %attention.6.refs_0_ = bf16[8,2,128,512]{3,2,1,0:T(8,128)(2,1)} custom-call(s32[8]{0:T(128)} %length_ref.3, bf16[8,2,576,128]{3,2,1,0:T(8,128)(2,1)S(1)} %bitcast.8, bf16[8,576,256]{2,1,0:T(8,128)(2,1)S(1)} %bitcast.12, bf16[8,2,576]{2,1,0:T(2,128)(2,1)S(1)} %copy-done.2, bf16[8,2,128,512]{3,2,1,0:T(8,128)(2,1)} %attention.5.refs_0_), custom_call_target="tpu_custom_call", output_to_operand_aliasing={{}: (4, {})} | custom-call | flops 1048576 | bytes 65536 | tf_op jit(solution)/shard_map/attention/pallas_call | solution.py:75
  37.1 1.0 %collective-permute-start.18 = (bf16[16,3584]{1,0:T(8,128)(2,1)S(1)}, bf16[16,3584]{1,0:T(8,128)(2,1)S(1)}, u32[]{:S(2)}, u32[]{:S(2)}) collective-permute-start(bf16[16,3584]{1,0:T(8,128)(2,1)S(1)} %fusion), channel_id=1, source_target_pairs={{0,4},{1,3},{2,6},{3,1},{4,0},{5,7},{6,2},{7,5},{8,12},{9,11},{10,... | collective-permute-start | bytes 344072 | tf_op jit(solution)/shard_map/ppermute | solution.py:193
  38.1 3.9 %collective-permute-done.18 = bf16[16,3584]{1,0:T(8,128)(2,1)S(1)} collective-permute-done((bf16[16,3584]{1,0:T(8,128)(2,1)S(1)}, bf16[16,3584]{1,0:T(8,128)(2,1)S(1)}, u32[]{:S(2)}, u32[]{:S(2)}) %collective-permute-start.18) | collective-permute-done | bytes 114720 | tf_op jit(solution)/shard_map/ppermute | solution.py:193
  42.0 2.1 %collective-permute-start.19 = (bf16[16,3584]{1,0:T(8,128)(2,1)S(1)}, bf16[16,3584]{1,0:T(8,128)(2,1)S(1)}, u32[]{:S(2)}, u32[]{:S(2)}) collective-permute-start(bf16[16,3584]{1,0:T(8,128)(2,1)S(1)} %add_convert_fusion.2), channel_id=1, source_target_pairs={{0,8},{1,9},{2,10},{3,11},{4,12},{5,13},{6,14},{7,15},{8,0},{9,1},... | collective-permute-start | bytes 344072 | tf_op jit(solution)/shard_map/ppermute | solution.py:193
  44.1 0.8 %collective-permute-start.20 = (bf16[16,3584]{1,0:T(8,128)(2,1)S(1)}, bf16[16,3584]{1,0:T(8,128)(2,1)S(1)}, u32[]{:S(2)}, u32[]{:S(2)}) collective-permute-start(bf16[16,3584]{1,0:T(8,128)(2,1)S(1)} %add_convert_fusion.1), channel_id=1, source_target_pairs={{0,4},{1,3},{2,6},{3,1},{4,0},{5,7},{6,2},{7,5},{8,12},{9,11},{10,... | collective-permute-start | bytes 344072 | tf_op jit(solution)/shard_map/ppermute | solution.py:193
  44.9 2.7 %attention.7 = bf16[8,2,128,512]{3,2,1,0:T(8,128)(2,1)} custom-call(s32[8]{0:T(128)} %length_ref.3, bf16[8,2,576,128]{3,2,1,0:T(8,128)(2,1)S(1)} %bitcast.9, bf16[8,576,256]{2,1,0:T(8,128)(2,1)S(1)} %bitcast.13, bf16[8,2,576]{2,1,0:T(2,128)(2,1)S(1)} %copy-done.2, bf16[8,2,128,512]{3,2,1,0:T(8,128)(2,1)} %attention.6.refs_0_), custom_call_target="tpu_custom_call", output_to_operand_aliasing={{}: (4, {})} | custom-call | flops 1048576 | bytes 65536 | tf_op jit(solution)/shard_map/attention/pallas_call | solution.py:75
  47.6 1.9 %collective-permute-done.19 = bf16[16,3584]{1,0:T(8,128)(2,1)S(1)} collective-permute-done((bf16[16,3584]{1,0:T(8,128)(2,1)S(1)}, bf16[16,3584]{1,0:T(8,128)(2,1)S(1)}, u32[]{:S(2)}, u32[]{:S(2)}) %collective-permute-start.19) | collective-permute-done | bytes 114720 | tf_op jit(solution)/shard_map/ppermute | solution.py:193
  50.2 0.7 %add_convert_fusion = bf16[16,3584]{1,0:T(8,128)(2,1)} fusion(bf16[16,3584]{1,0:T(8,128)(2,1)S(1)} %collective-permute-done.19, bf16[16,3584]{1,0:T(8,128)(2,1)S(1)} %collective-permute-done.20, bf16[16,3584]{1,0:T(8,128)(2,1)S(1)} %collective-permute-done.13, f32[64,3584]{1,0:T(8,128)S(1)} %convert_add_fusion), kind=kLoop, calls=%fused_computation.6 | loop fusion | flops 401408 | bytes 688128 | tf_op jit(solution)/shard_map/convert_element_type | solution.py:295
  (61 shorter events, 5.5 us)
Async XLA Ops:
  0.6 15.7 %slice-start = ((s8[7340032]{0:T(1024)(128)(4,1)}), s8[4194304]{0:T(1024)(128)(4,1)S(1)}, s32[]{:S(2)}) async-start(s8[7340032]{0:T(1024)(128)(4,1)} %bitcast.14), calls=%async_computation | async-start | bytes 8388608
  0.6 15.7 %slice-start.2 = ((s8[7340032]{0:T(1024)(128)(4,1)}), s8[4194304]{0:T(1024)(128)(4,1)S(1)}, s32[]{:S(2)}) async-start(s8[7340032]{0:T(1024)(128)(4,1)} %bitcast.16), calls=%async_computation.2 | async-start | bytes 8388608
  0.7 15.7 %slice-start.4 = ((s8[7340032]{0:T(1024)(128)(4,1)}), s8[4194304]{0:T(1024)(128)(4,1)S(1)}, s32[]{:S(2)}) async-start(s8[7340032]{0:T(1024)(128)(4,1)} %bitcast.18), calls=%async_computation.4 | async-start | bytes 8388608
  2.0 10.6 %collective-permute-start.2 = (bf16[16,3712]{1,0:T(8,128)(2,1)S(1)}, bf16[16,3712]{1,0:T(8,128)(2,1)S(1)}, u32[]{:S(2)}, u32[]{:S(2)}) collective-permute-start(bf16[16,3712]{1,0:T(8,128)(2,1)S(1)} %route.1), channel_id=1, source_target_pairs={{0,8},{1,9},{2,10},{3,11},{4,12},{5,13},{6,14},{7,15},{8,0},{9,1},... | collective-permute-start | bytes 356360 | tf_op jit(solution)/shard_map/ppermute | solution.py:193
  6.0 7.3 %collective-permute-start.1 = (bf16[16,3712]{1,0:T(8,128)(2,1)S(1)}, bf16[16,3712]{1,0:T(8,128)(2,1)S(1)}, u32[]{:S(2)}, u32[]{:S(2)}) collective-permute-start(bf16[16,3712]{1,0:T(8,128)(2,1)S(1)} %route.1), channel_id=1, source_target_pairs={{0,4},{1,3},{2,6},{3,1},{4,0},{5,7},{6,2},{7,5},{8,12},{9,11},{10,... | collective-permute-start | bytes 356360 | tf_op jit(solution)/shard_map/ppermute | solution.py:193
  7.6 5.7 %collective-permute-start = (bf16[16,3712]{1,0:T(8,128)(2,1)S(1)}, bf16[16,3712]{1,0:T(8,128)(2,1)S(1)}, u32[]{:S(2)}, u32[]{:S(2)}) collective-permute-start(bf16[16,3712]{1,0:T(8,128)(2,1)S(1)} %route.1), channel_id=1, source_target_pairs={{0,2},{1,5},{2,0},{3,7},{4,6},{5,1},{6,4},{7,3},{8,10},{9,13},{10,... | collective-permute-start | bytes 356360 | tf_op jit(solution)/shard_map/ppermute | solution.py:193
  13.4 3.0 %collective-permute-start.7 = (bf16[32,3712]{1,0:T(8,128)(2,1)S(1)}, bf16[32,3712]{1,0:T(8,128)(2,1)S(1)}, u32[]{:S(2)}, u32[]{:S(2)}) collective-permute-start(bf16[32,3712]{1,0:T(8,128)(2,1)S(1)} %constant_dynamic-update-slice_fusion.2.refs_1_), channel_id=1, source_target_pairs={{0,1},{1,0},{2,3},{3,2},{4,5},{5,4},{6,7},{7,6},{8,9},{9,8},{10,11... | collective-permute-start | bytes 712712 | tf_op jit(solution)/shard_map/ppermute | solution.py:197
  13.5 2.9 %collective-permute-start.6 = (bf16[32,3712]{1,0:T(8,128)(2,1)S(1)}, bf16[32,3712]{1,0:T(8,128)(2,1)S(1)}, u32[]{:S(2)}, u32[]{:S(2)}) collective-permute-start(bf16[32,3712]{1,0:T(8,128)(2,1)S(1)} %constant_dynamic-update-slice_fusion.refs_0_), channel_id=1, source_target_pairs={{0,1},{1,0},{2,3},{3,2},{4,5},{5,4},{6,7},{7,6},{8,9},{9,8},{10,11... | collective-permute-start | bytes 712712 | tf_op jit(solution)/shard_map/ppermute | solution.py:197
  14.0 5.6 %collective-permute-start.3 = (bf16[16,3712]{1,0:T(8,128)(2,1)S(1)}, bf16[16,3712]{1,0:T(8,128)(2,1)S(1)}, u32[]{:S(2)}, u32[]{:S(2)}) collective-permute-start(bf16[16,3712]{1,0:T(8,128)(2,1)S(1)} %collective-permute-done.1), channel_id=1, source_target_pairs={{0,2},{1,5},{2,0},{3,7},{4,6},{5,1},{6,4},{7,3},{8,10},{9,13},{10,... | collective-permute-start | bytes 356360 | tf_op jit(solution)/shard_map/ppermute | solution.py:193
  14.7 5.9 %collective-permute-start.5 = (bf16[16,3712]{1,0:T(8,128)(2,1)S(1)}, bf16[16,3712]{1,0:T(8,128)(2,1)S(1)}, u32[]{:S(2)}, u32[]{:S(2)}) collective-permute-start(bf16[16,3712]{1,0:T(8,128)(2,1)S(1)} %collective-permute-done.2), channel_id=1, source_target_pairs={{0,4},{1,3},{2,6},{3,1},{4,0},{5,7},{6,2},{7,5},{8,12},{9,11},{10,... | collective-permute-start | bytes 356360 | tf_op jit(solution)/shard_map/ppermute | solution.py:193
  15.8 4.8 %collective-permute-start.4 = (bf16[16,3712]{1,0:T(8,128)(2,1)S(1)}, bf16[16,3712]{1,0:T(8,128)(2,1)S(1)}, u32[]{:S(2)}, u32[]{:S(2)}) collective-permute-start(bf16[16,3712]{1,0:T(8,128)(2,1)S(1)} %collective-permute-done.2), channel_id=1, source_target_pairs={{0,2},{1,5},{2,0},{3,7},{4,6},{5,1},{6,4},{7,3},{8,10},{9,13},{10,... | collective-permute-start | bytes 356360 | tf_op jit(solution)/shard_map/ppermute | solution.py:193
  20.6 4.8 %collective-permute-start.8 = (bf16[16,3712]{1,0:T(8,128)(2,1)S(1)}, bf16[16,3712]{1,0:T(8,128)(2,1)S(1)}, u32[]{:S(2)}, u32[]{:S(2)}) collective-permute-start(bf16[16,3712]{1,0:T(8,128)(2,1)S(1)} %collective-permute-done.5), channel_id=1, source_target_pairs={{0,2},{1,5},{2,0},{3,7},{4,6},{5,1},{6,4},{7,3},{8,10},{9,13},{10,... | collective-permute-start | bytes 356360 | tf_op jit(solution)/shard_map/ppermute | solution.py:193
  22.0 3.6 %collective-permute-start.10 = (bf16[16,3712]{1,0:T(8,128)(2,1)S(1)}, bf16[16,3712]{1,0:T(8,128)(2,1)S(1)}, u32[]{:S(2)}, u32[]{:S(2)}) collective-permute-start(bf16[16,3712]{1,0:T(8,128)(2,1)S(1)} %collective-permute-done.3.refs_1_), channel_id=1, source_target_pairs={{0,1},{1,0},{2,3},{3,2},{4,5},{5,4},{6,7},{7,6},{8,9},{9,8},{10,11... | collective-permute-start | bytes 356360 | tf_op jit(solution)/shard_map/ppermute | solution.py:197
  22.0 3.5 %collective-permute-start.11 = (bf16[64,3584]{1,0:T(8,128)(2,1)S(1)}, bf16[64,3584]{1,0:T(8,128)(2,1)S(1)}, u32[]{:S(2)}, u32[]{:S(2)}) collective-permute-start(bf16[64,3584]{1,0:T(8,128)(2,1)S(1)} %get-tuple-element.87), channel_id=1, source_target_pairs={{0,1},{1,0},{2,3},{3,2},{4,5},{5,4},{6,7},{7,6},{8,9},{9,8},{10,11... | collective-permute-start | bytes 1376264 | tf_op jit(solution)/shard_map/ppermute | solution.py:197
  22.5 3.0 %collective-permute-start.9 = (bf16[32,3712]{1,0:T(8,128)(2,1)S(1)}, bf16[32,3712]{1,0:T(8,128)(2,1)S(1)}, u32[]{:S(2)}, u32[]{:S(2)}) collective-permute-start(bf16[32,3712]{1,0:T(8,128)(2,1)S(1)} %constant_dynamic-update-slice_fusion.4.refs_0_), channel_id=1, source_target_pairs={{0,1},{1,0},{2,3},{3,2},{4,5},{5,4},{6,7},{7,6},{8,9},{9,8},{10,11... | collective-permute-start | bytes 712712 | tf_op jit(solution)/shard_map/ppermute | solution.py:197
  25.6 1.5 %collective-permute-start.12 = (bf16[16,3712]{1,0:T(8,128)(2,1)S(1)}, bf16[16,3712]{1,0:T(8,128)(2,1)S(1)}, u32[]{:S(2)}, u32[]{:S(2)}) collective-permute-start(bf16[16,3712]{1,0:T(8,128)(2,1)S(1)} %collective-permute-done.8.refs_2_), channel_id=1, source_target_pairs={{0,1},{1,0},{2,3},{3,2},{4,5},{5,4},{6,7},{7,6},{8,9},{9,8},{10,11... | collective-permute-start | bytes 356360 | tf_op jit(solution)/shard_map/ppermute | solution.py:197
  26.0 4.9 %collective-permute-start.13 = (bf16[16,3584]{1,0:T(8,128)(2,1)S(1)}, bf16[16,3584]{1,0:T(8,128)(2,1)S(1)}, u32[]{:S(2)}, u32[]{:S(2)}) collective-permute-start(bf16[16,3584]{1,0:T(8,128)(2,1)S(1)} %slice.48), channel_id=1, source_target_pairs={{0,2},{1,5},{2,0},{3,7},{4,6},{5,1},{6,4},{7,3},{8,10},{9,13},{10,... | collective-permute-start | bytes 344072 | tf_op jit(solution)/shard_map/ppermute | solution.py:193
  30.9 1.3 %collective-permute-start.16 = (bf16[16,3584]{1,0:T(8,128)(2,1)S(1)}, bf16[16,3584]{1,0:T(8,128)(2,1)S(1)}, u32[]{:S(2)}, u32[]{:S(2)}) collective-permute-start(bf16[16,3584]{1,0:T(8,128)(2,1)S(1)} %get-tuple-element.99), channel_id=1, source_target_pairs={{0,1},{1,0},{2,3},{3,2},{4,5},{5,4},{6,7},{7,6},{8,9},{9,8},{10,11... | collective-permute-start | bytes 344072 | tf_op jit(solution)/shard_map/ppermute | solution.py:197
  30.9 2.4 %collective-permute-start.14 = (bf16[48,3584]{1,0:T(8,128)(2,1)S(1)}, bf16[48,3584]{1,0:T(8,128)(2,1)S(1)}, u32[]{:S(2)}, u32[]{:S(2)}) collective-permute-start(bf16[48,3584]{1,0:T(8,128)(2,1)S(1)} %get-tuple-element.97), channel_id=1, source_target_pairs={{0,1},{1,0},{2,3},{3,2},{4,5},{5,4},{6,7},{7,6},{8,9},{9,8},{10,11... | collective-permute-start | bytes 1032200 | tf_op jit(solution)/shard_map/ppermute | solution.py:197
  32.2 4.9 %collective-permute-start.17 = (bf16[16,3584]{1,0:T(8,128)(2,1)S(1)}, bf16[16,3584]{1,0:T(8,128)(2,1)S(1)}, u32[]{:S(2)}, u32[]{:S(2)}) collective-permute-start(bf16[16,3584]{1,0:T(8,128)(2,1)S(1)} %add_convert_fusion.3), channel_id=1, source_target_pairs={{0,2},{1,5},{2,0},{3,7},{4,6},{5,1},{6,4},{7,3},{8,10},{9,13},{10,... | collective-permute-start | bytes 344072 | tf_op jit(solution)/shard_map/ppermute | solution.py:193
  33.4 8.5 %collective-permute-start.15 = (bf16[32,3584]{1,0:T(8,128)(2,1)S(1)}, bf16[32,3584]{1,0:T(8,128)(2,1)S(1)}, u32[]{:S(2)}, u32[]{:S(2)}) collective-permute-start(bf16[32,3584]{1,0:T(8,128)(2,1)S(1)} %slice.47), channel_id=1, source_target_pairs={{0,2},{1,5},{2,0},{3,7},{4,6},{5,1},{6,4},{7,3},{8,10},{9,13},{10,... | collective-permute-start | bytes 688136 | tf_op jit(solution)/shard_map/ppermute | solution.py:193
  37.1 4.9 %collective-permute-start.18 = (bf16[16,3584]{1,0:T(8,128)(2,1)S(1)}, bf16[16,3584]{1,0:T(8,128)(2,1)S(1)}, u32[]{:S(2)}, u32[]{:S(2)}) collective-permute-start(bf16[16,3584]{1,0:T(8,128)(2,1)S(1)} %fusion), channel_id=1, source_target_pairs={{0,4},{1,3},{2,6},{3,1},{4,0},{5,7},{6,2},{7,5},{8,12},{9,11},{10,... | collective-permute-start | bytes 344072 | tf_op jit(solution)/shard_map/ppermute | solution.py:193
  42.0 7.5 %collective-permute-start.19 = (bf16[16,3584]{1,0:T(8,128)(2,1)S(1)}, bf16[16,3584]{1,0:T(8,128)(2,1)S(1)}, u32[]{:S(2)}, u32[]{:S(2)}) collective-permute-start(bf16[16,3584]{1,0:T(8,128)(2,1)S(1)} %add_convert_fusion.2), channel_id=1, source_target_pairs={{0,8},{1,9},{2,10},{3,11},{4,12},{5,13},{6,14},{7,15},{8,0},{9,1},... | collective-permute-start | bytes 344072 | tf_op jit(solution)/shard_map/ppermute | solution.py:193
  44.1 6.0 %collective-permute-start.20 = (bf16[16,3584]{1,0:T(8,128)(2,1)S(1)}, bf16[16,3584]{1,0:T(8,128)(2,1)S(1)}, u32[]{:S(2)}, u32[]{:S(2)}) collective-permute-start(bf16[16,3584]{1,0:T(8,128)(2,1)S(1)} %add_convert_fusion.1), channel_id=1, source_target_pairs={{0,4},{1,3},{2,6},{3,1},{4,0},{5,7},{6,2},{7,5},{8,12},{9,11},{10,... | collective-permute-start | bytes 344072 | tf_op jit(solution)/shard_map/ppermute | solution.py:193
  (6 other events, 72.4 us)

commit v10 on v9

--- a/solution.py
+++ b/solution.py
@@ -88,7 +88,7 @@
     )(*operands)
 
 
-def route_kernel(place_ref, rows_ref, score_ref, expert_ref, out_ref, *, experts, slots):
+def route_kernel(place_ref, rows_ref, score_ref, expert_ref, out_ref, table_ref, *, experts):
     tokens, width = rows_ref.shape
     sigmoid = jax.nn.sigmoid(score_ref[...])
     weights = ROUTE_SCALE * sigmoid / jnp.sum(sigmoid, axis=0, keepdims=True)
@@ -107,18 +107,20 @@
     row = lax.broadcasted_iota(jnp.int32, (tokens, tokens), 0)
     column = lax.broadcasted_iota(jnp.int32, (tokens, tokens), 1)
     unit = jnp.where(row == column, 1.0, 0.0).astype(BF16)
+    table = contract(unit, table.astype(BF16), 1, 1).astype(BF16)
     out_ref[:, :width] = rows_ref[...]
-    out_ref[:, width:] = contract(unit, table.astype(BF16), 1, 1).astype(BF16)
-
-
-def route(placement, rows, scores, expert_ids, slots):
+    out_ref[:, width:] = table
+    table_ref[...] = table
+
+
+def route(placement, rows, scores, expert_ids):
     tokens, width = rows.shape
     vmem = pl.BlockSpec(memory_space=pltpu.VMEM)
     return pl.pallas_call(
-        functools.partial(route_kernel, experts=placement.shape[0], slots=slots),
+        functools.partial(route_kernel, experts=placement.shape[0]),
         in_specs=[pl.BlockSpec(memory_space=pltpu.SMEM), vmem, vmem, vmem],
-        out_specs=vmem,
-        out_shape=jax.ShapeDtypeStruct((tokens, width + LANES), BF16),
+        out_specs=[vmem] * 2,
+        out_shape=[jax.ShapeDtypeStruct((tokens, n), BF16) for n in (width + LANES, LANES)],
         compiler_params=pltpu.CompilerParams(vmem_limit_bytes=4 << 20),
         cost_estimate=pl.CostEstimate(flops=1 << 34, bytes_accessed=1 << 25, transcendentals=0),
         name="route",
@@ -224,7 +226,6 @@
     requests, width = queries.shape[0], moe_input.shape[1]
     inputs = [queries.transpose(0, 1, 3, 2), latent_cache.transpose(0, 2, 1), new_latent]
     chip = lax.axis_index("ep").astype(jnp.int32)[None]
-    slots = ep * w_gate.shape[0]
     barrier = lax.optimization_barrier
     chip, gate_scores, lengths = barrier((chip, gate_scores, lengths))
 
@@ -245,21 +246,26 @@
         tie, out, inputs = barrier((tie, out, inputs))
         return tie
 
-    own = route(placement, moe_input, gate_scores, expert_ids, slots)
-    for turn in range(turns - 3):
-        own = jnp.concatenate([own, hop(own, ep, sub, masks, turn)], axis=0)
+    own, table = route(placement, moe_input, gate_scores, expert_ids)
+    a = jnp.concatenate([hop(x, ep, sub, masks, 0) for x in (moe_input, table)], axis=1)
     hop_a, hop_b, hop_c = (
         functools.partial(hop, ep=ep, sub=sub, masks=masks, turn=turn)
         for turn in range(turns - 3, turns)
     )
+    if turns > 3:
+        own = jnp.concatenate([own, a], axis=0)
+        for turn in range(1, turns - 3):
+            own = jnp.concatenate([own, hop(own, ep, sub, masks, turn)], axis=0)
+        a = hop_a(own)
     n = own.shape[0]
     own, inputs = barrier((own, inputs))
-    c, b, a = attend(3, (hop_c(own), hop_b(own), hop_a(own)))
-    bc, ac, ab = hop_c(b), hop_c(a), hop_b(a)
+    c = hop_c(own)
+    b, a = attend(2, (hop_b(own), a))
+    ab, bc, ac = hop_b(a), hop_c(b), hop_c(a)
     near_rows = [jnp.concatenate(x, axis=0) for x in ((own, a), (b, c))]
     near_rows += [swap(x) for x in near_rows]
     near_own, near_other = experts(near_rows, gate, up, down, chip, [4 * n])
-    bc, ac, ab, near_own, near_other = barrier((bc, ac, ab, near_own, near_other))
+    ab, bc, ac, near_own, near_other = barrier((ab, bc, ac, near_own, near_other))
     abc = hop_c(ab)
     ab, inputs = barrier((ab, inputs))
     abc = attend(2, abc)
@@ -270,7 +276,6 @@
     abc, early_swap, late_swap, near = barrier((abc, early_swap, late_swap, near))
     far_rows = [early, bc, abc, early_swap, late_swap, swap(abc)]
     far_own, far_other = experts(far_rows, gate, up, down, chip, [3 * n, n])
-    far_own, far_other, got_c = barrier((far_own, far_other, got_c))
 
     sent = add(far_own[1], swap(far_other[1])).astype(BF16)
     far = add(far_own[0], swap(far_other[0]))

time: 51 us -> 50.4 us (0.988)
  waiting for transfers between devices: 9.93 us -> 9.21 us
    ppermute x13 -> x14, waiting for transfers between devices: 9.1 us -> 7.06 us  [hop(): return lax.ppermute(x, ('ep', 'sub'), pairs)]
    ppermute x8, waiting for transfers between devices: 0.83 us -> 2.15 us  [swap(): return lax.ppermute(x, 'sub', [(0, 1), (1, 0)])]
    ppermute x13 -> x14, starting transfers between devices: 17.9 us -> 18.2 us  [hop(): return lax.ppermute(x, ('ep', 'sub'), pairs)]
  transfers between devices with their start and end apart: 21 -> 22, of which waited for: 10 -> 10; matrix products, arithmetic and copies ran while one was open for 1% -> 1% of each run, Pallas kernels for 34% -> 31%
where the time goes in v10:
time: 50.4 us; the launch traced here: 50.3 us
  starting transfers between devices  20.1 us (40%)
  Pallas kernels  18.9 us (38%)
  waiting for transfers between devices  9.21 us (18%)
  other arithmetic  1.02 us (2%)
  between operations  0.94 us (2%)
    ppermute x14, starting transfers between devices, hop(): return lax.ppermute(x, ('ep', 'sub'), pairs)  18.2 us
    pallas_call x4, Pallas kernels, attention(): pl.pallas_call(functools.partial(attention_kernel, first=first, count=cou...  11.1 us
    ppermute x14, waiting for transfers between devices, hop(): return lax.ppermute(x, ('ep', 'sub'), pairs)  7.06 us
    pallas_call x2, Pallas kernels, experts(): pl.pallas_call(functools.partial(experts_kernel, parts=len(parts), groups...  6.48 us
    ppermute x8, waiting for transfers between devices, swap(): return lax.ppermute(x, 'sub', [(0, 1), (1, 0)])  2.15 us
    ppermute x8, starting transfers between devices, swap(): return lax.ppermute(x, 'sub', [(0, 1), (1, 0)])  1.92 us
    pallas_call x1, Pallas kernels, route(): pl.pallas_call(functools.partial(route_kernel, experts=placement.shape[0]...  1.26 us
  transfers between devices with their start and end apart: 22, of which 10 were waited for; matrix products, arithmetic and copies ran while one was open for 1% of the time, Pallas kernels for 31%

profile of v10, /device:TPU:0, one launch (start us, length us, event | category | flops | bytes accessed | tf_op | source)
XLA Modules:
  0.0 50.3 jit_solution(18341764978721235283)
XLA Ops:
  0.6 4.1 %collective-permute-start.1 = (bf16[16,3584]{1,0:T(8,128)(2,1)}, bf16[16,3584]{1,0:T(8,128)(2,1)S(1)}, u32[]{:S(2)}, u32[]{:S(2)}) collective-permute-start(bf16[16,3584]{1,0:T(8,128)(2,1)} %rows_ref.1), channel_id=1, source_target_pairs={{0,8},{1,9},{2,10},{3,11},{4,12},{5,13},{6,14},{7,15},{8,0},{9,1},... | collective-permute-start | bytes 344072 | tf_op jit(solution)/shard_map/ppermute | solution.py:195
  4.8 1.3 %route.1 = (bf16[16,3712]{1,0:T(8,128)(2,1)S(1)}, bf16[16,128]{1,0:T(8,128)(2,1)S(1)}) custom-call(s32[2,14]{1,0:T(2,128)} %bitcast.22, bf16[16,3584]{1,0:T(8,128)(2,1)} %rows_ref.1, f32[8,16]{1,0:T(8,128)} %bitcast.20, s32[8,16]{1,0:T(8,128)} %bitcast.21), custom_call_target="tpu_custom_call" | custom-call | flops 17179869184 | bytes 33554432 | tf_op jit(solution)/shard_map/route/pallas_call | solution.py:119
  6.1 1.6 %collective-permute-start = (bf16[16,3712]{1,0:T(8,128)(2,1)S(1)}, bf16[16,3712]{1,0:T(8,128)(2,1)S(1)}, u32[]{:S(2)}, u32[]{:S(2)}) collective-permute-start(bf16[16,3712]{1,0:T(8,128)(2,1)S(1)} %get-tuple-element.60), channel_id=1, source_target_pairs={{0,4},{1,3},{2,6},{3,1},{4,0},{5,7},{6,2},{7,5},{8,12},{9,11},{10,... | collective-permute-start | bytes 356360 | tf_op jit(solution)/shard_map/ppermute | solution.py:195
  7.6 1.5 %collective-permute-start.6 = (bf16[16,3712]{1,0:T(8,128)(2,1)S(1)}, bf16[16,3712]{1,0:T(8,128)(2,1)S(1)}, u32[]{:S(2)}, u32[]{:S(2)}) collective-permute-start(bf16[16,3712]{1,0:T(8,128)(2,1)S(1)} %get-tuple-element.60), channel_id=1, source_target_pairs={{0,2},{1,5},{2,0},{3,7},{4,6},{5,1},{6,4},{7,3},{8,10},{9,13},{10,... | collective-permute-start | bytes 356360 | tf_op jit(solution)/shard_map/ppermute | solution.py:195
  9.5 2.8 %attention.4.refs_0_ = bf16[8,2,128,512]{3,2,1,0:T(8,128)(2,1)} custom-call(s32[8]{0:T(128)} %length_ref.3, bf16[8,2,576,128]{3,2,1,0:T(8,128)(2,1)S(1)} %bitcast.6, bf16[8,576,256]{2,1,0:T(8,128)(2,1)S(1)} %bitcast.10, bf16[8,2,576]{2,1,0:T(2,128)(2,1)S(1)} %copy-done.2), custom_call_target="tpu_custom_call" | custom-call | flops 1048576 | bytes 65536 | tf_op jit(solution)/shard_map/attention/pallas_call | solution.py:75
  12.4 1.3 %collective-permute-done.2 = bf16[16,128]{1,0:T(8,128)(2,1)S(1)} collective-permute-done((bf16[16,128]{1,0:T(8,128)(2,1)S(1)}, bf16[16,128]{1,0:T(8,128)(2,1)S(1)}, u32[]{:S(2)}, u32[]{:S(2)}) %collective-permute-start.2) | collective-permute-done | bytes 4128 | tf_op jit(solution)/shard_map/ppermute | solution.py:195
  15.3 1.5 %collective-permute-start.5 = (bf16[16,3712]{1,0:T(8,128)(2,1)S(1)}, bf16[16,3712]{1,0:T(8,128)(2,1)S(1)}, u32[]{:S(2)}, u32[]{:S(2)}) collective-permute-start(bf16[16,3712]{1,0:T(8,128)(2,1)S(1)} %pad_maximum_fusion), channel_id=1, source_target_pairs={{0,2},{1,5},{2,0},{3,7},{4,6},{5,1},{6,4},{7,3},{8,10},{9,13},{10,... | collective-permute-start | bytes 356360 | tf_op jit(solution)/shard_map/ppermute | solution.py:195
  17.0 3.2 %experts.2 = (f32[64,3584]{1,0:T(8,128)S(1)}, bf16[64,3584]{1,0:T(8,128)(2,1)S(1)}) custom-call(bf16[32,3712]{1,0:T(8,128)(2,1)S(1)} %constant_dynamic-update-slice_fusion.refs_0_, bf16[32,3712]{1,0:T(8,128)(2,1)S(1)} %constant_dynamic-update-slice_fusion.2.refs_1_, bf16[32,3712]{1,0:T(8,128)(2,1)S(1)} %collective-permute-done.7.refs_2_, ...), custom_call_target="tpu_custom_call" | custom-call | flops 1048576 | bytes 65536 | tf_op jit(solution)/shard_map/experts/pallas_call | solution.py:163
  21.0 0.8 %collective-permute-start.9 = (bf16[16,3712]{1,0:T(8,128)(2,1)S(1)}, bf16[16,3712]{1,0:T(8,128)(2,1)S(1)}, u32[]{:S(2)}, u32[]{:S(2)}) collective-permute-start(bf16[16,3712]{1,0:T(8,128)(2,1)S(1)} %collective-permute-done.3), channel_id=1, source_target_pairs={{0,2},{1,5},{2,0},{3,7},{4,6},{5,1},{6,4},{7,3},{8,10},{9,13},{10,... | collective-permute-start | bytes 356360 | tf_op jit(solution)/shard_map/ppermute | solution.py:195
  22.4 2.7 %attention.5.refs_0_ = bf16[8,2,128,512]{3,2,1,0:T(8,128)(2,1)} custom-call(s32[8]{0:T(128)} %length_ref.3, bf16[8,2,576,128]{3,2,1,0:T(8,128)(2,1)S(1)} %bitcast.7, bf16[8,576,256]{2,1,0:T(8,128)(2,1)S(1)} %bitcast.11, bf16[8,2,576]{2,1,0:T(2,128)(2,1)S(1)} %copy-done.2, bf16[8,2,128,512]{3,2,1,0:T(8,128)(2,1)} %attention.4.refs_0_), custom_call_target="tpu_custom_call", output_to_operand_aliasing={{}: (4, {})} | custom-call | flops 1048576 | bytes 65536 | tf_op jit(solution)/shard_map/attention/pallas_call | solution.py:75
  25.1 0.7 %collective-permute-done.9.refs_2_ = bf16[16,3712]{1,0:T(8,128)(2,1)S(1)} collective-permute-done((bf16[16,3712]{1,0:T(8,128)(2,1)S(1)}, bf16[16,3712]{1,0:T(8,128)(2,1)S(1)}, u32[]{:S(2)}, u32[]{:S(2)}) %collective-permute-start.9) | collective-permute-done | bytes 118816 | tf_op jit(solution)/shard_map/ppermute | solution.py:195
  26.0 1.3 %collective-permute-done.13.refs_5_ = bf16[16,3712]{1,0:T(8,128)(2,1)S(1)} collective-permute-done((bf16[16,3712]{1,0:T(8,128)(2,1)S(1)}, bf16[16,3712]{1,0:T(8,128)(2,1)S(1)}, u32[]{:S(2)}, u32[]{:S(2)}) %collective-permute-start.13) | collective-permute-done | bytes 118816 | tf_op jit(solution)/shard_map/ppermute | solution.py:199
  27.3 3.3 %experts.3 = (f32[48,3584]{1,0:T(8,128)S(1)}, f32[16,3584]{1,0:T(8,128)S(1)}, bf16[48,3584]{1,0:T(8,128)(2,1)S(1)}, bf16[16,3584]{1,0:T(8,128)(2,1)S(1)}) custom-call(bf16[32,3712]{1,0:T(8,128)(2,1)S(1)} %constant_dynamic-update-slice_fusion.4.refs_0_, bf16[16,3712]{1,0:T(8,128)(2,1)S(1)} %collective-permute-done.4.refs_1_, ...), custom_call_target="tpu_custom_call" | custom-call | flops 1048576 | bytes 65536 | tf_op jit(solution)/shard_map/experts/pallas_call | solution.py:163
  31.2 0.8 %collective-permute-done.16 = bf16[16,3584]{1,0:T(8,128)(2,1)S(1)} collective-permute-done((bf16[16,3584]{1,0:T(8,128)(2,1)S(1)}, bf16[16,3584]{1,0:T(8,128)(2,1)S(1)}, u32[]{:S(2)}, u32[]{:S(2)}) %collective-permute-start.16) | collective-permute-done | bytes 114720 | tf_op jit(solution)/shard_map/ppermute | solution.py:199
  32.0 0.8 %collective-permute-start.17 = (bf16[16,3584]{1,0:T(8,128)(2,1)S(1)}, bf16[16,3584]{1,0:T(8,128)(2,1)S(1)}, u32[]{:S(2)}, u32[]{:S(2)}) collective-permute-start(bf16[16,3584]{1,0:T(8,128)(2,1)S(1)} %add_convert_fusion.3), channel_id=1, source_target_pairs={{0,2},{1,5},{2,0},{3,7},{4,6},{5,1},{6,4},{7,3},{8,10},{9,13},{10,... | collective-permute-start | bytes 344072 | tf_op jit(solution)/shard_map/ppermute | solution.py:195
  32.9 1.3 %collective-permute-start.15 = (bf16[32,3584]{1,0:T(8,128)(2,1)S(1)}, bf16[32,3584]{1,0:T(8,128)(2,1)S(1)}, u32[]{:S(2)}, u32[]{:S(2)}) collective-permute-start(bf16[32,3584]{1,0:T(8,128)(2,1)S(1)} %slice.47), channel_id=1, source_target_pairs={{0,2},{1,5},{2,0},{3,7},{4,6},{5,1},{6,4},{7,3},{8,10},{9,13},{10,... | collective-permute-start | bytes 688136 | tf_op jit(solution)/shard_map/ppermute | solution.py:195
  34.3 2.2 %attention.6.refs_0_ = bf16[8,2,128,512]{3,2,1,0:T(8,128)(2,1)} custom-call(s32[8]{0:T(128)} %length_ref.3, bf16[8,2,576,128]{3,2,1,0:T(8,128)(2,1)S(1)} %bitcast.8, bf16[8,576,256]{2,1,0:T(8,128)(2,1)S(1)} %bitcast.12, bf16[8,2,576]{2,1,0:T(2,128)(2,1)S(1)} %copy-done.2, bf16[8,2,128,512]{3,2,1,0:T(8,128)(2,1)} %attention.5.refs_0_), custom_call_target="tpu_custom_call", output_to_operand_aliasing={{}: (4, {})} | custom-call | flops 1048576 | bytes 65536 | tf_op jit(solution)/shard_map/attention/pallas_call | solution.py:75
  36.9 1.6 %collective-permute-start.18 = (bf16[16,3584]{1,0:T(8,128)(2,1)S(1)}, bf16[16,3584]{1,0:T(8,128)(2,1)S(1)}, u32[]{:S(2)}, u32[]{:S(2)}) collective-permute-start(bf16[16,3584]{1,0:T(8,128)(2,1)S(1)} %fusion), channel_id=1, source_target_pairs={{0,4},{1,3},{2,6},{3,1},{4,0},{5,7},{6,2},{7,5},{8,12},{9,11},{10,... | collective-permute-start | bytes 344072 | tf_op jit(solution)/shard_map/ppermute | solution.py:195
  38.5 0.9 %collective-permute-start.20 = (bf16[16,3584]{1,0:T(8,128)(2,1)S(1)}, bf16[16,3584]{1,0:T(8,128)(2,1)S(1)}, u32[]{:S(2)}, u32[]{:S(2)}) collective-permute-start(bf16[16,3584]{1,0:T(8,128)(2,1)S(1)} %slice.48), channel_id=1, source_target_pairs={{0,2},{1,5},{2,0},{3,7},{4,6},{5,1},{6,4},{7,3},{8,10},{9,13},{10,... | collective-permute-start | bytes 344072 | tf_op jit(solution)/shard_map/ppermute | solution.py:195
  39.4 2.9 %collective-permute-done.18 = bf16[16,3584]{1,0:T(8,128)(2,1)S(1)} collective-permute-done((bf16[16,3584]{1,0:T(8,128)(2,1)S(1)}, bf16[16,3584]{1,0:T(8,128)(2,1)S(1)}, u32[]{:S(2)}, u32[]{:S(2)}) %collective-permute-start.18) | collective-permute-done | bytes 114720 | tf_op jit(solution)/shard_map/ppermute | solution.py:195
  42.3 2.0 %collective-permute-start.19 = (bf16[16,3584]{1,0:T(8,128)(2,1)S(1)}, bf16[16,3584]{1,0:T(8,128)(2,1)S(1)}, u32[]{:S(2)}, u32[]{:S(2)}) collective-permute-start(bf16[16,3584]{1,0:T(8,128)(2,1)S(1)} %add_convert_fusion.2), channel_id=1, source_target_pairs={{0,8},{1,9},{2,10},{3,11},{4,12},{5,13},{6,14},{7,15},{8,0},{9,1},... | collective-permute-start | bytes 344072 | tf_op jit(solution)/shard_map/ppermute | solution.py:195
  44.3 0.8 %collective-permute-start.21 = (bf16[16,3584]{1,0:T(8,128)(2,1)S(1)}, bf16[16,3584]{1,0:T(8,128)(2,1)S(1)}, u32[]{:S(2)}, u32[]{:S(2)}) collective-permute-start(bf16[16,3584]{1,0:T(8,128)(2,1)S(1)} %add_convert_fusion.1), channel_id=1, source_target_pairs={{0,4},{1,3},{2,6},{3,1},{4,0},{5,7},{6,2},{7,5},{8,12},{9,11},{10,... | collective-permute-start | bytes 344072 | tf_op jit(solution)/shard_map/ppermute | solution.py:195
  45.1 3.4 %attention.7 = bf16[8,2,128,512]{3,2,1,0:T(8,128)(2,1)} custom-call(s32[8]{0:T(128)} %length_ref.3, bf16[8,2,576,128]{3,2,1,0:T(8,128)(2,1)S(1)} %bitcast.9, bf16[8,576,256]{2,1,0:T(8,128)(2,1)S(1)} %bitcast.13, bf16[8,2,576]{2,1,0:T(2,128)(2,1)S(1)} %copy-done.2, bf16[8,2,128,512]{3,2,1,0:T(8,128)(2,1)} %attention.6.refs_0_), custom_call_target="tpu_custom_call", output_to_operand_aliasing={{}: (4, {})} | custom-call | flops 1048576 | bytes 65536 | tf_op jit(solution)/shard_map/attention/pallas_call | solution.py:75
  48.5 0.9 %collective-permute-done.19 = bf16[16,3584]{1,0:T(8,128)(2,1)S(1)} collective-permute-done((bf16[16,3584]{1,0:T(8,128)(2,1)S(1)}, bf16[16,3584]{1,0:T(8,128)(2,1)S(1)}, u32[]{:S(2)}, u32[]{:S(2)}) %collective-permute-start.19) | collective-permute-done | bytes 114720 | tf_op jit(solution)/shard_map/ppermute | solution.py:195
  (64 shorter events, 5.7 us)
Async XLA Ops:
  0.6 13.0 %collective-permute-start.1 = (bf16[16,3584]{1,0:T(8,128)(2,1)}, bf16[16,3584]{1,0:T(8,128)(2,1)S(1)}, u32[]{:S(2)}, u32[]{:S(2)}) collective-permute-start(bf16[16,3584]{1,0:T(8,128)(2,1)} %rows_ref.1), channel_id=1, source_target_pairs={{0,8},{1,9},{2,10},{3,11},{4,12},{5,13},{6,14},{7,15},{8,0},{9,1},... | collective-permute-start | bytes 344072 | tf_op jit(solution)/shard_map/ppermute | solution.py:195
  4.7 12.1 %slice-start.2 = ((s8[7340032]{0:T(1024)(128)(4,1)}), s8[4194304]{0:T(1024)(128)(4,1)S(1)}, s32[]{:S(2)}) async-start(s8[7340032]{0:T(1024)(128)(4,1)} %bitcast.16), calls=%async_computation.2 | async-start | bytes 8388608
  4.7 12.2 %slice-start.4 = ((s8[7340032]{0:T(1024)(128)(4,1)}), s8[4194304]{0:T(1024)(128)(4,1)S(1)}, s32[]{:S(2)}) async-start(s8[7340032]{0:T(1024)(128)(4,1)} %bitcast.18), calls=%async_computation.4 | async-start | bytes 8388608
  6.1 7.6 %collective-permute-start = (bf16[16,3712]{1,0:T(8,128)(2,1)S(1)}, bf16[16,3712]{1,0:T(8,128)(2,1)S(1)}, u32[]{:S(2)}, u32[]{:S(2)}) collective-permute-start(bf16[16,3712]{1,0:T(8,128)(2,1)S(1)} %get-tuple-element.60), channel_id=1, source_target_pairs={{0,4},{1,3},{2,6},{3,1},{4,0},{5,7},{6,2},{7,5},{8,12},{9,11},{10,... | collective-permute-start | bytes 356360 | tf_op jit(solution)/shard_map/ppermute | solution.py:195
  7.6 6.2 %collective-permute-start.6 = (bf16[16,3712]{1,0:T(8,128)(2,1)S(1)}, bf16[16,3712]{1,0:T(8,128)(2,1)S(1)}, u32[]{:S(2)}, u32[]{:S(2)}) collective-permute-start(bf16[16,3712]{1,0:T(8,128)(2,1)S(1)} %get-tuple-element.60), channel_id=1, source_target_pairs={{0,2},{1,5},{2,0},{3,7},{4,6},{5,1},{6,4},{7,3},{8,10},{9,13},{10,... | collective-permute-start | bytes 356360 | tf_op jit(solution)/shard_map/ppermute | solution.py:195
  9.2 4.5 %collective-permute-start.2 = (bf16[16,128]{1,0:T(8,128)(2,1)S(1)}, bf16[16,128]{1,0:T(8,128)(2,1)S(1)}, u32[]{:S(2)}, u32[]{:S(2)}) collective-permute-start(bf16[16,128]{1,0:T(8,128)(2,1)S(1)} %get-tuple-element.61), channel_id=1, source_target_pairs={{0,8},{1,9},{2,10},{3,11},{4,12},{5,13},{6,14},{7,15},{8,0},{9,1},... | collective-permute-start | bytes 12296 | tf_op jit(solution)/shard_map/ppermute | solution.py:195
  13.7 3.1 %collective-permute-start.7 = (bf16[32,3712]{1,0:T(8,128)(2,1)S(1)}, bf16[32,3712]{1,0:T(8,128)(2,1)S(1)}, u32[]{:S(2)}, u32[]{:S(2)}) collective-permute-start(bf16[32,3712]{1,0:T(8,128)(2,1)S(1)} %constant_dynamic-update-slice_fusion.refs_0_), channel_id=1, source_target_pairs={{0,1},{1,0},{2,3},{3,2},{4,5},{5,4},{6,7},{7,6},{8,9},{9,8},{10,11... | collective-permute-start | bytes 712712 | tf_op jit(solution)/shard_map/ppermute | solution.py:199
  13.8 3.0 %collective-permute-start.8 = (bf16[32,3712]{1,0:T(8,128)(2,1)S(1)}, bf16[32,3712]{1,0:T(8,128)(2,1)S(1)}, u32[]{:S(2)}, u32[]{:S(2)}) collective-permute-start(bf16[32,3712]{1,0:T(8,128)(2,1)S(1)} %constant_dynamic-update-slice_fusion.2.refs_1_), channel_id=1, source_target_pairs={{0,1},{1,0},{2,3},{3,2},{4,5},{5,4},{6,7},{7,6},{8,9},{9,8},{10,11... | collective-permute-start | bytes 712712 | tf_op jit(solution)/shard_map/ppermute | solution.py:199
  14.4 6.1 %collective-permute-start.3 = (bf16[16,3712]{1,0:T(8,128)(2,1)S(1)}, bf16[16,3712]{1,0:T(8,128)(2,1)S(1)}, u32[]{:S(2)}, u32[]{:S(2)}) collective-permute-start(bf16[16,3712]{1,0:T(8,128)(2,1)S(1)} %pad_maximum_fusion), channel_id=1, source_target_pairs={{0,4},{1,3},{2,6},{3,1},{4,0},{5,7},{6,2},{7,5},{8,12},{9,11},{10,... | collective-permute-start | bytes 356360 | tf_op jit(solution)/shard_map/ppermute | solution.py:195
  14.8 5.6 %collective-permute-start.4 = (bf16[16,3712]{1,0:T(8,128)(2,1)S(1)}, bf16[16,3712]{1,0:T(8,128)(2,1)S(1)}, u32[]{:S(2)}, u32[]{:S(2)}) collective-permute-start(bf16[16,3712]{1,0:T(8,128)(2,1)S(1)} %collective-permute-done), channel_id=1, source_target_pairs={{0,2},{1,5},{2,0},{3,7},{4,6},{5,1},{6,4},{7,3},{8,10},{9,13},{10,... | collective-permute-start | bytes 356360 | tf_op jit(solution)/shard_map/ppermute | solution.py:195
  15.3 5.6 %collective-permute-start.5 = (bf16[16,3712]{1,0:T(8,128)(2,1)S(1)}, bf16[16,3712]{1,0:T(8,128)(2,1)S(1)}, u32[]{:S(2)}, u32[]{:S(2)}) collective-permute-start(bf16[16,3712]{1,0:T(8,128)(2,1)S(1)} %pad_maximum_fusion), channel_id=1, source_target_pairs={{0,2},{1,5},{2,0},{3,7},{4,6},{5,1},{6,4},{7,3},{8,10},{9,13},{10,... | collective-permute-start | bytes 356360 | tf_op jit(solution)/shard_map/ppermute | solution.py:195
  21.0 4.8 %collective-permute-start.9 = (bf16[16,3712]{1,0:T(8,128)(2,1)S(1)}, bf16[16,3712]{1,0:T(8,128)(2,1)S(1)}, u32[]{:S(2)}, u32[]{:S(2)}) collective-permute-start(bf16[16,3712]{1,0:T(8,128)(2,1)S(1)} %collective-permute-done.3), channel_id=1, source_target_pairs={{0,2},{1,5},{2,0},{3,7},{4,6},{5,1},{6,4},{7,3},{8,10},{9,13},{10,... | collective-permute-start | bytes 356360 | tf_op jit(solution)/shard_map/ppermute | solution.py:195
  21.7 4.1 %collective-permute-start.12 = (bf16[64,3584]{1,0:T(8,128)(2,1)S(1)}, bf16[64,3584]{1,0:T(8,128)(2,1)S(1)}, u32[]{:S(2)}, u32[]{:S(2)}) collective-permute-start(bf16[64,3584]{1,0:T(8,128)(2,1)S(1)} %get-tuple-element.84), channel_id=1, source_target_pairs={{0,1},{1,0},{2,3},{3,2},{4,5},{5,4},{6,7},{7,6},{8,9},{9,8},{10,11... | collective-permute-start | bytes 1376264 | tf_op jit(solution)/shard_map/ppermute | solution.py:199
  21.7 4.2 %collective-permute-start.10 = (bf16[32,3712]{1,0:T(8,128)(2,1)S(1)}, bf16[32,3712]{1,0:T(8,128)(2,1)S(1)}, u32[]{:S(2)}, u32[]{:S(2)}) collective-permute-start(bf16[32,3712]{1,0:T(8,128)(2,1)S(1)} %constant_dynamic-update-slice_fusion.4.refs_0_), channel_id=1, source_target_pairs={{0,1},{1,0},{2,3},{3,2},{4,5},{5,4},{6,7},{7,6},{8,9},{9,8},{10,11... | collective-permute-start | bytes 712712 | tf_op jit(solution)/shard_map/ppermute | solution.py:199
  22.3 3.6 %collective-permute-start.11 = (bf16[16,3712]{1,0:T(8,128)(2,1)S(1)}, bf16[16,3712]{1,0:T(8,128)(2,1)S(1)}, u32[]{:S(2)}, u32[]{:S(2)}) collective-permute-start(bf16[16,3712]{1,0:T(8,128)(2,1)S(1)} %collective-permute-done.4.refs_1_), channel_id=1, source_target_pairs={{0,1},{1,0},{2,3},{3,2},{4,5},{5,4},{6,7},{7,6},{8,9},{9,8},{10,11... | collective-permute-start | bytes 356360 | tf_op jit(solution)/shard_map/ppermute | solution.py:199
  25.9 1.4 %collective-permute-start.13 = (bf16[16,3712]{1,0:T(8,128)(2,1)S(1)}, bf16[16,3712]{1,0:T(8,128)(2,1)S(1)}, u32[]{:S(2)}, u32[]{:S(2)}) collective-permute-start(bf16[16,3712]{1,0:T(8,128)(2,1)S(1)} %collective-permute-done.9.refs_2_), channel_id=1, source_target_pairs={{0,1},{1,0},{2,3},{3,2},{4,5},{5,4},{6,7},{7,6},{8,9},{9,8},{10,11... | collective-permute-start | bytes 356360 | tf_op jit(solution)/shard_map/ppermute | solution.py:199
  30.6 1.4 %collective-permute-start.16 = (bf16[16,3584]{1,0:T(8,128)(2,1)S(1)}, bf16[16,3584]{1,0:T(8,128)(2,1)S(1)}, u32[]{:S(2)}, u32[]{:S(2)}) collective-permute-start(bf16[16,3584]{1,0:T(8,128)(2,1)S(1)} %get-tuple-element.92), channel_id=1, source_target_pairs={{0,1},{1,0},{2,3},{3,2},{4,5},{5,4},{6,7},{7,6},{8,9},{9,8},{10,11... | collective-permute-start | bytes 344072 | tf_op jit(solution)/shard_map/ppermute | solution.py:199
  30.8 2.0 %collective-permute-start.14 = (bf16[48,3584]{1,0:T(8,128)(2,1)S(1)}, bf16[48,3584]{1,0:T(8,128)(2,1)S(1)}, u32[]{:S(2)}, u32[]{:S(2)}) collective-permute-start(bf16[48,3584]{1,0:T(8,128)(2,1)S(1)} %get-tuple-element.90), channel_id=1, source_target_pairs={{0,1},{1,0},{2,3},{3,2},{4,5},{5,4},{6,7},{7,6},{8,9},{9,8},{10,11... | collective-permute-start | bytes 1032200 | tf_op jit(solution)/shard_map/ppermute | solution.py:199
  32.0 4.9 %collective-permute-start.17 = (bf16[16,3584]{1,0:T(8,128)(2,1)S(1)}, bf16[16,3584]{1,0:T(8,128)(2,1)S(1)}, u32[]{:S(2)}, u32[]{:S(2)}) collective-permute-start(bf16[16,3584]{1,0:T(8,128)(2,1)S(1)} %add_convert_fusion.3), channel_id=1, source_target_pairs={{0,2},{1,5},{2,0},{3,7},{4,6},{5,1},{6,4},{7,3},{8,10},{9,13},{10,... | collective-permute-start | bytes 344072 | tf_op jit(solution)/shard_map/ppermute | solution.py:195
  32.9 9.3 %collective-permute-start.15 = (bf16[32,3584]{1,0:T(8,128)(2,1)S(1)}, bf16[32,3584]{1,0:T(8,128)(2,1)S(1)}, u32[]{:S(2)}, u32[]{:S(2)}) collective-permute-start(bf16[32,3584]{1,0:T(8,128)(2,1)S(1)} %slice.47), channel_id=1, source_target_pairs={{0,2},{1,5},{2,0},{3,7},{4,6},{5,1},{6,4},{7,3},{8,10},{9,13},{10,... | collective-permute-start | bytes 688136 | tf_op jit(solution)/shard_map/ppermute | solution.py:195
  36.9 5.4 %collective-permute-start.18 = (bf16[16,3584]{1,0:T(8,128)(2,1)S(1)}, bf16[16,3584]{1,0:T(8,128)(2,1)S(1)}, u32[]{:S(2)}, u32[]{:S(2)}) collective-permute-start(bf16[16,3584]{1,0:T(8,128)(2,1)S(1)} %fusion), channel_id=1, source_target_pairs={{0,4},{1,3},{2,6},{3,1},{4,0},{5,7},{6,2},{7,5},{8,12},{9,11},{10,... | collective-permute-start | bytes 344072 | tf_op jit(solution)/shard_map/ppermute | solution.py:195
  38.5 10.9 %collective-permute-start.20 = (bf16[16,3584]{1,0:T(8,128)(2,1)S(1)}, bf16[16,3584]{1,0:T(8,128)(2,1)S(1)}, u32[]{:S(2)}, u32[]{:S(2)}) collective-permute-start(bf16[16,3584]{1,0:T(8,128)(2,1)S(1)} %slice.48), channel_id=1, source_target_pairs={{0,2},{1,5},{2,0},{3,7},{4,6},{5,1},{6,4},{7,3},{8,10},{9,13},{10,... | collective-permute-start | bytes 344072 | tf_op jit(solution)/shard_map/ppermute | solution.py:195
  42.3 7.1 %collective-permute-start.19 = (bf16[16,3584]{1,0:T(8,128)(2,1)S(1)}, bf16[16,3584]{1,0:T(8,128)(2,1)S(1)}, u32[]{:S(2)}, u32[]{:S(2)}) collective-permute-start(bf16[16,3584]{1,0:T(8,128)(2,1)S(1)} %add_convert_fusion.2), channel_id=1, source_target_pairs={{0,8},{1,9},{2,10},{3,11},{4,12},{5,13},{6,14},{7,15},{8,0},{9,1},... | collective-permute-start | bytes 344072 | tf_op jit(solution)/shard_map/ppermute | solution.py:195
  44.3 5.2 %collective-permute-start.21 = (bf16[16,3584]{1,0:T(8,128)(2,1)S(1)}, bf16[16,3584]{1,0:T(8,128)(2,1)S(1)}, u32[]{:S(2)}, u32[]{:S(2)}) collective-permute-start(bf16[16,3584]{1,0:T(8,128)(2,1)S(1)} %add_convert_fusion.1), channel_id=1, source_target_pairs={{0,4},{1,3},{2,6},{3,1},{4,0},{5,7},{6,2},{7,5},{8,12},{9,11},{10,... | collective-permute-start | bytes 344072 | tf_op jit(solution)/shard_map/ppermute | solution.py:195
  (7 other events, 62.9 us)

commit v11 on v10

--- a/solution.py
+++ b/solution.py
@@ -247,20 +247,22 @@
         return tie
 
     own, table = route(placement, moe_input, gate_scores, expert_ids)
-    a = jnp.concatenate([hop(x, ep, sub, masks, 0) for x in (moe_input, table)], axis=1)
+    first = [moe_input, table]
+    for turn in range(turns - 3):
+        got = [hop(x, ep, sub, masks, turn) for x in first]
+        first = [jnp.concatenate(x, axis=0) for x in zip(first, got)]
     hop_a, hop_b, hop_c = (
         functools.partial(hop, ep=ep, sub=sub, masks=masks, turn=turn)
         for turn in range(turns - 3, turns)
     )
     if turns > 3:
-        own = jnp.concatenate([own, a], axis=0)
-        for turn in range(1, turns - 3):
-            own = jnp.concatenate([own, hop(own, ep, sub, masks, turn)], axis=0)
-        a = hop_a(own)
+        own = jnp.concatenate(first, axis=1)
     n = own.shape[0]
     own, inputs = barrier((own, inputs))
+    a, b = [[h(x) for x in first] for h in (hop_a, hop_b)]
     c = hop_c(own)
-    b, a = attend(2, (hop_b(own), a))
+    a, b = attend(2, (a, b))
+    a, b = [jnp.concatenate(x, axis=1) for x in (a, b)]
     ab, bc, ac = hop_b(a), hop_c(b), hop_c(a)
     near_rows = [jnp.concatenate(x, axis=0) for x in ((own, a), (b, c))]
     near_rows += [swap(x) for x in near_rows]

time: 50.4 us -> 51.9 us (1.030)
  starting transfers between devices: 20.1 us -> 22.9 us
  waiting for transfers between devices: 9.21 us -> 7.84 us
    ppermute x14 -> x15, starting transfers between devices: 18.2 us -> 20.7 us  [hop(): return lax.ppermute(x, ('ep', 'sub'), pairs)]
    ppermute x14 -> x15, waiting for transfers between devices: 7.06 us -> 5.95 us  [hop(): return lax.ppermute(x, ('ep', 'sub'), pairs)]
  transfers between devices with their start and end apart: 22 -> 23, of which waited for: 10 -> 8; matrix products, arithmetic and copies ran while one was open for 1% -> 1% of each run, Pallas kernels for 31% -> 30%
where the time goes in v11:
time: 51.9 us; the launch traced here: 51.8 us
  starting transfers between devices  22.9 us (44%)
  Pallas kernels  18.9 us (36%)
  waiting for transfers between devices  7.84 us (15%)
  other arithmetic  1.07 us (2%)
  between operations  0.94 us (2%)
    ppermute x15, starting transfers between devices, hop(): return lax.ppermute(x, ('ep', 'sub'), pairs)  20.7 us
    pallas_call x4, Pallas kernels, attention(): pl.pallas_call(functools.partial(attention_kernel, first=first, count=cou...  11.1 us
    pallas_call x2, Pallas kernels, experts(): pl.pallas_call(functools.partial(experts_kernel, parts=len(parts), groups...  6.52 us
    ppermute x15, waiting for transfers between devices, hop(): return lax.ppermute(x, ('ep', 'sub'), pairs)  5.95 us
    ppermute x8, starting transfers between devices, swap(): return lax.ppermute(x, 'sub', [(0, 1), (1, 0)])  2.17 us
    ppermute x8, waiting for transfers between devices, swap(): return lax.ppermute(x, 'sub', [(0, 1), (1, 0)])  1.89 us
    pallas_call x1, Pallas kernels, route(): pl.pallas_call(functools.partial(route_kernel, experts=placement.shape[0]...  1.26 us
  transfers between devices with their start and end apart: 23, of which 8 were waited for; matrix products, arithmetic and copies ran while one was open for 1% of the time, Pallas kernels for 30%

profile of v11, /device:TPU:0, one launch (start us, length us, event | category | flops | bytes accessed | tf_op | source)
XLA Modules:
  0.0 51.8 jit_solution(4225077855954902230)
XLA Ops:
  0.6 4.1 %collective-permute-start = (bf16[16,3584]{1,0:T(8,128)(2,1)}, bf16[16,3584]{1,0:T(8,128)(2,1)S(1)}, u32[]{:S(2)}, u32[]{:S(2)}) collective-permute-start(bf16[16,3584]{1,0:T(8,128)(2,1)} %rows_ref.1), channel_id=1, source_target_pairs={{0,8},{1,9},{2,10},{3,11},{4,12},{5,13},{6,14},{7,15},{8,0},{9,1},... | collective-permute-start | bytes 344072 | tf_op jit(solution)/shard_map/ppermute | solution.py:195
  4.7 1.6 %collective-permute-start.2 = (bf16[16,3584]{1,0:T(8,128)(2,1)}, bf16[16,3584]{1,0:T(8,128)(2,1)S(1)}, u32[]{:S(2)}, u32[]{:S(2)}) collective-permute-start(bf16[16,3584]{1,0:T(8,128)(2,1)} %rows_ref.1), channel_id=1, source_target_pairs={{0,4},{1,3},{2,6},{3,1},{4,0},{5,7},{6,2},{7,5},{8,12},{9,11},{10,... | collective-permute-start | bytes 344072 | tf_op jit(solution)/shard_map/ppermute | solution.py:195
  6.4 1.3 %route.1 = (bf16[16,3712]{1,0:T(8,128)(2,1)S(1)}, bf16[16,128]{1,0:T(8,128)(2,1)S(1)}) custom-call(s32[2,14]{1,0:T(2,128)} %bitcast.22, bf16[16,3584]{1,0:T(8,128)(2,1)} %rows_ref.1, f32[8,16]{1,0:T(8,128)} %bitcast.20, s32[8,16]{1,0:T(8,128)} %bitcast.21), custom_call_target="tpu_custom_call" | custom-call | flops 17179869184 | bytes 33554432 | tf_op jit(solution)/shard_map/route/pallas_call | solution.py:119
  8.2 1.8 %collective-permute-start.7 = (bf16[16,3712]{1,0:T(8,128)(2,1)S(1)}, bf16[16,3712]{1,0:T(8,128)(2,1)S(1)}, u32[]{:S(2)}, u32[]{:S(2)}) collective-permute-start(bf16[16,3712]{1,0:T(8,128)(2,1)S(1)} %get-tuple-element.71), channel_id=1, source_target_pairs={{0,2},{1,5},{2,0},{3,7},{4,6},{5,1},{6,4},{7,3},{8,10},{9,13},{10,... | collective-permute-start | bytes 356360 | tf_op jit(solution)/shard_map/ppermute | solution.py:195
  10.0 2.8 %attention.4.refs_0_ = bf16[8,2,128,512]{3,2,1,0:T(8,128)(2,1)} custom-call(s32[8]{0:T(128)} %length_ref.3, bf16[8,2,576,128]{3,2,1,0:T(8,128)(2,1)S(1)} %bitcast.6, bf16[8,576,256]{2,1,0:T(8,128)(2,1)S(1)} %bitcast.10, bf16[8,2,576]{2,1,0:T(2,128)(2,1)S(1)} %copy-done.2), custom_call_target="tpu_custom_call" | custom-call | flops 1048576 | bytes 65536 | tf_op jit(solution)/shard_map/attention/pallas_call | solution.py:75
  13.6 1.6 %collective-permute-start.4 = (bf16[16,3712]{1,0:T(8,128)(2,1)S(1)}, bf16[16,3712]{1,0:T(8,128)(2,1)S(1)}, u32[]{:S(2)}, u32[]{:S(2)}) collective-permute-start(bf16[16,3712]{1,0:T(8,128)(2,1)S(1)} %constant_dynamic-update-slice_fusion), channel_id=1, source_target_pairs={{0,4},{1,3},{2,6},{3,1},{4,0},{5,7},{6,2},{7,5},{8,12},{9,11},{10,... | collective-permute-start | bytes 356360 | tf_op jit(solution)/shard_map/ppermute | solution.py:195
  15.2 1.4 %collective-permute-start.5 = (bf16[16,3712]{1,0:T(8,128)(2,1)S(1)}, bf16[16,3712]{1,0:T(8,128)(2,1)S(1)}, u32[]{:S(2)}, u32[]{:S(2)}) collective-permute-start(bf16[16,3712]{1,0:T(8,128)(2,1)S(1)} %constant_dynamic-update-slice_fusion.2), channel_id=1, source_target_pairs={{0,2},{1,5},{2,0},{3,7},{4,6},{5,1},{6,4},{7,3},{8,10},{9,13},{10,... | collective-permute-start | bytes 356360 | tf_op jit(solution)/shard_map/ppermute | solution.py:195
  17.3 3.3 %experts.2 = (f32[64,3584]{1,0:T(8,128)S(1)}, bf16[64,3584]{1,0:T(8,128)(2,1)S(1)}) custom-call(bf16[32,3712]{1,0:T(8,128)(2,1)S(1)} %pad_maximum_fusion.refs_0_, bf16[32,3712]{1,0:T(8,128)(2,1)S(1)} %pad_maximum_fusion.1.refs_1_, bf16[32,3712]{1,0:T(8,128)(2,1)S(1)} %collective-permute-done.8.refs_2_, bf16[32,3712]{1,0:T(8,128)(2,1)S(1)} %collective-permute-done.9.refs_3_, ...), custom_call_target="tpu_custom_call" | custom-call | flops 1048576 | bytes 65536 | tf_op jit(solution)/shard_map/experts/pallas_call | solution.py:163
  20.6 0.8 %collective-permute-done.6 = bf16[16,3712]{1,0:T(8,128)(2,1)S(1)} collective-permute-done((bf16[16,3712]{1,0:T(8,128)(2,1)S(1)}, bf16[16,3712]{1,0:T(8,128)(2,1)S(1)}, u32[]{:S(2)}, u32[]{:S(2)}) %collective-permute-start.6) | collective-permute-done | bytes 118816 | tf_op jit(solution)/shard_map/ppermute | solution.py:195
  21.4 1.3 %collective-permute-start.10 = (bf16[16,3712]{1,0:T(8,128)(2,1)S(1)}, bf16[16,3712]{1,0:T(8,128)(2,1)S(1)}, u32[]{:S(2)}, u32[]{:S(2)}) collective-permute-start(bf16[16,3712]{1,0:T(8,128)(2,1)S(1)} %collective-permute-done.4), channel_id=1, source_target_pairs={{0,2},{1,5},{2,0},{3,7},{4,6},{5,1},{6,4},{7,3},{8,10},{9,13},{10,... | collective-permute-start | bytes 356360 | tf_op jit(solution)/shard_map/ppermute | solution.py:195
  23.3 2.7 %attention.5.refs_0_ = bf16[8,2,128,512]{3,2,1,0:T(8,128)(2,1)} custom-call(s32[8]{0:T(128)} %length_ref.3, bf16[8,2,576,128]{3,2,1,0:T(8,128)(2,1)S(1)} %bitcast.7, bf16[8,576,256]{2,1,0:T(8,128)(2,1)S(1)} %bitcast.11, bf16[8,2,576]{2,1,0:T(2,128)(2,1)S(1)} %copy-done.2, bf16[8,2,128,512]{3,2,1,0:T(8,128)(2,1)} %attention.4.refs_0_), custom_call_target="tpu_custom_call", output_to_operand_aliasing={{}: (4, {})} | custom-call | flops 1048576 | bytes 65536 | tf_op jit(solution)/shard_map/attention/pallas_call | solution.py:75
  26.7 1.1 %collective-permute-done.14.refs_5_ = bf16[16,3712]{1,0:T(8,128)(2,1)S(1)} collective-permute-done((bf16[16,3712]{1,0:T(8,128)(2,1)S(1)}, bf16[16,3712]{1,0:T(8,128)(2,1)S(1)}, u32[]{:S(2)}, u32[]{:S(2)}) %collective-permute-start.14) | collective-permute-done | bytes 118816 | tf_op jit(solution)/shard_map/ppermute | solution.py:199
  27.7 3.3 %experts.3 = (f32[48,3584]{1,0:T(8,128)S(1)}, f32[16,3584]{1,0:T(8,128)S(1)}, bf16[48,3584]{1,0:T(8,128)(2,1)S(1)}, bf16[16,3584]{1,0:T(8,128)(2,1)S(1)}) custom-call(bf16[32,3712]{1,0:T(8,128)(2,1)S(1)} %constant_dynamic-update-slice_fusion.4.refs_0_, bf16[16,3712]{1,0:T(8,128)(2,1)S(1)} %collective-permute-done.5.refs_1_, ...), custom_call_target="tpu_custom_call" | custom-call | flops 1048576 | bytes 65536 | tf_op jit(solution)/shard_map/experts/pallas_call | solution.py:163
  31.6 0.8 %collective-permute-done.17 = bf16[16,3584]{1,0:T(8,128)(2,1)S(1)} collective-permute-done((bf16[16,3584]{1,0:T(8,128)(2,1)S(1)}, bf16[16,3584]{1,0:T(8,128)(2,1)S(1)}, u32[]{:S(2)}, u32[]{:S(2)}) %collective-permute-start.17) | collective-permute-done | bytes 114720 | tf_op jit(solution)/shard_map/ppermute | solution.py:199
  32.4 1.3 %collective-permute-start.18 = (bf16[16,3584]{1,0:T(8,128)(2,1)S(1)}, bf16[16,3584]{1,0:T(8,128)(2,1)S(1)}, u32[]{:S(2)}, u32[]{:S(2)}) collective-permute-start(bf16[16,3584]{1,0:T(8,128)(2,1)S(1)} %add_convert_fusion.3), channel_id=1, source_target_pairs={{0,2},{1,5},{2,0},{3,7},{4,6},{5,1},{6,4},{7,3},{8,10},{9,13},{10,... | collective-permute-start | bytes 344072 | tf_op jit(solution)/shard_map/ppermute | solution.py:195
  33.9 0.8 %collective-permute-start.16 = (bf16[32,3584]{1,0:T(8,128)(2,1)S(1)}, bf16[32,3584]{1,0:T(8,128)(2,1)S(1)}, u32[]{:S(2)}, u32[]{:S(2)}) collective-permute-start(bf16[32,3584]{1,0:T(8,128)(2,1)S(1)} %slice.47), channel_id=1, source_target_pairs={{0,2},{1,5},{2,0},{3,7},{4,6},{5,1},{6,4},{7,3},{8,10},{9,13},{10,... | collective-permute-start | bytes 688136 | tf_op jit(solution)/shard_map/ppermute | solution.py:195
  34.7 2.2 %attention.6.refs_0_ = bf16[8,2,128,512]{3,2,1,0:T(8,128)(2,1)} custom-call(s32[8]{0:T(128)} %length_ref.3, bf16[8,2,576,128]{3,2,1,0:T(8,128)(2,1)S(1)} %bitcast.8, bf16[8,576,256]{2,1,0:T(8,128)(2,1)S(1)} %bitcast.12, bf16[8,2,576]{2,1,0:T(2,128)(2,1)S(1)} %copy-done.2, bf16[8,2,128,512]{3,2,1,0:T(8,128)(2,1)} %attention.5.refs_0_), custom_call_target="tpu_custom_call", output_to_operand_aliasing={{}: (4, {})} | custom-call | flops 1048576 | bytes 65536 | tf_op jit(solution)/shard_map/attention/pallas_call | solution.py:75
  37.3 0.7 %collective-permute-start.19 = (bf16[16,3584]{1,0:T(8,128)(2,1)S(1)}, bf16[16,3584]{1,0:T(8,128)(2,1)S(1)}, u32[]{:S(2)}, u32[]{:S(2)}) collective-permute-start(bf16[16,3584]{1,0:T(8,128)(2,1)S(1)} %fusion), channel_id=1, source_target_pairs={{0,4},{1,3},{2,6},{3,1},{4,0},{5,7},{6,2},{7,5},{8,12},{9,11},{10,... | collective-permute-start | bytes 344072 | tf_op jit(solution)/shard_map/ppermute | solution.py:195
  38.0 1.4 %collective-permute-start.21 = (bf16[16,3584]{1,0:T(8,128)(2,1)S(1)}, bf16[16,3584]{1,0:T(8,128)(2,1)S(1)}, u32[]{:S(2)}, u32[]{:S(2)}) collective-permute-start(bf16[16,3584]{1,0:T(8,128)(2,1)S(1)} %slice.48), channel_id=1, source_target_pairs={{0,2},{1,5},{2,0},{3,7},{4,6},{5,1},{6,4},{7,3},{8,10},{9,13},{10,... | collective-permute-start | bytes 344072 | tf_op jit(solution)/shard_map/ppermute | solution.py:195
  39.5 3.3 %collective-permute-done.19 = bf16[16,3584]{1,0:T(8,128)(2,1)S(1)} collective-permute-done((bf16[16,3584]{1,0:T(8,128)(2,1)S(1)}, bf16[16,3584]{1,0:T(8,128)(2,1)S(1)}, u32[]{:S(2)}, u32[]{:S(2)}) %collective-permute-start.19) | collective-permute-done | bytes 114720 | tf_op jit(solution)/shard_map/ppermute | solution.py:195
  42.8 2.7 %collective-permute-start.20 = (bf16[16,3584]{1,0:T(8,128)(2,1)S(1)}, bf16[16,3584]{1,0:T(8,128)(2,1)S(1)}, u32[]{:S(2)}, u32[]{:S(2)}) collective-permute-start(bf16[16,3584]{1,0:T(8,128)(2,1)S(1)} %add_convert_fusion.2), channel_id=1, source_target_pairs={{0,8},{1,9},{2,10},{3,11},{4,12},{5,13},{6,14},{7,15},{8,0},{9,1},... | collective-permute-start | bytes 344072 | tf_op jit(solution)/shard_map/ppermute | solution.py:195
  45.5 0.9 %collective-permute-start.22 = (bf16[16,3584]{1,0:T(8,128)(2,1)S(1)}, bf16[16,3584]{1,0:T(8,128)(2,1)S(1)}, u32[]{:S(2)}, u32[]{:S(2)}) collective-permute-start(bf16[16,3584]{1,0:T(8,128)(2,1)S(1)} %add_convert_fusion.1), channel_id=1, source_target_pairs={{0,4},{1,3},{2,6},{3,1},{4,0},{5,7},{6,2},{7,5},{8,12},{9,11},{10,... | collective-permute-start | bytes 344072 | tf_op jit(solution)/shard_map/ppermute | solution.py:195
  46.4 3.4 %attention.7 = bf16[8,2,128,512]{3,2,1,0:T(8,128)(2,1)} custom-call(s32[8]{0:T(128)} %length_ref.3, bf16[8,2,576,128]{3,2,1,0:T(8,128)(2,1)S(1)} %bitcast.9, bf16[8,576,256]{2,1,0:T(8,128)(2,1)S(1)} %bitcast.13, bf16[8,2,576]{2,1,0:T(2,128)(2,1)S(1)} %copy-done.2, bf16[8,2,128,512]{3,2,1,0:T(8,128)(2,1)} %attention.6.refs_0_), custom_call_target="tpu_custom_call", output_to_operand_aliasing={{}: (4, {})} | custom-call | flops 1048576 | bytes 65536 | tf_op jit(solution)/shard_map/attention/pallas_call | solution.py:75
  49.9 1.2 %collective-permute-done.22 = bf16[16,3584]{1,0:T(8,128)(2,1)S(1)} collective-permute-done((bf16[16,3584]{1,0:T(8,128)(2,1)S(1)}, bf16[16,3584]{1,0:T(8,128)(2,1)S(1)}, u32[]{:S(2)}, u32[]{:S(2)}) %collective-permute-start.22) | collective-permute-done | bytes 114720 | tf_op jit(solution)/shard_map/ppermute | solution.py:195
  (67 shorter events, 5.2 us)
Async XLA Ops:
  0.6 12.2 %collective-permute-start = (bf16[16,3584]{1,0:T(8,128)(2,1)}, bf16[16,3584]{1,0:T(8,128)(2,1)S(1)}, u32[]{:S(2)}, u32[]{:S(2)}) collective-permute-start(bf16[16,3584]{1,0:T(8,128)(2,1)} %rows_ref.1), channel_id=1, source_target_pairs={{0,8},{1,9},{2,10},{3,11},{4,12},{5,13},{6,14},{7,15},{8,0},{9,1},... | collective-permute-start | bytes 344072 | tf_op jit(solution)/shard_map/ppermute | solution.py:195
  4.7 8.1 %collective-permute-start.2 = (bf16[16,3584]{1,0:T(8,128)(2,1)}, bf16[16,3584]{1,0:T(8,128)(2,1)S(1)}, u32[]{:S(2)}, u32[]{:S(2)}) collective-permute-start(bf16[16,3584]{1,0:T(8,128)(2,1)} %rows_ref.1), channel_id=1, source_target_pairs={{0,4},{1,3},{2,6},{3,1},{4,0},{5,7},{6,2},{7,5},{8,12},{9,11},{10,... | collective-permute-start | bytes 344072 | tf_op jit(solution)/shard_map/ppermute | solution.py:195
  6.3 10.9 %slice-start.4 = ((s8[7340032]{0:T(1024)(128)(4,1)}), s8[4194304]{0:T(1024)(128)(4,1)S(1)}, s32[]{:S(2)}) async-start(s8[7340032]{0:T(1024)(128)(4,1)} %bitcast.18), calls=%async_computation.4 | async-start | bytes 8388608
  7.6 5.1 %collective-permute-start.1 = (bf16[16,128]{1,0:T(8,128)(2,1)S(1)}, bf16[16,128]{1,0:T(8,128)(2,1)S(1)}, u32[]{:S(2)}, u32[]{:S(2)}) collective-permute-start(bf16[16,128]{1,0:T(8,128)(2,1)S(1)} %get-tuple-element.61), channel_id=1, source_target_pairs={{0,8},{1,9},{2,10},{3,11},{4,12},{5,13},{6,14},{7,15},{8,0},{9,1},... | collective-permute-start | bytes 12296 | tf_op jit(solution)/shard_map/ppermute | solution.py:195
  8.0 4.8 %collective-permute-start.3 = (bf16[16,128]{1,0:T(8,128)(2,1)S(1)}, bf16[16,128]{1,0:T(8,128)(2,1)S(1)}, u32[]{:S(2)}, u32[]{:S(2)}) collective-permute-start(bf16[16,128]{1,0:T(8,128)(2,1)S(1)} %get-tuple-element.61), channel_id=1, source_target_pairs={{0,4},{1,3},{2,6},{3,1},{4,0},{5,7},{6,2},{7,5},{8,12},{9,11},{10,... | collective-permute-start | bytes 12296 | tf_op jit(solution)/shard_map/ppermute | solution.py:195
  8.2 4.8 %collective-permute-start.7 = (bf16[16,3712]{1,0:T(8,128)(2,1)S(1)}, bf16[16,3712]{1,0:T(8,128)(2,1)S(1)}, u32[]{:S(2)}, u32[]{:S(2)}) collective-permute-start(bf16[16,3712]{1,0:T(8,128)(2,1)S(1)} %get-tuple-element.71), channel_id=1, source_target_pairs={{0,2},{1,5},{2,0},{3,7},{4,6},{5,1},{6,4},{7,3},{8,10},{9,13},{10,... | collective-permute-start | bytes 356360 | tf_op jit(solution)/shard_map/ppermute | solution.py:195
  12.9 4.3 %collective-permute-start.8 = (bf16[32,3712]{1,0:T(8,128)(2,1)S(1)}, bf16[32,3712]{1,0:T(8,128)(2,1)S(1)}, u32[]{:S(2)}, u32[]{:S(2)}) collective-permute-start(bf16[32,3712]{1,0:T(8,128)(2,1)S(1)} %pad_maximum_fusion.refs_0_), channel_id=1, source_target_pairs={{0,1},{1,0},{2,3},{3,2},{4,5},{5,4},{6,7},{7,6},{8,9},{9,8},{10,11... | collective-permute-start | bytes 712712 | tf_op jit(solution)/shard_map/ppermute | solution.py:199
  13.0 4.1 %collective-permute-start.9 = (bf16[32,3712]{1,0:T(8,128)(2,1)S(1)}, bf16[32,3712]{1,0:T(8,128)(2,1)S(1)}, u32[]{:S(2)}, u32[]{:S(2)}) collective-permute-start(bf16[32,3712]{1,0:T(8,128)(2,1)S(1)} %pad_maximum_fusion.1.refs_1_), channel_id=1, source_target_pairs={{0,1},{1,0},{2,3},{3,2},{4,5},{5,4},{6,7},{7,6},{8,9},{9,8},{10,11... | collective-permute-start | bytes 712712 | tf_op jit(solution)/shard_map/ppermute | solution.py:199
  13.6 7.0 %collective-permute-start.4 = (bf16[16,3712]{1,0:T(8,128)(2,1)S(1)}, bf16[16,3712]{1,0:T(8,128)(2,1)S(1)}, u32[]{:S(2)}, u32[]{:S(2)}) collective-permute-start(bf16[16,3712]{1,0:T(8,128)(2,1)S(1)} %constant_dynamic-update-slice_fusion), channel_id=1, source_target_pairs={{0,4},{1,3},{2,6},{3,1},{4,0},{5,7},{6,2},{7,5},{8,12},{9,11},{10,... | collective-permute-start | bytes 356360 | tf_op jit(solution)/shard_map/ppermute | solution.py:195
  15.2 5.4 %collective-permute-start.5 = (bf16[16,3712]{1,0:T(8,128)(2,1)S(1)}, bf16[16,3712]{1,0:T(8,128)(2,1)S(1)}, u32[]{:S(2)}, u32[]{:S(2)}) collective-permute-start(bf16[16,3712]{1,0:T(8,128)(2,1)S(1)} %constant_dynamic-update-slice_fusion.2), channel_id=1, source_target_pairs={{0,2},{1,5},{2,0},{3,7},{4,6},{5,1},{6,4},{7,3},{8,10},{9,13},{10,... | collective-permute-start | bytes 356360 | tf_op jit(solution)/shard_map/ppermute | solution.py:195
  16.5 4.8 %collective-permute-start.6 = (bf16[16,3712]{1,0:T(8,128)(2,1)S(1)}, bf16[16,3712]{1,0:T(8,128)(2,1)S(1)}, u32[]{:S(2)}, u32[]{:S(2)}) collective-permute-start(bf16[16,3712]{1,0:T(8,128)(2,1)S(1)} %constant_dynamic-update-slice_fusion), channel_id=1, source_target_pairs={{0,2},{1,5},{2,0},{3,7},{4,6},{5,1},{6,4},{7,3},{8,10},{9,13},{10,... | collective-permute-start | bytes 356360 | tf_op jit(solution)/shard_map/ppermute | solution.py:195
  21.4 4.8 %collective-permute-start.10 = (bf16[16,3712]{1,0:T(8,128)(2,1)S(1)}, bf16[16,3712]{1,0:T(8,128)(2,1)S(1)}, u32[]{:S(2)}, u32[]{:S(2)}) collective-permute-start(bf16[16,3712]{1,0:T(8,128)(2,1)S(1)} %collective-permute-done.4), channel_id=1, source_target_pairs={{0,2},{1,5},{2,0},{3,7},{4,6},{5,1},{6,4},{7,3},{8,10},{9,13},{10,... | collective-permute-start | bytes 356360 | tf_op jit(solution)/shard_map/ppermute | solution.py:195
  22.6 3.6 %collective-permute-start.13 = (bf16[64,3584]{1,0:T(8,128)(2,1)S(1)}, bf16[64,3584]{1,0:T(8,128)(2,1)S(1)}, u32[]{:S(2)}, u32[]{:S(2)}) collective-permute-start(bf16[64,3584]{1,0:T(8,128)(2,1)S(1)} %get-tuple-element.88), channel_id=1, source_target_pairs={{0,1},{1,0},{2,3},{3,2},{4,5},{5,4},{6,7},{7,6},{8,9},{9,8},{10,11... | collective-permute-start | bytes 1376264 | tf_op jit(solution)/shard_map/ppermute | solution.py:199
  22.7 3.6 %collective-permute-start.11 = (bf16[32,3712]{1,0:T(8,128)(2,1)S(1)}, bf16[32,3712]{1,0:T(8,128)(2,1)S(1)}, u32[]{:S(2)}, u32[]{:S(2)}) collective-permute-start(bf16[32,3712]{1,0:T(8,128)(2,1)S(1)} %constant_dynamic-update-slice_fusion.4.refs_0_), channel_id=1, source_target_pairs={{0,1},{1,0},{2,3},{3,2},{4,5},{5,4},{6,7},{7,6},{8,9},{9,8},{10,11... | collective-permute-start | bytes 712712 | tf_op jit(solution)/shard_map/ppermute | solution.py:199
  23.2 3.1 %collective-permute-start.12 = (bf16[16,3712]{1,0:T(8,128)(2,1)S(1)}, bf16[16,3712]{1,0:T(8,128)(2,1)S(1)}, u32[]{:S(2)}, u32[]{:S(2)}) collective-permute-start(bf16[16,3712]{1,0:T(8,128)(2,1)S(1)} %collective-permute-done.5.refs_1_), channel_id=1, source_target_pairs={{0,1},{1,0},{2,3},{3,2},{4,5},{5,4},{6,7},{7,6},{8,9},{9,8},{10,11... | collective-permute-start | bytes 356360 | tf_op jit(solution)/shard_map/ppermute | solution.py:199
  26.3 1.4 %collective-permute-start.14 = (bf16[16,3712]{1,0:T(8,128)(2,1)S(1)}, bf16[16,3712]{1,0:T(8,128)(2,1)S(1)}, u32[]{:S(2)}, u32[]{:S(2)}) collective-permute-start(bf16[16,3712]{1,0:T(8,128)(2,1)S(1)} %collective-permute-done.10.refs_2_), channel_id=1, source_target_pairs={{0,1},{1,0},{2,3},{3,2},{4,5},{5,4},{6,7},{7,6},{8,9},{9,8},{10,11... | collective-permute-start | bytes 356360 | tf_op jit(solution)/shard_map/ppermute | solution.py:199
  31.0 1.4 %collective-permute-start.17 = (bf16[16,3584]{1,0:T(8,128)(2,1)S(1)}, bf16[16,3584]{1,0:T(8,128)(2,1)S(1)}, u32[]{:S(2)}, u32[]{:S(2)}) collective-permute-start(bf16[16,3584]{1,0:T(8,128)(2,1)S(1)} %get-tuple-element.96), channel_id=1, source_target_pairs={{0,1},{1,0},{2,3},{3,2},{4,5},{5,4},{6,7},{7,6},{8,9},{9,8},{10,11... | collective-permute-start | bytes 344072 | tf_op jit(solution)/shard_map/ppermute | solution.py:199
  31.3 2.4 %collective-permute-start.15 = (bf16[48,3584]{1,0:T(8,128)(2,1)S(1)}, bf16[48,3584]{1,0:T(8,128)(2,1)S(1)}, u32[]{:S(2)}, u32[]{:S(2)}) collective-permute-start(bf16[48,3584]{1,0:T(8,128)(2,1)S(1)} %get-tuple-element.94), channel_id=1, source_target_pairs={{0,1},{1,0},{2,3},{3,2},{4,5},{5,4},{6,7},{7,6},{8,9},{9,8},{10,11... | collective-permute-start | bytes 1032200 | tf_op jit(solution)/shard_map/ppermute | solution.py:199
  32.4 4.9 %collective-permute-start.18 = (bf16[16,3584]{1,0:T(8,128)(2,1)S(1)}, bf16[16,3584]{1,0:T(8,128)(2,1)S(1)}, u32[]{:S(2)}, u32[]{:S(2)}) collective-permute-start(bf16[16,3584]{1,0:T(8,128)(2,1)S(1)} %add_convert_fusion.3), channel_id=1, source_target_pairs={{0,2},{1,5},{2,0},{3,7},{4,6},{5,1},{6,4},{7,3},{8,10},{9,13},{10,... | collective-permute-start | bytes 344072 | tf_op jit(solution)/shard_map/ppermute | solution.py:195
  33.9 8.9 %collective-permute-start.16 = (bf16[32,3584]{1,0:T(8,128)(2,1)S(1)}, bf16[32,3584]{1,0:T(8,128)(2,1)S(1)}, u32[]{:S(2)}, u32[]{:S(2)}) collective-permute-start(bf16[32,3584]{1,0:T(8,128)(2,1)S(1)} %slice.47), channel_id=1, source_target_pairs={{0,2},{1,5},{2,0},{3,7},{4,6},{5,1},{6,4},{7,3},{8,10},{9,13},{10,... | collective-permute-start | bytes 688136 | tf_op jit(solution)/shard_map/ppermute | solution.py:195
  37.3 5.5 %collective-permute-start.19 = (bf16[16,3584]{1,0:T(8,128)(2,1)S(1)}, bf16[16,3584]{1,0:T(8,128)(2,1)S(1)}, u32[]{:S(2)}, u32[]{:S(2)}) collective-permute-start(bf16[16,3584]{1,0:T(8,128)(2,1)S(1)} %fusion), channel_id=1, source_target_pairs={{0,4},{1,3},{2,6},{3,1},{4,0},{5,7},{6,2},{7,5},{8,12},{9,11},{10,... | collective-permute-start | bytes 344072 | tf_op jit(solution)/shard_map/ppermute | solution.py:195
  38.0 11.9 %collective-permute-start.21 = (bf16[16,3584]{1,0:T(8,128)(2,1)S(1)}, bf16[16,3584]{1,0:T(8,128)(2,1)S(1)}, u32[]{:S(2)}, u32[]{:S(2)}) collective-permute-start(bf16[16,3584]{1,0:T(8,128)(2,1)S(1)} %slice.48), channel_id=1, source_target_pairs={{0,2},{1,5},{2,0},{3,7},{4,6},{5,1},{6,4},{7,3},{8,10},{9,13},{10,... | collective-permute-start | bytes 344072 | tf_op jit(solution)/shard_map/ppermute | solution.py:195
  42.8 7.1 %collective-permute-start.20 = (bf16[16,3584]{1,0:T(8,128)(2,1)S(1)}, bf16[16,3584]{1,0:T(8,128)(2,1)S(1)}, u32[]{:S(2)}, u32[]{:S(2)}) collective-permute-start(bf16[16,3584]{1,0:T(8,128)(2,1)S(1)} %add_convert_fusion.2), channel_id=1, source_target_pairs={{0,8},{1,9},{2,10},{3,11},{4,12},{5,13},{6,14},{7,15},{8,0},{9,1},... | collective-permute-start | bytes 344072 | tf_op jit(solution)/shard_map/ppermute | solution.py:195
  45.5 5.5 %collective-permute-start.22 = (bf16[16,3584]{1,0:T(8,128)(2,1)S(1)}, bf16[16,3584]{1,0:T(8,128)(2,1)S(1)}, u32[]{:S(2)}, u32[]{:S(2)}) collective-permute-start(bf16[16,3584]{1,0:T(8,128)(2,1)S(1)} %add_convert_fusion.1), channel_id=1, source_target_pairs={{0,4},{1,3},{2,6},{3,1},{4,0},{5,7},{6,2},{7,5},{8,12},{9,11},{10,... | collective-permute-start | bytes 344072 | tf_op jit(solution)/shard_map/ppermute | solution.py:195
  (8 other events, 65.3 us)

commit v12 on v10

--- a/solution.py
+++ b/solution.py
@@ -260,7 +260,7 @@
     n = own.shape[0]
     own, inputs = barrier((own, inputs))
     c = hop_c(own)
-    b, a = attend(2, (hop_b(own), a))
+    b, a = attend(3, (hop_b(own), a))
     ab, bc, ac = hop_b(a), hop_c(b), hop_c(a)
     near_rows = [jnp.concatenate(x, axis=0) for x in ((own, a), (b, c))]
     near_rows += [swap(x) for x in near_rows]
@@ -282,10 +282,10 @@
     rest = far[n:].astype(BF16)
     got_ab = hop_c(sent)
     got = hop_c(rest)
-    rest, inputs = barrier((rest, inputs))
-    got_ab = attend(1, got_ab)
     sent = add(far[:n], got_ab).astype(BF16)
     got_a = hop_b(sent)
+    sent, inputs = barrier((sent, inputs))
+    got_a = attend(1, got_a)
     got, got_a = barrier((got, got_a))
     sent = add(near[n : 2 * n], got[:n], got_a).astype(BF16)
     sent, got = barrier((sent, got))

time: 50.4 us -> 50.7 us (level)
  starting transfers between devices: 20.1 us -> 21.2 us
  waiting for transfers between devices: 9.21 us -> 8.3 us
    ppermute x14, waiting for transfers between devices: 7.06 us -> 6.31 us  [hop(): return lax.ppermute(x, ('ep', 'sub'), pairs)]
    ppermute x14, starting transfers between devices: 18.2 us -> 18.9 us  [hop(): return lax.ppermute(x, ('ep', 'sub'), pairs)]
where the time goes in v12:
time: 50.7 us; the launch traced here: 50.5 us
  starting transfers between devices  21.2 us (42%)
  Pallas kernels  18.9 us (37%)
  waiting for transfers between devices  8.3 us (16%)
  other arithmetic  1.02 us (2%)
  between operations  0.93 us (2%)
    ppermute x14, starting transfers between devices, hop(): return lax.ppermute(x, ('ep', 'sub'), pairs)  18.9 us
    pallas_call x4, Pallas kernels, attention(): pl.pallas_call(functools.partial(attention_kernel, first=first, count=cou...  11.1 us
    pallas_call x2, Pallas kernels, experts(): pl.pallas_call(functools.partial(experts_kernel, parts=len(parts), groups...  6.48 us
    ppermute x14, waiting for transfers between devices, hop(): return lax.ppermute(x, ('ep', 'sub'), pairs)  6.31 us
    ppermute x8, starting transfers between devices, swap(): return lax.ppermute(x, 'sub', [(0, 1), (1, 0)])  2.35 us
    ppermute x8, waiting for transfers between devices, swap(): return lax.ppermute(x, 'sub', [(0, 1), (1, 0)])  1.99 us
    pallas_call x1, Pallas kernels, route(): pl.pallas_call(functools.partial(route_kernel, experts=placement.shape[0]...  1.26 us
  transfers between devices with their start and end apart: 22, of which 10 were waited for; matrix products, arithmetic and copies ran while one was open for 1% of the time, Pallas kernels for 31%

profile of v12, /device:TPU:0, one launch (start us, length us, event | category | flops | bytes accessed | tf_op | source)
XLA Modules:
  0.0 50.5 jit_solution(12913362341264445289)
XLA Ops:
  0.6 4.1 %collective-permute-start.1 = (bf16[16,3584]{1,0:T(8,128)(2,1)}, bf16[16,3584]{1,0:T(8,128)(2,1)S(1)}, u32[]{:S(2)}, u32[]{:S(2)}) collective-permute-start(bf16[16,3584]{1,0:T(8,128)(2,1)} %rows_ref.1), channel_id=1, source_target_pairs={{0,8},{1,9},{2,10},{3,11},{4,12},{5,13},{6,14},{7,15},{8,0},{9,1},... | collective-permute-start | bytes 344072 | tf_op jit(solution)/shard_map/ppermute | solution.py:195
  4.8 1.3 %route.1 = (bf16[16,3712]{1,0:T(8,128)(2,1)S(1)}, bf16[16,128]{1,0:T(8,128)(2,1)S(1)}) custom-call(s32[2,14]{1,0:T(2,128)} %bitcast.22, bf16[16,3584]{1,0:T(8,128)(2,1)} %rows_ref.1, f32[8,16]{1,0:T(8,128)} %bitcast.20, s32[8,16]{1,0:T(8,128)} %bitcast.21), custom_call_target="tpu_custom_call" | custom-call | flops 17179869184 | bytes 33554432 | tf_op jit(solution)/shard_map/route/pallas_call | solution.py:119
  6.1 1.6 %collective-permute-start = (bf16[16,3712]{1,0:T(8,128)(2,1)S(1)}, bf16[16,3712]{1,0:T(8,128)(2,1)S(1)}, u32[]{:S(2)}, u32[]{:S(2)}) collective-permute-start(bf16[16,3712]{1,0:T(8,128)(2,1)S(1)} %get-tuple-element.60), channel_id=1, source_target_pairs={{0,4},{1,3},{2,6},{3,1},{4,0},{5,7},{6,2},{7,5},{8,12},{9,11},{10,... | collective-permute-start | bytes 356360 | tf_op jit(solution)/shard_map/ppermute | solution.py:195
  7.6 1.5 %collective-permute-start.6 = (bf16[16,3712]{1,0:T(8,128)(2,1)S(1)}, bf16[16,3712]{1,0:T(8,128)(2,1)S(1)}, u32[]{:S(2)}, u32[]{:S(2)}) collective-permute-start(bf16[16,3712]{1,0:T(8,128)(2,1)S(1)} %get-tuple-element.60), channel_id=1, source_target_pairs={{0,2},{1,5},{2,0},{3,7},{4,6},{5,1},{6,4},{7,3},{8,10},{9,13},{10,... | collective-permute-start | bytes 356360 | tf_op jit(solution)/shard_map/ppermute | solution.py:195
  9.5 3.5 %attention.4.refs_0_ = bf16[8,2,128,512]{3,2,1,0:T(8,128)(2,1)} custom-call(s32[8]{0:T(128)} %length_ref.3, bf16[8,2,576,128]{3,2,1,0:T(8,128)(2,1)S(1)} %bitcast.6, bf16[8,576,256]{2,1,0:T(8,128)(2,1)S(1)} %bitcast.10, bf16[8,2,576]{2,1,0:T(2,128)(2,1)S(1)} %copy-done.2), custom_call_target="tpu_custom_call" | custom-call | flops 1048576 | bytes 65536 | tf_op jit(solution)/shard_map/attention/pallas_call | solution.py:75
  15.4 1.5 %collective-permute-start.4 = (bf16[16,3712]{1,0:T(8,128)(2,1)S(1)}, bf16[16,3712]{1,0:T(8,128)(2,1)S(1)}, u32[]{:S(2)}, u32[]{:S(2)}) collective-permute-start(bf16[16,3712]{1,0:T(8,128)(2,1)S(1)} %collective-permute-done), channel_id=1, source_target_pairs={{0,2},{1,5},{2,0},{3,7},{4,6},{5,1},{6,4},{7,3},{8,10},{9,13},{10,... | collective-permute-start | bytes 356360 | tf_op jit(solution)/shard_map/ppermute | solution.py:195
  17.0 3.2 %experts.2 = (f32[64,3584]{1,0:T(8,128)S(1)}, bf16[64,3584]{1,0:T(8,128)(2,1)S(1)}) custom-call(bf16[32,3712]{1,0:T(8,128)(2,1)S(1)} %constant_dynamic-update-slice_fusion.refs_0_, bf16[32,3712]{1,0:T(8,128)(2,1)S(1)} %constant_dynamic-update-slice_fusion.2.refs_1_, bf16[32,3712]{1,0:T(8,128)(2,1)S(1)} %collective-permute-done.7.refs_2_, ...), custom_call_target="tpu_custom_call" | custom-call | flops 1048576 | bytes 65536 | tf_op jit(solution)/shard_map/experts/pallas_call | solution.py:163
  21.1 1.0 %collective-permute-start.9 = (bf16[16,3712]{1,0:T(8,128)(2,1)S(1)}, bf16[16,3712]{1,0:T(8,128)(2,1)S(1)}, u32[]{:S(2)}, u32[]{:S(2)}) collective-permute-start(bf16[16,3712]{1,0:T(8,128)(2,1)S(1)} %collective-permute-done.3), channel_id=1, source_target_pairs={{0,2},{1,5},{2,0},{3,7},{4,6},{5,1},{6,4},{7,3},{8,10},{9,13},{10,... | collective-permute-start | bytes 356360 | tf_op jit(solution)/shard_map/ppermute | solution.py:195
  22.1 0.7 %collective-permute-start.10 = (bf16[32,3712]{1,0:T(8,128)(2,1)S(1)}, bf16[32,3712]{1,0:T(8,128)(2,1)S(1)}, u32[]{:S(2)}, u32[]{:S(2)}) collective-permute-start(bf16[32,3712]{1,0:T(8,128)(2,1)S(1)} %constant_dynamic-update-slice_fusion.4.refs_0_), channel_id=1, source_target_pairs={{0,1},{1,0},{2,3},{3,2},{4,5},{5,4},{6,7},{7,6},{8,9},{9,8},{10,11... | collective-permute-start | bytes 712712 | tf_op jit(solution)/shard_map/ppermute | solution.py:199
  22.9 2.7 %attention.5.refs_0_ = bf16[8,2,128,512]{3,2,1,0:T(8,128)(2,1)} custom-call(s32[8]{0:T(128)} %length_ref.3, bf16[8,2,576,128]{3,2,1,0:T(8,128)(2,1)S(1)} %bitcast.7, bf16[8,576,256]{2,1,0:T(8,128)(2,1)S(1)} %bitcast.11, bf16[8,2,576]{2,1,0:T(2,128)(2,1)S(1)} %copy-done.2, bf16[8,2,128,512]{3,2,1,0:T(8,128)(2,1)} %attention.4.refs_0_), custom_call_target="tpu_custom_call", output_to_operand_aliasing={{}: (4, {})} | custom-call | flops 1048576 | bytes 65536 | tf_op jit(solution)/shard_map/attention/pallas_call | solution.py:75
  26.3 1.2 %collective-permute-done.13.refs_5_ = bf16[16,3712]{1,0:T(8,128)(2,1)S(1)} collective-permute-done((bf16[16,3712]{1,0:T(8,128)(2,1)S(1)}, bf16[16,3712]{1,0:T(8,128)(2,1)S(1)}, u32[]{:S(2)}, u32[]{:S(2)}) %collective-permute-start.13) | collective-permute-done | bytes 118816 | tf_op jit(solution)/shard_map/ppermute | solution.py:199
  27.4 3.3 %experts.3 = (f32[48,3584]{1,0:T(8,128)S(1)}, f32[16,3584]{1,0:T(8,128)S(1)}, bf16[48,3584]{1,0:T(8,128)(2,1)S(1)}, bf16[16,3584]{1,0:T(8,128)(2,1)S(1)}) custom-call(bf16[32,3712]{1,0:T(8,128)(2,1)S(1)} %constant_dynamic-update-slice_fusion.4.refs_0_, bf16[16,3712]{1,0:T(8,128)(2,1)S(1)} %collective-permute-done.4.refs_1_, ...), custom_call_target="tpu_custom_call" | custom-call | flops 1048576 | bytes 65536 | tf_op jit(solution)/shard_map/experts/pallas_call | solution.py:163
  31.3 0.8 %collective-permute-done.16 = bf16[16,3584]{1,0:T(8,128)(2,1)S(1)} collective-permute-done((bf16[16,3584]{1,0:T(8,128)(2,1)S(1)}, bf16[16,3584]{1,0:T(8,128)(2,1)S(1)}, u32[]{:S(2)}, u32[]{:S(2)}) %collective-permute-start.16) | collective-permute-done | bytes 114720 | tf_op jit(solution)/shard_map/ppermute | solution.py:199
  32.1 1.1 %collective-permute-start.17 = (bf16[16,3584]{1,0:T(8,128)(2,1)S(1)}, bf16[16,3584]{1,0:T(8,128)(2,1)S(1)}, u32[]{:S(2)}, u32[]{:S(2)}) collective-permute-start(bf16[16,3584]{1,0:T(8,128)(2,1)S(1)} %add_convert_fusion.3), channel_id=1, source_target_pairs={{0,2},{1,5},{2,0},{3,7},{4,6},{5,1},{6,4},{7,3},{8,10},{9,13},{10,... | collective-permute-start | bytes 344072 | tf_op jit(solution)/shard_map/ppermute | solution.py:195
  33.3 1.1 %collective-permute-start.15 = (bf16[32,3584]{1,0:T(8,128)(2,1)S(1)}, bf16[32,3584]{1,0:T(8,128)(2,1)S(1)}, u32[]{:S(2)}, u32[]{:S(2)}) collective-permute-start(bf16[32,3584]{1,0:T(8,128)(2,1)S(1)} %slice.47), channel_id=1, source_target_pairs={{0,2},{1,5},{2,0},{3,7},{4,6},{5,1},{6,4},{7,3},{8,10},{9,13},{10,... | collective-permute-start | bytes 688136 | tf_op jit(solution)/shard_map/ppermute | solution.py:195
  34.4 2.6 %collective-permute-done.17 = bf16[16,3584]{1,0:T(8,128)(2,1)S(1)} collective-permute-done((bf16[16,3584]{1,0:T(8,128)(2,1)S(1)}, bf16[16,3584]{1,0:T(8,128)(2,1)S(1)}, u32[]{:S(2)}, u32[]{:S(2)}) %collective-permute-start.17) | collective-permute-done | bytes 114720 | tf_op jit(solution)/shard_map/ppermute | solution.py:195
  37.0 1.5 %collective-permute-start.18 = (bf16[16,3584]{1,0:T(8,128)(2,1)S(1)}, bf16[16,3584]{1,0:T(8,128)(2,1)S(1)}, u32[]{:S(2)}, u32[]{:S(2)}) collective-permute-start(bf16[16,3584]{1,0:T(8,128)(2,1)S(1)} %fusion), channel_id=1, source_target_pairs={{0,4},{1,3},{2,6},{3,1},{4,0},{5,7},{6,2},{7,5},{8,12},{9,11},{10,... | collective-permute-start | bytes 344072 | tf_op jit(solution)/shard_map/ppermute | solution.py:195
  38.6 0.8 %collective-permute-start.20 = (bf16[16,3584]{1,0:T(8,128)(2,1)S(1)}, bf16[16,3584]{1,0:T(8,128)(2,1)S(1)}, u32[]{:S(2)}, u32[]{:S(2)}) collective-permute-start(bf16[16,3584]{1,0:T(8,128)(2,1)S(1)} %slice.48), channel_id=1, source_target_pairs={{0,2},{1,5},{2,0},{3,7},{4,6},{5,1},{6,4},{7,3},{8,10},{9,13},{10,... | collective-permute-start | bytes 344072 | tf_op jit(solution)/shard_map/ppermute | solution.py:195
  39.4 2.2 %attention.6.refs_0_ = bf16[8,2,128,512]{3,2,1,0:T(8,128)(2,1)} custom-call(s32[8]{0:T(128)} %length_ref.3, bf16[8,2,576,128]{3,2,1,0:T(8,128)(2,1)S(1)} %bitcast.8, bf16[8,576,256]{2,1,0:T(8,128)(2,1)S(1)} %bitcast.12, bf16[8,2,576]{2,1,0:T(2,128)(2,1)S(1)} %copy-done.2, bf16[8,2,128,512]{3,2,1,0:T(8,128)(2,1)} %attention.5.refs_0_), custom_call_target="tpu_custom_call", output_to_operand_aliasing={{}: (4, {})} | custom-call | flops 1048576 | bytes 65536 | tf_op jit(solution)/shard_map/attention/pallas_call | solution.py:75
  42.3 2.1 %collective-permute-start.19 = (bf16[16,3584]{1,0:T(8,128)(2,1)S(1)}, bf16[16,3584]{1,0:T(8,128)(2,1)S(1)}, u32[]{:S(2)}, u32[]{:S(2)}) collective-permute-start(bf16[16,3584]{1,0:T(8,128)(2,1)S(1)} %add_convert_fusion.2), channel_id=1, source_target_pairs={{0,8},{1,9},{2,10},{3,11},{4,12},{5,13},{6,14},{7,15},{8,0},{9,1},... | collective-permute-start | bytes 344072 | tf_op jit(solution)/shard_map/ppermute | solution.py:195
  44.4 1.3 %collective-permute-start.21 = (bf16[16,3584]{1,0:T(8,128)(2,1)S(1)}, bf16[16,3584]{1,0:T(8,128)(2,1)S(1)}, u32[]{:S(2)}, u32[]{:S(2)}) collective-permute-start(bf16[16,3584]{1,0:T(8,128)(2,1)S(1)} %add_convert_fusion.1), channel_id=1, source_target_pairs={{0,4},{1,3},{2,6},{3,1},{4,0},{5,7},{6,2},{7,5},{8,12},{9,11},{10,... | collective-permute-start | bytes 344072 | tf_op jit(solution)/shard_map/ppermute | solution.py:195
  45.7 2.7 %attention.7 = bf16[8,2,128,512]{3,2,1,0:T(8,128)(2,1)} custom-call(s32[8]{0:T(128)} %length_ref.3, bf16[8,2,576,128]{3,2,1,0:T(8,128)(2,1)S(1)} %bitcast.9, bf16[8,576,256]{2,1,0:T(8,128)(2,1)S(1)} %bitcast.13, bf16[8,2,576]{2,1,0:T(2,128)(2,1)S(1)} %copy-done.2, bf16[8,2,128,512]{3,2,1,0:T(8,128)(2,1)} %attention.6.refs_0_), custom_call_target="tpu_custom_call", output_to_operand_aliasing={{}: (4, {})} | custom-call | flops 1048576 | bytes 65536 | tf_op jit(solution)/shard_map/attention/pallas_call | solution.py:75
  48.3 1.1 %collective-permute-done.19 = bf16[16,3584]{1,0:T(8,128)(2,1)S(1)} collective-permute-done((bf16[16,3584]{1,0:T(8,128)(2,1)S(1)}, bf16[16,3584]{1,0:T(8,128)(2,1)S(1)}, u32[]{:S(2)}, u32[]{:S(2)}) %collective-permute-start.19) | collective-permute-done | bytes 114720 | tf_op jit(solution)/shard_map/ppermute | solution.py:195
  49.8 0.7 %add_convert_fusion = bf16[16,3584]{1,0:T(8,128)(2,1)} fusion(bf16[16,3584]{1,0:T(8,128)(2,1)S(1)} %collective-permute-done.19, bf16[16,3584]{1,0:T(8,128)(2,1)S(1)} %collective-permute-done.21, bf16[16,3584]{1,0:T(8,128)(2,1)S(1)} %collective-permute-done.20, f32[64,3584]{1,0:T(8,128)S(1)} %convert_add_fusion), kind=kLoop, calls=%fused_computation.6 | loop fusion | flops 401408 | bytes 688128 | tf_op jit(solution)/shard_map/convert_element_type | solution.py:300
  (64 shorter events, 6.1 us)
Async XLA Ops:
  0.6 13.0 %collective-permute-start.1 = (bf16[16,3584]{1,0:T(8,128)(2,1)}, bf16[16,3584]{1,0:T(8,128)(2,1)S(1)}, u32[]{:S(2)}, u32[]{:S(2)}) collective-permute-start(bf16[16,3584]{1,0:T(8,128)(2,1)} %rows_ref.1), channel_id=1, source_target_pairs={{0,8},{1,9},{2,10},{3,11},{4,12},{5,13},{6,14},{7,15},{8,0},{9,1},... | collective-permute-start | bytes 344072 | tf_op jit(solution)/shard_map/ppermute | solution.py:195
  4.7 12.2 %slice-start.2 = ((s8[7340032]{0:T(1024)(128)(4,1)}), s8[4194304]{0:T(1024)(128)(4,1)S(1)}, s32[]{:S(2)}) async-start(s8[7340032]{0:T(1024)(128)(4,1)} %bitcast.16), calls=%async_computation.2 | async-start | bytes 8388608
  4.7 12.2 %slice-start.4 = ((s8[7340032]{0:T(1024)(128)(4,1)}), s8[4194304]{0:T(1024)(128)(4,1)S(1)}, s32[]{:S(2)}) async-start(s8[7340032]{0:T(1024)(128)(4,1)} %bitcast.18), calls=%async_computation.4 | async-start | bytes 8388608
  6.1 7.6 %collective-permute-start = (bf16[16,3712]{1,0:T(8,128)(2,1)S(1)}, bf16[16,3712]{1,0:T(8,128)(2,1)S(1)}, u32[]{:S(2)}, u32[]{:S(2)}) collective-permute-start(bf16[16,3712]{1,0:T(8,128)(2,1)S(1)} %get-tuple-element.60), channel_id=1, source_target_pairs={{0,4},{1,3},{2,6},{3,1},{4,0},{5,7},{6,2},{7,5},{8,12},{9,11},{10,... | collective-permute-start | bytes 356360 | tf_op jit(solution)/shard_map/ppermute | solution.py:195
  7.6 6.2 %collective-permute-start.6 = (bf16[16,3712]{1,0:T(8,128)(2,1)S(1)}, bf16[16,3712]{1,0:T(8,128)(2,1)S(1)}, u32[]{:S(2)}, u32[]{:S(2)}) collective-permute-start(bf16[16,3712]{1,0:T(8,128)(2,1)S(1)} %get-tuple-element.60), channel_id=1, source_target_pairs={{0,2},{1,5},{2,0},{3,7},{4,6},{5,1},{6,4},{7,3},{8,10},{9,13},{10,... | collective-permute-start | bytes 356360 | tf_op jit(solution)/shard_map/ppermute | solution.py:195
  9.2 4.5 %collective-permute-start.2 = (bf16[16,128]{1,0:T(8,128)(2,1)S(1)}, bf16[16,128]{1,0:T(8,128)(2,1)S(1)}, u32[]{:S(2)}, u32[]{:S(2)}) collective-permute-start(bf16[16,128]{1,0:T(8,128)(2,1)S(1)} %get-tuple-element.61), channel_id=1, source_target_pairs={{0,8},{1,9},{2,10},{3,11},{4,12},{5,13},{6,14},{7,15},{8,0},{9,1},... | collective-permute-start | bytes 12296 | tf_op jit(solution)/shard_map/ppermute | solution.py:195
  13.7 3.2 %collective-permute-start.7 = (bf16[32,3712]{1,0:T(8,128)(2,1)S(1)}, bf16[32,3712]{1,0:T(8,128)(2,1)S(1)}, u32[]{:S(2)}, u32[]{:S(2)}) collective-permute-start(bf16[32,3712]{1,0:T(8,128)(2,1)S(1)} %constant_dynamic-update-slice_fusion.refs_0_), channel_id=1, source_target_pairs={{0,1},{1,0},{2,3},{3,2},{4,5},{5,4},{6,7},{7,6},{8,9},{9,8},{10,11... | collective-permute-start | bytes 712712 | tf_op jit(solution)/shard_map/ppermute | solution.py:199
  13.8 3.0 %collective-permute-start.8 = (bf16[32,3712]{1,0:T(8,128)(2,1)S(1)}, bf16[32,3712]{1,0:T(8,128)(2,1)S(1)}, u32[]{:S(2)}, u32[]{:S(2)}) collective-permute-start(bf16[32,3712]{1,0:T(8,128)(2,1)S(1)} %constant_dynamic-update-slice_fusion.2.refs_1_), channel_id=1, source_target_pairs={{0,1},{1,0},{2,3},{3,2},{4,5},{5,4},{6,7},{7,6},{8,9},{9,8},{10,11... | collective-permute-start | bytes 712712 | tf_op jit(solution)/shard_map/ppermute | solution.py:199
  14.4 6.1 %collective-permute-start.3 = (bf16[16,3712]{1,0:T(8,128)(2,1)S(1)}, bf16[16,3712]{1,0:T(8,128)(2,1)S(1)}, u32[]{:S(2)}, u32[]{:S(2)}) collective-permute-start(bf16[16,3712]{1,0:T(8,128)(2,1)S(1)} %pad_maximum_fusion), channel_id=1, source_target_pairs={{0,4},{1,3},{2,6},{3,1},{4,0},{5,7},{6,2},{7,5},{8,12},{9,11},{10,... | collective-permute-start | bytes 356360 | tf_op jit(solution)/shard_map/ppermute | solution.py:195
  14.8 5.6 %collective-permute-start.5 = (bf16[16,3712]{1,0:T(8,128)(2,1)S(1)}, bf16[16,3712]{1,0:T(8,128)(2,1)S(1)}, u32[]{:S(2)}, u32[]{:S(2)}) collective-permute-start(bf16[16,3712]{1,0:T(8,128)(2,1)S(1)} %pad_maximum_fusion), channel_id=1, source_target_pairs={{0,2},{1,5},{2,0},{3,7},{4,6},{5,1},{6,4},{7,3},{8,10},{9,13},{10,... | collective-permute-start | bytes 356360 | tf_op jit(solution)/shard_map/ppermute | solution.py:195
  15.4 5.6 %collective-permute-start.4 = (bf16[16,3712]{1,0:T(8,128)(2,1)S(1)}, bf16[16,3712]{1,0:T(8,128)(2,1)S(1)}, u32[]{:S(2)}, u32[]{:S(2)}) collective-permute-start(bf16[16,3712]{1,0:T(8,128)(2,1)S(1)} %collective-permute-done), channel_id=1, source_target_pairs={{0,2},{1,5},{2,0},{3,7},{4,6},{5,1},{6,4},{7,3},{8,10},{9,13},{10,... | collective-permute-start | bytes 356360 | tf_op jit(solution)/shard_map/ppermute | solution.py:195
  21.0 5.0 %collective-permute-start.12 = (bf16[64,3584]{1,0:T(8,128)(2,1)S(1)}, bf16[64,3584]{1,0:T(8,128)(2,1)S(1)}, u32[]{:S(2)}, u32[]{:S(2)}) collective-permute-start(bf16[64,3584]{1,0:T(8,128)(2,1)S(1)} %get-tuple-element.84), channel_id=1, source_target_pairs={{0,1},{1,0},{2,3},{3,2},{4,5},{5,4},{6,7},{7,6},{8,9},{9,8},{10,11... | collective-permute-start | bytes 1376264 | tf_op jit(solution)/shard_map/ppermute | solution.py:199
  21.1 4.8 %collective-permute-start.9 = (bf16[16,3712]{1,0:T(8,128)(2,1)S(1)}, bf16[16,3712]{1,0:T(8,128)(2,1)S(1)}, u32[]{:S(2)}, u32[]{:S(2)}) collective-permute-start(bf16[16,3712]{1,0:T(8,128)(2,1)S(1)} %collective-permute-done.3), channel_id=1, source_target_pairs={{0,2},{1,5},{2,0},{3,7},{4,6},{5,1},{6,4},{7,3},{8,10},{9,13},{10,... | collective-permute-start | bytes 356360 | tf_op jit(solution)/shard_map/ppermute | solution.py:195
  22.1 3.9 %collective-permute-start.10 = (bf16[32,3712]{1,0:T(8,128)(2,1)S(1)}, bf16[32,3712]{1,0:T(8,128)(2,1)S(1)}, u32[]{:S(2)}, u32[]{:S(2)}) collective-permute-start(bf16[32,3712]{1,0:T(8,128)(2,1)S(1)} %constant_dynamic-update-slice_fusion.4.refs_0_), channel_id=1, source_target_pairs={{0,1},{1,0},{2,3},{3,2},{4,5},{5,4},{6,7},{7,6},{8,9},{9,8},{10,11... | collective-permute-start | bytes 712712 | tf_op jit(solution)/shard_map/ppermute | solution.py:199
  22.9 3.2 %collective-permute-start.11 = (bf16[16,3712]{1,0:T(8,128)(2,1)S(1)}, bf16[16,3712]{1,0:T(8,128)(2,1)S(1)}, u32[]{:S(2)}, u32[]{:S(2)}) collective-permute-start(bf16[16,3712]{1,0:T(8,128)(2,1)S(1)} %collective-permute-done.4.refs_1_), channel_id=1, source_target_pairs={{0,1},{1,0},{2,3},{3,2},{4,5},{5,4},{6,7},{7,6},{8,9},{9,8},{10,11... | collective-permute-start | bytes 356360 | tf_op jit(solution)/shard_map/ppermute | solution.py:199
  26.0 1.4 %collective-permute-start.13 = (bf16[16,3712]{1,0:T(8,128)(2,1)S(1)}, bf16[16,3712]{1,0:T(8,128)(2,1)S(1)}, u32[]{:S(2)}, u32[]{:S(2)}) collective-permute-start(bf16[16,3712]{1,0:T(8,128)(2,1)S(1)} %collective-permute-done.9.refs_2_), channel_id=1, source_target_pairs={{0,1},{1,0},{2,3},{3,2},{4,5},{5,4},{6,7},{7,6},{8,9},{9,8},{10,11... | collective-permute-start | bytes 356360 | tf_op jit(solution)/shard_map/ppermute | solution.py:199
  30.7 1.4 %collective-permute-start.16 = (bf16[16,3584]{1,0:T(8,128)(2,1)S(1)}, bf16[16,3584]{1,0:T(8,128)(2,1)S(1)}, u32[]{:S(2)}, u32[]{:S(2)}) collective-permute-start(bf16[16,3584]{1,0:T(8,128)(2,1)S(1)} %get-tuple-element.92), channel_id=1, source_target_pairs={{0,1},{1,0},{2,3},{3,2},{4,5},{5,4},{6,7},{7,6},{8,9},{9,8},{10,11... | collective-permute-start | bytes 344072 | tf_op jit(solution)/shard_map/ppermute | solution.py:199
  30.9 2.3 %collective-permute-start.14 = (bf16[48,3584]{1,0:T(8,128)(2,1)S(1)}, bf16[48,3584]{1,0:T(8,128)(2,1)S(1)}, u32[]{:S(2)}, u32[]{:S(2)}) collective-permute-start(bf16[48,3584]{1,0:T(8,128)(2,1)S(1)} %get-tuple-element.90), channel_id=1, source_target_pairs={{0,1},{1,0},{2,3},{3,2},{4,5},{5,4},{6,7},{7,6},{8,9},{9,8},{10,11... | collective-permute-start | bytes 1032200 | tf_op jit(solution)/shard_map/ppermute | solution.py:199
  32.1 4.9 %collective-permute-start.17 = (bf16[16,3584]{1,0:T(8,128)(2,1)S(1)}, bf16[16,3584]{1,0:T(8,128)(2,1)S(1)}, u32[]{:S(2)}, u32[]{:S(2)}) collective-permute-start(bf16[16,3584]{1,0:T(8,128)(2,1)S(1)} %add_convert_fusion.3), channel_id=1, source_target_pairs={{0,2},{1,5},{2,0},{3,7},{4,6},{5,1},{6,4},{7,3},{8,10},{9,13},{10,... | collective-permute-start | bytes 344072 | tf_op jit(solution)/shard_map/ppermute | solution.py:195
  33.3 8.9 %collective-permute-start.15 = (bf16[32,3584]{1,0:T(8,128)(2,1)S(1)}, bf16[32,3584]{1,0:T(8,128)(2,1)S(1)}, u32[]{:S(2)}, u32[]{:S(2)}) collective-permute-start(bf16[32,3584]{1,0:T(8,128)(2,1)S(1)} %slice.47), channel_id=1, source_target_pairs={{0,2},{1,5},{2,0},{3,7},{4,6},{5,1},{6,4},{7,3},{8,10},{9,13},{10,... | collective-permute-start | bytes 688136 | tf_op jit(solution)/shard_map/ppermute | solution.py:195
  37.0 5.3 %collective-permute-start.18 = (bf16[16,3584]{1,0:T(8,128)(2,1)S(1)}, bf16[16,3584]{1,0:T(8,128)(2,1)S(1)}, u32[]{:S(2)}, u32[]{:S(2)}) collective-permute-start(bf16[16,3584]{1,0:T(8,128)(2,1)S(1)} %fusion), channel_id=1, source_target_pairs={{0,4},{1,3},{2,6},{3,1},{4,0},{5,7},{6,2},{7,5},{8,12},{9,11},{10,... | collective-permute-start | bytes 344072 | tf_op jit(solution)/shard_map/ppermute | solution.py:195
  38.6 10.9 %collective-permute-start.20 = (bf16[16,3584]{1,0:T(8,128)(2,1)S(1)}, bf16[16,3584]{1,0:T(8,128)(2,1)S(1)}, u32[]{:S(2)}, u32[]{:S(2)}) collective-permute-start(bf16[16,3584]{1,0:T(8,128)(2,1)S(1)} %slice.48), channel_id=1, source_target_pairs={{0,2},{1,5},{2,0},{3,7},{4,6},{5,1},{6,4},{7,3},{8,10},{9,13},{10,... | collective-permute-start | bytes 344072 | tf_op jit(solution)/shard_map/ppermute | solution.py:195
  42.3 7.1 %collective-permute-start.19 = (bf16[16,3584]{1,0:T(8,128)(2,1)S(1)}, bf16[16,3584]{1,0:T(8,128)(2,1)S(1)}, u32[]{:S(2)}, u32[]{:S(2)}) collective-permute-start(bf16[16,3584]{1,0:T(8,128)(2,1)S(1)} %add_convert_fusion.2), channel_id=1, source_target_pairs={{0,8},{1,9},{2,10},{3,11},{4,12},{5,13},{6,14},{7,15},{8,0},{9,1},... | collective-permute-start | bytes 344072 | tf_op jit(solution)/shard_map/ppermute | solution.py:195
  44.4 5.4 %collective-permute-start.21 = (bf16[16,3584]{1,0:T(8,128)(2,1)S(1)}, bf16[16,3584]{1,0:T(8,128)(2,1)S(1)}, u32[]{:S(2)}, u32[]{:S(2)}) collective-permute-start(bf16[16,3584]{1,0:T(8,128)(2,1)S(1)} %add_convert_fusion.1), channel_id=1, source_target_pairs={{0,4},{1,3},{2,6},{3,1},{4,0},{5,7},{6,2},{7,5},{8,12},{9,11},{10,... | collective-permute-start | bytes 344072 | tf_op jit(solution)/shard_map/ppermute | solution.py:195
  (7 other events, 62.9 us)

commit v13 on v9

--- a/solution.py
+++ b/solution.py
@@ -270,7 +270,6 @@
     abc, early_swap, late_swap, near = barrier((abc, early_swap, late_swap, near))
     far_rows = [early, bc, abc, early_swap, late_swap, swap(abc)]
     far_own, far_other = experts(far_rows, gate, up, down, chip, [3 * n, n])
-    far_own, far_other, got_c = barrier((far_own, far_other, got_c))
 
     sent = add(far_own[1], swap(far_other[1])).astype(BF16)
     far = add(far_own[0], swap(far_other[0]))

time: 51 us -> 52.3 us (1.025)
  waiting for transfers between devices: 9.93 us -> 13.2 us
  starting transfers between devices: 20.1 us -> 18.1 us
    ppermute x13, waiting for transfers between devices: 9.1 us -> 11 us  [hop(): return lax.ppermute(x, ('ep', 'sub'), pairs)]
    ppermute x13, starting transfers between devices: 17.9 us -> 16.2 us  [hop(): return lax.ppermute(x, ('ep', 'sub'), pairs)]
    ppermute x8, waiting for transfers between devices: 0.83 us -> 2.15 us  [swap(): return lax.ppermute(x, 'sub', [(0, 1), (1, 0)])]
  transfers between devices with their start and end apart: 21 -> 21, of which waited for: 10 -> 10; matrix products, arithmetic and copies ran while one was open for 1% -> 1% of each run, Pallas kernels for 34% -> 27%
where the time goes in v13:
time: 52.3 us; the launch traced here: 52.2 us
  Pallas kernels  18.7 us (36%)
  starting transfers between devices  18.1 us (35%)
  waiting for transfers between devices  13.2 us (25%)
  other arithmetic  1.01 us (2%)
  between operations  0.97 us (2%)
    ppermute x13, starting transfers between devices, hop(): return lax.ppermute(x, ('ep', 'sub'), pairs)  16.2 us
    ppermute x13, waiting for transfers between devices, hop(): return lax.ppermute(x, ('ep', 'sub'), pairs)  11 us
    pallas_call x4, Pallas kernels, attention(): pl.pallas_call(functools.partial(attention_kernel, first=first, count=cou...  11 us
    pallas_call x2, Pallas kernels, experts(): pl.pallas_call(functools.partial(experts_kernel, parts=len(parts), groups...  6.48 us
    ppermute x8, waiting for transfers between devices, swap(): return lax.ppermute(x, 'sub', [(0, 1), (1, 0)])  2.15 us
    ppermute x8, starting transfers between devices, swap(): return lax.ppermute(x, 'sub', [(0, 1), (1, 0)])  1.93 us
    pallas_call x1, Pallas kernels, route(): pl.pallas_call(functools.partial(route_kernel, experts=placement.shape[0]...  1.27 us
  transfers between devices with their start and end apart: 21, of which 10 were waited for; matrix products, arithmetic and copies ran while one was open for 1% of the time, Pallas kernels for 27%

profile of v13, /device:TPU:0, one launch (start us, length us, event | category | flops | bytes accessed | tf_op | source)
XLA Modules:
  0.0 52.2 jit_solution(17664265591619680103)
XLA Ops:
  0.7 1.3 %route.1 = bf16[16,3712]{1,0:T(8,128)(2,1)S(1)} custom-call(s32[2,14]{1,0:T(2,128)} %bitcast.22, bf16[16,3584]{1,0:T(8,128)(2,1)} %rows_ref.1, f32[8,16]{1,0:T(8,128)} %bitcast.20, s32[8,16]{1,0:T(8,128)} %bitcast.21), custom_call_target="tpu_custom_call" | custom-call | flops 17179869184 | bytes 33554432 | tf_op jit(solution)/shard_map/route/pallas_call | solution.py:117
  2.0 3.0 %collective-permute-start = (bf16[16,3712]{1,0:T(8,128)(2,1)S(1)}, bf16[16,3712]{1,0:T(8,128)(2,1)S(1)}, u32[]{:S(2)}, u32[]{:S(2)}) collective-permute-start(bf16[16,3712]{1,0:T(8,128)(2,1)S(1)} %route.1), channel_id=1, source_target_pairs={{0,2},{1,5},{2,0},{3,7},{4,6},{5,1},{6,4},{7,3},{8,10},{9,13},{10,... | collective-permute-start | bytes 356360 | tf_op jit(solution)/shard_map/ppermute | solution.py:193
  5.0 1.6 %collective-permute-start.1 = (bf16[16,3712]{1,0:T(8,128)(2,1)S(1)}, bf16[16,3712]{1,0:T(8,128)(2,1)S(1)}, u32[]{:S(2)}, u32[]{:S(2)}) collective-permute-start(bf16[16,3712]{1,0:T(8,128)(2,1)S(1)} %route.1), channel_id=1, source_target_pairs={{0,4},{1,3},{2,6},{3,1},{4,0},{5,7},{6,2},{7,5},{8,12},{9,11},{10,... | collective-permute-start | bytes 356360 | tf_op jit(solution)/shard_map/ppermute | solution.py:193
  6.6 2.6 %collective-permute-start.2 = (bf16[16,3712]{1,0:T(8,128)(2,1)S(1)}, bf16[16,3712]{1,0:T(8,128)(2,1)S(1)}, u32[]{:S(2)}, u32[]{:S(2)}) collective-permute-start(bf16[16,3712]{1,0:T(8,128)(2,1)S(1)} %route.1), channel_id=1, source_target_pairs={{0,8},{1,9},{2,10},{3,11},{4,12},{5,13},{6,14},{7,15},{8,0},{9,1},... | collective-permute-start | bytes 356360 | tf_op jit(solution)/shard_map/ppermute | solution.py:193
  9.2 3.4 %attention.4.refs_0_ = bf16[8,2,128,512]{3,2,1,0:T(8,128)(2,1)} custom-call(s32[8]{0:T(128)} %length_ref.3, bf16[8,2,576,128]{3,2,1,0:T(8,128)(2,1)S(1)} %bitcast.6, bf16[8,576,256]{2,1,0:T(8,128)(2,1)S(1)} %bitcast.10, bf16[8,2,576]{2,1,0:T(2,128)(2,1)S(1)} %copy-done.2), custom_call_target="tpu_custom_call" | custom-call | flops 1048576 | bytes 65536 | tf_op jit(solution)/shard_map/attention/pallas_call | solution.py:75
  12.6 1.7 %collective-permute-done.2 = bf16[16,3712]{1,0:T(8,128)(2,1)S(1)} collective-permute-done((bf16[16,3712]{1,0:T(8,128)(2,1)S(1)}, bf16[16,3712]{1,0:T(8,128)(2,1)S(1)}, u32[]{:S(2)}, u32[]{:S(2)}) %collective-permute-start.2) | collective-permute-done | bytes 118816 | tf_op jit(solution)/shard_map/ppermute | solution.py:193
  15.6 1.4 %collective-permute-start.4 = (bf16[16,3712]{1,0:T(8,128)(2,1)S(1)}, bf16[16,3712]{1,0:T(8,128)(2,1)S(1)}, u32[]{:S(2)}, u32[]{:S(2)}) collective-permute-start(bf16[16,3712]{1,0:T(8,128)(2,1)S(1)} %collective-permute-done.2), channel_id=1, source_target_pairs={{0,2},{1,5},{2,0},{3,7},{4,6},{5,1},{6,4},{7,3},{8,10},{9,13},{10,... | collective-permute-start | bytes 356360 | tf_op jit(solution)/shard_map/ppermute | solution.py:193
  17.1 3.2 %experts.2 = (f32[64,3584]{1,0:T(8,128)S(1)}, bf16[64,3584]{1,0:T(8,128)(2,1)S(1)}) custom-call(bf16[32,3712]{1,0:T(8,128)(2,1)S(1)} %constant_dynamic-update-slice_fusion.refs_0_, bf16[32,3712]{1,0:T(8,128)(2,1)S(1)} %constant_dynamic-update-slice_fusion.2.refs_1_, bf16[32,3712]{1,0:T(8,128)(2,1)S(1)} %collective-permute-done.6.refs_2_, ...), custom_call_target="tpu_custom_call" | custom-call | flops 1048576 | bytes 65536 | tf_op jit(solution)/shard_map/experts/pallas_call | solution.py:161
  20.6 1.8 %collective-permute-done.4 = bf16[16,3712]{1,0:T(8,128)(2,1)S(1)} collective-permute-done((bf16[16,3712]{1,0:T(8,128)(2,1)S(1)}, bf16[16,3712]{1,0:T(8,128)(2,1)S(1)}, u32[]{:S(2)}, u32[]{:S(2)}) %collective-permute-start.4) | collective-permute-done | bytes 118816 | tf_op jit(solution)/shard_map/ppermute | solution.py:193
  23.7 2.7 %attention.5.refs_0_ = bf16[8,2,128,512]{3,2,1,0:T(8,128)(2,1)} custom-call(s32[8]{0:T(128)} %length_ref.3, bf16[8,2,576,128]{3,2,1,0:T(8,128)(2,1)S(1)} %bitcast.7, bf16[8,576,256]{2,1,0:T(8,128)(2,1)S(1)} %bitcast.11, bf16[8,2,576]{2,1,0:T(2,128)(2,1)S(1)} %copy-done.2, bf16[8,2,128,512]{3,2,1,0:T(8,128)(2,1)} %attention.4.refs_0_), custom_call_target="tpu_custom_call", output_to_operand_aliasing={{}: (4, {})} | custom-call | flops 1048576 | bytes 65536 | tf_op jit(solution)/shard_map/attention/pallas_call | solution.py:75
  26.4 0.8 %collective-permute-done.8.refs_2_ = bf16[16,3712]{1,0:T(8,128)(2,1)S(1)} collective-permute-done((bf16[16,3712]{1,0:T(8,128)(2,1)S(1)}, bf16[16,3712]{1,0:T(8,128)(2,1)S(1)}, u32[]{:S(2)}, u32[]{:S(2)}) %collective-permute-start.8) | collective-permute-done | bytes 118816 | tf_op jit(solution)/shard_map/ppermute | solution.py:193
  27.4 1.3 %collective-permute-done.12.refs_5_ = bf16[16,3712]{1,0:T(8,128)(2,1)S(1)} collective-permute-done((bf16[16,3712]{1,0:T(8,128)(2,1)S(1)}, bf16[16,3712]{1,0:T(8,128)(2,1)S(1)}, u32[]{:S(2)}, u32[]{:S(2)}) %collective-permute-start.12) | collective-permute-done | bytes 118816 | tf_op jit(solution)/shard_map/ppermute | solution.py:197
  28.7 3.3 %experts.3 = (f32[48,3584]{1,0:T(8,128)S(1)}, f32[16,3584]{1,0:T(8,128)S(1)}, bf16[48,3584]{1,0:T(8,128)(2,1)S(1)}, bf16[16,3584]{1,0:T(8,128)(2,1)S(1)}) custom-call(bf16[32,3712]{1,0:T(8,128)(2,1)S(1)} %constant_dynamic-update-slice_fusion.4.refs_0_, bf16[16,3712]{1,0:T(8,128)(2,1)S(1)} %collective-permute-done.3.refs_1_, ...), custom_call_target="tpu_custom_call" | custom-call | flops 1048576 | bytes 65536 | tf_op jit(solution)/shard_map/experts/pallas_call | solution.py:161
  32.6 0.8 %collective-permute-done.15 = bf16[16,3584]{1,0:T(8,128)(2,1)S(1)} collective-permute-done((bf16[16,3584]{1,0:T(8,128)(2,1)S(1)}, bf16[16,3584]{1,0:T(8,128)(2,1)S(1)}, u32[]{:S(2)}, u32[]{:S(2)}) %collective-permute-start.15) | collective-permute-done | bytes 114720 | tf_op jit(solution)/shard_map/ppermute | solution.py:197
  33.4 0.7 %collective-permute-start.16 = (bf16[16,3584]{1,0:T(8,128)(2,1)S(1)}, bf16[16,3584]{1,0:T(8,128)(2,1)S(1)}, u32[]{:S(2)}, u32[]{:S(2)}) collective-permute-start(bf16[16,3584]{1,0:T(8,128)(2,1)S(1)} %add_convert_fusion.3), channel_id=1, source_target_pairs={{0,2},{1,5},{2,0},{3,7},{4,6},{5,1},{6,4},{7,3},{8,10},{9,13},{10,... | collective-permute-start | bytes 344072 | tf_op jit(solution)/shard_map/ppermute | solution.py:193
  34.3 1.4 %collective-permute-start.14 = (bf16[32,3584]{1,0:T(8,128)(2,1)S(1)}, bf16[32,3584]{1,0:T(8,128)(2,1)S(1)}, u32[]{:S(2)}, u32[]{:S(2)}) collective-permute-start(bf16[32,3584]{1,0:T(8,128)(2,1)S(1)} %slice.47), channel_id=1, source_target_pairs={{0,2},{1,5},{2,0},{3,7},{4,6},{5,1},{6,4},{7,3},{8,10},{9,13},{10,... | collective-permute-start | bytes 688136 | tf_op jit(solution)/shard_map/ppermute | solution.py:193
  35.7 2.2 %attention.6.refs_0_ = bf16[8,2,128,512]{3,2,1,0:T(8,128)(2,1)} custom-call(s32[8]{0:T(128)} %length_ref.3, bf16[8,2,576,128]{3,2,1,0:T(8,128)(2,1)S(1)} %bitcast.8, bf16[8,576,256]{2,1,0:T(8,128)(2,1)S(1)} %bitcast.12, bf16[8,2,576]{2,1,0:T(2,128)(2,1)S(1)} %copy-done.2, bf16[8,2,128,512]{3,2,1,0:T(8,128)(2,1)} %attention.5.refs_0_), custom_call_target="tpu_custom_call", output_to_operand_aliasing={{}: (4, {})} | custom-call | flops 1048576 | bytes 65536 | tf_op jit(solution)/shard_map/attention/pallas_call | solution.py:75
  38.4 0.8 %collective-permute-start.19 = (bf16[16,3584]{1,0:T(8,128)(2,1)S(1)}, bf16[16,3584]{1,0:T(8,128)(2,1)S(1)}, u32[]{:S(2)}, u32[]{:S(2)}) collective-permute-start(bf16[16,3584]{1,0:T(8,128)(2,1)S(1)} %slice.48), channel_id=1, source_target_pairs={{0,2},{1,5},{2,0},{3,7},{4,6},{5,1},{6,4},{7,3},{8,10},{9,13},{10,... | collective-permute-start | bytes 344072 | tf_op jit(solution)/shard_map/ppermute | solution.py:193
  39.2 4.1 %collective-permute-done.17 = bf16[16,3584]{1,0:T(8,128)(2,1)S(1)} collective-permute-done((bf16[16,3584]{1,0:T(8,128)(2,1)S(1)}, bf16[16,3584]{1,0:T(8,128)(2,1)S(1)}, u32[]{:S(2)}, u32[]{:S(2)}) %collective-permute-start.17) | collective-permute-done | bytes 114720 | tf_op jit(solution)/shard_map/ppermute | solution.py:193
  43.4 1.9 %collective-permute-start.18 = (bf16[16,3584]{1,0:T(8,128)(2,1)S(1)}, bf16[16,3584]{1,0:T(8,128)(2,1)S(1)}, u32[]{:S(2)}, u32[]{:S(2)}) collective-permute-start(bf16[16,3584]{1,0:T(8,128)(2,1)S(1)} %add_convert_fusion.2), channel_id=1, source_target_pairs={{0,8},{1,9},{2,10},{3,11},{4,12},{5,13},{6,14},{7,15},{8,0},{9,1},... | collective-permute-start | bytes 344072 | tf_op jit(solution)/shard_map/ppermute | solution.py:193
  45.4 1.4 %collective-permute-start.20 = (bf16[16,3584]{1,0:T(8,128)(2,1)S(1)}, bf16[16,3584]{1,0:T(8,128)(2,1)S(1)}, u32[]{:S(2)}, u32[]{:S(2)}) collective-permute-start(bf16[16,3584]{1,0:T(8,128)(2,1)S(1)} %add_convert_fusion.1), channel_id=1, source_target_pairs={{0,4},{1,3},{2,6},{3,1},{4,0},{5,7},{6,2},{7,5},{8,12},{9,11},{10,... | collective-permute-start | bytes 344072 | tf_op jit(solution)/shard_map/ppermute | solution.py:193
  46.8 2.7 %attention.7 = bf16[8,2,128,512]{3,2,1,0:T(8,128)(2,1)} custom-call(s32[8]{0:T(128)} %length_ref.3, bf16[8,2,576,128]{3,2,1,0:T(8,128)(2,1)S(1)} %bitcast.9, bf16[8,576,256]{2,1,0:T(8,128)(2,1)S(1)} %bitcast.13, bf16[8,2,576]{2,1,0:T(2,128)(2,1)S(1)} %copy-done.2, bf16[8,2,128,512]{3,2,1,0:T(8,128)(2,1)} %attention.6.refs_0_), custom_call_target="tpu_custom_call", output_to_operand_aliasing={{}: (4, {})} | custom-call | flops 1048576 | bytes 65536 | tf_op jit(solution)/shard_map/attention/pallas_call | solution.py:75
  49.5 1.2 %collective-permute-done.18 = bf16[16,3584]{1,0:T(8,128)(2,1)S(1)} collective-permute-done((bf16[16,3584]{1,0:T(8,128)(2,1)S(1)}, bf16[16,3584]{1,0:T(8,128)(2,1)S(1)}, u32[]{:S(2)}, u32[]{:S(2)}) %collective-permute-start.18) | collective-permute-done | bytes 114720 | tf_op jit(solution)/shard_map/ppermute | solution.py:193
  50.7 0.7 %collective-permute-done.20 = bf16[16,3584]{1,0:T(8,128)(2,1)S(1)} collective-permute-done((bf16[16,3584]{1,0:T(8,128)(2,1)S(1)}, bf16[16,3584]{1,0:T(8,128)(2,1)S(1)}, u32[]{:S(2)}, u32[]{:S(2)}) %collective-permute-start.20) | collective-permute-done | bytes 114720 | tf_op jit(solution)/shard_map/ppermute | solution.py:193
  (61 shorter events, 5.1 us)
Async XLA Ops:
  0.6 16.4 %slice-start = ((s8[7340032]{0:T(1024)(128)(4,1)}), s8[4194304]{0:T(1024)(128)(4,1)S(1)}, s32[]{:S(2)}) async-start(s8[7340032]{0:T(1024)(128)(4,1)} %bitcast.14), calls=%async_computation | async-start | bytes 8388608
  0.6 16.4 %slice-start.2 = ((s8[7340032]{0:T(1024)(128)(4,1)}), s8[4194304]{0:T(1024)(128)(4,1)S(1)}, s32[]{:S(2)}) async-start(s8[7340032]{0:T(1024)(128)(4,1)} %bitcast.16), calls=%async_computation.2 | async-start | bytes 8388608
  0.7 16.4 %slice-start.4 = ((s8[7340032]{0:T(1024)(128)(4,1)}), s8[4194304]{0:T(1024)(128)(4,1)S(1)}, s32[]{:S(2)}) async-start(s8[7340032]{0:T(1024)(128)(4,1)} %bitcast.18), calls=%async_computation.4 | async-start | bytes 8388608
  2.0 10.6 %collective-permute-start = (bf16[16,3712]{1,0:T(8,128)(2,1)S(1)}, bf16[16,3712]{1,0:T(8,128)(2,1)S(1)}, u32[]{:S(2)}, u32[]{:S(2)}) collective-permute-start(bf16[16,3712]{1,0:T(8,128)(2,1)S(1)} %route.1), channel_id=1, source_target_pairs={{0,2},{1,5},{2,0},{3,7},{4,6},{5,1},{6,4},{7,3},{8,10},{9,13},{10,... | collective-permute-start | bytes 356360 | tf_op jit(solution)/shard_map/ppermute | solution.py:193
  5.0 7.6 %collective-permute-start.1 = (bf16[16,3712]{1,0:T(8,128)(2,1)S(1)}, bf16[16,3712]{1,0:T(8,128)(2,1)S(1)}, u32[]{:S(2)}, u32[]{:S(2)}) collective-permute-start(bf16[16,3712]{1,0:T(8,128)(2,1)S(1)} %route.1), channel_id=1, source_target_pairs={{0,4},{1,3},{2,6},{3,1},{4,0},{5,7},{6,2},{7,5},{8,12},{9,11},{10,... | collective-permute-start | bytes 356360 | tf_op jit(solution)/shard_map/ppermute | solution.py:193
  6.6 7.7 %collective-permute-start.2 = (bf16[16,3712]{1,0:T(8,128)(2,1)S(1)}, bf16[16,3712]{1,0:T(8,128)(2,1)S(1)}, u32[]{:S(2)}, u32[]{:S(2)}) collective-permute-start(bf16[16,3712]{1,0:T(8,128)(2,1)S(1)} %route.1), channel_id=1, source_target_pairs={{0,8},{1,9},{2,10},{3,11},{4,12},{5,13},{6,14},{7,15},{8,0},{9,1},... | collective-permute-start | bytes 356360 | tf_op jit(solution)/shard_map/ppermute | solution.py:193
  14.3 2.7 %collective-permute-start.6 = (bf16[32,3712]{1,0:T(8,128)(2,1)S(1)}, bf16[32,3712]{1,0:T(8,128)(2,1)S(1)}, u32[]{:S(2)}, u32[]{:S(2)}) collective-permute-start(bf16[32,3712]{1,0:T(8,128)(2,1)S(1)} %constant_dynamic-update-slice_fusion.refs_0_), channel_id=1, source_target_pairs={{0,1},{1,0},{2,3},{3,2},{4,5},{5,4},{6,7},{7,6},{8,9},{9,8},{10,11... | collective-permute-start | bytes 712712 | tf_op jit(solution)/shard_map/ppermute | solution.py:197
  14.4 2.6 %collective-permute-start.7 = (bf16[32,3712]{1,0:T(8,128)(2,1)S(1)}, bf16[32,3712]{1,0:T(8,128)(2,1)S(1)}, u32[]{:S(2)}, u32[]{:S(2)}) collective-permute-start(bf16[32,3712]{1,0:T(8,128)(2,1)S(1)} %constant_dynamic-update-slice_fusion.2.refs_1_), channel_id=1, source_target_pairs={{0,1},{1,0},{2,3},{3,2},{4,5},{5,4},{6,7},{7,6},{8,9},{9,8},{10,11... | collective-permute-start | bytes 712712 | tf_op jit(solution)/shard_map/ppermute | solution.py:197
  15.0 5.6 %collective-permute-start.3 = (bf16[16,3712]{1,0:T(8,128)(2,1)S(1)}, bf16[16,3712]{1,0:T(8,128)(2,1)S(1)}, u32[]{:S(2)}, u32[]{:S(2)}) collective-permute-start(bf16[16,3712]{1,0:T(8,128)(2,1)S(1)} %collective-permute-done.1), channel_id=1, source_target_pairs={{0,2},{1,5},{2,0},{3,7},{4,6},{5,1},{6,4},{7,3},{8,10},{9,13},{10,... | collective-permute-start | bytes 356360 | tf_op jit(solution)/shard_map/ppermute | solution.py:193
  15.6 6.8 %collective-permute-start.4 = (bf16[16,3712]{1,0:T(8,128)(2,1)S(1)}, bf16[16,3712]{1,0:T(8,128)(2,1)S(1)}, u32[]{:S(2)}, u32[]{:S(2)}) collective-permute-start(bf16[16,3712]{1,0:T(8,128)(2,1)S(1)} %collective-permute-done.2), channel_id=1, source_target_pairs={{0,2},{1,5},{2,0},{3,7},{4,6},{5,1},{6,4},{7,3},{8,10},{9,13},{10,... | collective-permute-start | bytes 356360 | tf_op jit(solution)/shard_map/ppermute | solution.py:193
  17.0 5.4 %collective-permute-start.5 = (bf16[16,3712]{1,0:T(8,128)(2,1)S(1)}, bf16[16,3712]{1,0:T(8,128)(2,1)S(1)}, u32[]{:S(2)}, u32[]{:S(2)}) collective-permute-start(bf16[16,3712]{1,0:T(8,128)(2,1)S(1)} %collective-permute-done.2), channel_id=1, source_target_pairs={{0,4},{1,3},{2,6},{3,1},{4,0},{5,7},{6,2},{7,5},{8,12},{9,11},{10,... | collective-permute-start | bytes 356360 | tf_op jit(solution)/shard_map/ppermute | solution.py:193
  22.4 4.8 %collective-permute-start.8 = (bf16[16,3712]{1,0:T(8,128)(2,1)S(1)}, bf16[16,3712]{1,0:T(8,128)(2,1)S(1)}, u32[]{:S(2)}, u32[]{:S(2)}) collective-permute-start(bf16[16,3712]{1,0:T(8,128)(2,1)S(1)} %collective-permute-done.5), channel_id=1, source_target_pairs={{0,2},{1,5},{2,0},{3,7},{4,6},{5,1},{6,4},{7,3},{8,10},{9,13},{10,... | collective-permute-start | bytes 356360 | tf_op jit(solution)/shard_map/ppermute | solution.py:193
  23.0 4.2 %collective-permute-start.11 = (bf16[64,3584]{1,0:T(8,128)(2,1)S(1)}, bf16[64,3584]{1,0:T(8,128)(2,1)S(1)}, u32[]{:S(2)}, u32[]{:S(2)}) collective-permute-start(bf16[64,3584]{1,0:T(8,128)(2,1)S(1)} %get-tuple-element.82), channel_id=1, source_target_pairs={{0,1},{1,0},{2,3},{3,2},{4,5},{5,4},{6,7},{7,6},{8,9},{9,8},{10,11... | collective-permute-start | bytes 1376264 | tf_op jit(solution)/shard_map/ppermute | solution.py:197
  23.0 4.3 %collective-permute-start.9 = (bf16[32,3712]{1,0:T(8,128)(2,1)S(1)}, bf16[32,3712]{1,0:T(8,128)(2,1)S(1)}, u32[]{:S(2)}, u32[]{:S(2)}) collective-permute-start(bf16[32,3712]{1,0:T(8,128)(2,1)S(1)} %constant_dynamic-update-slice_fusion.4.refs_0_), channel_id=1, source_target_pairs={{0,1},{1,0},{2,3},{3,2},{4,5},{5,4},{6,7},{7,6},{8,9},{9,8},{10,11... | collective-permute-start | bytes 712712 | tf_op jit(solution)/shard_map/ppermute | solution.py:197
  23.6 3.7 %collective-permute-start.10 = (bf16[16,3712]{1,0:T(8,128)(2,1)S(1)}, bf16[16,3712]{1,0:T(8,128)(2,1)S(1)}, u32[]{:S(2)}, u32[]{:S(2)}) collective-permute-start(bf16[16,3712]{1,0:T(8,128)(2,1)S(1)} %collective-permute-done.3.refs_1_), channel_id=1, source_target_pairs={{0,1},{1,0},{2,3},{3,2},{4,5},{5,4},{6,7},{7,6},{8,9},{9,8},{10,11... | collective-permute-start | bytes 356360 | tf_op jit(solution)/shard_map/ppermute | solution.py:197
  27.3 1.4 %collective-permute-start.12 = (bf16[16,3712]{1,0:T(8,128)(2,1)S(1)}, bf16[16,3712]{1,0:T(8,128)(2,1)S(1)}, u32[]{:S(2)}, u32[]{:S(2)}) collective-permute-start(bf16[16,3712]{1,0:T(8,128)(2,1)S(1)} %collective-permute-done.8.refs_2_), channel_id=1, source_target_pairs={{0,1},{1,0},{2,3},{3,2},{4,5},{5,4},{6,7},{7,6},{8,9},{9,8},{10,11... | collective-permute-start | bytes 356360 | tf_op jit(solution)/shard_map/ppermute | solution.py:197
  32.0 1.4 %collective-permute-start.15 = (bf16[16,3584]{1,0:T(8,128)(2,1)S(1)}, bf16[16,3584]{1,0:T(8,128)(2,1)S(1)}, u32[]{:S(2)}, u32[]{:S(2)}) collective-permute-start(bf16[16,3584]{1,0:T(8,128)(2,1)S(1)} %get-tuple-element.90), channel_id=1, source_target_pairs={{0,1},{1,0},{2,3},{3,2},{4,5},{5,4},{6,7},{7,6},{8,9},{9,8},{10,11... | collective-permute-start | bytes 344072 | tf_op jit(solution)/shard_map/ppermute | solution.py:197
  32.2 1.9 %collective-permute-start.13 = (bf16[48,3584]{1,0:T(8,128)(2,1)S(1)}, bf16[48,3584]{1,0:T(8,128)(2,1)S(1)}, u32[]{:S(2)}, u32[]{:S(2)}) collective-permute-start(bf16[48,3584]{1,0:T(8,128)(2,1)S(1)} %get-tuple-element.88), channel_id=1, source_target_pairs={{0,1},{1,0},{2,3},{3,2},{4,5},{5,4},{6,7},{7,6},{8,9},{9,8},{10,11... | collective-permute-start | bytes 1032200 | tf_op jit(solution)/shard_map/ppermute | solution.py:197
  33.4 4.9 %collective-permute-start.16 = (bf16[16,3584]{1,0:T(8,128)(2,1)S(1)}, bf16[16,3584]{1,0:T(8,128)(2,1)S(1)}, u32[]{:S(2)}, u32[]{:S(2)}) collective-permute-start(bf16[16,3584]{1,0:T(8,128)(2,1)S(1)} %add_convert_fusion.3), channel_id=1, source_target_pairs={{0,2},{1,5},{2,0},{3,7},{4,6},{5,1},{6,4},{7,3},{8,10},{9,13},{10,... | collective-permute-start | bytes 344072 | tf_op jit(solution)/shard_map/ppermute | solution.py:193
  34.3 9.1 %collective-permute-start.14 = (bf16[32,3584]{1,0:T(8,128)(2,1)S(1)}, bf16[32,3584]{1,0:T(8,128)(2,1)S(1)}, u32[]{:S(2)}, u32[]{:S(2)}) collective-permute-start(bf16[32,3584]{1,0:T(8,128)(2,1)S(1)} %slice.47), channel_id=1, source_target_pairs={{0,2},{1,5},{2,0},{3,7},{4,6},{5,1},{6,4},{7,3},{8,10},{9,13},{10,... | collective-permute-start | bytes 688136 | tf_op jit(solution)/shard_map/ppermute | solution.py:193
  38.3 5.1 %collective-permute-start.17 = (bf16[16,3584]{1,0:T(8,128)(2,1)S(1)}, bf16[16,3584]{1,0:T(8,128)(2,1)S(1)}, u32[]{:S(2)}, u32[]{:S(2)}) collective-permute-start(bf16[16,3584]{1,0:T(8,128)(2,1)S(1)} %fusion), channel_id=1, source_target_pairs={{0,4},{1,3},{2,6},{3,1},{4,0},{5,7},{6,2},{7,5},{8,12},{9,11},{10,... | collective-permute-start | bytes 344072 | tf_op jit(solution)/shard_map/ppermute | solution.py:193
  38.4 12.3 %collective-permute-start.19 = (bf16[16,3584]{1,0:T(8,128)(2,1)S(1)}, bf16[16,3584]{1,0:T(8,128)(2,1)S(1)}, u32[]{:S(2)}, u32[]{:S(2)}) collective-permute-start(bf16[16,3584]{1,0:T(8,128)(2,1)S(1)} %slice.48), channel_id=1, source_target_pairs={{0,2},{1,5},{2,0},{3,7},{4,6},{5,1},{6,4},{7,3},{8,10},{9,13},{10,... | collective-permute-start | bytes 344072 | tf_op jit(solution)/shard_map/ppermute | solution.py:193
  43.4 7.3 %collective-permute-start.18 = (bf16[16,3584]{1,0:T(8,128)(2,1)S(1)}, bf16[16,3584]{1,0:T(8,128)(2,1)S(1)}, u32[]{:S(2)}, u32[]{:S(2)}) collective-permute-start(bf16[16,3584]{1,0:T(8,128)(2,1)S(1)} %add_convert_fusion.2), channel_id=1, source_target_pairs={{0,8},{1,9},{2,10},{3,11},{4,12},{5,13},{6,14},{7,15},{8,0},{9,1},... | collective-permute-start | bytes 344072 | tf_op jit(solution)/shard_map/ppermute | solution.py:193
  45.4 6.1 %collective-permute-start.20 = (bf16[16,3584]{1,0:T(8,128)(2,1)S(1)}, bf16[16,3584]{1,0:T(8,128)(2,1)S(1)}, u32[]{:S(2)}, u32[]{:S(2)}) collective-permute-start(bf16[16,3584]{1,0:T(8,128)(2,1)S(1)} %add_convert_fusion.1), channel_id=1, source_target_pairs={{0,4},{1,3},{2,6},{3,1},{4,0},{5,7},{6,2},{7,5},{8,12},{9,11},{10,... | collective-permute-start | bytes 344072 | tf_op jit(solution)/shard_map/ppermute | solution.py:193
  (6 other events, 74.5 us)

commit v14 on v10

--- a/solution.py
+++ b/solution.py
@@ -261,11 +261,11 @@
     own, inputs = barrier((own, inputs))
     c = hop_c(own)
     b, a = attend(2, (hop_b(own), a))
-    ab, bc, ac = hop_b(a), hop_c(b), hop_c(a)
+    bc, ab, ac = hop_c(b), hop_b(a), hop_c(a)
     near_rows = [jnp.concatenate(x, axis=0) for x in ((own, a), (b, c))]
     near_rows += [swap(x) for x in near_rows]
     near_own, near_other = experts(near_rows, gate, up, down, chip, [4 * n])
-    ab, bc, ac, near_own, near_other = barrier((ab, bc, ac, near_own, near_other))
+    bc, ab, ac, near_own, near_other = barrier((bc, ab, ac, near_own, near_other))
     abc = hop_c(ab)
     ab, inputs = barrier((ab, inputs))
     abc = attend(2, abc)

time: 50.4 us -> 50.5 us (level)
  no operation moved by 1% of the time
where the time goes in v14:
time: 50.5 us; the launch traced here: 50.3 us
  starting transfers between devices  20 us (40%)
  Pallas kernels  18.9 us (37%)
  waiting for transfers between devices  9.4 us (19%)
  other arithmetic  1.02 us (2%)
  between operations  0.94 us (2%)
    ppermute x14, starting transfers between devices, hop(): return lax.ppermute(x, ('ep', 'sub'), pairs)  18 us
    pallas_call x4, Pallas kernels, attention(): pl.pallas_call(functools.partial(attention_kernel, first=first, count=cou...  11.1 us
    ppermute x14, waiting for transfers between devices, hop(): return lax.ppermute(x, ('ep', 'sub'), pairs)  7.26 us
    pallas_call x2, Pallas kernels, experts(): pl.pallas_call(functools.partial(experts_kernel, parts=len(parts), groups...  6.48 us
    ppermute x8, waiting for transfers between devices, swap(): return lax.ppermute(x, 'sub', [(0, 1), (1, 0)])  2.15 us
    ppermute x8, starting transfers between devices, swap(): return lax.ppermute(x, 'sub', [(0, 1), (1, 0)])  1.92 us
    pallas_call x1, Pallas kernels, route(): pl.pallas_call(functools.partial(route_kernel, experts=placement.shape[0]...  1.26 us
  transfers between devices with their start and end apart: 22, of which 10 were waited for; matrix products, arithmetic and copies ran while one was open for 1% of the time, Pallas kernels for 31%

profile of v14, /device:TPU:0, one launch (start us, length us, event | category | flops | bytes accessed | tf_op | source)
XLA Modules:
  0.0 50.3 jit_solution(1549218766196996512)
XLA Ops:
  0.6 4.1 %collective-permute-start.1 = (bf16[16,3584]{1,0:T(8,128)(2,1)}, bf16[16,3584]{1,0:T(8,128)(2,1)S(1)}, u32[]{:S(2)}, u32[]{:S(2)}) collective-permute-start(bf16[16,3584]{1,0:T(8,128)(2,1)} %rows_ref.1), channel_id=1, source_target_pairs={{0,8},{1,9},{2,10},{3,11},{4,12},{5,13},{6,14},{7,15},{8,0},{9,1},... | collective-permute-start | bytes 344072 | tf_op jit(solution)/shard_map/ppermute | solution.py:195
  4.8 1.3 %route.1 = (bf16[16,3712]{1,0:T(8,128)(2,1)S(1)}, bf16[16,128]{1,0:T(8,128)(2,1)S(1)}) custom-call(s32[2,14]{1,0:T(2,128)} %bitcast.22, bf16[16,3584]{1,0:T(8,128)(2,1)} %rows_ref.1, f32[8,16]{1,0:T(8,128)} %bitcast.20, s32[8,16]{1,0:T(8,128)} %bitcast.21), custom_call_target="tpu_custom_call" | custom-call | flops 17179869184 | bytes 33554432 | tf_op jit(solution)/shard_map/route/pallas_call | solution.py:119
  6.1 1.6 %collective-permute-start = (bf16[16,3712]{1,0:T(8,128)(2,1)S(1)}, bf16[16,3712]{1,0:T(8,128)(2,1)S(1)}, u32[]{:S(2)}, u32[]{:S(2)}) collective-permute-start(bf16[16,3712]{1,0:T(8,128)(2,1)S(1)} %get-tuple-element.60), channel_id=1, source_target_pairs={{0,4},{1,3},{2,6},{3,1},{4,0},{5,7},{6,2},{7,5},{8,12},{9,11},{10,... | collective-permute-start | bytes 356360 | tf_op jit(solution)/shard_map/ppermute | solution.py:195
  7.6 1.5 %collective-permute-start.6 = (bf16[16,3712]{1,0:T(8,128)(2,1)S(1)}, bf16[16,3712]{1,0:T(8,128)(2,1)S(1)}, u32[]{:S(2)}, u32[]{:S(2)}) collective-permute-start(bf16[16,3712]{1,0:T(8,128)(2,1)S(1)} %get-tuple-element.60), channel_id=1, source_target_pairs={{0,2},{1,5},{2,0},{3,7},{4,6},{5,1},{6,4},{7,3},{8,10},{9,13},{10,... | collective-permute-start | bytes 356360 | tf_op jit(solution)/shard_map/ppermute | solution.py:195
  9.5 2.8 %attention.4.refs_0_ = bf16[8,2,128,512]{3,2,1,0:T(8,128)(2,1)} custom-call(s32[8]{0:T(128)} %length_ref.3, bf16[8,2,576,128]{3,2,1,0:T(8,128)(2,1)S(1)} %bitcast.6, bf16[8,576,256]{2,1,0:T(8,128)(2,1)S(1)} %bitcast.10, bf16[8,2,576]{2,1,0:T(2,128)(2,1)S(1)} %copy-done.2), custom_call_target="tpu_custom_call" | custom-call | flops 1048576 | bytes 65536 | tf_op jit(solution)/shard_map/attention/pallas_call | solution.py:75
  12.4 1.3 %collective-permute-done.2 = bf16[16,128]{1,0:T(8,128)(2,1)S(1)} collective-permute-done((bf16[16,128]{1,0:T(8,128)(2,1)S(1)}, bf16[16,128]{1,0:T(8,128)(2,1)S(1)}, u32[]{:S(2)}, u32[]{:S(2)}) %collective-permute-start.2) | collective-permute-done | bytes 4128 | tf_op jit(solution)/shard_map/ppermute | solution.py:195
  15.3 1.5 %collective-permute-start.5 = (bf16[16,3712]{1,0:T(8,128)(2,1)S(1)}, bf16[16,3712]{1,0:T(8,128)(2,1)S(1)}, u32[]{:S(2)}, u32[]{:S(2)}) collective-permute-start(bf16[16,3712]{1,0:T(8,128)(2,1)S(1)} %pad_maximum_fusion), channel_id=1, source_target_pairs={{0,2},{1,5},{2,0},{3,7},{4,6},{5,1},{6,4},{7,3},{8,10},{9,13},{10,... | collective-permute-start | bytes 356360 | tf_op jit(solution)/shard_map/ppermute | solution.py:195
  17.0 3.2 %experts.2 = (f32[64,3584]{1,0:T(8,128)S(1)}, bf16[64,3584]{1,0:T(8,128)(2,1)S(1)}) custom-call(bf16[32,3712]{1,0:T(8,128)(2,1)S(1)} %constant_dynamic-update-slice_fusion.refs_0_, bf16[32,3712]{1,0:T(8,128)(2,1)S(1)} %constant_dynamic-update-slice_fusion.2.refs_1_, bf16[32,3712]{1,0:T(8,128)(2,1)S(1)} %collective-permute-done.7.refs_2_, ...), custom_call_target="tpu_custom_call" | custom-call | flops 1048576 | bytes 65536 | tf_op jit(solution)/shard_map/experts/pallas_call | solution.py:163
  22.4 2.7 %attention.5.refs_0_ = bf16[8,2,128,512]{3,2,1,0:T(8,128)(2,1)} custom-call(s32[8]{0:T(128)} %length_ref.3, bf16[8,2,576,128]{3,2,1,0:T(8,128)(2,1)S(1)} %bitcast.7, bf16[8,576,256]{2,1,0:T(8,128)(2,1)S(1)} %bitcast.11, bf16[8,2,576]{2,1,0:T(2,128)(2,1)S(1)} %copy-done.2, bf16[8,2,128,512]{3,2,1,0:T(8,128)(2,1)} %attention.4.refs_0_), custom_call_target="tpu_custom_call", output_to_operand_aliasing={{}: (4, {})} | custom-call | flops 1048576 | bytes 65536 | tf_op jit(solution)/shard_map/attention/pallas_call | solution.py:75
  25.1 0.8 %collective-permute-done.9.refs_2_ = bf16[16,3712]{1,0:T(8,128)(2,1)S(1)} collective-permute-done((bf16[16,3712]{1,0:T(8,128)(2,1)S(1)}, bf16[16,3712]{1,0:T(8,128)(2,1)S(1)}, u32[]{:S(2)}, u32[]{:S(2)}) %collective-permute-start.9) | collective-permute-done | bytes 118816 | tf_op jit(solution)/shard_map/ppermute | solution.py:195
  26.1 1.3 %collective-permute-done.13.refs_5_ = bf16[16,3712]{1,0:T(8,128)(2,1)S(1)} collective-permute-done((bf16[16,3712]{1,0:T(8,128)(2,1)S(1)}, bf16[16,3712]{1,0:T(8,128)(2,1)S(1)}, u32[]{:S(2)}, u32[]{:S(2)}) %collective-permute-start.13) | collective-permute-done | bytes 118816 | tf_op jit(solution)/shard_map/ppermute | solution.py:199
  27.4 3.3 %experts.3 = (f32[48,3584]{1,0:T(8,128)S(1)}, f32[16,3584]{1,0:T(8,128)S(1)}, bf16[48,3584]{1,0:T(8,128)(2,1)S(1)}, bf16[16,3584]{1,0:T(8,128)(2,1)S(1)}) custom-call(bf16[32,3712]{1,0:T(8,128)(2,1)S(1)} %constant_dynamic-update-slice_fusion.4.refs_0_, bf16[16,3712]{1,0:T(8,128)(2,1)S(1)} %collective-permute-done.3.refs_1_, ...), custom_call_target="tpu_custom_call" | custom-call | flops 1048576 | bytes 65536 | tf_op jit(solution)/shard_map/experts/pallas_call | solution.py:163
  31.3 0.8 %collective-permute-done.16 = bf16[16,3584]{1,0:T(8,128)(2,1)S(1)} collective-permute-done((bf16[16,3584]{1,0:T(8,128)(2,1)S(1)}, bf16[16,3584]{1,0:T(8,128)(2,1)S(1)}, u32[]{:S(2)}, u32[]{:S(2)}) %collective-permute-start.16) | collective-permute-done | bytes 114720 | tf_op jit(solution)/shard_map/ppermute | solution.py:199
  32.1 0.7 %collective-permute-start.17 = (bf16[16,3584]{1,0:T(8,128)(2,1)S(1)}, bf16[16,3584]{1,0:T(8,128)(2,1)S(1)}, u32[]{:S(2)}, u32[]{:S(2)}) collective-permute-start(bf16[16,3584]{1,0:T(8,128)(2,1)S(1)} %add_convert_fusion.3), channel_id=1, source_target_pairs={{0,2},{1,5},{2,0},{3,7},{4,6},{5,1},{6,4},{7,3},{8,10},{9,13},{10,... | collective-permute-start | bytes 344072 | tf_op jit(solution)/shard_map/ppermute | solution.py:195
  32.9 1.4 %collective-permute-start.15 = (bf16[32,3584]{1,0:T(8,128)(2,1)S(1)}, bf16[32,3584]{1,0:T(8,128)(2,1)S(1)}, u32[]{:S(2)}, u32[]{:S(2)}) collective-permute-start(bf16[32,3584]{1,0:T(8,128)(2,1)S(1)} %slice.47), channel_id=1, source_target_pairs={{0,2},{1,5},{2,0},{3,7},{4,6},{5,1},{6,4},{7,3},{8,10},{9,13},{10,... | collective-permute-start | bytes 688136 | tf_op jit(solution)/shard_map/ppermute | solution.py:195
  34.4 2.2 %attention.6.refs_0_ = bf16[8,2,128,512]{3,2,1,0:T(8,128)(2,1)} custom-call(s32[8]{0:T(128)} %length_ref.3, bf16[8,2,576,128]{3,2,1,0:T(8,128)(2,1)S(1)} %bitcast.8, bf16[8,576,256]{2,1,0:T(8,128)(2,1)S(1)} %bitcast.12, bf16[8,2,576]{2,1,0:T(2,128)(2,1)S(1)} %copy-done.2, bf16[8,2,128,512]{3,2,1,0:T(8,128)(2,1)} %attention.5.refs_0_), custom_call_target="tpu_custom_call", output_to_operand_aliasing={{}: (4, {})} | custom-call | flops 1048576 | bytes 65536 | tf_op jit(solution)/shard_map/attention/pallas_call | solution.py:75
  37.0 1.2 %collective-permute-start.18 = (bf16[16,3584]{1,0:T(8,128)(2,1)S(1)}, bf16[16,3584]{1,0:T(8,128)(2,1)S(1)}, u32[]{:S(2)}, u32[]{:S(2)}) collective-permute-start(bf16[16,3584]{1,0:T(8,128)(2,1)S(1)} %fusion), channel_id=1, source_target_pairs={{0,4},{1,3},{2,6},{3,1},{4,0},{5,7},{6,2},{7,5},{8,12},{9,11},{10,... | collective-permute-start | bytes 344072 | tf_op jit(solution)/shard_map/ppermute | solution.py:195
  38.2 1.1 %collective-permute-start.20 = (bf16[16,3584]{1,0:T(8,128)(2,1)S(1)}, bf16[16,3584]{1,0:T(8,128)(2,1)S(1)}, u32[]{:S(2)}, u32[]{:S(2)}) collective-permute-start(bf16[16,3584]{1,0:T(8,128)(2,1)S(1)} %slice.48), channel_id=1, source_target_pairs={{0,2},{1,5},{2,0},{3,7},{4,6},{5,1},{6,4},{7,3},{8,10},{9,13},{10,... | collective-permute-start | bytes 344072 | tf_op jit(solution)/shard_map/ppermute | solution.py:195
  39.4 2.9 %collective-permute-done.18 = bf16[16,3584]{1,0:T(8,128)(2,1)S(1)} collective-permute-done((bf16[16,3584]{1,0:T(8,128)(2,1)S(1)}, bf16[16,3584]{1,0:T(8,128)(2,1)S(1)}, u32[]{:S(2)}, u32[]{:S(2)}) %collective-permute-start.18) | collective-permute-done | bytes 114720 | tf_op jit(solution)/shard_map/ppermute | solution.py:195
  42.3 1.9 %collective-permute-start.19 = (bf16[16,3584]{1,0:T(8,128)(2,1)S(1)}, bf16[16,3584]{1,0:T(8,128)(2,1)S(1)}, u32[]{:S(2)}, u32[]{:S(2)}) collective-permute-start(bf16[16,3584]{1,0:T(8,128)(2,1)S(1)} %add_convert_fusion.2), channel_id=1, source_target_pairs={{0,8},{1,9},{2,10},{3,11},{4,12},{5,13},{6,14},{7,15},{8,0},{9,1},... | collective-permute-start | bytes 344072 | tf_op jit(solution)/shard_map/ppermute | solution.py:195
  44.3 0.9 %collective-permute-start.21 = (bf16[16,3584]{1,0:T(8,128)(2,1)S(1)}, bf16[16,3584]{1,0:T(8,128)(2,1)S(1)}, u32[]{:S(2)}, u32[]{:S(2)}) collective-permute-start(bf16[16,3584]{1,0:T(8,128)(2,1)S(1)} %add_convert_fusion.1), channel_id=1, source_target_pairs={{0,4},{1,3},{2,6},{3,1},{4,0},{5,7},{6,2},{7,5},{8,12},{9,11},{10,... | collective-permute-start | bytes 344072 | tf_op jit(solution)/shard_map/ppermute | solution.py:195
  45.2 3.4 %attention.7 = bf16[8,2,128,512]{3,2,1,0:T(8,128)(2,1)} custom-call(s32[8]{0:T(128)} %length_ref.3, bf16[8,2,576,128]{3,2,1,0:T(8,128)(2,1)S(1)} %bitcast.9, bf16[8,576,256]{2,1,0:T(8,128)(2,1)S(1)} %bitcast.13, bf16[8,2,576]{2,1,0:T(2,128)(2,1)S(1)} %copy-done.2, bf16[8,2,128,512]{3,2,1,0:T(8,128)(2,1)} %attention.6.refs_0_), custom_call_target="tpu_custom_call", output_to_operand_aliasing={{}: (4, {})} | custom-call | flops 1048576 | bytes 65536 | tf_op jit(solution)/shard_map/attention/pallas_call | solution.py:75
  48.6 0.8 %collective-permute-done.19 = bf16[16,3584]{1,0:T(8,128)(2,1)S(1)} collective-permute-done((bf16[16,3584]{1,0:T(8,128)(2,1)S(1)}, bf16[16,3584]{1,0:T(8,128)(2,1)S(1)}, u32[]{:S(2)}, u32[]{:S(2)}) %collective-permute-start.19) | collective-permute-done | bytes 114720 | tf_op jit(solution)/shard_map/ppermute | solution.py:195
  49.6 0.7 %add_convert_fusion = bf16[16,3584]{1,0:T(8,128)(2,1)} fusion(bf16[16,3584]{1,0:T(8,128)(2,1)S(1)} %collective-permute-done.19, bf16[16,3584]{1,0:T(8,128)(2,1)S(1)} %collective-permute-done.21, bf16[16,3584]{1,0:T(8,128)(2,1)S(1)} %collective-permute-done.20, f32[64,3584]{1,0:T(8,128)S(1)} %convert_add_fusion), kind=kLoop, calls=%fused_computation.6 | loop fusion | flops 401408 | bytes 688128 | tf_op jit(solution)/shard_map/convert_element_type | solution.py:300
  (64 shorter events, 5.8 us)
Async XLA Ops:
  0.6 13.0 %collective-permute-start.1 = (bf16[16,3584]{1,0:T(8,128)(2,1)}, bf16[16,3584]{1,0:T(8,128)(2,1)S(1)}, u32[]{:S(2)}, u32[]{:S(2)}) collective-permute-start(bf16[16,3584]{1,0:T(8,128)(2,1)} %rows_ref.1), channel_id=1, source_target_pairs={{0,8},{1,9},{2,10},{3,11},{4,12},{5,13},{6,14},{7,15},{8,0},{9,1},... | collective-permute-start | bytes 344072 | tf_op jit(solution)/shard_map/ppermute | solution.py:195
  4.7 12.1 %slice-start.2 = ((s8[7340032]{0:T(1024)(128)(4,1)}), s8[4194304]{0:T(1024)(128)(4,1)S(1)}, s32[]{:S(2)}) async-start(s8[7340032]{0:T(1024)(128)(4,1)} %bitcast.16), calls=%async_computation.2 | async-start | bytes 8388608
  4.7 12.2 %slice-start.4 = ((s8[7340032]{0:T(1024)(128)(4,1)}), s8[4194304]{0:T(1024)(128)(4,1)S(1)}, s32[]{:S(2)}) async-start(s8[7340032]{0:T(1024)(128)(4,1)} %bitcast.18), calls=%async_computation.4 | async-start | bytes 8388608
  6.1 7.6 %collective-permute-start = (bf16[16,3712]{1,0:T(8,128)(2,1)S(1)}, bf16[16,3712]{1,0:T(8,128)(2,1)S(1)}, u32[]{:S(2)}, u32[]{:S(2)}) collective-permute-start(bf16[16,3712]{1,0:T(8,128)(2,1)S(1)} %get-tuple-element.60), channel_id=1, source_target_pairs={{0,4},{1,3},{2,6},{3,1},{4,0},{5,7},{6,2},{7,5},{8,12},{9,11},{10,... | collective-permute-start | bytes 356360 | tf_op jit(solution)/shard_map/ppermute | solution.py:195
  7.6 6.2 %collective-permute-start.6 = (bf16[16,3712]{1,0:T(8,128)(2,1)S(1)}, bf16[16,3712]{1,0:T(8,128)(2,1)S(1)}, u32[]{:S(2)}, u32[]{:S(2)}) collective-permute-start(bf16[16,3712]{1,0:T(8,128)(2,1)S(1)} %get-tuple-element.60), channel_id=1, source_target_pairs={{0,2},{1,5},{2,0},{3,7},{4,6},{5,1},{6,4},{7,3},{8,10},{9,13},{10,... | collective-permute-start | bytes 356360 | tf_op jit(solution)/shard_map/ppermute | solution.py:195
  9.2 4.5 %collective-permute-start.2 = (bf16[16,128]{1,0:T(8,128)(2,1)S(1)}, bf16[16,128]{1,0:T(8,128)(2,1)S(1)}, u32[]{:S(2)}, u32[]{:S(2)}) collective-permute-start(bf16[16,128]{1,0:T(8,128)(2,1)S(1)} %get-tuple-element.61), channel_id=1, source_target_pairs={{0,8},{1,9},{2,10},{3,11},{4,12},{5,13},{6,14},{7,15},{8,0},{9,1},... | collective-permute-start | bytes 12296 | tf_op jit(solution)/shard_map/ppermute | solution.py:195
  13.7 3.1 %collective-permute-start.7 = (bf16[32,3712]{1,0:T(8,128)(2,1)S(1)}, bf16[32,3712]{1,0:T(8,128)(2,1)S(1)}, u32[]{:S(2)}, u32[]{:S(2)}) collective-permute-start(bf16[32,3712]{1,0:T(8,128)(2,1)S(1)} %constant_dynamic-update-slice_fusion.refs_0_), channel_id=1, source_target_pairs={{0,1},{1,0},{2,3},{3,2},{4,5},{5,4},{6,7},{7,6},{8,9},{9,8},{10,11... | collective-permute-start | bytes 712712 | tf_op jit(solution)/shard_map/ppermute | solution.py:199
  13.8 3.0 %collective-permute-start.8 = (bf16[32,3712]{1,0:T(8,128)(2,1)S(1)}, bf16[32,3712]{1,0:T(8,128)(2,1)S(1)}, u32[]{:S(2)}, u32[]{:S(2)}) collective-permute-start(bf16[32,3712]{1,0:T(8,128)(2,1)S(1)} %constant_dynamic-update-slice_fusion.2.refs_1_), channel_id=1, source_target_pairs={{0,1},{1,0},{2,3},{3,2},{4,5},{5,4},{6,7},{7,6},{8,9},{9,8},{10,11... | collective-permute-start | bytes 712712 | tf_op jit(solution)/shard_map/ppermute | solution.py:199
  14.4 5.8 %collective-permute-start.3 = (bf16[16,3712]{1,0:T(8,128)(2,1)S(1)}, bf16[16,3712]{1,0:T(8,128)(2,1)S(1)}, u32[]{:S(2)}, u32[]{:S(2)}) collective-permute-start(bf16[16,3712]{1,0:T(8,128)(2,1)S(1)} %collective-permute-done), channel_id=1, source_target_pairs={{0,2},{1,5},{2,0},{3,7},{4,6},{5,1},{6,4},{7,3},{8,10},{9,13},{10,... | collective-permute-start | bytes 356360 | tf_op jit(solution)/shard_map/ppermute | solution.py:195
  14.9 6.0 %collective-permute-start.4 = (bf16[16,3712]{1,0:T(8,128)(2,1)S(1)}, bf16[16,3712]{1,0:T(8,128)(2,1)S(1)}, u32[]{:S(2)}, u32[]{:S(2)}) collective-permute-start(bf16[16,3712]{1,0:T(8,128)(2,1)S(1)} %pad_maximum_fusion), channel_id=1, source_target_pairs={{0,4},{1,3},{2,6},{3,1},{4,0},{5,7},{6,2},{7,5},{8,12},{9,11},{10,... | collective-permute-start | bytes 356360 | tf_op jit(solution)/shard_map/ppermute | solution.py:195
  15.3 5.7 %collective-permute-start.5 = (bf16[16,3712]{1,0:T(8,128)(2,1)S(1)}, bf16[16,3712]{1,0:T(8,128)(2,1)S(1)}, u32[]{:S(2)}, u32[]{:S(2)}) collective-permute-start(bf16[16,3712]{1,0:T(8,128)(2,1)S(1)} %pad_maximum_fusion), channel_id=1, source_target_pairs={{0,2},{1,5},{2,0},{3,7},{4,6},{5,1},{6,4},{7,3},{8,10},{9,13},{10,... | collective-permute-start | bytes 356360 | tf_op jit(solution)/shard_map/ppermute | solution.py:195
  21.1 4.8 %collective-permute-start.9 = (bf16[16,3712]{1,0:T(8,128)(2,1)S(1)}, bf16[16,3712]{1,0:T(8,128)(2,1)S(1)}, u32[]{:S(2)}, u32[]{:S(2)}) collective-permute-start(bf16[16,3712]{1,0:T(8,128)(2,1)S(1)} %collective-permute-done.4), channel_id=1, source_target_pairs={{0,2},{1,5},{2,0},{3,7},{4,6},{5,1},{6,4},{7,3},{8,10},{9,13},{10,... | collective-permute-start | bytes 356360 | tf_op jit(solution)/shard_map/ppermute | solution.py:195
  21.7 4.2 %collective-permute-start.12 = (bf16[64,3584]{1,0:T(8,128)(2,1)S(1)}, bf16[64,3584]{1,0:T(8,128)(2,1)S(1)}, u32[]{:S(2)}, u32[]{:S(2)}) collective-permute-start(bf16[64,3584]{1,0:T(8,128)(2,1)S(1)} %get-tuple-element.84), channel_id=1, source_target_pairs={{0,1},{1,0},{2,3},{3,2},{4,5},{5,4},{6,7},{7,6},{8,9},{9,8},{10,11... | collective-permute-start | bytes 1376264 | tf_op jit(solution)/shard_map/ppermute | solution.py:199
  21.7 4.3 %collective-permute-start.10 = (bf16[32,3712]{1,0:T(8,128)(2,1)S(1)}, bf16[32,3712]{1,0:T(8,128)(2,1)S(1)}, u32[]{:S(2)}, u32[]{:S(2)}) collective-permute-start(bf16[32,3712]{1,0:T(8,128)(2,1)S(1)} %constant_dynamic-update-slice_fusion.4.refs_0_), channel_id=1, source_target_pairs={{0,1},{1,0},{2,3},{3,2},{4,5},{5,4},{6,7},{7,6},{8,9},{9,8},{10,11... | collective-permute-start | bytes 712712 | tf_op jit(solution)/shard_map/ppermute | solution.py:199
  22.3 3.7 %collective-permute-start.11 = (bf16[16,3712]{1,0:T(8,128)(2,1)S(1)}, bf16[16,3712]{1,0:T(8,128)(2,1)S(1)}, u32[]{:S(2)}, u32[]{:S(2)}) collective-permute-start(bf16[16,3712]{1,0:T(8,128)(2,1)S(1)} %collective-permute-done.3.refs_1_), channel_id=1, source_target_pairs={{0,1},{1,0},{2,3},{3,2},{4,5},{5,4},{6,7},{7,6},{8,9},{9,8},{10,11... | collective-permute-start | bytes 356360 | tf_op jit(solution)/shard_map/ppermute | solution.py:199
  26.0 1.4 %collective-permute-start.13 = (bf16[16,3712]{1,0:T(8,128)(2,1)S(1)}, bf16[16,3712]{1,0:T(8,128)(2,1)S(1)}, u32[]{:S(2)}, u32[]{:S(2)}) collective-permute-start(bf16[16,3712]{1,0:T(8,128)(2,1)S(1)} %collective-permute-done.9.refs_2_), channel_id=1, source_target_pairs={{0,1},{1,0},{2,3},{3,2},{4,5},{5,4},{6,7},{7,6},{8,9},{9,8},{10,11... | collective-permute-start | bytes 356360 | tf_op jit(solution)/shard_map/ppermute | solution.py:199
  30.7 1.4 %collective-permute-start.16 = (bf16[16,3584]{1,0:T(8,128)(2,1)S(1)}, bf16[16,3584]{1,0:T(8,128)(2,1)S(1)}, u32[]{:S(2)}, u32[]{:S(2)}) collective-permute-start(bf16[16,3584]{1,0:T(8,128)(2,1)S(1)} %get-tuple-element.92), channel_id=1, source_target_pairs={{0,1},{1,0},{2,3},{3,2},{4,5},{5,4},{6,7},{7,6},{8,9},{9,8},{10,11... | collective-permute-start | bytes 344072 | tf_op jit(solution)/shard_map/ppermute | solution.py:199
  30.9 1.9 %collective-permute-start.14 = (bf16[48,3584]{1,0:T(8,128)(2,1)S(1)}, bf16[48,3584]{1,0:T(8,128)(2,1)S(1)}, u32[]{:S(2)}, u32[]{:S(2)}) collective-permute-start(bf16[48,3584]{1,0:T(8,128)(2,1)S(1)} %get-tuple-element.90), channel_id=1, source_target_pairs={{0,1},{1,0},{2,3},{3,2},{4,5},{5,4},{6,7},{7,6},{8,9},{9,8},{10,11... | collective-permute-start | bytes 1032200 | tf_op jit(solution)/shard_map/ppermute | solution.py:199
  32.1 4.9 %collective-permute-start.17 = (bf16[16,3584]{1,0:T(8,128)(2,1)S(1)}, bf16[16,3584]{1,0:T(8,128)(2,1)S(1)}, u32[]{:S(2)}, u32[]{:S(2)}) collective-permute-start(bf16[16,3584]{1,0:T(8,128)(2,1)S(1)} %add_convert_fusion.3), channel_id=1, source_target_pairs={{0,2},{1,5},{2,0},{3,7},{4,6},{5,1},{6,4},{7,3},{8,10},{9,13},{10,... | collective-permute-start | bytes 344072 | tf_op jit(solution)/shard_map/ppermute | solution.py:195
  32.9 9.3 %collective-permute-start.15 = (bf16[32,3584]{1,0:T(8,128)(2,1)S(1)}, bf16[32,3584]{1,0:T(8,128)(2,1)S(1)}, u32[]{:S(2)}, u32[]{:S(2)}) collective-permute-start(bf16[32,3584]{1,0:T(8,128)(2,1)S(1)} %slice.47), channel_id=1, source_target_pairs={{0,2},{1,5},{2,0},{3,7},{4,6},{5,1},{6,4},{7,3},{8,10},{9,13},{10,... | collective-permute-start | bytes 688136 | tf_op jit(solution)/shard_map/ppermute | solution.py:195
  37.0 5.3 %collective-permute-start.18 = (bf16[16,3584]{1,0:T(8,128)(2,1)S(1)}, bf16[16,3584]{1,0:T(8,128)(2,1)S(1)}, u32[]{:S(2)}, u32[]{:S(2)}) collective-permute-start(bf16[16,3584]{1,0:T(8,128)(2,1)S(1)} %fusion), channel_id=1, source_target_pairs={{0,4},{1,3},{2,6},{3,1},{4,0},{5,7},{6,2},{7,5},{8,12},{9,11},{10,... | collective-permute-start | bytes 344072 | tf_op jit(solution)/shard_map/ppermute | solution.py:195
  38.2 11.2 %collective-permute-start.20 = (bf16[16,3584]{1,0:T(8,128)(2,1)S(1)}, bf16[16,3584]{1,0:T(8,128)(2,1)S(1)}, u32[]{:S(2)}, u32[]{:S(2)}) collective-permute-start(bf16[16,3584]{1,0:T(8,128)(2,1)S(1)} %slice.48), channel_id=1, source_target_pairs={{0,2},{1,5},{2,0},{3,7},{4,6},{5,1},{6,4},{7,3},{8,10},{9,13},{10,... | collective-permute-start | bytes 344072 | tf_op jit(solution)/shard_map/ppermute | solution.py:195
  42.3 7.1 %collective-permute-start.19 = (bf16[16,3584]{1,0:T(8,128)(2,1)S(1)}, bf16[16,3584]{1,0:T(8,128)(2,1)S(1)}, u32[]{:S(2)}, u32[]{:S(2)}) collective-permute-start(bf16[16,3584]{1,0:T(8,128)(2,1)S(1)} %add_convert_fusion.2), channel_id=1, source_target_pairs={{0,8},{1,9},{2,10},{3,11},{4,12},{5,13},{6,14},{7,15},{8,0},{9,1},... | collective-permute-start | bytes 344072 | tf_op jit(solution)/shard_map/ppermute | solution.py:195
  44.3 5.4 %collective-permute-start.21 = (bf16[16,3584]{1,0:T(8,128)(2,1)S(1)}, bf16[16,3584]{1,0:T(8,128)(2,1)S(1)}, u32[]{:S(2)}, u32[]{:S(2)}) collective-permute-start(bf16[16,3584]{1,0:T(8,128)(2,1)S(1)} %add_convert_fusion.1), channel_id=1, source_target_pairs={{0,4},{1,3},{2,6},{3,1},{4,0},{5,7},{6,2},{7,5},{8,12},{9,11},{10,... | collective-permute-start | bytes 344072 | tf_op jit(solution)/shard_map/ppermute | solution.py:195
  (7 other events, 62.9 us)
